TPU v7x, 1024 devices: a whole 4x8x16 slice. The times are simulated.
1024 devices in a mesh: dom: 64 (over z, y_lo, core), rows: 16 (over x, y_hi).
Axes of the slice: x: 4, y: 8 (y_hi: 4, y_lo: 2; y = y_hi * 2 + y_lo), z: 16, core: 2. Of those that a mesh axis runs over, the one named last changes fastest.
Arguments:
- features: bfloat16 [524288, 256], P(('dom', 'rows')), may hold values from -6 to 6
- weight: bfloat16 [256, 256], replicated, may hold values from -0.375 to 0.375
- tile_values: bfloat16 [1024, 5, 4, 128, 128], P(('dom', 'rows')), may hold values from -0.1875 to 0.1875
- tile_source: int32 [1024, 5, 4], P(('dom', 'rows')), may hold values from 0 to 3
- tile_slot: int32 [1024, 5, 4], P(('dom', 'rows')), may hold values from 0 to 31
- slot_block: int32 [1024, 32], P(('dom', 'rows')), may hold values from 0 to 3
- tile_count: int32 [1024, 5], P(('dom', 'rows')), may hold values from 1 to 4
- cotangent: bfloat16 [524288, 256], P(('dom', 'rows')), may hold values from -6 to 6
Outputs:
- activations: bfloat16 [524288, 256], P(('dom', 'rows'))
- feature_grad: bfloat16 [524288, 256], P(('dom', 'rows'))
- weight_grad: float32 [256, 256], replicated
Inputs may be any that keep to these rules, and one draw needn't show every extreme that they name: Tiles of index tile_count[g, k] and above at offset index k are padding; their tile_values, tile_source and tile_slot count for nothing.
All inputs are finite; a program needn't handle non-finite values.
Results may differ from a plain program's by a relative error of at most 0.019.
Values may be sent and summed in bfloat16 or wider, within the bound.
No kernel may reach another device: no remote copies, remote signals or barrier semaphores. Data moves between devices by JAX's collectives and lax.ppermute only.
A program may use at most 32 MiB of HBM per device.

v0:
```python
import jax
import jax.numpy as jnp
from jax import lax
from jax.sharding import PartitionSpec as P

BLOCK = 128
HALF = 2
CAP = 2


def shifted(value, axis, steps):
    count = lax.axis_size(axis)
    pairs = [(source, (source + steps) % count) for source in range(count)]
    return lax.ppermute(value, axis, pairs)


def pass_features(visiting, offset_by):
    return shifted(visiting, "dom", offset_by)


def pass_sums(carried, offset_by):
    return shifted(carried, "dom", offset_by)


def per_device(
    features, weight, tile_values, tile_source, tile_slot, slot_block, tile_count, cotangent
):
    channels = features.shape[1]
    blocks_dev = features.shape[0] // BLOCK
    row_count = lax.axis_size("rows")
    values = tile_values[0]
    sources = tile_source[0]
    slot_ids = tile_slot[0]
    targets = slot_block[0]
    counts = tile_count[0]
    num_steps = values.shape[0]
    tiles_step = values.shape[1]
    slot_total = targets.shape[0]
    reach = HALF
    live_mask = jnp.arange(tiles_step, dtype=jnp.int32)[None, :] < counts[:, None]
    slot_onehot = (
        (slot_ids[..., None] == jnp.arange(slot_total, dtype=jnp.int32)) & live_mask[..., None]
    ).astype(jnp.float32)
    source_onehot = (
        (sources[..., None] == jnp.arange(blocks_dev, dtype=jnp.int32)) & live_mask[..., None]
    ).astype(jnp.float32)
    own_blocks = features.reshape(blocks_dev, BLOCK, channels)
    products = [None] * num_steps
    visiting = pass_features(own_blocks, reach)
    for step_idx in range(num_steps):
        if step_idx > 0:
            visiting = pass_features(visiting, -1)
        tile_picked = jnp.take(visiting, sources[step_idx], axis=0)
        products[step_idx] = jnp.einsum(
            "tij,tjf->tif", values[step_idx], tile_picked, preferred_element_type=jnp.float32
        )
    stacked = jnp.concatenate(products, axis=0)
    slot_sums = jnp.einsum("ts,tif->sif", slot_onehot.reshape(-1, slot_total), stacked)
    partials = slot_sums.astype(jnp.bfloat16).reshape(row_count, CAP, BLOCK, channels)
    ids_wire = targets.reshape(row_count, CAP).astype(jnp.bfloat16)
    received, received_ids = (
        lax.all_to_all(partials, "rows", split_axis=0, concat_axis=0, tiled=True),
        lax.all_to_all(ids_wire, "rows", split_axis=0, concat_axis=0, tiled=True),
    )
    block_codes = jnp.arange(blocks_dev, dtype=jnp.int32).astype(jnp.bfloat16)
    owner_onehot = (received_ids[..., None] == block_codes).astype(jnp.bfloat16)
    aggregate = jnp.einsum(
        "rcb,rcif->bif", owner_onehot, received, preferred_element_type=jnp.float32
    )
    aggregate = aggregate.astype(jnp.bfloat16).reshape(blocks_dev * BLOCK, channels)
    pre_act = jnp.dot(aggregate, weight, preferred_element_type=jnp.float32)
    activations = jax.nn.silu(pre_act).astype(jnp.bfloat16)
    sigmoid_pre = jax.nn.sigmoid(pre_act)
    slope_factor = sigmoid_pre * (1.0 + pre_act * (1.0 - sigmoid_pre))
    pre_grad = (cotangent.astype(jnp.float32) * slope_factor).astype(jnp.bfloat16)
    local_grad = lax.dot_general(
        aggregate, pre_grad, (((0,), (0,)), ((), ())), preferred_element_type=jnp.float32
    )
    weight_grad = lax.psum(local_grad, ("dom", "rows"))
    agg_grad = lax.dot_general(
        pre_grad, weight, (((1,), (1,)), ((), ())), preferred_element_type=jnp.float32
    )
    agg_grad = agg_grad.astype(jnp.bfloat16).reshape(blocks_dev, BLOCK, channels)
    reply_blocks = jnp.take(agg_grad, received_ids.astype(jnp.int32), axis=0)
    returned = lax.all_to_all(
        reply_blocks, "rows", split_axis=0, concat_axis=0, tiled=True
    ).reshape(slot_total, BLOCK, channels)

    def source_terms(step_idx):
        picked = jnp.take(returned, slot_ids[step_idx], axis=0)
        product = jnp.einsum(
            "tji,tjf->tif", values[step_idx], picked, preferred_element_type=jnp.float32
        )
        return jnp.einsum("tb,tif->bif", source_onehot[step_idx], product)

    carried = source_terms(num_steps - 1)
    for step_idx in range(num_steps - 2, -1, -1):
        carried = pass_sums(carried, 1) + source_terms(step_idx)
    source_grad = pass_sums(carried, -reach)
    feature_grad = source_grad.astype(jnp.bfloat16).reshape(blocks_dev * BLOCK, channels)
    return (activations, feature_grad, weight_grad)


def solution(mesh):
    return jax.shard_map(
        per_device,
        mesh=mesh,
        in_specs=(
            P(("dom", "rows"), None),
            P(),
            P(("dom", "rows"), None, None, None, None),
            P(("dom", "rows"), None, None),
            P(("dom", "rows"), None, None),
            P(("dom", "rows"), None),
            P(("dom", "rows"), None),
            P(("dom", "rows"), None),
        ),
        out_specs=(P(("dom", "rows"), None), P(("dom", "rows"), None), P()),
        check_vma=False,
    )
```

profile of v0, /device:TPU:1, one launch (start us, length us, event | category | flops | bytes accessed | tf_op | source)
XLA Modules:
  0.0 749.3 jit_solution(16741442685429104850)
XLA Ops:
  8.6 10.2 %all-to-all-start = ((bf16[16,1,2]{2,1,0:T(2,128)(2,1)}), bf16[16,1,2]{2,1,0:T(2,128)(2,1)S(1)}, u32[]{:S(2)}, u32[]{:S(2)}) async-start(bf16[16,1,2]{2,1,0:T(2,128)(2,1)} %convert_element_type.75), calls=%async_computation | async-start | bytes 16384 | tf_op jit(solution)/shard_map/all_to_all | solution.py:63
  18.9 2.3 collective-permute-start
  22.5 20.4 %collective-permute-done = bf16[4,128,256]{2,1,0:T(8,128)(2,1)S(1)} collective-permute-done((bf16[4,128,256]{2,1,0:T(8,128)(2,1)}, bf16[4,128,256]{2,1,0:T(8,128)(2,1)S(1)}, u32[]{:S(2)}, u32[]{:S(2)}) %collective-permute-start) | collective-permute-done | bytes 262176 | tf_op jit(solution)/shard_map/ppermute | solution.py:14
  42.8 3.4 collective-permute-start.1
  47.0 3.5 collective-permute-done.1
  54.0 4.2 collective-permute-done.2
  58.2 3.8 collective-permute-start.3
  65.9 5.9 collective-permute-start.4
  78.5 2.2 reshape.145
  80.8 4.8 copy.100
  85.6 8.7 %all-to-all-start.1 = ((bf16[16,2,128,256]{3,1,2,0:T(2,128)(2,1)}), bf16[16,2,128,256]{3,1,2,0:T(2,128)(2,1)S(1)}, u32[]{:S(2)}, u32[]{:S(2)}) async-start(bf16[16,2,128,256]{3,1,2,0:T(2,128)(2,1)} %copy.100), calls=%async_computation.1 | async-start | bytes 4194304 | tf_op jit(solution)/shard_map/all_to_all | solution.py:62
  94.7 50.1 %all-to-all-done.1 = bf16[16,2,128,256]{3,1,2,0:T(2,128)(2,1)S(1)} async-done(((bf16[16,2,128,256]{3,1,2,0:T(2,128)(2,1)}), bf16[16,2,128,256]{3,1,2,0:T(2,128)(2,1)S(1)}, u32[]{:S(2)}, u32[]{:S(2)}) %all-to-all-start.1) | async-done | bytes 2097184 | tf_op jit(solution)/shard_map/all_to_all | solution.py:62
  151.3 5.9 all-to-all-start.2
  157.7 47.1 %all-to-all-done.2 = bf16[16,2,128,256]{3,2,1,0:T(8,128)(2,1)S(1)} async-done(((bf16[16,2,128,256]{3,2,1,0:T(8,128)(2,1)}), bf16[16,2,128,256]{3,2,1,0:T(8,128)(2,1)S(1)}, u32[]{:S(2)}, u32[]{:S(2)}) %all-to-all-start.2) | async-done | bytes 2097184 | tf_op jit(solution)/shard_map/all_to_all | solution.py:85
  213.5 3.6 collective-permute-done.5
  219.3 4.4 collective-permute-start.6
  226.8 3.3 collective-permute-done.6
  232.2 4.3 collective-permute-start.7
  239.6 5.5 collective-permute-done.7
  247.1 2.3 collective-permute-start.8
  252.5 7.6 %collective-permute-done.8 = f32[4,128,256]{2,0,1:T(4,128)} collective-permute-done((f32[4,128,256]{2,0,1:T(4,128)}, f32[4,128,256]{2,0,1:T(4,128)}, u32[]{:S(2)}, u32[]{:S(2)}) %collective-permute-start.8) | collective-permute-done | bytes 524320 | tf_op jit(solution)/shard_map/ppermute | solution.py:14
  261.3 10.1 %collective-permute-start.9 = (bf16[4,128,256]{2,0,1:T(4,128)(2,1)S(1)}, bf16[4,128,256]{2,0,1:T(4,128)(2,1)S(1)}, u32[]{:S(2)}, u32[]{:S(2)}) collective-permute-start(bf16[4,128,256]{2,0,1:T(4,128)(2,1)S(1)} %add.58), channel_id=1, source_target_pairs={{0,992},{16,1008},{32,0},{48,16},{64,32},{80,48},{96,64},{112,80},... | collective-permute-start | bytes 786440 | tf_op jit(solution)/shard_map/ppermute | solution.py:14
  272.4 3.6 collective-permute-done.9
  276.7 464.0 %all-reduce.2.cloned.1.call-done = f32[256,256]{1,0:T(8,128)} async-done(((f32[256,256]{1,0:T(8,128)}), f32[256,256]{1,0:T(8,128)}) %all-reduce.2.cloned.1.call-update) | async-done | bytes 262160 | tf_op jit(solution)/shard_map/psum | solution.py:79
  (107 shorter events, 53.3 us)
Async XLA Ops:
  7.2 139.0 %copy-start = (bf16[256,256]{1,0:T(8,128)(2,1)S(1)}, bf16[256,256]{1,0:T(8,128)(2,1)}, u32[]{:S(2)}) copy-start(bf16[256,256]{1,0:T(8,128)(2,1)} %param.13) | copy-start | bytes 393220
  7.2 56.6 %copy-start.1 = (bf16[1,5,4,128,128]{4,3,2,1,0:T(8,128)(2,1)S(1)}, bf16[1,5,4,128,128]{4,3,2,1,0:T(8,128)(2,1)}, u32[]{:S(2)}) copy-start(bf16[1,5,4,128,128]{4,3,2,1,0:T(8,128)(2,1)} %param.14) | copy-start | bytes 1966084
  8.6 76.9 %all-to-all-start = ((bf16[16,1,2]{2,1,0:T(2,128)(2,1)}), bf16[16,1,2]{2,1,0:T(2,128)(2,1)S(1)}, u32[]{:S(2)}, u32[]{:S(2)}) async-start(bf16[16,1,2]{2,1,0:T(2,128)(2,1)} %convert_element_type.75), calls=%async_computation | async-start | bytes 16384 | tf_op jit(solution)/shard_map/all_to_all | solution.py:63
  18.9 24.0 %collective-permute-start = (bf16[4,128,256]{2,1,0:T(8,128)(2,1)}, bf16[4,128,256]{2,1,0:T(8,128)(2,1)S(1)}, u32[]{:S(2)}, u32[]{:S(2)}) collective-permute-start(bf16[4,128,256]{2,1,0:T(8,128)(2,1)} %bitcast.132), channel_id=1, source_target_pairs={{0,32},{16,48},{32,64},{48,80},{64,96},{80,112},{96,128},{112,144}... | collective-permute-start | bytes 786440 | tf_op jit(solution)/shard_map/ppermute | solution.py:14
  42.8 7.7 %collective-permute-start.1 = (bf16[4,128,256]{2,1,0:T(8,128)(2,1)S(1)}, bf16[4,128,256]{2,1,0:T(8,128)(2,1)S(1)}, u32[]{:S(2)}, u32[]{:S(2)}) collective-permute-start(bf16[4,128,256]{2,1,0:T(8,128)(2,1)S(1)} %collective-permute-done), channel_id=1, source_target_pairs={{0,1008},{16,0},{32,16},{48,32},{64,48},{80,64},{96,80},{112,96},{... | collective-permute-start | bytes 786440 | tf_op jit(solution)/shard_map/ppermute | solution.py:14
  50.5 7.7 %collective-permute-start.2 = (bf16[4,128,256]{2,1,0:T(8,128)(2,1)S(1)}, bf16[4,128,256]{2,1,0:T(8,128)(2,1)S(1)}, u32[]{:S(2)}, u32[]{:S(2)}) collective-permute-start(bf16[4,128,256]{2,1,0:T(8,128)(2,1)S(1)} %collective-permute-done.1), channel_id=1, source_target_pairs={{0,1008},{16,0},{32,16},{48,32},{64,48},{80,64},{96,80},{112,96},{... | collective-permute-start | bytes 786440 | tf_op jit(solution)/shard_map/ppermute | solution.py:14
  58.2 7.7 %collective-permute-start.3 = (bf16[4,128,256]{2,1,0:T(8,128)(2,1)S(1)}, bf16[4,128,256]{2,1,0:T(8,128)(2,1)S(1)}, u32[]{:S(2)}, u32[]{:S(2)}) collective-permute-start(bf16[4,128,256]{2,1,0:T(8,128)(2,1)S(1)} %collective-permute-done.2), channel_id=1, source_target_pairs={{0,1008},{16,0},{32,16},{48,32},{64,48},{80,64},{96,80},{112,96},{... | collective-permute-start | bytes 786440 | tf_op jit(solution)/shard_map/ppermute | solution.py:14
  65.9 7.7 %collective-permute-start.4 = (bf16[4,128,256]{2,1,0:T(8,128)(2,1)S(1)}, bf16[4,128,256]{2,1,0:T(8,128)(2,1)S(1)}, u32[]{:S(2)}, u32[]{:S(2)}) collective-permute-start(bf16[4,128,256]{2,1,0:T(8,128)(2,1)S(1)} %collective-permute-done.3), channel_id=1, source_target_pairs={{0,1008},{16,0},{32,16},{48,32},{64,48},{80,64},{96,80},{112,96},{... | collective-permute-start | bytes 786440 | tf_op jit(solution)/shard_map/ppermute | solution.py:14
  85.6 59.2 %all-to-all-start.1 = ((bf16[16,2,128,256]{3,1,2,0:T(2,128)(2,1)}), bf16[16,2,128,256]{3,1,2,0:T(2,128)(2,1)S(1)}, u32[]{:S(2)}, u32[]{:S(2)}) async-start(bf16[16,2,128,256]{3,1,2,0:T(2,128)(2,1)} %copy.100), calls=%async_computation.1 | async-start | bytes 4194304 | tf_op jit(solution)/shard_map/all_to_all | solution.py:62
  148.3 0.7 copy-start.2
  151.3 5.9 copy-start.4
  151.3 6.0 copy-start.5
  151.3 53.6 %all-to-all-start.2 = ((bf16[16,2,128,256]{3,2,1,0:T(8,128)(2,1)}), bf16[16,2,128,256]{3,2,1,0:T(8,128)(2,1)S(1)}, u32[]{:S(2)}, u32[]{:S(2)}) async-start(bf16[16,2,128,256]{3,2,1,0:T(8,128)(2,1)} %broadcast_select_fusion), calls=%async_computation.2 | async-start | bytes 4194304 | tf_op jit(solution)/shard_map/all_to_all | solution.py:85
  157.2 583.6 %all-reduce.2.cloned.1.call-start = ((), (), s32[]{:S(2)}) async-start(), calls=%async_computation.3 | async-start | bytes 524288 | tf_op jit(solution)/shard_map/psum | solution.py:79
  208.8 8.3 %collective-permute-start.5 = (f32[4,128,256]{2,0,1:T(4,128)}, f32[4,128,256]{2,0,1:T(4,128)}, u32[]{:S(2)}, u32[]{:S(2)}) collective-permute-start(f32[4,128,256]{2,0,1:T(4,128)} %fusion.74), channel_id=1, source_target_pairs={{0,16},{16,32},{32,48},{48,64},{64,80},{80,96},{96,112},{112,128},... | collective-permute-start | bytes 1572872 | tf_op jit(solution)/shard_map/ppermute | solution.py:14
  219.3 10.9 %collective-permute-start.6 = (f32[4,128,256]{2,0,1:T(4,128)}, f32[4,128,256]{2,0,1:T(4,128)}, u32[]{:S(2)}, u32[]{:S(2)}) collective-permute-start(f32[4,128,256]{2,0,1:T(4,128)} %convolution_add_fusion), channel_id=1, source_target_pairs={{0,16},{16,32},{32,48},{48,64},{64,80},{80,96},{96,112},{112,128},... | collective-permute-start | bytes 1572872 | tf_op jit(solution)/shard_map/ppermute | solution.py:14
  232.2 12.9 %collective-permute-start.7 = (f32[4,128,256]{2,0,1:T(4,128)}, f32[4,128,256]{2,0,1:T(4,128)}, u32[]{:S(2)}, u32[]{:S(2)}) collective-permute-start(f32[4,128,256]{2,0,1:T(4,128)} %add.56), channel_id=1, source_target_pairs={{0,16},{16,32},{32,48},{48,64},{64,80},{80,96},{96,112},{112,128},... | collective-permute-start | bytes 1572872 | tf_op jit(solution)/shard_map/ppermute | solution.py:14
  247.1 24.3 %copy-start.3 = (bf16[512,256]{1,0:T(8,128)(2,1)S(1)}, bf16[512,256]{1,0:T(8,128)(2,1)}, u32[]{:S(2)}) copy-start(bf16[512,256]{1,0:T(8,128)(2,1)} %copy-done.2) | copy-start | bytes 786436
  247.1 13.0 %collective-permute-start.8 = (f32[4,128,256]{2,0,1:T(4,128)}, f32[4,128,256]{2,0,1:T(4,128)}, u32[]{:S(2)}, u32[]{:S(2)}) collective-permute-start(f32[4,128,256]{2,0,1:T(4,128)} %add.57), channel_id=1, source_target_pairs={{0,16},{16,32},{32,48},{48,64},{64,80},{80,96},{96,112},{112,128},... | collective-permute-start | bytes 1572872 | tf_op jit(solution)/shard_map/ppermute | solution.py:14
  261.3 14.7 %collective-permute-start.9 = (bf16[4,128,256]{2,0,1:T(4,128)(2,1)S(1)}, bf16[4,128,256]{2,0,1:T(4,128)(2,1)S(1)}, u32[]{:S(2)}, u32[]{:S(2)}) collective-permute-start(bf16[4,128,256]{2,0,1:T(4,128)(2,1)S(1)} %add.58), channel_id=1, source_target_pairs={{0,992},{16,1008},{32,0},{48,16},{64,32},{80,48},{96,64},{112,80},... | collective-permute-start | bytes 786440 | tf_op jit(solution)/shard_map/ppermute | solution.py:14
Sparse Core Ops, SparseCore 0:
  272.5 468.2 all-reduce.1
where the time goes:
time: 752 us; the launch traced here: 749 us
  waiting for transfers between devices  615 us (82%)
  starting transfers between devices  65.2 us (9%)
  local copies, waits for them, and re-layouts  26.9 us (4%)
  matrix products  19.5 us (3%)
  between operations  14.6 us (2%)
  other arithmetic  8.5 us (1%)
    psum x1, waiting for transfers between devices, per_device(): weight_grad = lax.psum(local_grad, ('dom', 'rows'))  464 us
    ppermute x10, waiting for transfers between devices, shifted(): return lax.ppermute(value, axis, pairs)  53.3 us
    all_to_all x1, waiting for transfers between devices, per_device(): lax.all_to_all(partials, 'rows', split_axis=0, concat_axis=0, tiled=True)  50.1 us
    all_to_all x1, waiting for transfers between devices, per_device(): lax.all_to_all(reply_blocks, 'rows', split_axis=0, concat_axis=0, tiled=T...  47.1 us
    ppermute x10, starting transfers between devices, shifted(): return lax.ppermute(value, axis, pairs)  40.3 us
  transfers between devices with their start and end apart: 14, of which 13 were waited for; matrix products, arithmetic and copies ran while one was open for 5% of the time, Pallas kernels for 0%

commit v1 on v0

v1 whole, which is shorter than its diff:
```python
import functools

import jax
import jax.numpy as jnp
from jax import lax
from jax.experimental import pallas as pl
from jax.experimental.pallas import tpu as pltpu
from jax.sharding import PartitionSpec as P

BLOCK = 128
HALF = 2
CAP = 2
XN = 4
YN = 4
LANES = 128
ID_ROWS = 16

OFFSETS = (-2, -1, 1, 2)
VMEM = pl.BlockSpec(memory_space=pltpu.VMEM)
SMEM = pl.BlockSpec(memory_space=pltpu.SMEM)
BF16 = jnp.bfloat16
F32 = jnp.float32


def params():
    return pltpu.CompilerParams(vmem_limit_bytes=24 * 1024 * 1024)


def cost(flops, nbytes):
    return pl.CostEstimate(flops=flops, bytes_accessed=nbytes, transcendentals=0)


def dom_shift(value, steps):
    count = lax.axis_size("dom")
    return lax.ppermute(value, "dom", [(i, (i + steps) % count) for i in range(count)])


def y_shift(value, steps):
    pairs = [(x * YN + y, x * YN + (y + steps) % YN) for x in range(XN) for y in range(YN)]
    return lax.ppermute(value, "rows", pairs)


X_GROUPS = [[x * YN + y for x in range(XN)] for y in range(YN)]


def x_exchange(value):
    return lax.all_to_all(
        value, "rows", split_axis=0, concat_axis=0, tiled=True, axis_index_groups=X_GROUPS
    )


def grouped_sum(value, axis, groups):
    size = len(groups[0])
    spread = jnp.broadcast_to(value[None], (size,) + value.shape)
    return jnp.sum(
        lax.all_to_all(
            spread, axis, split_axis=0, concat_axis=0, tiled=True, axis_index_groups=groups
        ),
        axis=0,
    )


def forward_kernel(with_ids, src, slot, cnt, fm2, fm1, f0, fp1, fp2, vals, ids, out, acc):
    acc[...] = jnp.zeros_like(acc)
    feats = (fm2, fm1, f0, fp1, fp2)
    tiles_step = vals.shape[0] // len(feats)
    for k, feat in enumerate(feats):
        for t in range(tiles_step):
            n = k * tiles_step + t

            @pl.when(t < cnt[0, k])
            def _():
                block = feat[src[k, t]]
                acc[slot[k, t]] += jnp.dot(vals[n], block, preferred_element_type=F32)

    per_x = acc.shape[0] // XN
    for s in range(acc.shape[0]):
        out[s // per_x, pl.ds((s % per_x) * BLOCK, BLOCK), :] = acc[s].astype(BF16)
    if with_ids:
        for x in range(XN):
            out[x, pl.ds(per_x * BLOCK, ID_ROWS), :] = ids[x]


def forward_products(src, slot, cnt, feats, vals, ids, with_ids):
    slots = XN * YN * CAP
    rows = YN * CAP * BLOCK + (ID_ROWS if with_ids else 0)
    return pl.pallas_call(
        functools.partial(forward_kernel, with_ids),
        out_shape=jax.ShapeDtypeStruct((XN, rows, LANES), BF16),
        in_specs=[SMEM] * 3 + [VMEM] * 7,
        out_specs=VMEM,
        scratch_shapes=[pltpu.VMEM((slots, BLOCK, LANES), F32)],
        compiler_params=params(),
        cost_estimate=cost(vals.shape[0] * 2 * BLOCK * BLOCK * LANES, 4 << 20),
        name="tile_forward",
    )(src, slot, cnt, *feats, vals, ids)


def gather_kernel(blocks_dev, recv, ids, out):
    for y in range(YN):
        for b in range(blocks_dev):
            total = jnp.zeros((BLOCK, LANES), F32)
            for x in range(XN):
                for c in range(CAP):
                    j = y * CAP + c
                    hit = ids[pl.ds(x * 8 + j, 1), :] == float(b)
                    part = recv[x, pl.ds(j * BLOCK, BLOCK), :].astype(F32)
                    total = total + jnp.where(hit, part, 0.0)
            out[y, pl.ds(b * BLOCK, BLOCK), :] = total.astype(BF16)


def gather_blocks(recv, ids, blocks_dev):
    return pl.pallas_call(
        functools.partial(gather_kernel, blocks_dev),
        out_shape=jax.ShapeDtypeStruct((YN, blocks_dev * BLOCK, LANES), BF16),
        in_specs=[VMEM, VMEM],
        out_specs=VMEM,
        compiler_params=params(),
        cost_estimate=cost(1 << 20, 2 << 20),
        name="block_sums",
    )(recv, ids)


def dense_kernel(*refs):
    own = refs[0:2]
    far = refs[2:8]
    me, weight, cot, act, g0, g1, wgrad = refs[8:]
    y = me[0]
    halves = []
    for h in range(2):
        total = own[h][y].astype(F32)
        for k in range(3):
            total = total + far[h * 3 + k][...].astype(F32)
        halves.append(total.astype(BF16))
    agg = jnp.concatenate(halves, axis=1)
    w = weight[...]
    pre = jnp.dot(agg, w, preferred_element_type=F32)
    sig = 1.0 / (1.0 + jnp.exp(-pre))
    act[...] = (pre * sig).astype(BF16)
    slope = sig * (1.0 + pre * (1.0 - sig))
    pre_grad = (cot[...].astype(F32) * slope).astype(BF16)
    grad = lax.dot_general(
        pre_grad, w, (((1,), (1,)), ((), ())), preferred_element_type=F32
    ).astype(BF16)
    g0[...] = grad[:, :LANES]
    g1[...] = grad[:, LANES:]
    wgrad[...] = lax.dot_general(
        agg, pre_grad, (((0,), (0,)), ((), ())), preferred_element_type=F32
    )


def dense(own, far, me, weight, cot):
    nodes, channels = cot.shape
    return pl.pallas_call(
        dense_kernel,
        out_shape=(
            jax.ShapeDtypeStruct((nodes, channels), BF16),
            jax.ShapeDtypeStruct((nodes, LANES), BF16),
            jax.ShapeDtypeStruct((nodes, LANES), BF16),
            jax.ShapeDtypeStruct((channels, channels), F32),
        ),
        in_specs=[VMEM] * 8 + [SMEM] + [VMEM] * 2,
        out_specs=(VMEM,) * 4,
        compiler_params=params(),
        cost_estimate=cost(6 * nodes * channels * channels, 4 << 20),
        name="dense_layer",
    )(*own, *far, me, weight, cot)


def reply_kernel(blocks_dev, me, g0, g1, g2, g3, ids, out):
    for k, grads in enumerate((g0, g1, g2, g3)):
        y = lax.rem(me[0] - k + YN, YN)
        blocks = [grads[pl.ds(b * BLOCK, BLOCK), :].astype(F32) for b in range(blocks_dev)]
        for x in range(XN):
            for c in range(CAP):
                j = y * CAP + c
                row = ids[pl.ds(x * 8 + j, 1), :]
                picked = jnp.where(row == 0.0, blocks[0], 0.0)
                for b in range(1, blocks_dev):
                    picked = jnp.where(row == float(b), blocks[b], picked)
                start = pl.multiple_of(j * BLOCK, BLOCK)
                out[x, pl.ds(start, BLOCK), :] = picked.astype(BF16)


def reply_blocks(me, grads, ids, blocks_dev):
    return pl.pallas_call(
        functools.partial(reply_kernel, blocks_dev),
        out_shape=jax.ShapeDtypeStruct((XN, YN * CAP * BLOCK, LANES), BF16),
        in_specs=[SMEM] + [VMEM] * 5,
        out_specs=VMEM,
        compiler_params=params(),
        cost_estimate=cost(1 << 20, 2 << 20),
        name="slot_replies",
    )(me, *grads, ids)


def backward_kernel(src, slot, cnt, ret, vals, om2, om1, o0, op1, op2, acc):
    outs = (om2, om1, o0, op1, op2)
    tiles_step = vals.shape[0] // len(outs)
    per_x = ret.shape[1] // BLOCK
    for k, out in enumerate(outs):
        acc[...] = jnp.zeros_like(acc)
        for t in range(tiles_step):
            n = k * tiles_step + t

            @pl.when(t < cnt[0, k])
            def _():
                s = slot[k, t]
                start = pl.multiple_of((s % per_x) * BLOCK, BLOCK)
                block = ret[s // per_x, pl.ds(start, BLOCK), :]
                acc[src[k, t]] += lax.dot_general(
                    vals[n], block, (((0,), (0,)), ((), ())), preferred_element_type=F32
                )

        for b in range(acc.shape[0]):
            out[pl.ds(b * BLOCK, BLOCK), :] = acc[b].astype(out.dtype)


def backward_products(src, slot, cnt, ret, vals, blocks_dev):
    half = jax.ShapeDtypeStruct((blocks_dev * BLOCK, LANES), BF16)
    full = jax.ShapeDtypeStruct((blocks_dev * BLOCK, LANES), F32)
    return pl.pallas_call(
        backward_kernel,
        out_shape=(half, half, full, half, half),
        in_specs=[SMEM] * 3 + [VMEM] * 2,
        out_specs=(VMEM,) * 5,
        scratch_shapes=[pltpu.VMEM((blocks_dev, BLOCK, LANES), F32)],
        compiler_params=params(),
        cost_estimate=cost(vals.shape[0] * 2 * BLOCK * BLOCK * LANES, 4 << 20),
        name="tile_backward",
    )(src, slot, cnt, ret, vals)


def final_kernel(*refs):
    out = refs[-1]
    for h in range(2):
        total = refs[h * 5][...]
        for k in range(1, 5):
            total = total + refs[h * 5 + k][...].astype(F32)
        out[:, h * LANES : (h + 1) * LANES] = total.astype(BF16)


def final_sum(parts):
    nodes = parts[0].shape[0]
    return pl.pallas_call(
        final_kernel,
        out_shape=jax.ShapeDtypeStruct((nodes, 2 * LANES), BF16),
        in_specs=[VMEM] * len(parts),
        out_specs=VMEM,
        compiler_params=params(),
        cost_estimate=cost(1 << 20, 2 << 20),
        name="grad_sum",
    )(*parts)


def per_device(
    features, weight, tile_values, tile_source, tile_slot, slot_block, tile_count, cotangent
):
    blocks_dev = features.shape[0] // BLOCK
    dom_count = lax.axis_size("dom")
    vals = tile_values.reshape(-1, BLOCK, BLOCK)
    src, slot, cnt = tile_source[0], tile_slot[0], tile_count
    me = (lax.axis_index("rows") % YN).astype(jnp.int32).reshape(1)
    id_rows = jnp.broadcast_to(
        jnp.pad(slot_block.reshape(XN, -1), ((0, 0), (0, ID_ROWS - YN * CAP)))[..., None],
        (XN, ID_ROWS, LANES),
    ).astype(BF16)

    own = [features[:, h * LANES : (h + 1) * LANES] for h in range(2)]
    near = [[dom_shift(own[h], -o) for o in OFFSETS] for h in range(2)]
    arrived = []
    for h in range(2):
        feats = [near[h][0], near[h][1], own[h], near[h][2], near[h][3]]
        feats = [f.reshape(blocks_dev, BLOCK, LANES) for f in feats]
        sent = forward_products(src, slot, cnt, feats, vals, id_rows, h == 0)
        arrived.append(x_exchange(sent))
    ids = arrived[0][:, YN * CAP * BLOCK :, :][:, : YN * CAP].astype(F32)
    ids = ids.reshape(XN * YN * CAP, LANES)
    sums, far = [], []
    for h in range(2):
        blocks = gather_blocks(arrived[h], ids, blocks_dev)
        sums.append(blocks)
        for k in (1, 2, 3):
            to = lax.dynamic_index_in_dim(blocks, (me[0] + k) % YN, 0, keepdims=False)
            far.append(y_shift(to, k))
    activations, g0, g1, local_grad = dense(sums, far, me, weight, cotangent)

    parts = []
    for g in (g0, g1):
        grads = [g] + [y_shift(g, k) for k in (1, 2, 3)]
        back = x_exchange(reply_blocks(me, grads, ids, blocks_dev))
        terms = backward_products(src, slot, cnt, back, vals, blocks_dev)
        parts.append(terms[2])
        for term, o in zip((terms[0], terms[1], terms[3], terms[4]), OFFSETS):
            parts.append(dom_shift(term, o))
    feature_grad = final_sum(parts)

    rows = lax.axis_size("rows")
    channels = local_grad.shape[0]
    pieces = local_grad.reshape(rows, channels // rows, channels)
    piece = jnp.sum(
        lax.all_to_all(pieces, "rows", split_axis=0, concat_axis=0, tiled=True), axis=0
    )
    inner = 8
    outer = dom_count // inner
    near_groups = [[i * inner + j for j in range(inner)] for i in range(outer)]
    far_groups = [[i * inner + j for i in range(outer)] for j in range(inner)]
    piece = grouped_sum(piece, "dom", near_groups)
    piece = grouped_sum(piece, "dom", far_groups)
    whole = jnp.broadcast_to(piece[None], pieces.shape)
    weight_grad = lax.all_to_all(whole, "rows", split_axis=0, concat_axis=0, tiled=True)
    weight_grad = weight_grad.reshape(channels, channels)
    return (activations, feature_grad, weight_grad)


def solution(mesh):
    return jax.shard_map(
        per_device,
        mesh=mesh,
        in_specs=(
            P(("dom", "rows"), None),
            P(),
            P(("dom", "rows"), None, None, None, None),
            P(("dom", "rows"), None, None),
            P(("dom", "rows"), None, None),
            P(("dom", "rows"), None),
            P(("dom", "rows"), None),
            P(("dom", "rows"), None),
        ),
        out_specs=(P(("dom", "rows"), None), P(("dom", "rows"), None), P()),
        check_vma=False,
    )
```

time: 752 us -> 279 us (0.37)
  waiting for transfers between devices: 615 us -> 88.6 us
  starting transfers between devices: 65.2 us -> 146 us
  matrix products: 19.5 us -> 0 us
  local copies, waits for them, and re-layouts: 26.9 us -> 9.24 us
  Pallas kernels: 0 us -> 17.5 us
  blocking collectives: 0 us -> 13.7 us
  between operations: 14.6 us -> 1.14 us
  other arithmetic: 8.5 us -> 0.73 us
    psum x1 -> x0, waiting for transfers between devices: 464 us -> none  [per_device(): weight_grad = lax.psum(local_grad, ('dom', 'rows'))]
    ppermute x10 -> x28, starting transfers between devices: 40.3 us -> 114 us  [the longest x16 71.7 us: dom_shift(): lax.ppermute(value, 'dom', [(i, (i + steps) % count) for i in range(count)])]
    all_to_all x3 -> x7, waiting for transfers between devices: 97.2 us -> 40 us  [the longest x4 40 us: x_exchange(): lax.all_to_all(value, 'rows', split_axis=0, concat_axis=0, tiled=True, ax...]
    dot_general x20 -> x0, matrix products: 19.5 us -> none  [the longest x5 5.52 us: source_terms(): jnp.einsum('tji,tjf->tif', values[step_idx], picked, preferred_element_ty...]
    pallas_call x0 -> x10, Pallas kernels: none -> 17.5 us  [the longest x2 6.08 us: backward_products(): pl.pallas_call(backward_kernel, out_shape=(half, half, full, half, half),...]
    all_to_all x0 -> x1, blocking collectives: none -> 13.7 us  [per_device(): lax.all_to_all(pieces, 'rows', split_axis=0, concat_axis=0, tiled=True)]
    all_to_all x3 -> x7, starting transfers between devices: 24.8 us -> 32.3 us  [the longest x4 16.5 us: x_exchange(): lax.all_to_all(value, 'rows', split_axis=0, concat_axis=0, tiled=True, ax...]
    ppermute x10 -> x28, waiting for transfers between devices: 53.3 us -> 48.6 us  [the longest x12 31 us: y_shift(): return lax.ppermute(value, 'rows', pairs)]
  transfers between devices with their start and end apart: 14 -> 35, of which waited for: 13 -> 13; matrix products, arithmetic and copies ran while one was open for 5% -> 1% of each run, Pallas kernels for 0% -> 4%
where the time goes in v1:
time: 279 us; the launch traced here: 277 us
  starting transfers between devices  146 us (52%)
  waiting for transfers between devices  88.6 us (32%)
  Pallas kernels  17.5 us (6%)
  blocking collectives  13.7 us (5%)
  local copies, waits for them, and re-layouts  9.24 us (3%)
    ppermute x16, starting transfers between devices, dom_shift(): lax.ppermute(value, 'dom', [(i, (i + steps) % count) for i in range(count)])  71.7 us
    ppermute x12, starting transfers between devices, y_shift(): return lax.ppermute(value, 'rows', pairs)  41.8 us
    all_to_all x4, waiting for transfers between devices, x_exchange(): lax.all_to_all(value, 'rows', split_axis=0, concat_axis=0, tiled=True, ax...  40 us
    ppermute x12, waiting for transfers between devices, y_shift(): return lax.ppermute(value, 'rows', pairs)  31 us
    ppermute x16, waiting for transfers between devices, dom_shift(): lax.ppermute(value, 'dom', [(i, (i + steps) % count) for i in range(count)])  17.6 us
    all_to_all x4, starting transfers between devices, x_exchange(): lax.all_to_all(value, 'rows', split_axis=0, concat_axis=0, tiled=True, ax...  16.5 us
    all_to_all x1, blocking collectives, per_device(): lax.all_to_all(pieces, 'rows', split_axis=0, concat_axis=0, tiled=True)  13.7 us
    all_to_all x2, starting transfers between devices, grouped_sum(): lax.all_to_all(spread, axis, split_axis=0, concat_axis=0, tiled=True, axi...  11.5 us
  transfers between devices with their start and end apart: 35, of which 13 were waited for; matrix products, arithmetic and copies ran while one was open for 1% of the time, Pallas kernels for 4%

profile of v1, /device:TPU:1, one launch (start us, length us, event | category | flops | bytes accessed | tf_op | source)
XLA Modules:
  0.0 276.8 jit_solution(11246542606833846064)
XLA Ops:
  1.6 19.8 %collective-permute-start.3 = (bf16[512,128]{1,0:T(8,128)(2,1)S(1)}, bf16[512,128]{1,0:T(8,128)(2,1)S(1)}, u32[]{:S(2)}, u32[]{:S(2)}) collective-permute-start(bf16[512,128]{1,0:T(8,128)(2,1)S(1)} %get-tuple-element.38), channel_id=1, source_target_pairs={{0,992},{16,1008},{32,0},{48,16},{64,32},{80,48},{96,64},{112,80},... | collective-permute-start | bytes 393224 | tf_op jit(solution)/shard_map/ppermute | solution.py:35
  31.3 5.1 %collective-permute-done = bf16[512,128]{1,0:T(8,128)(2,1)S(1)} collective-permute-done((bf16[512,128]{1,0:T(8,128)(2,1)S(1)}, bf16[512,128]{1,0:T(8,128)(2,1)S(1)}, u32[]{:S(2)}, u32[]{:S(2)}) %collective-permute-start) | collective-permute-done | bytes 131104 | tf_op jit(solution)/shard_map/ppermute | solution.py:35
  41.6 4.6 %all-to-all-start = ((bf16[4,1040,128]{2,1,0:T(8,128)(2,1)}), bf16[4,1040,128]{2,1,0:T(8,128)(2,1)S(1)}, u32[]{:S(2)}, u32[]{:S(2)}) async-start(bf16[4,1040,128]{2,1,0:T(8,128)(2,1)} %tile_forward.2), calls=%async_computation | async-start | bytes 2129920 | tf_op jit(solution)/shard_map/all_to_all | solution.py:47
  58.0 5.1 %collective-permute-done.4 = bf16[512,128]{1,0:T(8,128)(2,1)S(1)} collective-permute-done((bf16[512,128]{1,0:T(8,128)(2,1)S(1)}, bf16[512,128]{1,0:T(8,128)(2,1)S(1)}, u32[]{:S(2)}, u32[]{:S(2)}) %collective-permute-start.4) | collective-permute-done | bytes 131104 | tf_op jit(solution)/shard_map/ppermute | solution.py:35
  66.6 4.9 %all-to-all-start.1 = ((bf16[4,1024,128]{2,1,0:T(8,128)(2,1)}), bf16[4,1024,128]{2,1,0:T(8,128)(2,1)S(1)}, u32[]{:S(2)}, u32[]{:S(2)}) async-start(bf16[4,1024,128]{2,1,0:T(8,128)(2,1)} %copy-done.3), calls=%async_computation.1 | async-start | bytes 2097152 | tf_op jit(solution)/shard_map/all_to_all | solution.py:47
  71.5 14.7 %all-to-all-done.1.recv = bf16[4,1024,128]{2,1,0:T(8,128)(2,1)S(1)} async-done(((bf16[4,1024,128]{2,1,0:T(8,128)(2,1)}), bf16[4,1024,128]{2,1,0:T(8,128)(2,1)S(1)}, u32[]{:S(2)}, u32[]{:S(2)}) %all-to-all-start.1) | async-done | bytes 1048608 | tf_op jit(solution)/shard_map/all_to_all | solution.py:47
  87.2 5.8 %collective-permute-start.13 = (bf16[512,128]{1,0:T(8,128)(2,1)S(1)}, bf16[512,128]{1,0:T(8,128)(2,1)S(1)}, u32[]{:S(2)}, u32[]{:S(2)}) collective-permute-start(bf16[512,128]{1,0:T(8,128)(2,1)S(1)} %get-tuple-element.31), channel_id=1, source_target_pairs={{0,3},{1,0},{2,1},{3,2},{4,7},{5,4},{6,5},{7,6},{8,11},{9,8},{10,9... | collective-permute-start | bytes 393224 | tf_op jit(solution)/shard_map/ppermute | solution.py:40
  100.4 4.5 %collective-permute-start.10 = (bf16[512,128]{1,0:T(8,128)(2,1)S(1)}, bf16[512,128]{1,0:T(8,128)(2,1)S(1)}, u32[]{:S(2)}, u32[]{:S(2)}) collective-permute-start(bf16[512,128]{1,0:T(8,128)(2,1)S(1)} %get-tuple-element.34), channel_id=1, source_target_pairs={{0,3},{1,0},{2,1},{3,2},{4,7},{5,4},{6,5},{7,6},{8,11},{9,8},{10,9... | collective-permute-start | bytes 393224 | tf_op jit(solution)/shard_map/ppermute | solution.py:40
  104.9 5.7 %collective-permute-start.9 = (bf16[512,128]{1,0:T(8,128)(2,1)S(1)}, bf16[512,128]{1,0:T(8,128)(2,1)S(1)}, u32[]{:S(2)}, u32[]{:S(2)}) collective-permute-start(bf16[512,128]{1,0:T(8,128)(2,1)S(1)} %get-tuple-element.35), channel_id=1, source_target_pairs={{0,2},{1,3},{2,0},{3,1},{4,6},{5,7},{6,4},{7,5},{8,10},{9,11},{10,... | collective-permute-start | bytes 393224 | tf_op jit(solution)/shard_map/ppermute | solution.py:40
  114.7 4.9 %collective-permute-done.9.refs_3_ = bf16[512,128]{1,0:T(8,128)(2,1)S(1)} collective-permute-done((bf16[512,128]{1,0:T(8,128)(2,1)S(1)}, bf16[512,128]{1,0:T(8,128)(2,1)S(1)}, u32[]{:S(2)}, u32[]{:S(2)}) %collective-permute-start.9) | collective-permute-done | bytes 131104 | tf_op jit(solution)/shard_map/ppermute | solution.py:40
  124.9 13.7 %all_to_all.40 = f32[16,16,256]{2,1,0:T(8,128)S(1)} all-to-all(f32[16,16,256]{2,1,0:T(8,128)S(1)} %bitcast.39), channel_id=1, replica_groups=mesh['dom'=64,'rows'=16] {'rows'}, dimensions={0} | all-to-all | bytes 524288 | tf_op jit(solution)/shard_map/all_to_all | solution.py:302
  139.3 6.2 %all-to-all-start.5 = ((f32[8,16,256]{2,1,0:T(8,128)}), f32[8,16,256]{2,1,0:T(8,128)S(1)}, u32[]{:S(2)}, u32[]{:S(2)}) async-start(f32[8,16,256]{2,1,0:T(8,128)} %broadcast_in_dim.9), calls=%async_computation.5 | async-start | bytes 262144 | tf_op jit(solution)/shard_map/all_to_all | solution.py:56
  147.5 5.4 %collective-permute-start.22 = (bf16[512,128]{1,0:T(8,128)(2,1)S(1)}, bf16[512,128]{1,0:T(8,128)(2,1)S(1)}, u32[]{:S(2)}, u32[]{:S(2)}) collective-permute-start(bf16[512,128]{1,0:T(8,128)(2,1)S(1)} %get-tuple-element.24.g0), channel_id=1, source_target_pairs={{0,2},{1,3},{2,0},{3,1},{4,6},{5,7},{6,4},{7,5},{8,10},{9,11},{10,... | collective-permute-start | bytes 393224 | tf_op jit(solution)/shard_map/ppermute | solution.py:40
  154.8 6.6 %collective-permute-done.22.g2 = bf16[512,128]{1,0:T(8,128)(2,1)S(1)} collective-permute-done((bf16[512,128]{1,0:T(8,128)(2,1)S(1)}, bf16[512,128]{1,0:T(8,128)(2,1)S(1)}, u32[]{:S(2)}, u32[]{:S(2)}) %collective-permute-start.22) | collective-permute-done | bytes 131104 | tf_op jit(solution)/shard_map/ppermute | solution.py:40
  169.8 14.7 %all-to-all-done.3.ret = bf16[4,1024,128]{2,1,0:T(8,128)(2,1)S(1)} async-done(((bf16[4,1024,128]{2,1,0:T(8,128)(2,1)}), bf16[4,1024,128]{2,1,0:T(8,128)(2,1)S(1)}, u32[]{:S(2)}, u32[]{:S(2)}) %all-to-all-start.3) | async-done | bytes 1048608 | tf_op jit(solution)/shard_map/all_to_all | solution.py:47
  185.2 5.2 %all-to-all-start.6 = ((f32[8,16,256]{2,1,0:T(8,128)}), f32[8,16,256]{2,1,0:T(8,128)S(1)}, u32[]{:S(2)}, u32[]{:S(2)}) async-start(f32[8,16,256]{2,1,0:T(8,128)} %broadcast_in_dim.10), calls=%async_computation.6 | async-start | bytes 262144 | tf_op jit(solution)/shard_map/all_to_all | solution.py:56
  194.3 4.3 %collective-permute-start.14 = (bf16[512,128]{1,0:T(8,128)(2,1)S(1)}, bf16[512,128]{1,0:T(8,128)(2,1)S(1)}, u32[]{:S(2)}, u32[]{:S(2)}) collective-permute-start(bf16[512,128]{1,0:T(8,128)(2,1)S(1)} %get-tuple-element.18.g0), channel_id=1, source_target_pairs={{0,1},{1,2},{2,3},{3,0},{4,5},{5,6},{6,7},{7,4},{8,9},{9,10},{10,1... | collective-permute-start | bytes 393224 | tf_op jit(solution)/shard_map/ppermute | solution.py:40
  198.6 5.2 %collective-permute-done.15.g2 = bf16[512,128]{1,0:T(8,128)(2,1)S(1)} collective-permute-done((bf16[512,128]{1,0:T(8,128)(2,1)S(1)}, bf16[512,128]{1,0:T(8,128)(2,1)S(1)}, u32[]{:S(2)}, u32[]{:S(2)}) %collective-permute-start.15) | collective-permute-done | bytes 131104 | tf_op jit(solution)/shard_map/ppermute | solution.py:40
  203.8 4.5 %collective-permute-done.14.g1 = bf16[512,128]{1,0:T(8,128)(2,1)S(1)} collective-permute-done((bf16[512,128]{1,0:T(8,128)(2,1)S(1)}, bf16[512,128]{1,0:T(8,128)(2,1)S(1)}, u32[]{:S(2)}, u32[]{:S(2)}) %collective-permute-start.14) | collective-permute-done | bytes 131104 | tf_op jit(solution)/shard_map/ppermute | solution.py:40
  213.3 10.6 %all-to-all-done.2.ret = bf16[4,1024,128]{2,1,0:T(8,128)(2,1)S(1)} async-done(((bf16[4,1024,128]{2,1,0:T(8,128)(2,1)}), bf16[4,1024,128]{2,1,0:T(8,128)(2,1)S(1)}, u32[]{:S(2)}, u32[]{:S(2)}) %all-to-all-start.2) | async-done | bytes 1048608 | tf_op jit(solution)/shard_map/all_to_all | solution.py:47
  224.6 4.3 %all-to-all-start.7 = ((f32[16,16,256]{2,1,0:T(8,128)}), f32[16,16,256]{2,1,0:T(8,128)S(1)}, u32[]{:S(2)}, u32[]{:S(2)}) async-start(f32[16,16,256]{2,1,0:T(8,128)} %broadcast_in_dim.11), calls=%async_computation.7 | async-start | bytes 524288 | tf_op jit(solution)/shard_map/all_to_all | solution.py:311
  232.0 12.0 %collective-permute-start.24 = (bf16[512,128]{1,0:T(8,128)(2,1)S(1)}, bf16[512,128]{1,0:T(8,128)(2,1)S(1)}, u32[]{:S(2)}, u32[]{:S(2)}) collective-permute-start(bf16[512,128]{1,0:T(8,128)(2,1)S(1)} %get-tuple-element.26), channel_id=1, source_target_pairs={{0,992},{16,1008},{32,0},{48,16},{64,32},{80,48},{96,64},{112,80},... | collective-permute-start | bytes 393224 | tf_op jit(solution)/shard_map/ppermute | solution.py:35
  255.0 5.3 %collective-permute-start.17 = (bf16[512,128]{1,0:T(8,128)(2,1)S(1)}, bf16[512,128]{1,0:T(8,128)(2,1)S(1)}, u32[]{:S(2)}, u32[]{:S(2)}) collective-permute-start(bf16[512,128]{1,0:T(8,128)(2,1)S(1)} %get-tuple-element.20), channel_id=1, source_target_pairs={{0,992},{16,1008},{32,0},{48,16},{64,32},{80,48},{96,64},{112,80},... | collective-permute-start | bytes 393224 | tf_op jit(solution)/shard_map/ppermute | solution.py:35
  267.9 7.3 %collective-permute-done.20.refs_4_ = bf16[512,128]{1,0:T(8,128)(2,1)S(1)} collective-permute-done((bf16[512,128]{1,0:T(8,128)(2,1)S(1)}, bf16[512,128]{1,0:T(8,128)(2,1)S(1)}, u32[]{:S(2)}, u32[]{:S(2)}) %collective-permute-start.20) | collective-permute-done | bytes 131104 | tf_op jit(solution)/shard_map/ppermute | solution.py:35
  (90 shorter events, 95.0 us)
Async XLA Ops:
  1.6 29.6 %collective-permute-start.3 = (bf16[512,128]{1,0:T(8,128)(2,1)S(1)}, bf16[512,128]{1,0:T(8,128)(2,1)S(1)}, u32[]{:S(2)}, u32[]{:S(2)}) collective-permute-start(bf16[512,128]{1,0:T(8,128)(2,1)S(1)} %get-tuple-element.38), channel_id=1, source_target_pairs={{0,992},{16,1008},{32,0},{48,16},{64,32},{80,48},{96,64},{112,80},... | collective-permute-start | bytes 393224 | tf_op jit(solution)/shard_map/ppermute | solution.py:35
  41.6 25.0 %all-to-all-start = ((bf16[4,1040,128]{2,1,0:T(8,128)(2,1)}), bf16[4,1040,128]{2,1,0:T(8,128)(2,1)S(1)}, u32[]{:S(2)}, u32[]{:S(2)}) async-start(bf16[4,1040,128]{2,1,0:T(8,128)(2,1)} %tile_forward.2), calls=%async_computation | async-start | bytes 2129920 | tf_op jit(solution)/shard_map/all_to_all | solution.py:47
  46.2 11.8 %collective-permute-start.7 = (bf16[512,128]{1,0:T(8,128)(2,1)S(1)}, bf16[512,128]{1,0:T(8,128)(2,1)S(1)}, u32[]{:S(2)}, u32[]{:S(2)}) collective-permute-start(bf16[512,128]{1,0:T(8,128)(2,1)S(1)} %get-tuple-element.37), channel_id=1, source_target_pairs={{0,992},{16,1008},{32,0},{48,16},{64,32},{80,48},{96,64},{112,80},... | collective-permute-start | bytes 393224 | tf_op jit(solution)/shard_map/ppermute | solution.py:35
  66.6 19.6 %all-to-all-start.1 = ((bf16[4,1024,128]{2,1,0:T(8,128)(2,1)}), bf16[4,1024,128]{2,1,0:T(8,128)(2,1)S(1)}, u32[]{:S(2)}, u32[]{:S(2)}) async-start(bf16[4,1024,128]{2,1,0:T(8,128)(2,1)} %copy-done.3), calls=%async_computation.1 | async-start | bytes 2097152 | tf_op jit(solution)/shard_map/all_to_all | solution.py:47
  87.2 23.5 %collective-permute-start.13 = (bf16[512,128]{1,0:T(8,128)(2,1)S(1)}, bf16[512,128]{1,0:T(8,128)(2,1)S(1)}, u32[]{:S(2)}, u32[]{:S(2)}) collective-permute-start(bf16[512,128]{1,0:T(8,128)(2,1)S(1)} %get-tuple-element.31), channel_id=1, source_target_pairs={{0,3},{1,0},{2,1},{3,2},{4,7},{5,4},{6,5},{7,6},{8,11},{9,8},{10,9... | collective-permute-start | bytes 393224 | tf_op jit(solution)/shard_map/ppermute | solution.py:40
  93.0 19.6 %collective-permute-start.12 = (bf16[512,128]{1,0:T(8,128)(2,1)S(1)}, bf16[512,128]{1,0:T(8,128)(2,1)S(1)}, u32[]{:S(2)}, u32[]{:S(2)}) collective-permute-start(bf16[512,128]{1,0:T(8,128)(2,1)S(1)} %get-tuple-element.32), channel_id=1, source_target_pairs={{0,2},{1,3},{2,0},{3,1},{4,6},{5,7},{6,4},{7,5},{8,10},{9,11},{10,... | collective-permute-start | bytes 393224 | tf_op jit(solution)/shard_map/ppermute | solution.py:40
  96.4 16.1 %collective-permute-start.11 = (bf16[512,128]{1,0:T(8,128)(2,1)S(1)}, bf16[512,128]{1,0:T(8,128)(2,1)S(1)}, u32[]{:S(2)}, u32[]{:S(2)}) collective-permute-start(bf16[512,128]{1,0:T(8,128)(2,1)S(1)} %get-tuple-element.33), channel_id=1, source_target_pairs={{0,1},{1,2},{2,3},{3,0},{4,5},{5,6},{6,7},{7,4},{8,9},{9,10},{10,1... | collective-permute-start | bytes 393224 | tf_op jit(solution)/shard_map/ppermute | solution.py:40
  100.4 14.2 %collective-permute-start.10 = (bf16[512,128]{1,0:T(8,128)(2,1)S(1)}, bf16[512,128]{1,0:T(8,128)(2,1)S(1)}, u32[]{:S(2)}, u32[]{:S(2)}) collective-permute-start(bf16[512,128]{1,0:T(8,128)(2,1)S(1)} %get-tuple-element.34), channel_id=1, source_target_pairs={{0,3},{1,0},{2,1},{3,2},{4,7},{5,4},{6,5},{7,6},{8,11},{9,8},{10,9... | collective-permute-start | bytes 393224 | tf_op jit(solution)/shard_map/ppermute | solution.py:40
  104.9 14.7 %collective-permute-start.9 = (bf16[512,128]{1,0:T(8,128)(2,1)S(1)}, bf16[512,128]{1,0:T(8,128)(2,1)S(1)}, u32[]{:S(2)}, u32[]{:S(2)}) collective-permute-start(bf16[512,128]{1,0:T(8,128)(2,1)S(1)} %get-tuple-element.35), channel_id=1, source_target_pairs={{0,2},{1,3},{2,0},{3,1},{4,6},{5,7},{6,4},{7,5},{8,10},{9,11},{10,... | collective-permute-start | bytes 393224 | tf_op jit(solution)/shard_map/ppermute | solution.py:40
  110.6 13.1 %collective-permute-start.8 = (bf16[512,128]{1,0:T(8,128)(2,1)S(1)}, bf16[512,128]{1,0:T(8,128)(2,1)S(1)}, u32[]{:S(2)}, u32[]{:S(2)}) collective-permute-start(bf16[512,128]{1,0:T(8,128)(2,1)S(1)} %get-tuple-element.36), channel_id=1, source_target_pairs={{0,1},{1,2},{2,3},{3,0},{4,5},{5,6},{6,7},{7,4},{8,9},{9,10},{10,1... | collective-permute-start | bytes 393224 | tf_op jit(solution)/shard_map/ppermute | solution.py:40
  139.3 27.0 %all-to-all-start.5 = ((f32[8,16,256]{2,1,0:T(8,128)}), f32[8,16,256]{2,1,0:T(8,128)S(1)}, u32[]{:S(2)}, u32[]{:S(2)}) async-start(f32[8,16,256]{2,1,0:T(8,128)} %broadcast_in_dim.9), calls=%async_computation.5 | async-start | bytes 262144 | tf_op jit(solution)/shard_map/all_to_all | solution.py:56
  147.5 14.0 %collective-permute-start.22 = (bf16[512,128]{1,0:T(8,128)(2,1)S(1)}, bf16[512,128]{1,0:T(8,128)(2,1)S(1)}, u32[]{:S(2)}, u32[]{:S(2)}) collective-permute-start(bf16[512,128]{1,0:T(8,128)(2,1)S(1)} %get-tuple-element.24.g0), channel_id=1, source_target_pairs={{0,2},{1,3},{2,0},{3,1},{4,6},{5,7},{6,4},{7,5},{8,10},{9,11},{10,... | collective-permute-start | bytes 393224 | tf_op jit(solution)/shard_map/ppermute | solution.py:40
  152.9 12.0 %collective-permute-start.21 = (bf16[512,128]{1,0:T(8,128)(2,1)S(1)}, bf16[512,128]{1,0:T(8,128)(2,1)S(1)}, u32[]{:S(2)}, u32[]{:S(2)}) collective-permute-start(bf16[512,128]{1,0:T(8,128)(2,1)S(1)} %get-tuple-element.24.g0), channel_id=1, source_target_pairs={{0,1},{1,2},{2,3},{3,0},{4,5},{5,6},{6,7},{7,4},{8,9},{9,10},{10,1... | collective-permute-start | bytes 393224 | tf_op jit(solution)/shard_map/ppermute | solution.py:40
  166.3 18.3 %all-to-all-start.3 = ((bf16[4,1024,128]{2,1,0:T(8,128)(2,1)}), bf16[4,1024,128]{2,1,0:T(8,128)(2,1)S(1)}, u32[]{:S(2)}, u32[]{:S(2)}) async-start(bf16[4,1024,128]{2,1,0:T(8,128)(2,1)} %slot_replies.3), calls=%async_computation.3 | async-start | bytes 2097152 | tf_op jit(solution)/shard_map/all_to_all | solution.py:47
  185.2 24.6 %all-to-all-start.6 = ((f32[8,16,256]{2,1,0:T(8,128)}), f32[8,16,256]{2,1,0:T(8,128)S(1)}, u32[]{:S(2)}, u32[]{:S(2)}) async-start(f32[8,16,256]{2,1,0:T(8,128)} %broadcast_in_dim.10), calls=%async_computation.6 | async-start | bytes 262144 | tf_op jit(solution)/shard_map/all_to_all | solution.py:56
  192.3 11.4 %collective-permute-start.15 = (bf16[512,128]{1,0:T(8,128)(2,1)S(1)}, bf16[512,128]{1,0:T(8,128)(2,1)S(1)}, u32[]{:S(2)}, u32[]{:S(2)}) collective-permute-start(bf16[512,128]{1,0:T(8,128)(2,1)S(1)} %get-tuple-element.18.g0), channel_id=1, source_target_pairs={{0,2},{1,3},{2,0},{3,1},{4,6},{5,7},{6,4},{7,5},{8,10},{9,11},{10,... | collective-permute-start | bytes 393224 | tf_op jit(solution)/shard_map/ppermute | solution.py:40
  194.3 14.1 %collective-permute-start.14 = (bf16[512,128]{1,0:T(8,128)(2,1)S(1)}, bf16[512,128]{1,0:T(8,128)(2,1)S(1)}, u32[]{:S(2)}, u32[]{:S(2)}) collective-permute-start(bf16[512,128]{1,0:T(8,128)(2,1)S(1)} %get-tuple-element.18.g0), channel_id=1, source_target_pairs={{0,1},{1,2},{2,3},{3,0},{4,5},{5,6},{6,7},{7,4},{8,9},{9,10},{10,1... | collective-permute-start | bytes 393224 | tf_op jit(solution)/shard_map/ppermute | solution.py:40
  209.8 14.1 %all-to-all-start.2 = ((bf16[4,1024,128]{2,1,0:T(8,128)(2,1)}), bf16[4,1024,128]{2,1,0:T(8,128)(2,1)S(1)}, u32[]{:S(2)}, u32[]{:S(2)}) async-start(bf16[4,1024,128]{2,1,0:T(8,128)(2,1)} %copy-done.2), calls=%async_computation.2 | async-start | bytes 2097152 | tf_op jit(solution)/shard_map/all_to_all | solution.py:47
  224.6 51.4 %all-to-all-start.7 = ((f32[16,16,256]{2,1,0:T(8,128)}), f32[16,16,256]{2,1,0:T(8,128)S(1)}, u32[]{:S(2)}, u32[]{:S(2)}) async-start(f32[16,16,256]{2,1,0:T(8,128)} %broadcast_in_dim.11), calls=%async_computation.7 | async-start | bytes 524288 | tf_op jit(solution)/shard_map/all_to_all | solution.py:311
  232.0 28.3 %collective-permute-start.24 = (bf16[512,128]{1,0:T(8,128)(2,1)S(1)}, bf16[512,128]{1,0:T(8,128)(2,1)S(1)}, u32[]{:S(2)}, u32[]{:S(2)}) collective-permute-start(bf16[512,128]{1,0:T(8,128)(2,1)S(1)} %get-tuple-element.26), channel_id=1, source_target_pairs={{0,992},{16,1008},{32,0},{48,16},{64,32},{80,48},{96,64},{112,80},... | collective-permute-start | bytes 393224 | tf_op jit(solution)/shard_map/ppermute | solution.py:35
  244.0 19.3 %collective-permute-start.25 = (bf16[512,128]{1,0:T(8,128)(2,1)S(1)}, bf16[512,128]{1,0:T(8,128)(2,1)S(1)}, u32[]{:S(2)}, u32[]{:S(2)}) collective-permute-start(bf16[512,128]{1,0:T(8,128)(2,1)S(1)} %get-tuple-element.27), channel_id=1, source_target_pairs={{0,1008},{16,0},{32,16},{48,32},{64,48},{80,64},{96,80},{112,96},{... | collective-permute-start | bytes 393224 | tf_op jit(solution)/shard_map/ppermute | solution.py:35
  248.1 17.8 %collective-permute-start.26 = (bf16[512,128]{1,0:T(8,128)(2,1)S(1)}, bf16[512,128]{1,0:T(8,128)(2,1)S(1)}, u32[]{:S(2)}, u32[]{:S(2)}) collective-permute-start(bf16[512,128]{1,0:T(8,128)(2,1)S(1)} %get-tuple-element.28), channel_id=1, source_target_pairs={{0,16},{16,32},{32,48},{48,64},{64,80},{80,96},{96,112},{112,128},... | collective-permute-start | bytes 393224 | tf_op jit(solution)/shard_map/ppermute | solution.py:35
  250.1 17.8 %collective-permute-start.27 = (bf16[512,128]{1,0:T(8,128)(2,1)S(1)}, bf16[512,128]{1,0:T(8,128)(2,1)S(1)}, u32[]{:S(2)}, u32[]{:S(2)}) collective-permute-start(bf16[512,128]{1,0:T(8,128)(2,1)S(1)} %get-tuple-element.29), channel_id=1, source_target_pairs={{0,32},{16,48},{32,64},{48,80},{64,96},{80,112},{96,128},{112,144}... | collective-permute-start | bytes 393224 | tf_op jit(solution)/shard_map/ppermute | solution.py:35
  255.0 12.9 %collective-permute-start.17 = (bf16[512,128]{1,0:T(8,128)(2,1)S(1)}, bf16[512,128]{1,0:T(8,128)(2,1)S(1)}, u32[]{:S(2)}, u32[]{:S(2)}) collective-permute-start(bf16[512,128]{1,0:T(8,128)(2,1)S(1)} %get-tuple-element.20), channel_id=1, source_target_pairs={{0,992},{16,1008},{32,0},{48,16},{64,32},{80,48},{96,64},{112,80},... | collective-permute-start | bytes 393224 | tf_op jit(solution)/shard_map/ppermute | solution.py:35
  (19 other events, 191.8 us)

commit v2 on v1

v2 whole, which is shorter than its diff:
```python
import functools

import jax
import jax.numpy as jnp
from jax import lax
from jax.experimental import pallas as pl
from jax.experimental.pallas import tpu as pltpu
from jax.sharding import PartitionSpec as P

BLOCK = 128
HALF = 2
CAP = 2
XN = 4
YN = 4
LANES = 128
ID_ROWS = 16

OFFSETS = (-2, -1, 1, 2)
VMEM = pl.BlockSpec(memory_space=pltpu.VMEM)
SMEM = pl.BlockSpec(memory_space=pltpu.SMEM)
BF16 = jnp.bfloat16
F32 = jnp.float32


def params():
    return pltpu.CompilerParams(vmem_limit_bytes=24 * 1024 * 1024)


def cost(flops, nbytes):
    return pl.CostEstimate(flops=flops, bytes_accessed=nbytes, transcendentals=0)


def dom_shift(value, steps):
    count = lax.axis_size("dom")
    return lax.ppermute(value, "dom", [(i, (i + steps) % count) for i in range(count)])


def y_shift(value, steps):
    pairs = [(x * YN + y, x * YN + (y + steps) % YN) for x in range(XN) for y in range(YN)]
    return lax.ppermute(value, "rows", pairs)


X_GROUPS = [[x * YN + y for x in range(XN)] for y in range(YN)]


def x_exchange(value):
    return lax.all_to_all(
        value, "rows", split_axis=0, concat_axis=0, tiled=True, axis_index_groups=X_GROUPS
    )


def x_shift(value, steps):
    pairs = [(x * YN + y, (x + steps) % XN * YN + y) for x in range(XN) for y in range(YN)]
    return lax.ppermute(value, "rows", pairs)


def forward_kernel(half, src, slot, cnt, fm2, fm1, f0, fp1, fp2, vals, ids, out, acc):
    acc[...] = jnp.zeros_like(acc)
    feats = (fm2, fm1, f0, fp1, fp2)
    tiles_step = vals.shape[0] // len(feats)
    for k, feat in enumerate(feats):
        for t in range(tiles_step):
            n = k * tiles_step + t

            @pl.when(t < cnt[0, k])
            def _():
                block = feat[src[k, t], :, half * LANES : (half + 1) * LANES]
                acc[slot[k, t]] += jnp.dot(vals[n], block, preferred_element_type=F32)

    per_x = acc.shape[0] // XN
    for s in range(acc.shape[0]):
        out[s // per_x, pl.ds((s % per_x) * BLOCK, BLOCK), :] = acc[s].astype(BF16)
    if half == 0:
        for x in range(XN):
            out[x, pl.ds(per_x * BLOCK, ID_ROWS), :] = ids[x]


def forward_products(src, slot, cnt, feats, vals, ids, half):
    slots = XN * YN * CAP
    rows = YN * CAP * BLOCK + (ID_ROWS if half == 0 else 0)
    return pl.pallas_call(
        functools.partial(forward_kernel, half),
        out_shape=jax.ShapeDtypeStruct((XN, rows, LANES), BF16),
        in_specs=[SMEM] * 3 + [VMEM] * 7,
        out_specs=VMEM,
        scratch_shapes=[pltpu.VMEM((slots, BLOCK, LANES), F32)],
        compiler_params=params(),
        cost_estimate=cost(vals.shape[0] * 2 * BLOCK * BLOCK * LANES, 9 << 20),
        name="tile_forward",
    )(src, slot, cnt, *feats, vals, ids)


def gather_kernel(blocks_dev, me, recv, ids, *refs):
    if len(refs) > 4:
        total = refs[0][...]
        for k in (1, 2, 3):
            total = total + refs[k][...].astype(F32)
        refs[4][...] = total.astype(BF16)
        refs = refs[5:]
    for k, out in enumerate(refs):
        y = lax.rem(me[0] + k, YN)
        for b in range(blocks_dev):
            total = jnp.zeros((BLOCK, LANES), F32)
            for x in range(XN):
                for c in range(CAP):
                    j = y * CAP + c
                    hit = ids[pl.ds(x * YN * CAP + j, 1), :] == float(b)
                    start = pl.multiple_of(j * BLOCK, BLOCK)
                    part = recv[x, pl.ds(start, BLOCK), :].astype(F32)
                    total = total + jnp.where(hit, part, 0.0)
            out[pl.ds(b * BLOCK, BLOCK), :] = total.astype(out.dtype)


def gather_blocks(me, recv, ids, blocks_dev, earlier=()):
    nodes = blocks_dev * BLOCK
    half = jax.ShapeDtypeStruct((nodes, LANES), BF16)
    own = jax.ShapeDtypeStruct((nodes, LANES), F32)
    outs = (own, half, half, half)
    if earlier:
        outs = (half,) + outs
    return pl.pallas_call(
        functools.partial(gather_kernel, blocks_dev),
        out_shape=outs,
        in_specs=[SMEM] + [VMEM] * (2 + len(earlier)),
        out_specs=(VMEM,) * len(outs),
        compiler_params=params(),
        cost_estimate=cost(1 << 20, 4 << 20),
        name="block_sums",
    )(me, recv, ids, *earlier)


def dense_kernel(me, agg0, own, far1, far2, far3, weight, cot, act, g0, g1, s1, s2, s3, mine, wg):
    total = own[...]
    for far in (far1, far2, far3):
        total = total + far[...].astype(F32)
    agg = jnp.concatenate([agg0[...], total.astype(BF16)], axis=1)
    w = weight[...]
    pre = jnp.dot(agg, w, preferred_element_type=F32)
    sig = 1.0 / (1.0 + jnp.exp(-pre))
    act[...] = (pre * sig).astype(BF16)
    slope = sig * (1.0 + pre * (1.0 - sig))
    pre_grad = (cot[...].astype(F32) * slope).astype(BF16)
    grad = lax.dot_general(
        pre_grad, w, (((1,), (1,)), ((), ())), preferred_element_type=F32
    ).astype(BF16)
    nodes = cot.shape[0]
    wg[...] = lax.dot_general(
        agg, pre_grad, (((0,), (0,)), ((), ())), preferred_element_type=F32
    )
    g0[...] = grad[:, :LANES]
    g1[...] = grad[:, LANES:]
    rows = wg.shape[0] // YN

    def piece(k):
        y = lax.rem(me[0] + k, YN)
        return wg[pl.ds(pl.multiple_of(y * rows, rows), rows), :]

    mine[...] = piece(0)
    for k, out in ((1, s1), (2, s2), (3, s3)):
        chunk = piece(k).astype(BF16)
        out[pl.ds(0, nodes), :] = grad[:, :LANES]
        out[pl.ds(nodes, rows), :] = chunk[:, :LANES]
        out[pl.ds(nodes + rows, rows), :] = chunk[:, LANES:]


def dense(me, agg0, own, far, weight, cot):
    nodes, channels = cot.shape
    rows = channels // YN
    half = jax.ShapeDtypeStruct((nodes, LANES), BF16)
    send = jax.ShapeDtypeStruct((nodes + 2 * rows, LANES), BF16)
    outs = (
        jax.ShapeDtypeStruct((nodes, channels), BF16),
        half,
        half,
        send,
        send,
        send,
        jax.ShapeDtypeStruct((rows, channels), F32),
    )
    return pl.pallas_call(
        dense_kernel,
        out_shape=outs,
        in_specs=[SMEM] + [VMEM] * 7,
        out_specs=(VMEM,) * len(outs),
        scratch_shapes=[pltpu.VMEM((channels, channels), F32)],
        compiler_params=params(),
        cost_estimate=cost(6 * nodes * channels * channels, 5 << 20),
        name="dense_layer",
    )(me, agg0, own, *far, weight, cot)


def pick_slots(blocks_dev, me, grads, ids, place):
    for k, grad in enumerate(grads):
        y = lax.rem(me[0] - k + YN, YN)
        blocks = [grad[pl.ds(b * BLOCK, BLOCK), :].astype(F32) for b in range(blocks_dev)]
        for c in range(CAP):
            j = y * CAP + c
            start = pl.multiple_of(j * BLOCK, BLOCK)
            for i in range(XN):
                x, out = place(i)
                row = ids[pl.ds(x * YN * CAP + j, 1), :]
                picked = jnp.where(row == 0.0, blocks[0], 0.0)
                for b in range(1, blocks_dev):
                    picked = jnp.where(row == float(b), blocks[b], picked)
                out[pl.ds(start, BLOCK), :] = picked.astype(BF16)


def reply0_kernel(blocks_dev, me, g0, r1, r2, r3, ids, mine, out):
    pick_slots(blocks_dev, me, (g0, r1, r2, r3), ids, lambda i: (i, out.at[i]))
    nodes = blocks_dev * BLOCK
    rows = mine.shape[0]
    left, right = mine[:, :LANES], mine[:, LANES:]
    for r in (r1, r2, r3):
        left = left + r[pl.ds(nodes, rows), :].astype(F32)
        right = right + r[pl.ds(nodes + rows, rows), :].astype(F32)
    base = YN * CAP * BLOCK
    per_x = rows // XN
    for x in range(XN):
        part = slice(x * per_x, (x + 1) * per_x)
        out[x, pl.ds(base, per_x), :] = left[part].astype(BF16)
        out[x, pl.ds(base + per_x, per_x), :] = right[part].astype(BF16)


def reply_first(me, grads, ids, mine, blocks_dev):
    rows = YN * CAP * BLOCK + 2 * (mine.shape[0] // XN)
    return pl.pallas_call(
        functools.partial(reply0_kernel, blocks_dev),
        out_shape=jax.ShapeDtypeStruct((XN, rows, LANES), BF16),
        in_specs=[SMEM] + [VMEM] * 6,
        out_specs=VMEM,
        compiler_params=params(),
        cost_estimate=cost(1 << 20, 4 << 20),
        name="slot_replies",
    )(me, *grads, ids, mine)


def reply1_kernel(blocks_dev, me, g0, r1, r2, r3, ids, *outs):
    pick_slots(
        blocks_dev, me, (g0, r1, r2, r3), ids, lambda i: (lax.rem(me[1] + i, XN), outs[i])
    )


def reply_second(me, grads, ids, blocks_dev):
    out = jax.ShapeDtypeStruct((YN * CAP * BLOCK, LANES), BF16)
    return pl.pallas_call(
        functools.partial(reply1_kernel, blocks_dev),
        out_shape=(out,) * XN,
        in_specs=[SMEM] + [VMEM] * 5,
        out_specs=(VMEM,) * XN,
        compiler_params=params(),
        cost_estimate=cost(1 << 20, 4 << 20),
        name="slot_replies",
    )(me, *grads, ids)


def tile_sums(src, slot, cnt, vals, acc, block_of, store):
    steps = cnt.shape[1]
    tiles_step = vals.shape[0] // steps
    for k in range(steps):
        acc[...] = jnp.zeros_like(acc)
        for t in range(tiles_step):
            n = k * tiles_step + t

            @pl.when(t < cnt[0, k])
            def _():
                acc[src[k, t]] += lax.dot_general(
                    vals[n],
                    block_of(slot[k, t]),
                    (((0,), (0,)), ((), ())),
                    preferred_element_type=F32,
                )

        store(k)


def backward0_kernel(src, slot, cnt, ret, vals, out, own, piece, acc):
    per_x = YN * CAP

    def block_of(s):
        start = pl.multiple_of(lax.rem(s, per_x) * BLOCK, BLOCK)
        return ret[lax.div(s, per_x), pl.ds(start, BLOCK), :]

    def store(k):
        for b in range(acc.shape[0]):
            if k == HALF:
                own[pl.ds(b * BLOCK, BLOCK), :] = acc[b]
            else:
                out[k, pl.ds(b * BLOCK, BLOCK), :] = acc[b].astype(BF16)

    tile_sums(src, slot, cnt, vals, acc, block_of, store)
    base = per_x * BLOCK
    rows = piece.shape[1]
    for side in range(2):
        total = ret[0, pl.ds(base + side * rows, rows), :].astype(F32)
        for x in range(1, XN):
            total = total + ret[x, pl.ds(base + side * rows, rows), :].astype(F32)
        for i in range(piece.shape[0]):
            piece[i, :, side * LANES : (side + 1) * LANES] = total


def backward_first(src, slot, cnt, ret, vals, blocks_dev, copies):
    nodes = blocks_dev * BLOCK
    rows = (ret.shape[1] - YN * CAP * BLOCK) // 2
    return pl.pallas_call(
        backward0_kernel,
        out_shape=(
            jax.ShapeDtypeStruct((2 * HALF + 1, nodes, LANES), BF16),
            jax.ShapeDtypeStruct((nodes, LANES), F32),
            jax.ShapeDtypeStruct((copies, rows, 2 * LANES), F32),
        ),
        in_specs=[SMEM] * 3 + [VMEM] * 2,
        out_specs=(VMEM,) * 3,
        scratch_shapes=[pltpu.VMEM((blocks_dev, BLOCK, LANES), F32)],
        compiler_params=params(),
        cost_estimate=cost(vals.shape[0] * 2 * BLOCK * BLOCK * LANES, 9 << 20),
        name="tile_backward",
    )(src, slot, cnt, ret, vals)


def backward1_kernel(
    src, slot, cnt, me, b0, b1, b2, b3, vals, first, om2, om1, op1, op2, own, acc, ret
):
    per_x = YN * CAP
    for k, back in enumerate((b0, b1, b2, b3)):
        ret[lax.rem(me[1] - k + XN, XN)] = back[...]
    outs = (om2, om1, own, op1, op2)

    def block_of(s):
        start = pl.multiple_of(lax.rem(s, per_x) * BLOCK, BLOCK)
        return ret[lax.div(s, per_x), pl.ds(start, BLOCK), :]

    def store(k):
        for b in range(acc.shape[0]):
            spot = pl.ds(b * BLOCK, BLOCK)
            if k == HALF:
                own[spot, :] = acc[b]
            else:
                outs[k][spot, :LANES] = first[k, spot, :]
                outs[k][spot, LANES:] = acc[b].astype(BF16)

    tile_sums(src, slot, cnt, vals, acc, block_of, store)


def backward_second(src, slot, cnt, me, back, vals, first, blocks_dev):
    nodes = blocks_dev * BLOCK
    send = jax.ShapeDtypeStruct((nodes, 2 * LANES), BF16)
    own = jax.ShapeDtypeStruct((nodes, LANES), F32)
    return pl.pallas_call(
        backward1_kernel,
        out_shape=(send,) * 4 + (own,),
        in_specs=[SMEM] * 4 + [VMEM] * 6,
        out_specs=(VMEM,) * 5,
        scratch_shapes=[
            pltpu.VMEM((blocks_dev, BLOCK, LANES), F32),
            pltpu.VMEM((XN, YN * CAP * BLOCK, LANES), BF16),
        ],
        compiler_params=params(),
        cost_estimate=cost(vals.shape[0] * 2 * BLOCK * BLOCK * LANES, 9 << 20),
        name="tile_backward",
    )(src, slot, cnt, me, *back, vals, first)


def final_kernel(own0, own1, r1, r2, r3, r4, out):
    for h, own in enumerate((own0, own1)):
        total = own[...]
        for r in (r1, r2, r3, r4):
            total = total + r[:, h * LANES : (h + 1) * LANES].astype(F32)
        out[:, h * LANES : (h + 1) * LANES] = total.astype(BF16)


def final_sum(*parts):
    return pl.pallas_call(
        final_kernel,
        out_shape=jax.ShapeDtypeStruct((parts[0].shape[0], 2 * LANES), BF16),
        in_specs=[VMEM] * len(parts),
        out_specs=VMEM,
        compiler_params=params(),
        cost_estimate=cost(1 << 20, 2 << 20),
        name="grad_sum",
    )(*parts)


def spread_kernel(parts, out):
    total = parts[0]
    for i in range(1, parts.shape[0]):
        total = total + parts[i]
    for i in range(out.shape[0]):
        out[i] = total


def sum_and_spread(parts, copies):
    return pl.pallas_call(
        spread_kernel,
        out_shape=jax.ShapeDtypeStruct((copies,) + parts.shape[1:], F32),
        in_specs=[VMEM],
        out_specs=VMEM,
        compiler_params=params(),
        cost_estimate=cost(1 << 16, 1 << 20),
        name="sum_and_spread",
    )(parts)


def dom_exchange(value, groups):
    return lax.all_to_all(
        value, "dom", split_axis=0, concat_axis=0, tiled=True, axis_index_groups=groups
    )


def per_device(
    features, weight, tile_values, tile_source, tile_slot, slot_block, tile_count, cotangent
):
    blocks_dev = features.shape[0] // BLOCK
    channels = features.shape[1]
    vals = tile_values.reshape(-1, BLOCK, BLOCK)
    src, slot, cnt = tile_source[0], tile_slot[0], tile_count
    rank = lax.axis_index("rows")
    me = jnp.stack([rank % YN, rank // YN]).astype(jnp.int32)
    id_rows = jnp.broadcast_to(
        jnp.pad(slot_block.reshape(XN, -1), ((0, 0), (0, ID_ROWS - YN * CAP)))[..., None],
        (XN, ID_ROWS, LANES),
    ).astype(BF16)
    inner = 8
    outer = lax.axis_size("dom") // inner
    near_groups = [[i * inner + j for j in range(inner)] for i in range(outer)]
    far_groups = [[i * inner + j for i in range(outer)] for j in range(inner)]

    near = [dom_shift(features, -o) for o in OFFSETS]
    feats = [near[0], near[1], features, near[2], near[3]]
    feats = [f.reshape(blocks_dev, BLOCK, channels) for f in feats]
    got0 = x_exchange(forward_products(src, slot, cnt, feats, vals, id_rows, 0))
    got1 = x_exchange(forward_products(src, slot, cnt, feats, vals, id_rows, 1))
    ids = got0[:, YN * CAP * BLOCK :, :][:, : YN * CAP].astype(F32)
    ids = ids.reshape(XN * YN * CAP, LANES)
    sums = gather_blocks(me, got0, ids, blocks_dev)
    far = [y_shift(sums[k], k) for k in (1, 2, 3)]
    agg0, *sums = gather_blocks(me, got1, ids, blocks_dev, (sums[0], *far))
    far = [y_shift(sums[k], k) for k in (1, 2, 3)]
    activations, g0, g1, s1, s2, s3, mine = dense(me, agg0, sums[0], far, weight, cotangent)

    grads = [g0] + [y_shift(s, k) for k, s in ((1, s1), (2, s2), (3, s3))]
    back0 = x_exchange(reply_first(me, grads, ids, mine, blocks_dev))
    grads = [g1] + [y_shift(g1, k) for k in (1, 2, 3)]
    reply = reply_second(me, grads, ids, blocks_dev)
    back1 = [reply[0]] + [x_shift(reply[k], k) for k in (1, 2, 3)]
    first, own0, piece = backward_first(src, slot, cnt, back0, vals, blocks_dev, inner)
    piece = sum_and_spread(dom_exchange(piece, near_groups), outer)
    *terms, own1 = backward_second(src, slot, cnt, me, back1, vals, first, blocks_dev)
    terms = [dom_shift(t, o) for t, o in zip(terms, OFFSETS)]
    piece = sum_and_spread(dom_exchange(piece, far_groups), XN * YN)
    whole = lax.all_to_all(piece, "rows", split_axis=0, concat_axis=0, tiled=True)
    whole = whole.reshape(XN, YN, channels // (XN * YN), channels)
    weight_grad = whole.transpose(1, 0, 2, 3).reshape(channels, channels)
    feature_grad = final_sum(own0, own1, *terms)
    return (activations, feature_grad, weight_grad)


def solution(mesh):
    return jax.shard_map(
        per_device,
        mesh=mesh,
        in_specs=(
            P(("dom", "rows"), None),
            P(),
            P(("dom", "rows"), None, None, None, None),
            P(("dom", "rows"), None, None),
            P(("dom", "rows"), None, None),
            P(("dom", "rows"), None),
            P(("dom", "rows"), None),
            P(("dom", "rows"), None),
        ),
        out_specs=(P(("dom", "rows"), None), P(("dom", "rows"), None), P()),
        check_vma=False,
    )
```

time: 279 us -> 245 us (0.88)
  starting transfers between devices: 146 us -> 115 us
  waiting for transfers between devices: 88.6 us -> 70.6 us
  blocking collectives: 13.7 us -> 28 us
  Pallas kernels: 17.5 us -> 22 us
  local copies, waits for them, and re-layouts: 9.24 us -> 6.1 us
    ppermute x16 -> x8, starting transfers between devices: 71.7 us -> 38 us  [dom_shift(): lax.ppermute(value, 'dom', [(i, (i + steps) % count) for i in range(count)])]
    all_to_all x4 -> x2, waiting for transfers between devices: 40 us -> 11 us  [x_exchange(): lax.all_to_all(value, 'rows', split_axis=0, concat_axis=0, tiled=True, ax...]
    all_to_all x1 -> x2, blocking collectives: 13.7 us -> 28 us  [the longest x1 18.8 us: x_exchange(): lax.all_to_all(value, 'rows', split_axis=0, concat_axis=0, tiled=True, ax...]
    all_to_all x4 -> x2, starting transfers between devices: 16.5 us -> 7.16 us  [x_exchange(): lax.all_to_all(value, 'rows', split_axis=0, concat_axis=0, tiled=True, ax...]
    ppermute x0 -> x3, starting transfers between devices: none -> 9.08 us  [x_shift(): return lax.ppermute(value, 'rows', pairs)]
    ppermute x12, waiting for transfers between devices: 31 us -> 38.8 us  [y_shift(): return lax.ppermute(value, 'rows', pairs)]
    pallas_call x10 -> x12, Pallas kernels: 17.5 us -> 22 us  [the longest x2 6.63 us: forward_products(): pl.pallas_call(functools.partial(forward_kernel, half), out_shape=jax.Sha...]
    ppermute x12, starting transfers between devices: 41.8 us -> 44.9 us  [y_shift(): return lax.ppermute(value, 'rows', pairs)]
  transfers between devices with their start and end apart: 35 -> 27, of which waited for: 13 -> 14; matrix products, arithmetic and copies ran while one was open for 1% -> 1% of each run, Pallas kernels for 4% -> 4%
where the time goes in v2:
time: 245 us; the launch traced here: 243 us
  starting transfers between devices  115 us (47%)
  waiting for transfers between devices  70.6 us (29%)
  blocking collectives  28 us (11%)
  Pallas kernels  22 us (9%)
  local copies, waits for them, and re-layouts  6.1 us (2%)
    ppermute x12, starting transfers between devices, y_shift(): return lax.ppermute(value, 'rows', pairs)  44.9 us
    ppermute x12, waiting for transfers between devices, y_shift(): return lax.ppermute(value, 'rows', pairs)  38.8 us
    ppermute x8, starting transfers between devices, dom_shift(): lax.ppermute(value, 'dom', [(i, (i + steps) % count) for i in range(count)])  38 us
    all_to_all x1, blocking collectives, x_exchange(): lax.all_to_all(value, 'rows', split_axis=0, concat_axis=0, tiled=True, ax...  18.8 us
    ppermute x8, waiting for transfers between devices, dom_shift(): lax.ppermute(value, 'dom', [(i, (i + steps) % count) for i in range(count)])  18.2 us
    all_to_all x2, waiting for transfers between devices, x_exchange(): lax.all_to_all(value, 'rows', split_axis=0, concat_axis=0, tiled=True, ax...  11 us
    all_to_all x1, starting transfers between devices, dom_exchange(): lax.all_to_all(value, 'dom', split_axis=0, concat_axis=0, tiled=True, axi...  9.51 us
    all_to_all x1, blocking collectives, dom_exchange(): lax.all_to_all(value, 'dom', split_axis=0, concat_axis=0, tiled=True, axi...  9.14 us
  transfers between devices with their start and end apart: 27, of which 14 were waited for; matrix products, arithmetic and copies ran while one was open for 1% of the time, Pallas kernels for 4%

profile of v2, /device:TPU:1, one launch (start us, length us, event | category | flops | bytes accessed | tf_op | source)
XLA Modules:
  0.0 243.1 jit_solution(12365524200629573138)
XLA Ops:
  0.6 4.0 %collective-permute-start = (bf16[512,256]{1,0:T(8,128)(2,1)}, bf16[512,256]{1,0:T(8,128)(2,1)S(1)}, u32[]{:S(2)}, u32[]{:S(2)}) collective-permute-start(bf16[512,256]{1,0:T(8,128)(2,1)} %param.8), channel_id=1, source_target_pairs={{0,32},{16,48},{32,64},{48,80},{64,96},{80,112},{96,128},{112,144}... | collective-permute-start | bytes 786440 | tf_op jit(solution)/shard_map/ppermute | solution.py:35
  4.7 4.7 %collective-permute-start.1 = (bf16[512,256]{1,0:T(8,128)(2,1)}, bf16[512,256]{1,0:T(8,128)(2,1)S(1)}, u32[]{:S(2)}, u32[]{:S(2)}) collective-permute-start(bf16[512,256]{1,0:T(8,128)(2,1)} %param.8), channel_id=1, source_target_pairs={{0,16},{16,32},{32,48},{48,64},{64,80},{80,96},{96,112},{112,128},... | collective-permute-start | bytes 786440 | tf_op jit(solution)/shard_map/ppermute | solution.py:35
  9.4 11.1 %collective-permute-start.2 = (bf16[512,256]{1,0:T(8,128)(2,1)}, bf16[512,256]{1,0:T(8,128)(2,1)S(1)}, u32[]{:S(2)}, u32[]{:S(2)}) collective-permute-start(bf16[512,256]{1,0:T(8,128)(2,1)} %param.8), channel_id=1, source_target_pairs={{0,1008},{16,0},{32,16},{48,32},{64,48},{80,64},{96,80},{112,96},{... | collective-permute-start | bytes 786440 | tf_op jit(solution)/shard_map/ppermute | solution.py:35
  20.6 6.3 %collective-permute-start.3 = (bf16[512,256]{1,0:T(8,128)(2,1)}, bf16[512,256]{1,0:T(8,128)(2,1)S(1)}, u32[]{:S(2)}, u32[]{:S(2)}) collective-permute-start(bf16[512,256]{1,0:T(8,128)(2,1)} %param.8), channel_id=1, source_target_pairs={{0,992},{16,1008},{32,0},{48,16},{64,32},{80,48},{96,64},{112,80},... | collective-permute-start | bytes 786440 | tf_op jit(solution)/shard_map/ppermute | solution.py:35
  29.2 6.6 %collective-permute-done.3 = bf16[512,256]{1,0:T(8,128)(2,1)S(1)} collective-permute-done((bf16[512,256]{1,0:T(8,128)(2,1)}, bf16[512,256]{1,0:T(8,128)(2,1)S(1)}, u32[]{:S(2)}, u32[]{:S(2)}) %collective-permute-start.3) | collective-permute-done | bytes 262176 | tf_op jit(solution)/shard_map/ppermute | solution.py:35
  41.9 3.6 %all-to-all-start.1 = ((bf16[4,1040,128]{2,1,0:T(8,128)(2,1)}), bf16[4,1040,128]{2,1,0:T(8,128)(2,1)S(1)}, u32[]{:S(2)}, u32[]{:S(2)}) async-start(bf16[4,1040,128]{2,1,0:T(8,128)(2,1)} %tile_forward.3), calls=%async_computation.1 | async-start | bytes 2129920 | tf_op jit(solution)/shard_map/all_to_all | solution.py:47
  48.9 11.0 %all-to-all-done.1.recv = bf16[4,1040,128]{2,1,0:T(8,128)(2,1)S(1)} async-done(((bf16[4,1040,128]{2,1,0:T(8,128)(2,1)}), bf16[4,1040,128]{2,1,0:T(8,128)(2,1)S(1)}, u32[]{:S(2)}, u32[]{:S(2)}) %all-to-all-start.1) | async-done | bytes 1064992 | tf_op jit(solution)/shard_map/all_to_all | solution.py:47
  67.0 4.5 %collective-permute-start.5 = (bf16[512,128]{1,0:T(8,128)(2,1)S(1)}, bf16[512,128]{1,0:T(8,128)(2,1)S(1)}, u32[]{:S(2)}, u32[]{:S(2)}) collective-permute-start(bf16[512,128]{1,0:T(8,128)(2,1)S(1)} %get-tuple-element.33), channel_id=1, source_target_pairs={{0,2},{1,3},{2,0},{3,1},{4,6},{5,7},{6,4},{7,5},{8,10},{9,11},{10,... | collective-permute-start | bytes 393224 | tf_op jit(solution)/shard_map/ppermute | solution.py:40
  71.5 5.5 %collective-permute-start.6 = (bf16[512,128]{1,0:T(8,128)(2,1)S(1)}, bf16[512,128]{1,0:T(8,128)(2,1)S(1)}, u32[]{:S(2)}, u32[]{:S(2)}) collective-permute-start(bf16[512,128]{1,0:T(8,128)(2,1)S(1)} %get-tuple-element.34), channel_id=1, source_target_pairs={{0,3},{1,0},{2,1},{3,2},{4,7},{5,4},{6,5},{7,6},{8,11},{9,8},{10,9... | collective-permute-start | bytes 393224 | tf_op jit(solution)/shard_map/ppermute | solution.py:40
  77.0 8.7 %collective-permute-done.6.refs_3_ = bf16[512,128]{1,0:T(8,128)(2,1)S(1)} collective-permute-done((bf16[512,128]{1,0:T(8,128)(2,1)S(1)}, bf16[512,128]{1,0:T(8,128)(2,1)S(1)}, u32[]{:S(2)}, u32[]{:S(2)}) %collective-permute-start.6) | collective-permute-done | bytes 131104 | tf_op jit(solution)/shard_map/ppermute | solution.py:40
  89.1 5.8 %collective-permute-start.8 = (bf16[512,128]{1,0:T(8,128)(2,1)S(1)}, bf16[512,128]{1,0:T(8,128)(2,1)S(1)}, u32[]{:S(2)}, u32[]{:S(2)}) collective-permute-start(bf16[512,128]{1,0:T(8,128)(2,1)S(1)} %get-tuple-element.38), channel_id=1, source_target_pairs={{0,2},{1,3},{2,0},{3,1},{4,6},{5,7},{6,4},{7,5},{8,10},{9,11},{10,... | collective-permute-start | bytes 393224 | tf_op jit(solution)/shard_map/ppermute | solution.py:40
  100.6 6.1 %collective-permute-done.9.far3 = bf16[512,128]{1,0:T(8,128)(2,1)S(1)} collective-permute-done((bf16[512,128]{1,0:T(8,128)(2,1)S(1)}, bf16[512,128]{1,0:T(8,128)(2,1)S(1)}, u32[]{:S(2)}, u32[]{:S(2)}) %collective-permute-start.9) | collective-permute-done | bytes 131104 | tf_op jit(solution)/shard_map/ppermute | solution.py:40
  110.7 4.6 %collective-permute-start.11 = (bf16[640,128]{1,0:T(8,128)(2,1)S(1)}, bf16[640,128]{1,0:T(8,128)(2,1)S(1)}, u32[]{:S(2)}, u32[]{:S(2)}) collective-permute-start(bf16[640,128]{1,0:T(8,128)(2,1)S(1)} %get-tuple-element.43), channel_id=1, source_target_pairs={{0,2},{1,3},{2,0},{3,1},{4,6},{5,7},{6,4},{7,5},{8,10},{9,11},{10,... | collective-permute-start | bytes 491528 | tf_op jit(solution)/shard_map/ppermute | solution.py:40
  115.4 3.6 %collective-permute-start.12 = (bf16[640,128]{1,0:T(8,128)(2,1)S(1)}, bf16[640,128]{1,0:T(8,128)(2,1)S(1)}, u32[]{:S(2)}, u32[]{:S(2)}) collective-permute-start(bf16[640,128]{1,0:T(8,128)(2,1)S(1)} %get-tuple-element.44), channel_id=1, source_target_pairs={{0,3},{1,0},{2,1},{3,2},{4,7},{5,4},{6,5},{7,6},{8,11},{9,8},{10,9... | collective-permute-start | bytes 491528 | tf_op jit(solution)/shard_map/ppermute | solution.py:40
  122.6 7.1 %collective-permute-done.12.r3 = bf16[640,128]{1,0:T(8,128)(2,1)S(1)} collective-permute-done((bf16[640,128]{1,0:T(8,128)(2,1)S(1)}, bf16[640,128]{1,0:T(8,128)(2,1)S(1)}, u32[]{:S(2)}, u32[]{:S(2)}) %collective-permute-start.12) | collective-permute-done | bytes 163872 | tf_op jit(solution)/shard_map/ppermute | solution.py:40
  130.7 18.8 %all_to_all.30.ret = bf16[4,1056,128]{2,1,0:T(8,128)(2,1)S(1)} all-to-all(bf16[4,1056,128]{2,1,0:T(8,128)(2,1)S(1)} %slot_replies.2), channel_id=1, replica_groups={{0,4,8,12},{1,5,9,13},{2,6,10,14},{3,7,11,15},{16,20,24,28},{17,21,25,2..., dimensions={0} | all-to-all | bytes 2162688 | tf_op jit(solution)/shard_map/all_to_all | solution.py:47
  152.4 9.1 %all_to_all.31.parts = f32[8,16,256]{2,1,0:T(8,128)S(1)} all-to-all(f32[8,16,256]{2,1,0:T(8,128)S(1)} %get-tuple-element.58), channel_id=1, replica_groups={{0,16,32,48,64,80,96,112},{128,144,160,176,192,208,224,240},{256,272,28..., dimensions={0} | all-to-all | bytes 262144 | tf_op jit(solution)/shard_map/all_to_all | solution.py:404
  162.2 9.5 %all-to-all-start.4 = ((f32[8,16,256]{2,1,0:T(8,128)}), f32[8,16,256]{2,1,0:T(8,128)S(1)}, u32[]{:S(2)}, u32[]{:S(2)}) async-start(f32[8,16,256]{2,1,0:T(8,128)} %sum_and_spread.2), calls=%async_computation.4 | async-start | bytes 262144 | tf_op jit(solution)/shard_map/all_to_all | solution.py:404
  174.8 6.0 %collective-permute-start.14 = (bf16[512,128]{1,0:T(8,128)(2,1)S(1)}, bf16[512,128]{1,0:T(8,128)(2,1)S(1)}, u32[]{:S(2)}, u32[]{:S(2)}) collective-permute-start(bf16[512,128]{1,0:T(8,128)(2,1)S(1)} %get-tuple-element.47.g0), channel_id=1, source_target_pairs={{0,2},{1,3},{2,0},{3,1},{4,6},{5,7},{6,4},{7,5},{8,10},{9,11},{10,... | collective-permute-start | bytes 393224 | tf_op jit(solution)/shard_map/ppermute | solution.py:40
  184.1 6.4 %collective-permute-done.14.r2 = bf16[512,128]{1,0:T(8,128)(2,1)S(1)} collective-permute-done((bf16[512,128]{1,0:T(8,128)(2,1)S(1)}, bf16[512,128]{1,0:T(8,128)(2,1)S(1)}, u32[]{:S(2)}, u32[]{:S(2)}) %collective-permute-start.14) | collective-permute-done | bytes 131104 | tf_op jit(solution)/shard_map/ppermute | solution.py:40
  198.4 4.2 %collective-permute-start.17 = (bf16[1024,128]{1,0:T(8,128)(2,1)S(1)}, bf16[1024,128]{1,0:T(8,128)(2,1)S(1)}, u32[]{:S(2)}, u32[]{:S(2)}) collective-permute-start(bf16[1024,128]{1,0:T(8,128)(2,1)S(1)} %get-tuple-element.50), channel_id=1, source_target_pairs={{0,8},{1,9},{2,10},{3,11},{4,12},{5,13},{6,14},{7,15},{8,0},{9,1},... | collective-permute-start | bytes 786440 | tf_op jit(solution)/shard_map/ppermute | solution.py:54
  205.5 6.0 %all-to-all-start.5 = ((f32[16,16,256]{2,1,0:T(8,128)}), f32[16,16,256]{2,1,0:T(8,128)}, u32[]{:S(2)}, u32[]{:S(2)}) async-start(f32[16,16,256]{2,1,0:T(8,128)} %sum_and_spread.3), calls=%async_computation.5 | async-start | bytes 524288 | tf_op jit(solution)/shard_map/all_to_all | solution.py:450
  219.1 4.3 %collective-permute-start.20 = (bf16[512,256]{1,0:T(8,128)(2,1)S(1)}, bf16[512,256]{1,0:T(8,128)(2,1)S(1)}, u32[]{:S(2)}, u32[]{:S(2)}) collective-permute-start(bf16[512,256]{1,0:T(8,128)(2,1)S(1)} %get-tuple-element.55), channel_id=1, source_target_pairs={{0,1008},{16,0},{32,16},{48,32},{64,48},{80,64},{96,80},{112,96},{... | collective-permute-start | bytes 786440 | tf_op jit(solution)/shard_map/ppermute | solution.py:35
  232.5 8.1 %collective-permute-done.22.r4 = bf16[512,256]{1,0:T(8,128)(2,1)S(1)} collective-permute-done((bf16[512,256]{1,0:T(8,128)(2,1)S(1)}, bf16[512,256]{1,0:T(8,128)(2,1)S(1)}, u32[]{:S(2)}, u32[]{:S(2)}) %collective-permute-start.22) | collective-permute-done | bytes 262176 | tf_op jit(solution)/shard_map/ppermute | solution.py:35
  (69 shorter events, 76.4 us)
Async XLA Ops:
  0.6 28.6 %collective-permute-start = (bf16[512,256]{1,0:T(8,128)(2,1)}, bf16[512,256]{1,0:T(8,128)(2,1)S(1)}, u32[]{:S(2)}, u32[]{:S(2)}) collective-permute-start(bf16[512,256]{1,0:T(8,128)(2,1)} %param.8), channel_id=1, source_target_pairs={{0,32},{16,48},{32,64},{48,80},{64,96},{80,112},{96,128},{112,144}... | collective-permute-start | bytes 786440 | tf_op jit(solution)/shard_map/ppermute | solution.py:35
  4.7 24.5 %collective-permute-start.1 = (bf16[512,256]{1,0:T(8,128)(2,1)}, bf16[512,256]{1,0:T(8,128)(2,1)S(1)}, u32[]{:S(2)}, u32[]{:S(2)}) collective-permute-start(bf16[512,256]{1,0:T(8,128)(2,1)} %param.8), channel_id=1, source_target_pairs={{0,16},{16,32},{32,48},{48,64},{64,80},{80,96},{96,112},{112,128},... | collective-permute-start | bytes 786440 | tf_op jit(solution)/shard_map/ppermute | solution.py:35
  9.4 19.8 %collective-permute-start.2 = (bf16[512,256]{1,0:T(8,128)(2,1)}, bf16[512,256]{1,0:T(8,128)(2,1)S(1)}, u32[]{:S(2)}, u32[]{:S(2)}) collective-permute-start(bf16[512,256]{1,0:T(8,128)(2,1)} %param.8), channel_id=1, source_target_pairs={{0,1008},{16,0},{32,16},{48,32},{64,48},{80,64},{96,80},{112,96},{... | collective-permute-start | bytes 786440 | tf_op jit(solution)/shard_map/ppermute | solution.py:35
  20.6 15.3 %collective-permute-start.3 = (bf16[512,256]{1,0:T(8,128)(2,1)}, bf16[512,256]{1,0:T(8,128)(2,1)S(1)}, u32[]{:S(2)}, u32[]{:S(2)}) collective-permute-start(bf16[512,256]{1,0:T(8,128)(2,1)} %param.8), channel_id=1, source_target_pairs={{0,992},{16,1008},{32,0},{48,16},{64,32},{80,48},{96,64},{112,80},... | collective-permute-start | bytes 786440 | tf_op jit(solution)/shard_map/ppermute | solution.py:35
  41.9 18.0 %all-to-all-start.1 = ((bf16[4,1040,128]{2,1,0:T(8,128)(2,1)}), bf16[4,1040,128]{2,1,0:T(8,128)(2,1)S(1)}, u32[]{:S(2)}, u32[]{:S(2)}) async-start(bf16[4,1040,128]{2,1,0:T(8,128)(2,1)} %tile_forward.3), calls=%async_computation.1 | async-start | bytes 2129920 | tf_op jit(solution)/shard_map/all_to_all | solution.py:47
  59.9 17.1 %all-to-all-start = ((bf16[4,1024,128]{2,1,0:T(8,128)(2,1)}), bf16[4,1024,128]{2,1,0:T(8,128)(2,1)S(1)}, u32[]{:S(2)}, u32[]{:S(2)}) async-start(bf16[4,1024,128]{2,1,0:T(8,128)(2,1)} %tile_forward.2), calls=%async_computation | async-start | bytes 2097152 | tf_op jit(solution)/shard_map/all_to_all | solution.py:47
  65.0 12.0 %collective-permute-start.4 = (bf16[512,128]{1,0:T(8,128)(2,1)S(1)}, bf16[512,128]{1,0:T(8,128)(2,1)S(1)}, u32[]{:S(2)}, u32[]{:S(2)}) collective-permute-start(bf16[512,128]{1,0:T(8,128)(2,1)S(1)} %get-tuple-element.32), channel_id=1, source_target_pairs={{0,1},{1,2},{2,3},{3,0},{4,5},{5,6},{6,7},{7,4},{8,9},{9,10},{10,1... | collective-permute-start | bytes 393224 | tf_op jit(solution)/shard_map/ppermute | solution.py:40
  71.5 14.2 %collective-permute-start.6 = (bf16[512,128]{1,0:T(8,128)(2,1)S(1)}, bf16[512,128]{1,0:T(8,128)(2,1)S(1)}, u32[]{:S(2)}, u32[]{:S(2)}) collective-permute-start(bf16[512,128]{1,0:T(8,128)(2,1)S(1)} %get-tuple-element.34), channel_id=1, source_target_pairs={{0,3},{1,0},{2,1},{3,2},{4,7},{5,4},{6,5},{7,6},{8,11},{9,8},{10,9... | collective-permute-start | bytes 393224 | tf_op jit(solution)/shard_map/ppermute | solution.py:40
  89.1 11.5 %collective-permute-start.8 = (bf16[512,128]{1,0:T(8,128)(2,1)S(1)}, bf16[512,128]{1,0:T(8,128)(2,1)S(1)}, u32[]{:S(2)}, u32[]{:S(2)}) collective-permute-start(bf16[512,128]{1,0:T(8,128)(2,1)S(1)} %get-tuple-element.38), channel_id=1, source_target_pairs={{0,2},{1,3},{2,0},{3,1},{4,6},{5,7},{6,4},{7,5},{8,10},{9,11},{10,... | collective-permute-start | bytes 393224 | tf_op jit(solution)/shard_map/ppermute | solution.py:40
  94.9 11.8 %collective-permute-start.9 = (bf16[512,128]{1,0:T(8,128)(2,1)S(1)}, bf16[512,128]{1,0:T(8,128)(2,1)S(1)}, u32[]{:S(2)}, u32[]{:S(2)}) collective-permute-start(bf16[512,128]{1,0:T(8,128)(2,1)S(1)} %get-tuple-element.39), channel_id=1, source_target_pairs={{0,3},{1,0},{2,1},{3,2},{4,7},{5,4},{6,5},{7,6},{8,11},{9,8},{10,9... | collective-permute-start | bytes 393224 | tf_op jit(solution)/shard_map/ppermute | solution.py:40
  108.5 10.5 %collective-permute-start.10 = (bf16[640,128]{1,0:T(8,128)(2,1)S(1)}, bf16[640,128]{1,0:T(8,128)(2,1)S(1)}, u32[]{:S(2)}, u32[]{:S(2)}) collective-permute-start(bf16[640,128]{1,0:T(8,128)(2,1)S(1)} %get-tuple-element.42), channel_id=1, source_target_pairs={{0,1},{1,2},{2,3},{3,0},{4,5},{5,6},{6,7},{7,4},{8,9},{9,10},{10,1... | collective-permute-start | bytes 491528 | tf_op jit(solution)/shard_map/ppermute | solution.py:40
  110.7 11.8 %collective-permute-start.11 = (bf16[640,128]{1,0:T(8,128)(2,1)S(1)}, bf16[640,128]{1,0:T(8,128)(2,1)S(1)}, u32[]{:S(2)}, u32[]{:S(2)}) collective-permute-start(bf16[640,128]{1,0:T(8,128)(2,1)S(1)} %get-tuple-element.43), channel_id=1, source_target_pairs={{0,2},{1,3},{2,0},{3,1},{4,6},{5,7},{6,4},{7,5},{8,10},{9,11},{10,... | collective-permute-start | bytes 491528 | tf_op jit(solution)/shard_map/ppermute | solution.py:40
  115.4 14.3 %collective-permute-start.12 = (bf16[640,128]{1,0:T(8,128)(2,1)S(1)}, bf16[640,128]{1,0:T(8,128)(2,1)S(1)}, u32[]{:S(2)}, u32[]{:S(2)}) collective-permute-start(bf16[640,128]{1,0:T(8,128)(2,1)S(1)} %get-tuple-element.44), channel_id=1, source_target_pairs={{0,3},{1,0},{2,1},{3,2},{4,7},{5,4},{6,5},{7,6},{8,11},{9,8},{10,9... | collective-permute-start | bytes 491528 | tf_op jit(solution)/shard_map/ppermute | solution.py:40
  162.2 42.6 %all-to-all-start.4 = ((f32[8,16,256]{2,1,0:T(8,128)}), f32[8,16,256]{2,1,0:T(8,128)S(1)}, u32[]{:S(2)}, u32[]{:S(2)}) async-start(f32[8,16,256]{2,1,0:T(8,128)} %sum_and_spread.2), calls=%async_computation.4 | async-start | bytes 262144 | tf_op jit(solution)/shard_map/all_to_all | solution.py:404
  171.7 12.4 %collective-permute-start.13 = (bf16[512,128]{1,0:T(8,128)(2,1)S(1)}, bf16[512,128]{1,0:T(8,128)(2,1)S(1)}, u32[]{:S(2)}, u32[]{:S(2)}) collective-permute-start(bf16[512,128]{1,0:T(8,128)(2,1)S(1)} %get-tuple-element.47.g0), channel_id=1, source_target_pairs={{0,1},{1,2},{2,3},{3,0},{4,5},{5,6},{6,7},{7,4},{8,9},{9,10},{10,1... | collective-permute-start | bytes 393224 | tf_op jit(solution)/shard_map/ppermute | solution.py:40
  174.8 15.7 %collective-permute-start.14 = (bf16[512,128]{1,0:T(8,128)(2,1)S(1)}, bf16[512,128]{1,0:T(8,128)(2,1)S(1)}, u32[]{:S(2)}, u32[]{:S(2)}) collective-permute-start(bf16[512,128]{1,0:T(8,128)(2,1)S(1)} %get-tuple-element.47.g0), channel_id=1, source_target_pairs={{0,2},{1,3},{2,0},{3,1},{4,6},{5,7},{6,4},{7,5},{8,10},{9,11},{10,... | collective-permute-start | bytes 393224 | tf_op jit(solution)/shard_map/ppermute | solution.py:40
  180.8 13.3 %collective-permute-start.15 = (bf16[512,128]{1,0:T(8,128)(2,1)S(1)}, bf16[512,128]{1,0:T(8,128)(2,1)S(1)}, u32[]{:S(2)}, u32[]{:S(2)}) collective-permute-start(bf16[512,128]{1,0:T(8,128)(2,1)S(1)} %get-tuple-element.47.g0), channel_id=1, source_target_pairs={{0,3},{1,0},{2,1},{3,2},{4,7},{5,4},{6,5},{7,6},{8,11},{9,8},{10,9... | collective-permute-start | bytes 393224 | tf_op jit(solution)/shard_map/ppermute | solution.py:40
  195.7 15.9 %collective-permute-start.16 = (bf16[1024,128]{1,0:T(8,128)(2,1)}, bf16[1024,128]{1,0:T(8,128)(2,1)S(1)}, u32[]{:S(2)}, u32[]{:S(2)}) collective-permute-start(bf16[1024,128]{1,0:T(8,128)(2,1)} %get-tuple-element.49), channel_id=1, source_target_pairs={{0,4},{1,5},{2,6},{3,7},{4,8},{5,9},{6,10},{7,11},{8,12},{9,13},{1... | collective-permute-start | bytes 786440 | tf_op jit(solution)/shard_map/ppermute | solution.py:54
  198.4 14.0 %collective-permute-start.17 = (bf16[1024,128]{1,0:T(8,128)(2,1)S(1)}, bf16[1024,128]{1,0:T(8,128)(2,1)S(1)}, u32[]{:S(2)}, u32[]{:S(2)}) collective-permute-start(bf16[1024,128]{1,0:T(8,128)(2,1)S(1)} %get-tuple-element.50), channel_id=1, source_target_pairs={{0,8},{1,9},{2,10},{3,11},{4,12},{5,13},{6,14},{7,15},{8,0},{9,1},... | collective-permute-start | bytes 786440 | tf_op jit(solution)/shard_map/ppermute | solution.py:54
  202.6 11.6 %collective-permute-start.18 = (bf16[1024,128]{1,0:T(8,128)(2,1)S(1)}, bf16[1024,128]{1,0:T(8,128)(2,1)S(1)}, u32[]{:S(2)}, u32[]{:S(2)}) collective-permute-start(bf16[1024,128]{1,0:T(8,128)(2,1)S(1)} %get-tuple-element.51), channel_id=1, source_target_pairs={{0,12},{1,13},{2,14},{3,15},{4,0},{5,1},{6,2},{7,3},{8,4},{9,5},{1... | collective-permute-start | bytes 786440 | tf_op jit(solution)/shard_map/ppermute | solution.py:54
  205.5 35.9 %all-to-all-start.5 = ((f32[16,16,256]{2,1,0:T(8,128)}), f32[16,16,256]{2,1,0:T(8,128)}, u32[]{:S(2)}, u32[]{:S(2)}) async-start(f32[16,16,256]{2,1,0:T(8,128)} %sum_and_spread.3), calls=%async_computation.5 | async-start | bytes 524288 | tf_op jit(solution)/shard_map/all_to_all | solution.py:450
  217.2 11.8 %collective-permute-start.19 = (bf16[512,256]{1,0:T(8,128)(2,1)S(1)}, bf16[512,256]{1,0:T(8,128)(2,1)S(1)}, u32[]{:S(2)}, u32[]{:S(2)}) collective-permute-start(bf16[512,256]{1,0:T(8,128)(2,1)S(1)} %get-tuple-element.54), channel_id=1, source_target_pairs={{0,992},{16,1008},{32,0},{48,16},{64,32},{80,48},{96,64},{112,80},... | collective-permute-start | bytes 786440 | tf_op jit(solution)/shard_map/ppermute | solution.py:35
  219.1 10.9 %collective-permute-start.20 = (bf16[512,256]{1,0:T(8,128)(2,1)S(1)}, bf16[512,256]{1,0:T(8,128)(2,1)S(1)}, u32[]{:S(2)}, u32[]{:S(2)}) collective-permute-start(bf16[512,256]{1,0:T(8,128)(2,1)S(1)} %get-tuple-element.55), channel_id=1, source_target_pairs={{0,1008},{16,0},{32,16},{48,32},{64,48},{80,64},{96,80},{112,96},{... | collective-permute-start | bytes 786440 | tf_op jit(solution)/shard_map/ppermute | solution.py:35
  227.0 13.6 %collective-permute-start.22 = (bf16[512,256]{1,0:T(8,128)(2,1)S(1)}, bf16[512,256]{1,0:T(8,128)(2,1)S(1)}, u32[]{:S(2)}, u32[]{:S(2)}) collective-permute-start(bf16[512,256]{1,0:T(8,128)(2,1)S(1)} %get-tuple-element.57), channel_id=1, source_target_pairs={{0,32},{16,48},{32,64},{48,80},{64,96},{80,112},{96,128},{112,144}... | collective-permute-start | bytes 786440 | tf_op jit(solution)/shard_map/ppermute | solution.py:35
  (11 other events, 126.3 us)

commit v3 on v0

v3 whole, which is shorter than its diff:
```python
import functools

import jax
import jax.numpy as jnp
from jax import lax
from jax.experimental import pallas as pl
from jax.experimental.pallas import tpu as pltpu
from jax.sharding import PartitionSpec as P

BLOCK = 128
HALF = 2
CAP = 2
XN = 4
YN = 4
LANES = 128
ID_ROWS = 16

OFFSETS = (-2, -1, 1, 2)
VMEM = pl.BlockSpec(memory_space=pltpu.VMEM)
ANY = pl.BlockSpec(memory_space=pl.ANY)
SMEM = pl.BlockSpec(memory_space=pltpu.SMEM)
GATHER_FLOPS = 10**11
REPLY_FLOPS = 10**11
BACK_FLOPS = 10**11
FINAL_FLOPS = 2*10**10
BF16 = jnp.bfloat16
F32 = jnp.float32


def params():
    return pltpu.CompilerParams(vmem_limit_bytes=24 * 1024 * 1024)


def cost(flops, nbytes):
    return pl.CostEstimate(flops=flops, bytes_accessed=nbytes, transcendentals=0)


def dom_shift(value, steps):
    count = lax.axis_size("dom")
    return lax.ppermute(value, "dom", [(i, (i + steps) % count) for i in range(count)])


Y_GROUPS = [[x * YN + y for y in range(YN)] for x in range(XN)]


def y_exchange(value):
    return lax.all_to_all(
        value, "rows", split_axis=0, concat_axis=0, tiled=True, axis_index_groups=Y_GROUPS
    )


def x_shift(value, steps):
    pairs = [(x * YN + y, (x + steps) % XN * YN + y) for x in range(XN) for y in range(YN)]
    return lax.ppermute(value, "rows", pairs)


def forward_kernel(src, slot, cnt, me, fm2, fm1, f0, fp1, fp2, vals, ids, *refs):
    outs, acc = refs[:-1], refs[-1]
    acc[...] = jnp.zeros_like(acc)
    feats = (fm2, fm1, f0, fp1, fp2)
    tiles_step = vals.shape[0] // len(feats)
    for k, feat in enumerate(feats):
        for t in range(tiles_step):
            live = t < cnt[0, k]
            block = feat[src[k, t]]
            block = jnp.where(live, block, jnp.zeros_like(block))
            acc[slot[k, t]] += jnp.dot(
                vals[k * tiles_step + t], block, preferred_element_type=F32
            )
    per_x = acc.shape[0] // XN
    for k in range(XN):
        x = lax.rem(me[1] + k, XN)
        for j in range(per_x):
            total = acc[x * per_x + j].astype(BF16)
            for h in range(2):
                part = total[:, h * LANES : (h + 1) * LANES]
                outs[h * XN + k][pl.ds(j * BLOCK, BLOCK), :] = part
        outs[k][pl.ds(per_x * BLOCK, ID_ROWS), :] = ids[x]


def forward_products(src, slot, cnt, me, feats, vals, ids):
    slots = XN * YN * CAP
    rows = YN * CAP * BLOCK
    first = jax.ShapeDtypeStruct((rows + ID_ROWS, LANES), BF16)
    second = jax.ShapeDtypeStruct((rows, LANES), BF16)
    return pl.pallas_call(
        forward_kernel,
        out_shape=(first,) * XN + (second,) * XN,
        in_specs=[SMEM] * 4 + [VMEM] * 7,
        out_specs=(VMEM,) * (2 * XN),
        scratch_shapes=[pltpu.VMEM((slots, BLOCK, 2 * LANES), F32)],
        compiler_params=params(),
        cost_estimate=cost(vals.shape[0] * 4 * BLOCK * BLOCK * LANES, 9 << 20),
        name="tile_forward",
    )(src, slot, cnt, me, *feats, vals, ids)


def id_row(ids, j):
    return ids[j : j + 1, :]


def gather_kernel(blocks_dev, n_after, *refs):
    recv, with_ids = refs[0:XN], refs[XN : 2 * XN]
    out = refs[2 * XN + n_after]
    base = YN * CAP * BLOCK
    ids = [w[pl.ds(base, ID_ROWS), :].astype(F32) for w in with_ids]
    for y in range(YN):
        totals = [jnp.zeros((BLOCK, LANES), F32) for _ in range(blocks_dev)]
        for k in range(XN):
            for c in range(CAP):
                j = y * CAP + c
                row = id_row(ids[k], j)
                part = recv[k][pl.ds(j * BLOCK, BLOCK), :].astype(F32)
                for b in range(blocks_dev):
                    totals[b] = totals[b] + jnp.where(row == float(b), part, 0.0)
        for b in range(blocks_dev):
            out[y, pl.ds(b * BLOCK, BLOCK), :] = totals[b].astype(BF16)


def gather_blocks(recv, with_ids, blocks_dev, after=()):
    return pl.pallas_call(
        functools.partial(gather_kernel, blocks_dev, len(after)),
        out_shape=jax.ShapeDtypeStruct((YN, blocks_dev * BLOCK, LANES), BF16),
        in_specs=[VMEM] * (2 * XN) + [ANY] * len(after),
        out_specs=VMEM,
        compiler_params=params(),
        cost_estimate=cost(GATHER_FLOPS, 4 << 20),
        name="block_sums",
    )(*recv, *with_ids, *after)


def dense_kernel(p0, p1, weight, cot, act, s0, s1, wg):
    halves = []
    for p in (p0, p1):
        total = p[0].astype(F32)
        for y in range(1, YN):
            total = total + p[y].astype(F32)
        halves.append(total.astype(BF16))
    agg = jnp.concatenate(halves, axis=1)
    w = weight[...]
    pre = jnp.dot(agg, w, preferred_element_type=F32)
    sig = 1.0 / (1.0 + jnp.exp(-pre))
    act[...] = (pre * sig).astype(BF16)
    slope = sig * (1.0 + pre * (1.0 - sig))
    pre_grad = (cot[...].astype(F32) * slope).astype(BF16)
    grad = lax.dot_general(
        pre_grad, w, (((1,), (1,)), ((), ())), preferred_element_type=F32
    ).astype(BF16)
    nodes = cot.shape[0]
    wg[...] = lax.dot_general(
        agg, pre_grad, (((0,), (0,)), ((), ())), preferred_element_type=F32
    )
    rows = wg.shape[0] // YN
    for y in range(YN):
        chunk = wg[pl.ds(y * rows, rows), :].astype(BF16)
        s0[y, pl.ds(0, nodes), :] = grad[:, :LANES]
        s0[y, pl.ds(nodes, rows), :] = chunk[:, :LANES]
        s0[y, pl.ds(nodes + rows, rows), :] = chunk[:, LANES:]
        s1[y] = grad[:, LANES:]


def dense(p0, p1, weight, cot):
    nodes, channels = cot.shape
    rows = channels // YN
    outs = (
        jax.ShapeDtypeStruct((nodes, channels), BF16),
        jax.ShapeDtypeStruct((YN, nodes + 2 * rows, LANES), BF16),
        jax.ShapeDtypeStruct((YN, nodes, LANES), BF16),
    )
    return pl.pallas_call(
        dense_kernel,
        out_shape=outs,
        in_specs=[VMEM] * 4,
        out_specs=(VMEM,) * len(outs),
        scratch_shapes=[pltpu.VMEM((channels, channels), F32)],
        compiler_params=params(),
        cost_estimate=cost(6 * nodes * channels * channels, 5 << 20),
        name="dense_layer",
    )(p0, p1, weight, cot)


def reply_kernel(blocks_dev, carries, n_after, *refs):
    me, grads, with_ids = refs[0], refs[1], refs[2 : 2 + XN]
    outs = refs[2 + XN + n_after :]
    nodes = blocks_dev * BLOCK
    base = YN * CAP * BLOCK
    ids = [w[pl.ds(base, ID_ROWS), :].astype(F32) for w in with_ids]
    for y in range(YN):
        blocks = [grads[y, pl.ds(b * BLOCK, BLOCK), :].astype(F32) for b in range(blocks_dev)]
        for c in range(CAP):
            j = y * CAP + c
            for k in range(XN):
                row = id_row(ids[k], j)
                picked = jnp.where(row == 0.0, blocks[0], 0.0)
                for b in range(1, blocks_dev):
                    picked = jnp.where(row == float(b), blocks[b], picked)
                outs[k][pl.ds(j * BLOCK, BLOCK), :] = picked.astype(BF16)
    if carries:
        total = refs[-1]
        outs = outs[:-1]
        rows = total.shape[0] // 2
        total[...] = grads[0, pl.ds(nodes, 2 * rows), :].astype(F32)
        for y in range(1, YN):
            total[...] += grads[y, pl.ds(nodes, 2 * rows), :].astype(F32)
        per_x = rows // XN
        for k in range(XN):
            start = pl.multiple_of(lax.rem(me[1] - k + XN, XN) * per_x, per_x)
            for side in range(2):
                part = total[pl.ds(side * rows + start, per_x), :].astype(BF16)
                outs[k][pl.ds(base + side * per_x, per_x), :] = part


def reply_slots(me, grads, with_ids, blocks_dev, carries, after=()):
    rows = YN * CAP * BLOCK
    extra = grads.shape[1] - blocks_dev * BLOCK
    out = jax.ShapeDtypeStruct((rows + extra // XN, LANES), BF16)
    return pl.pallas_call(
        functools.partial(reply_kernel, blocks_dev, carries, len(after)),
        out_shape=(out,) * XN,
        in_specs=[SMEM] + [VMEM] * (1 + XN) + [ANY] * len(after),
        out_specs=(VMEM,) * XN,
        scratch_shapes=[pltpu.VMEM((extra, LANES), F32)] if carries else [],
        compiler_params=params(),
        cost_estimate=cost(REPLY_FLOPS, 4 << 20),
        name="slot_replies",
    )(me, grads, *with_ids, *after)


def piece_kernel(b0, b1, b2, b3, after, out):
    base = YN * CAP * BLOCK
    rows = out.shape[1]
    for side in range(2):
        spot = pl.ds(base + side * rows, rows)
        total = b0[spot, :].astype(F32)
        for arrived in (b1, b2, b3):
            total = total + arrived[spot, :].astype(F32)
        for i in range(out.shape[0]):
            out[i, :, side * LANES : (side + 1) * LANES] = total


def piece_sum(back, copies, after):
    rows = (back[0].shape[0] - YN * CAP * BLOCK) // 2
    return pl.pallas_call(
        piece_kernel,
        out_shape=jax.ShapeDtypeStruct((copies, rows, 2 * LANES), F32),
        in_specs=[VMEM] * XN + [ANY],
        out_specs=VMEM,
        compiler_params=params(),
        cost_estimate=cost(1 << 16, 1 << 20),
        name="piece_sum",
    )(*back, after)


def backward_kernel(src, slot, cnt, me, *refs):
    back, vals, outs, (acc, ret) = refs[: 2 * XN], refs[2 * XN], refs[2 * XN + 1 : -2], refs[-2:]
    per_x = YN * CAP
    for k in range(XN):
        x = lax.rem(me[1] + k, XN)
        for h in range(2):
            for j in range(per_x):
                part = back[h * XN + k][pl.ds(j * BLOCK, BLOCK), :]
                ret[x * per_x + j, :, h * LANES : (h + 1) * LANES] = part
    steps = cnt.shape[1]
    tiles_step = vals.shape[0] // steps
    acc[...] = jnp.zeros_like(acc)
    for k in range(steps):
        for t in range(tiles_step):
            block = ret[slot[k, t]]
            block = jnp.where(t < cnt[0, k], block, jnp.zeros_like(block))
            acc[k, src[k, t]] += lax.dot_general(
                vals[k * tiles_step + t],
                block,
                (((0,), (0,)), ((), ())),
                preferred_element_type=F32,
            )
    for k, out in enumerate(outs):
        for b in range(acc.shape[1]):
            out[pl.ds(b * BLOCK, BLOCK), :] = acc[k, b].astype(out.dtype)


def backward_products(src, slot, cnt, me, back0, back1, vals, blocks_dev):
    nodes = blocks_dev * BLOCK
    steps = cnt.shape[1]
    send = jax.ShapeDtypeStruct((nodes, 2 * LANES), BF16)
    own = jax.ShapeDtypeStruct((nodes, 2 * LANES), F32)
    return pl.pallas_call(
        backward_kernel,
        out_shape=(send, send, own, send, send),
        in_specs=[SMEM] * 4 + [VMEM] * (2 * XN + 1),
        out_specs=(VMEM,) * 5,
        scratch_shapes=[
            pltpu.VMEM((steps, blocks_dev, BLOCK, 2 * LANES), F32),
            pltpu.VMEM((XN * YN * CAP, BLOCK, 2 * LANES), BF16),
        ],
        compiler_params=params(),
        cost_estimate=cost(BACK_FLOPS, 9 << 20),
        name="tile_backward",
    )(src, slot, cnt, me, *back0, *back1, vals)


def final_kernel(own, r1, r2, r3, r4, out):
    total = own[...]
    for r in (r1, r2, r3, r4):
        total = total + r[...].astype(F32)
    out[...] = total.astype(BF16)


def final_sum(*parts):
    return pl.pallas_call(
        final_kernel,
        out_shape=jax.ShapeDtypeStruct(parts[0].shape, BF16),
        in_specs=[VMEM] * len(parts),
        out_specs=VMEM,
        compiler_params=params(),
        cost_estimate=cost(FINAL_FLOPS, 2 << 20),
        name="grad_sum",
    )(*parts)


def spread_kernel(parts, out):
    total = parts[0]
    for i in range(1, parts.shape[0]):
        total = total + parts[i]
    for i in range(out.shape[0]):
        out[i] = total


def sum_and_spread(parts, copies):
    return pl.pallas_call(
        spread_kernel,
        out_shape=jax.ShapeDtypeStruct((copies,) + parts.shape[1:], F32),
        in_specs=[VMEM],
        out_specs=VMEM,
        compiler_params=params(),
        cost_estimate=cost(1 << 16, 1 << 20),
        name="sum_and_spread",
    )(parts)


def dom_exchange(value, groups):
    return lax.all_to_all(
        value, "dom", split_axis=0, concat_axis=0, tiled=True, axis_index_groups=groups
    )


def per_device(
    features, weight, tile_values, tile_source, tile_slot, slot_block, tile_count, cotangent
):
    blocks_dev = features.shape[0] // BLOCK
    channels = features.shape[1]
    vals = tile_values.reshape(-1, BLOCK, BLOCK)
    src, slot, cnt = tile_source[0], tile_slot[0], tile_count
    rank = lax.axis_index("rows")
    me = jnp.stack([rank % YN, rank // YN]).astype(jnp.int32)
    id_rows = jnp.broadcast_to(
        jnp.pad(slot_block.reshape(XN, -1), ((0, 0), (0, ID_ROWS - YN * CAP)))[..., None],
        (XN, ID_ROWS, LANES),
    ).astype(BF16)
    inner = 8
    outer = lax.axis_size("dom") // inner
    near_groups = [[i * inner + j for j in range(inner)] for i in range(outer)]
    far_groups = [[i * inner + j for i in range(outer)] for j in range(inner)]

    near = [dom_shift(features, -o) for o in OFFSETS]
    feats = [near[0], near[1], features, near[2], near[3]]
    feats = [f.reshape(blocks_dev, BLOCK, channels) for f in feats]
    sent = forward_products(src, slot, cnt, me, feats, vals, id_rows)
    got0 = [sent[0]] + [x_shift(sent[k], k) for k in range(1, XN)]
    got1 = [sent[XN]] + [x_shift(sent[XN + k], k) for k in range(1, XN)]
    sums0 = gather_blocks(got0, got0, blocks_dev)
    p0 = y_exchange(sums0)
    p1 = y_exchange(gather_blocks(got1, got0, blocks_dev, (sums0,)))
    activations, s0, s1 = dense(p0, p1, weight, cotangent)

    reply0 = reply_slots(me, y_exchange(s0), got0, blocks_dev, True)
    back0 = [reply0[0]] + [x_shift(reply0[k], -k) for k in range(1, XN)]
    reply1 = reply_slots(me, y_exchange(s1), got0, blocks_dev, False, (reply0[0],))
    back1 = [reply1[0]] + [x_shift(reply1[k], -k) for k in range(1, XN)]
    piece = piece_sum(back0, inner, reply1[0])
    terms = list(backward_products(src, slot, cnt, me, back0, back1, vals, blocks_dev))
    own = terms.pop(HALF)
    terms = [dom_shift(t, o) for t, o in zip(terms, OFFSETS)]
    piece = sum_and_spread(dom_exchange(piece, near_groups), outer)
    piece = sum_and_spread(dom_exchange(piece, far_groups), XN * YN)
    whole = lax.all_to_all(piece, "rows", split_axis=0, concat_axis=0, tiled=True)
    whole = whole.reshape(XN, YN, channels // (XN * YN), channels)
    weight_grad = whole.transpose(1, 0, 2, 3).reshape(channels, channels)
    feature_grad = final_sum(own, *terms)
    return (activations, feature_grad, weight_grad)


def solution(mesh):
    return jax.shard_map(
        per_device,
        mesh=mesh,
        in_specs=(
            P(("dom", "rows"), None),
            P(),
            P(("dom", "rows"), None, None, None, None),
            P(("dom", "rows"), None, None),
            P(("dom", "rows"), None, None),
            P(("dom", "rows"), None),
            P(("dom", "rows"), None),
            P(("dom", "rows"), None),
        ),
        out_specs=(P(("dom", "rows"), None), P(("dom", "rows"), None), P()),
        check_vma=False,
    )
```

time: 752 us -> 210 us (0.28)
  waiting for transfers between devices: 615 us -> 32.9 us
  starting transfers between devices: 65.2 us -> 112 us
  blocking collectives: 0 us -> 32 us
  matrix products: 19.5 us -> 0 us
  Pallas kernels: 0 us -> 14.7 us
  between operations: 14.6 us -> 1.07 us
  local copies, waits for them, and re-layouts: 26.9 us -> 15.7 us
  other arithmetic: 8.5 us -> 0.1 us
    psum x1 -> x0, waiting for transfers between devices: 464 us -> none  [per_device(): weight_grad = lax.psum(local_grad, ('dom', 'rows'))]
    all_to_all x3 -> x5, waiting for transfers between devices: 97.2 us -> 15 us  [the longest x1 10.1 us: per_device(): lax.all_to_all(piece, 'rows', split_axis=0, concat_axis=0, tiled=True)]
    ppermute x10 -> x20, starting transfers between devices: 40.3 us -> 76.5 us  [the longest x8 38.4 us: dom_shift(): lax.ppermute(value, 'dom', [(i, (i + steps) % count) for i in range(count)])]
    ppermute x10 -> x20, waiting for transfers between devices: 53.3 us -> 18 us  [the longest x12 10.3 us: x_shift(): return lax.ppermute(value, 'rows', pairs)]
    all_to_all x0 -> x2, blocking collectives: none -> 32 us  [y_exchange(): lax.all_to_all(value, 'rows', split_axis=0, concat_axis=0, tiled=True, ax...]
    dot_general x20 -> x0, matrix products: 19.5 us -> none  [the longest x5 5.52 us: source_terms(): jnp.einsum('tji,tjf->tif', values[step_idx], picked, preferred_element_ty...]
    pallas_call x0 -> x11, Pallas kernels: none -> 14.7 us  [the longest x2 3.03 us: gather_blocks(): pl.pallas_call(functools.partial(gather_kernel, blocks_dev, len(after)),...]
    unnamed x14 -> x72, local copies, waits for them, and re-layouts: 2.9 us -> 14.6 us
  transfers between devices with their start and end apart: 14 -> 25, of which waited for: 13 -> 10; matrix products, arithmetic and copies ran while one was open for 5% -> 0% of each run, Pallas kernels for 0% -> 5%
where the time goes in v3:
time: 210 us; the launch traced here: 208 us
  starting transfers between devices  112 us (53%)
  waiting for transfers between devices  32.9 us (16%)
  blocking collectives  32 us (15%)
  local copies, waits for them, and re-layouts  15.7 us (7%)
  Pallas kernels  14.7 us (7%)
    ppermute x8, starting transfers between devices, dom_shift(): lax.ppermute(value, 'dom', [(i, (i + steps) % count) for i in range(count)])  38.4 us
    ppermute x12, starting transfers between devices, x_shift(): return lax.ppermute(value, 'rows', pairs)  38.1 us
    all_to_all x2, blocking collectives, y_exchange(): lax.all_to_all(value, 'rows', split_axis=0, concat_axis=0, tiled=True, ax...  32 us
    all_to_all x2, starting transfers between devices, dom_exchange(): lax.all_to_all(value, 'dom', split_axis=0, concat_axis=0, tiled=True, axi...  20.1 us
    unnamed x72, local copies, waits for them, and re-layouts  14.6 us
    ppermute x12, waiting for transfers between devices, x_shift(): return lax.ppermute(value, 'rows', pairs)  10.3 us
    all_to_all x1, waiting for transfers between devices, per_device(): lax.all_to_all(piece, 'rows', split_axis=0, concat_axis=0, tiled=True)  10.1 us
    all_to_all x1, starting transfers between devices, per_device(): lax.all_to_all(piece, 'rows', split_axis=0, concat_axis=0, tiled=True)  7.86 us
  transfers between devices with their start and end apart: 25, of which 10 were waited for; matrix products, arithmetic and copies ran while one was open for 0% of the time, Pallas kernels for 5%

profile of v3, /device:TPU:1, one launch (start us, length us, event | category | flops | bytes accessed | tf_op | source)
XLA Modules:
  0.0 208.5 jit_solution(1860188245439473814)
XLA Ops:
  0.6 4.0 %collective-permute-start = (bf16[512,256]{1,0:T(8,128)(2,1)}, bf16[512,256]{1,0:T(8,128)(2,1)S(1)}, u32[]{:S(2)}, u32[]{:S(2)}) collective-permute-start(bf16[512,256]{1,0:T(8,128)(2,1)} %param.8), channel_id=1, source_target_pairs={{0,32},{16,48},{32,64},{48,80},{64,96},{80,112},{96,128},{112,144}... | collective-permute-start | bytes 786440 | tf_op jit(solution)/shard_map/ppermute | solution.py:40
  4.7 4.7 %collective-permute-start.1 = (bf16[512,256]{1,0:T(8,128)(2,1)}, bf16[512,256]{1,0:T(8,128)(2,1)S(1)}, u32[]{:S(2)}, u32[]{:S(2)}) collective-permute-start(bf16[512,256]{1,0:T(8,128)(2,1)} %param.8), channel_id=1, source_target_pairs={{0,16},{16,32},{32,48},{48,64},{64,80},{80,96},{96,112},{112,128},... | collective-permute-start | bytes 786440 | tf_op jit(solution)/shard_map/ppermute | solution.py:40
  9.4 11.1 %collective-permute-start.2 = (bf16[512,256]{1,0:T(8,128)(2,1)}, bf16[512,256]{1,0:T(8,128)(2,1)S(1)}, u32[]{:S(2)}, u32[]{:S(2)}) collective-permute-start(bf16[512,256]{1,0:T(8,128)(2,1)} %param.8), channel_id=1, source_target_pairs={{0,1008},{16,0},{32,16},{48,32},{64,48},{80,64},{96,80},{112,96},{... | collective-permute-start | bytes 786440 | tf_op jit(solution)/shard_map/ppermute | solution.py:40
  20.6 6.3 %collective-permute-start.3 = (bf16[512,256]{1,0:T(8,128)(2,1)}, bf16[512,256]{1,0:T(8,128)(2,1)S(1)}, u32[]{:S(2)}, u32[]{:S(2)}) collective-permute-start(bf16[512,256]{1,0:T(8,128)(2,1)} %param.8), channel_id=1, source_target_pairs={{0,992},{16,1008},{32,0},{48,16},{64,32},{80,48},{96,64},{112,80},... | collective-permute-start | bytes 786440 | tf_op jit(solution)/shard_map/ppermute | solution.py:40
  29.2 6.6 %collective-permute-done.3 = bf16[512,256]{1,0:T(8,128)(2,1)S(1)} collective-permute-done((bf16[512,256]{1,0:T(8,128)(2,1)}, bf16[512,256]{1,0:T(8,128)(2,1)S(1)}, u32[]{:S(2)}, u32[]{:S(2)}) %collective-permute-start.3) | collective-permute-done | bytes 262176 | tf_op jit(solution)/shard_map/ppermute | solution.py:40
  45.4 4.0 %collective-permute-start.6 = (bf16[1040,128]{1,0:T(8,128)(2,1)S(1)}, bf16[1040,128]{1,0:T(8,128)(2,1)S(1)}, u32[]{:S(2)}, u32[]{:S(2)}) collective-permute-start(bf16[1040,128]{1,0:T(8,128)(2,1)S(1)} %get-tuple-element.30), channel_id=1, source_target_pairs={{0,12},{1,13},{2,14},{3,15},{4,0},{5,1},{6,2},{7,3},{8,4},{9,5},{1... | collective-permute-start | bytes 798728 | tf_op jit(solution)/shard_map/ppermute | solution.py:54
  51.9 3.7 %collective-permute-start.8 = (bf16[1024,128]{1,0:T(8,128)(2,1)S(1)}, bf16[1024,128]{1,0:T(8,128)(2,1)S(1)}, u32[]{:S(2)}, u32[]{:S(2)}) collective-permute-start(bf16[1024,128]{1,0:T(8,128)(2,1)S(1)} %get-tuple-element.33), channel_id=1, source_target_pairs={{0,8},{1,9},{2,10},{3,11},{4,12},{5,13},{6,14},{7,15},{8,0},{9,1},... | collective-permute-start | bytes 786440 | tf_op jit(solution)/shard_map/ppermute | solution.py:54
  61.7 3.5 %all-to-all-start = ((bf16[4,512,128]{2,1,0:T(8,128)(2,1)}), bf16[4,512,128]{2,1,0:T(8,128)(2,1)S(1)}, u32[]{:S(2)}, u32[]{:S(2)}) async-start(bf16[4,512,128]{2,1,0:T(8,128)(2,1)} %block_sums.2.refs_8_), calls=%async_computation | async-start | bytes 1048576 | tf_op jit(solution)/shard_map/all_to_all | solution.py:47
  65.1 3.3 %collective-permute-done.7.refs_1_ = bf16[1024,128]{1,0:T(8,128)(2,1)S(1)} collective-permute-done((bf16[1024,128]{1,0:T(8,128)(2,1)}, bf16[1024,128]{1,0:T(8,128)(2,1)S(1)}, u32[]{:S(2)}, u32[]{:S(2)}) %collective-permute-start.7) | collective-permute-done | bytes 262176 | tf_op jit(solution)/shard_map/ppermute | solution.py:54
  74.4 4.8 %all-to-all-done.p0 = bf16[4,512,128]{2,1,0:T(8,128)(2,1)S(1)} async-done(((bf16[4,512,128]{2,1,0:T(8,128)(2,1)}), bf16[4,512,128]{2,1,0:T(8,128)(2,1)S(1)}, u32[]{:S(2)}, u32[]{:S(2)}) %all-to-all-start) | async-done | bytes 524320 | tf_op jit(solution)/shard_map/all_to_all | solution.py:47
  79.2 15.8 %all_to_all.35.p1 = bf16[4,512,128]{2,1,0:T(8,128)(2,1)S(1)} all-to-all(bf16[4,512,128]{2,1,0:T(8,128)(2,1)S(1)} %block_sums.3), channel_id=1, replica_groups={{0,1,2,3},{4,5,6,7},{8,9,10,11},{12,13,14,15},{16,17,18,19},{20,21,22,2..., dimensions={0} | all-to-all | bytes 1048576 | tf_op jit(solution)/shard_map/all_to_all | solution.py:47
  96.3 16.2 %all_to_all.36.refs_1_ = bf16[4,640,128]{2,1,0:T(8,128)(2,1)S(1)} all-to-all(bf16[4,640,128]{2,1,0:T(8,128)(2,1)S(1)} %get-tuple-element.36), channel_id=1, replica_groups={{0,1,2,3},{4,5,6,7},{8,9,10,11},{12,13,14,15},{16,17,18,19},{20,21,22,2..., dimensions={0} | all-to-all | bytes 1310720 | tf_op jit(solution)/shard_map/all_to_all | solution.py:47
  112.5 4.1 %all-to-all-start.3 = ((bf16[4,512,128]{2,1,0:T(8,128)(2,1)}), bf16[4,512,128]{2,1,0:T(8,128)(2,1)S(1)}, u32[]{:S(2)}, u32[]{:S(2)}) async-start(bf16[4,512,128]{2,1,0:T(8,128)(2,1)} %get-tuple-element.41), calls=%async_computation.3 | async-start | bytes 1048576 | tf_op jit(solution)/shard_map/all_to_all | solution.py:47
  117.7 8.0 %collective-permute-start.10 = (bf16[1056,128]{1,0:T(8,128)(2,1)S(1)}, bf16[1056,128]{1,0:T(8,128)(2,1)S(1)}, u32[]{:S(2)}, u32[]{:S(2)}) collective-permute-start(bf16[1056,128]{1,0:T(8,128)(2,1)S(1)} %get-tuple-element.38), channel_id=1, source_target_pairs={{0,12},{1,13},{2,14},{3,15},{4,0},{5,1},{6,2},{7,3},{8,4},{9,5},{1... | collective-permute-start | bytes 811016 | tf_op jit(solution)/shard_map/ppermute | solution.py:54
  138.0 11.8 %all-to-all-start.4 = ((f32[8,16,256]{2,1,0:T(8,128)}), f32[8,16,256]{2,1,0:T(8,128)S(1)}, u32[]{:S(2)}, u32[]{:S(2)}) async-start(f32[8,16,256]{2,1,0:T(8,128)} %piece_sum.1), calls=%async_computation.4 | async-start | bytes 262144 | tf_op jit(solution)/shard_map/all_to_all | solution.py:341
  149.8 3.8 %collective-permute-start.13 = (bf16[1024,128]{1,0:T(8,128)(2,1)S(1)}, bf16[1024,128]{1,0:T(8,128)(2,1)S(1)}, u32[]{:S(2)}, u32[]{:S(2)}) collective-permute-start(bf16[1024,128]{1,0:T(8,128)(2,1)S(1)} %copy-done.26), channel_id=1, source_target_pairs={{0,12},{1,13},{2,14},{3,15},{4,0},{5,1},{6,2},{7,3},{8,4},{9,5},{1... | collective-permute-start | bytes 786440 | tf_op jit(solution)/shard_map/ppermute | solution.py:54
  153.6 2.9 %collective-permute-start.14 = (bf16[1024,128]{1,0:T(8,128)(2,1)S(1)}, bf16[1024,128]{1,0:T(8,128)(2,1)}, u32[]{:S(2)}, u32[]{:S(2)}) collective-permute-start(bf16[1024,128]{1,0:T(8,128)(2,1)S(1)} %copy-done.24), channel_id=1, source_target_pairs={{0,8},{1,9},{2,10},{3,11},{4,12},{5,13},{6,14},{7,15},{8,0},{9,1},... | collective-permute-start | bytes 786440 | tf_op jit(solution)/shard_map/ppermute | solution.py:54
  159.2 8.3 %all-to-all-start.5 = ((f32[8,16,256]{2,1,0:T(8,128)}), f32[8,16,256]{2,1,0:T(8,128)S(1)}, u32[]{:S(2)}, u32[]{:S(2)}) async-start(f32[8,16,256]{2,1,0:T(8,128)} %sum_and_spread.2), calls=%async_computation.5 | async-start | bytes 262144 | tf_op jit(solution)/shard_map/all_to_all | solution.py:341
  167.5 3.4 %collective-permute-done.15.refs_7_ = bf16[1024,128]{1,0:T(8,128)(2,1)} collective-permute-done((bf16[1024,128]{1,0:T(8,128)(2,1)S(1)}, bf16[1024,128]{1,0:T(8,128)(2,1)}, u32[]{:S(2)}, u32[]{:S(2)}) %collective-permute-start.15) | collective-permute-done | bytes 262176 | tf_op jit(solution)/shard_map/ppermute | solution.py:54
  171.0 3.0 %tile_backward.1 = (bf16[512,256]{1,0:T(8,128)(2,1)}, bf16[512,256]{1,0:T(8,128)(2,1)S(1)}, f32[512,256]{1,0:T(8,128)S(1)}, bf16[512,256]{1,0:T(8,128)(2,1)S(1)}, bf16[512,256]{1,0:T(8,128)(2,1)S(1)}) custom-call(s32[5,4]{1,0:T(8,128)S(1)} %copy-done.6, s32[5,4]{1,0:T(8,128)S(1)} %copy-done.8, s32[1,5]{1,0:T(1,128)S(1)} %copy-done.10, s32[2]{0:T(128)S(1)} %copy-done.12, ...), custom_call_target="tpu_custom_call" | custom-call | flops 99999997952 | bytes 9437184 | tf_op jit(solution)/shard_map/tile_backward/pallas_call | solution.py:286
  174.8 3.9 %collective-permute-start.16 = (bf16[512,256]{1,0:T(8,128)(2,1)}, bf16[512,256]{1,0:T(8,128)(2,1)S(1)}, u32[]{:S(2)}, u32[]{:S(2)}) collective-permute-start(bf16[512,256]{1,0:T(8,128)(2,1)} %get-tuple-element.47), channel_id=1, source_target_pairs={{0,992},{16,1008},{32,0},{48,16},{64,32},{80,48},{96,64},{112,80},... | collective-permute-start | bytes 786440 | tf_op jit(solution)/shard_map/ppermute | solution.py:40
  178.7 3.1 %collective-permute-start.17 = (bf16[512,256]{1,0:T(8,128)(2,1)S(1)}, bf16[512,256]{1,0:T(8,128)(2,1)S(1)}, u32[]{:S(2)}, u32[]{:S(2)}) collective-permute-start(bf16[512,256]{1,0:T(8,128)(2,1)S(1)} %get-tuple-element.48), channel_id=1, source_target_pairs={{0,1008},{16,0},{32,16},{48,32},{64,48},{80,64},{96,80},{112,96},{... | collective-permute-start | bytes 786440 | tf_op jit(solution)/shard_map/ppermute | solution.py:40
  187.8 7.9 %all-to-all-start.6 = ((f32[16,16,256]{2,1,0:T(8,128)}), f32[16,16,256]{2,1,0:T(8,128)S(1)}, u32[]{:S(2)}, u32[]{:S(2)}) async-start(f32[16,16,256]{2,1,0:T(8,128)} %sum_and_spread.3), calls=%async_computation.6 | async-start | bytes 524288 | tf_op jit(solution)/shard_map/all_to_all | solution.py:385
  197.6 10.1 %all-to-all-done.6 = f32[16,16,256]{2,1,0:T(8,128)S(1)} async-done(((f32[16,16,256]{2,1,0:T(8,128)}), f32[16,16,256]{2,1,0:T(8,128)S(1)}, u32[]{:S(2)}, u32[]{:S(2)}) %all-to-all-start.6) | async-done | bytes 262176 | tf_op jit(solution)/shard_map/all_to_all | solution.py:385
  (119 shorter events, 52.8 us)
Async XLA Ops:
  0.6 28.6 %collective-permute-start = (bf16[512,256]{1,0:T(8,128)(2,1)}, bf16[512,256]{1,0:T(8,128)(2,1)S(1)}, u32[]{:S(2)}, u32[]{:S(2)}) collective-permute-start(bf16[512,256]{1,0:T(8,128)(2,1)} %param.8), channel_id=1, source_target_pairs={{0,32},{16,48},{32,64},{48,80},{64,96},{80,112},{96,128},{112,144}... | collective-permute-start | bytes 786440 | tf_op jit(solution)/shard_map/ppermute | solution.py:40
  4.7 24.5 %collective-permute-start.1 = (bf16[512,256]{1,0:T(8,128)(2,1)}, bf16[512,256]{1,0:T(8,128)(2,1)S(1)}, u32[]{:S(2)}, u32[]{:S(2)}) collective-permute-start(bf16[512,256]{1,0:T(8,128)(2,1)} %param.8), channel_id=1, source_target_pairs={{0,16},{16,32},{32,48},{48,64},{64,80},{80,96},{96,112},{112,128},... | collective-permute-start | bytes 786440 | tf_op jit(solution)/shard_map/ppermute | solution.py:40
  9.4 19.8 %collective-permute-start.2 = (bf16[512,256]{1,0:T(8,128)(2,1)}, bf16[512,256]{1,0:T(8,128)(2,1)S(1)}, u32[]{:S(2)}, u32[]{:S(2)}) collective-permute-start(bf16[512,256]{1,0:T(8,128)(2,1)} %param.8), channel_id=1, source_target_pairs={{0,1008},{16,0},{32,16},{48,32},{64,48},{80,64},{96,80},{112,96},{... | collective-permute-start | bytes 786440 | tf_op jit(solution)/shard_map/ppermute | solution.py:40
  20.6 15.3 %collective-permute-start.3 = (bf16[512,256]{1,0:T(8,128)(2,1)}, bf16[512,256]{1,0:T(8,128)(2,1)S(1)}, u32[]{:S(2)}, u32[]{:S(2)}) collective-permute-start(bf16[512,256]{1,0:T(8,128)(2,1)} %param.8), channel_id=1, source_target_pairs={{0,992},{16,1008},{32,0},{48,16},{64,32},{80,48},{96,64},{112,80},... | collective-permute-start | bytes 786440 | tf_op jit(solution)/shard_map/ppermute | solution.py:40
  41.0 16.3 %collective-permute-start.4 = (bf16[1040,128]{1,0:T(8,128)(2,1)S(1)}, bf16[1040,128]{1,0:T(8,128)(2,1)S(1)}, u32[]{:S(2)}, u32[]{:S(2)}) collective-permute-start(bf16[1040,128]{1,0:T(8,128)(2,1)S(1)} %get-tuple-element.28), channel_id=1, source_target_pairs={{0,4},{1,5},{2,6},{3,7},{4,8},{5,9},{6,10},{7,11},{8,12},{9,13},{1... | collective-permute-start | bytes 798728 | tf_op jit(solution)/shard_map/ppermute | solution.py:54
  42.9 16.7 %collective-permute-start.5 = (bf16[1040,128]{1,0:T(8,128)(2,1)S(1)}, bf16[1040,128]{1,0:T(8,128)(2,1)S(1)}, u32[]{:S(2)}, u32[]{:S(2)}) collective-permute-start(bf16[1040,128]{1,0:T(8,128)(2,1)S(1)} %get-tuple-element.29), channel_id=1, source_target_pairs={{0,8},{1,9},{2,10},{3,11},{4,12},{5,13},{6,14},{7,15},{8,0},{9,1},... | collective-permute-start | bytes 798728 | tf_op jit(solution)/shard_map/ppermute | solution.py:54
  45.4 14.8 %collective-permute-start.6 = (bf16[1040,128]{1,0:T(8,128)(2,1)S(1)}, bf16[1040,128]{1,0:T(8,128)(2,1)S(1)}, u32[]{:S(2)}, u32[]{:S(2)}) collective-permute-start(bf16[1040,128]{1,0:T(8,128)(2,1)S(1)} %get-tuple-element.30), channel_id=1, source_target_pairs={{0,12},{1,13},{2,14},{3,15},{4,0},{5,1},{6,2},{7,3},{8,4},{9,5},{1... | collective-permute-start | bytes 798728 | tf_op jit(solution)/shard_map/ppermute | solution.py:54
  49.4 19.1 %collective-permute-start.7 = (bf16[1024,128]{1,0:T(8,128)(2,1)}, bf16[1024,128]{1,0:T(8,128)(2,1)S(1)}, u32[]{:S(2)}, u32[]{:S(2)}) collective-permute-start(bf16[1024,128]{1,0:T(8,128)(2,1)} %get-tuple-element.32), channel_id=1, source_target_pairs={{0,4},{1,5},{2,6},{3,7},{4,8},{5,9},{6,10},{7,11},{8,12},{9,13},{1... | collective-permute-start | bytes 786440 | tf_op jit(solution)/shard_map/ppermute | solution.py:54
  51.9 17.3 %collective-permute-start.8 = (bf16[1024,128]{1,0:T(8,128)(2,1)S(1)}, bf16[1024,128]{1,0:T(8,128)(2,1)S(1)}, u32[]{:S(2)}, u32[]{:S(2)}) collective-permute-start(bf16[1024,128]{1,0:T(8,128)(2,1)S(1)} %get-tuple-element.33), channel_id=1, source_target_pairs={{0,8},{1,9},{2,10},{3,11},{4,12},{5,13},{6,14},{7,15},{8,0},{9,1},... | collective-permute-start | bytes 786440 | tf_op jit(solution)/shard_map/ppermute | solution.py:54
  57.3 13.6 %collective-permute-start.9 = (bf16[1024,128]{1,0:T(8,128)(2,1)S(1)}, bf16[1024,128]{1,0:T(8,128)(2,1)}, u32[]{:S(2)}, u32[]{:S(2)}) collective-permute-start(bf16[1024,128]{1,0:T(8,128)(2,1)S(1)} %get-tuple-element.34), channel_id=1, source_target_pairs={{0,12},{1,13},{2,14},{3,15},{4,0},{5,1},{6,2},{7,3},{8,4},{9,5},{1... | collective-permute-start | bytes 786440 | tf_op jit(solution)/shard_map/ppermute | solution.py:54
  61.7 17.5 %all-to-all-start = ((bf16[4,512,128]{2,1,0:T(8,128)(2,1)}), bf16[4,512,128]{2,1,0:T(8,128)(2,1)S(1)}, u32[]{:S(2)}, u32[]{:S(2)}) async-start(bf16[4,512,128]{2,1,0:T(8,128)(2,1)} %block_sums.2.refs_8_), calls=%async_computation | async-start | bytes 1048576 | tf_op jit(solution)/shard_map/all_to_all | solution.py:47
  112.5 17.6 %all-to-all-start.3 = ((bf16[4,512,128]{2,1,0:T(8,128)(2,1)}), bf16[4,512,128]{2,1,0:T(8,128)(2,1)S(1)}, u32[]{:S(2)}, u32[]{:S(2)}) async-start(bf16[4,512,128]{2,1,0:T(8,128)(2,1)} %get-tuple-element.41), calls=%async_computation.3 | async-start | bytes 1048576 | tf_op jit(solution)/shard_map/all_to_all | solution.py:47
  117.7 19.3 %collective-permute-start.10 = (bf16[1056,128]{1,0:T(8,128)(2,1)S(1)}, bf16[1056,128]{1,0:T(8,128)(2,1)S(1)}, u32[]{:S(2)}, u32[]{:S(2)}) collective-permute-start(bf16[1056,128]{1,0:T(8,128)(2,1)S(1)} %get-tuple-element.38), channel_id=1, source_target_pairs={{0,12},{1,13},{2,14},{3,15},{4,0},{5,1},{6,2},{7,3},{8,4},{9,5},{1... | collective-permute-start | bytes 811016 | tf_op jit(solution)/shard_map/ppermute | solution.py:54
  125.7 11.3 %collective-permute-start.11 = (bf16[1056,128]{1,0:T(8,128)(2,1)S(1)}, bf16[1056,128]{1,0:T(8,128)(2,1)S(1)}, u32[]{:S(2)}, u32[]{:S(2)}) collective-permute-start(bf16[1056,128]{1,0:T(8,128)(2,1)S(1)} %get-tuple-element.39), channel_id=1, source_target_pairs={{0,8},{1,9},{2,10},{3,11},{4,12},{5,13},{6,14},{7,15},{8,0},{9,1},... | collective-permute-start | bytes 811016 | tf_op jit(solution)/shard_map/ppermute | solution.py:54
  138.0 20.5 %all-to-all-start.4 = ((f32[8,16,256]{2,1,0:T(8,128)}), f32[8,16,256]{2,1,0:T(8,128)S(1)}, u32[]{:S(2)}, u32[]{:S(2)}) async-start(f32[8,16,256]{2,1,0:T(8,128)} %piece_sum.1), calls=%async_computation.4 | async-start | bytes 262144 | tf_op jit(solution)/shard_map/all_to_all | solution.py:341
  149.8 17.8 %collective-permute-start.13 = (bf16[1024,128]{1,0:T(8,128)(2,1)S(1)}, bf16[1024,128]{1,0:T(8,128)(2,1)S(1)}, u32[]{:S(2)}, u32[]{:S(2)}) collective-permute-start(bf16[1024,128]{1,0:T(8,128)(2,1)S(1)} %copy-done.26), channel_id=1, source_target_pairs={{0,12},{1,13},{2,14},{3,15},{4,0},{5,1},{6,2},{7,3},{8,4},{9,5},{1... | collective-permute-start | bytes 786440 | tf_op jit(solution)/shard_map/ppermute | solution.py:54
  153.6 13.9 %collective-permute-start.14 = (bf16[1024,128]{1,0:T(8,128)(2,1)S(1)}, bf16[1024,128]{1,0:T(8,128)(2,1)}, u32[]{:S(2)}, u32[]{:S(2)}) collective-permute-start(bf16[1024,128]{1,0:T(8,128)(2,1)S(1)} %copy-done.24), channel_id=1, source_target_pairs={{0,8},{1,9},{2,10},{3,11},{4,12},{5,13},{6,14},{7,15},{8,0},{9,1},... | collective-permute-start | bytes 786440 | tf_op jit(solution)/shard_map/ppermute | solution.py:54
  156.6 14.4 %collective-permute-start.15 = (bf16[1024,128]{1,0:T(8,128)(2,1)S(1)}, bf16[1024,128]{1,0:T(8,128)(2,1)}, u32[]{:S(2)}, u32[]{:S(2)}) collective-permute-start(bf16[1024,128]{1,0:T(8,128)(2,1)S(1)} %copy-done.22), channel_id=1, source_target_pairs={{0,4},{1,5},{2,6},{3,7},{4,8},{5,9},{6,10},{7,11},{8,12},{9,13},{1... | collective-permute-start | bytes 786440 | tf_op jit(solution)/shard_map/ppermute | solution.py:54
  159.2 27.8 %all-to-all-start.5 = ((f32[8,16,256]{2,1,0:T(8,128)}), f32[8,16,256]{2,1,0:T(8,128)S(1)}, u32[]{:S(2)}, u32[]{:S(2)}) async-start(f32[8,16,256]{2,1,0:T(8,128)} %sum_and_spread.2), calls=%async_computation.5 | async-start | bytes 262144 | tf_op jit(solution)/shard_map/all_to_all | solution.py:341
  174.8 20.8 %collective-permute-start.16 = (bf16[512,256]{1,0:T(8,128)(2,1)}, bf16[512,256]{1,0:T(8,128)(2,1)S(1)}, u32[]{:S(2)}, u32[]{:S(2)}) collective-permute-start(bf16[512,256]{1,0:T(8,128)(2,1)} %get-tuple-element.47), channel_id=1, source_target_pairs={{0,992},{16,1008},{32,0},{48,16},{64,32},{80,48},{96,64},{112,80},... | collective-permute-start | bytes 786440 | tf_op jit(solution)/shard_map/ppermute | solution.py:40
  178.7 17.0 %collective-permute-start.17 = (bf16[512,256]{1,0:T(8,128)(2,1)S(1)}, bf16[512,256]{1,0:T(8,128)(2,1)S(1)}, u32[]{:S(2)}, u32[]{:S(2)}) collective-permute-start(bf16[512,256]{1,0:T(8,128)(2,1)S(1)} %get-tuple-element.48), channel_id=1, source_target_pairs={{0,1008},{16,0},{32,16},{48,32},{64,48},{80,64},{96,80},{112,96},{... | collective-permute-start | bytes 786440 | tf_op jit(solution)/shard_map/ppermute | solution.py:40
  181.8 13.9 %collective-permute-start.18 = (bf16[512,256]{1,0:T(8,128)(2,1)S(1)}, bf16[512,256]{1,0:T(8,128)(2,1)S(1)}, u32[]{:S(2)}, u32[]{:S(2)}) collective-permute-start(bf16[512,256]{1,0:T(8,128)(2,1)S(1)} %get-tuple-element.49), channel_id=1, source_target_pairs={{0,16},{16,32},{32,48},{48,64},{64,80},{80,96},{96,112},{112,128},... | collective-permute-start | bytes 786440 | tf_op jit(solution)/shard_map/ppermute | solution.py:40
  184.3 12.5 %collective-permute-start.19 = (bf16[512,256]{1,0:T(8,128)(2,1)S(1)}, bf16[512,256]{1,0:T(8,128)(2,1)S(1)}, u32[]{:S(2)}, u32[]{:S(2)}) collective-permute-start(bf16[512,256]{1,0:T(8,128)(2,1)S(1)} %get-tuple-element.50), channel_id=1, source_target_pairs={{0,32},{16,48},{32,64},{48,80},{64,96},{80,112},{96,128},{112,144}... | collective-permute-start | bytes 786440 | tf_op jit(solution)/shard_map/ppermute | solution.py:40
  187.8 20.0 %all-to-all-start.6 = ((f32[16,16,256]{2,1,0:T(8,128)}), f32[16,16,256]{2,1,0:T(8,128)S(1)}, u32[]{:S(2)}, u32[]{:S(2)}) async-start(f32[16,16,256]{2,1,0:T(8,128)} %sum_and_spread.3), calls=%async_computation.6 | async-start | bytes 524288 | tf_op jit(solution)/shard_map/all_to_all | solution.py:385
  (37 other events, 479.2 us)

commit v4 on v0

v4 whole, which is shorter than its diff:
```python
import functools

import jax
import jax.numpy as jnp
from jax import lax
from jax.experimental import pallas as pl
from jax.experimental.pallas import tpu as pltpu
from jax.sharding import PartitionSpec as P

BLOCK = 128
HALF = 2
CAP = 2
XN = 4
YN = 4
INNER = 8
LANES = 128
ID_ROWS = 16

OFFSETS = (-2, -1, 1, 2)
VMEM = pl.BlockSpec(memory_space=pltpu.VMEM)
SMEM = pl.BlockSpec(memory_space=pltpu.SMEM)
BF16 = jnp.bfloat16
F32 = jnp.float32

GATHER_FLOPS = 1 << 20
DENSE_FLOPS = 1 << 28
REPLY_FLOPS = 10**10
BACK_FLOPS = 10**10
FINAL_FLOPS = 10**10
SPREAD_FLOPS = 1 << 16


def kernel_call(body, name, outs, ins, mib, flops, scratch=()):
    nbytes = sum(a.size * a.dtype.itemsize for _, a in ins)
    return pl.pallas_call(
        body,
        out_shape=outs,
        in_specs=[space for space, _ in ins],
        out_specs=jax.tree.map(lambda _: VMEM, outs),
        scratch_shapes=list(scratch),
        compiler_params=pltpu.CompilerParams(vmem_limit_bytes=mib << 20),
        cost_estimate=pl.CostEstimate(flops=flops, bytes_accessed=nbytes, transcendentals=0),
        name=name,
    )(*[a for _, a in ins])


def dom_shift(value, steps):
    count = lax.axis_size("dom")
    return lax.ppermute(value, "dom", [(i, (i + steps) % count) for i in range(count)])


def y_shift(value, steps):
    pairs = [(x * YN + y, x * YN + (y + steps) % YN) for x in range(XN) for y in range(YN)]
    return lax.ppermute(value, "rows", pairs)


def x_shift(value, steps):
    pairs = [(x * YN + y, (x + steps) % XN * YN + y) for x in range(XN) for y in range(YN)]
    return lax.ppermute(value, "rows", pairs)


X_GROUPS = [[x * YN + y for x in range(XN)] for y in range(YN)]
Y_GROUPS = [[x * YN + y for y in range(YN)] for x in range(XN)]


def exchange(value, axis, groups=None):
    return lax.all_to_all(
        value, axis, split_axis=0, concat_axis=0, tiled=True, axis_index_groups=groups
    )


def forward_kernel(src, slot, cnt, fm2, fm1, f0, fp1, fp2, vals, ids, out, acc):
    acc[...] = jnp.zeros_like(acc)
    feats = (fm2, fm1, f0, fp1, fp2)
    tiles_step = vals.shape[0] // len(feats)
    for k, feat in enumerate(feats):
        for t in range(tiles_step):
            block = feat[src[k, t]]
            block = jnp.where(t < cnt[0, k], block, jnp.zeros_like(block))
            acc[slot[k, t]] += jnp.dot(
                vals[k * tiles_step + t], block, preferred_element_type=F32
            )
    per_x = YN * CAP
    for x in range(XN):
        for j in range(per_x):
            out[x, pl.ds(j * BLOCK, BLOCK), :] = acc[x * per_x + j].astype(BF16)
        out[x, pl.ds(per_x * BLOCK, ID_ROWS), :] = ids[x]


def forward_products(src, slot, cnt, feats, vals, ids):
    channels = feats[0].shape[2]
    rows = YN * CAP * BLOCK + ID_ROWS
    ins = [(SMEM, src), (SMEM, slot), (SMEM, cnt)]
    ins += [(VMEM, a) for a in (*feats, vals, ids)]
    return kernel_call(
        forward_kernel,
        "tile_forward",
        jax.ShapeDtypeStruct((XN, rows, channels), BF16),
        ins,
        12,
        vals.size * 2 * channels,
        [pltpu.VMEM((XN * YN * CAP, BLOCK, channels), F32)],
    )


def gather_kernel(blocks_dev, recv, out, ids_out):
    base = YN * CAP * BLOCK
    for x in range(XN):
        ids = recv[x, pl.ds(base, ID_ROWS), :].astype(F32)
        ids_out[pl.ds(x * YN * CAP, YN * CAP), :] = ids[: YN * CAP]
    chunk = 32
    for y in range(YN):
        for start in range(0, BLOCK, chunk):
            totals = [jnp.zeros((chunk, out.shape[2]), F32) for _ in range(blocks_dev)]
            for x in range(XN):
                for c in range(CAP):
                    j = y * CAP + c
                    n = x * YN * CAP + j
                    row = ids_out[n : n + 1, :]
                    part = recv[x, pl.ds(j * BLOCK + start, chunk), :].astype(F32)
                    for b in range(blocks_dev):
                        totals[b] = totals[b] + jnp.where(row == float(b), part, 0.0)
            for b in range(blocks_dev):
                out[y, pl.ds(b * BLOCK + start, chunk), :] = totals[b].astype(BF16)


def gather_blocks(recv, blocks_dev):
    channels = recv.shape[2]
    return kernel_call(
        functools.partial(gather_kernel, blocks_dev),
        "block_sums",
        (
            jax.ShapeDtypeStruct((YN, blocks_dev * BLOCK, channels), BF16),
            jax.ShapeDtypeStruct((XN * YN * CAP, channels), F32),
        ),
        [(VMEM, recv)],
        6,
        GATHER_FLOPS,
    )


def dense_kernel(parts, weight, cot, act, grad, wgrad):
    total = parts[0].astype(F32)
    for y in range(1, YN):
        total = total + parts[y].astype(F32)
    agg = total.astype(BF16)
    w = weight[...]
    pre = jnp.dot(agg, w, preferred_element_type=F32)
    sig = 1.0 / (1.0 + jnp.exp(-pre))
    act[...] = (pre * sig).astype(BF16)
    slope = sig * (1.0 + pre * (1.0 - sig))
    pre_grad = (cot[...].astype(F32) * slope).astype(BF16)
    grad[...] = lax.dot_general(
        pre_grad, w, (((1,), (1,)), ((), ())), preferred_element_type=F32
    ).astype(BF16)
    wgrad[...] = lax.dot_general(
        agg, pre_grad, (((0,), (0,)), ((), ())), preferred_element_type=F32
    )


def dense(parts, weight, cot):
    nodes, channels = cot.shape
    full = jax.ShapeDtypeStruct((nodes, channels), BF16)
    return kernel_call(
        dense_kernel,
        "dense_layer",
        (full, full, jax.ShapeDtypeStruct((channels, channels), F32)),
        [(VMEM, parts), (VMEM, weight), (VMEM, cot)],
        10,
        DENSE_FLOPS,
    )


def reply_kernel(blocks_dev, me, g0, r1, r2, r3, ids, *outs):
    chunk = 32
    for k, grads in enumerate((g0, r1, r2, r3)):
        y = lax.rem(me[0] - k + YN, YN)
        rows = {}
        for i in range(XN):
            x = lax.rem(me[1] - i + XN, XN)
            for c in range(CAP):
                rows[i, c] = ids[pl.ds(x * YN * CAP + y * CAP + c, 1), :]
        for start in range(0, BLOCK, chunk):
            blocks = [
                grads[pl.ds(b * BLOCK + start, chunk), :].astype(F32) for b in range(blocks_dev)
            ]
            for (i, c), row in rows.items():
                picked = jnp.where(row == 0.0, blocks[0], 0.0)
                for b in range(1, blocks_dev):
                    picked = jnp.where(row == float(b), blocks[b], picked)
                spot = pl.multiple_of((y * CAP + c) * BLOCK + start, chunk)
                outs[i][pl.ds(spot, chunk), :] = picked.astype(BF16)


def reply_slots(me, grads, ids, blocks_dev):
    out = jax.ShapeDtypeStruct((YN * CAP * BLOCK, ids.shape[1]), BF16)
    return kernel_call(
        functools.partial(reply_kernel, blocks_dev),
        "slot_replies",
        (out,) * XN,
        [(SMEM, me)] + [(VMEM, a) for a in (*grads, ids)],
        6,
        REPLY_FLOPS,
    )


def backward_kernel(src, slot, cnt, me, b0, b1, b2, b3, vals, om2, om1, own, op1, op2, acc, ret):
    per_x = YN * CAP
    for k, back in enumerate((b0, b1, b2, b3)):
        x = lax.rem(me[1] + k, XN)
        for j in range(per_x):
            ret[x * per_x + j] = back[pl.ds(j * BLOCK, BLOCK), :]
    steps = cnt.shape[1]
    tiles_step = vals.shape[0] // steps
    acc[...] = jnp.zeros_like(acc)
    for k in range(steps):
        for t in range(tiles_step):
            block = ret[slot[k, t]]
            block = jnp.where(t < cnt[0, k], block, jnp.zeros_like(block))
            acc[k, src[k, t]] += lax.dot_general(
                vals[k * tiles_step + t],
                block,
                (((0,), (0,)), ((), ())),
                preferred_element_type=F32,
            )
    for k, out in enumerate((om2, om1, own, op1, op2)):
        for b in range(acc.shape[1]):
            out[pl.ds(b * BLOCK, BLOCK), :] = acc[k, b].astype(out.dtype)


def backward_products(src, slot, cnt, me, back, vals, blocks_dev):
    nodes, channels = blocks_dev * BLOCK, back[0].shape[1]
    steps = cnt.shape[1]
    send = jax.ShapeDtypeStruct((nodes, channels), BF16)
    own = jax.ShapeDtypeStruct((nodes, channels), F32)
    return kernel_call(
        backward_kernel,
        "tile_backward",
        (send, send, own, send, send),
        [(SMEM, a) for a in (src, slot, cnt, me)] + [(VMEM, a) for a in (*back, vals)],
        12,
        BACK_FLOPS,
        [
            pltpu.VMEM((steps, blocks_dev, BLOCK, channels), F32),
            pltpu.VMEM((XN * YN * CAP, BLOCK, channels), BF16),
        ],
    )


def final_kernel(own, r1, r2, r3, r4, out):
    total = own[...]
    for r in (r1, r2, r3, r4):
        total = total + r[...].astype(F32)
    out[...] = total.astype(BF16)


def final_sum(parts):
    return kernel_call(
        final_kernel,
        "grad_sum",
        jax.ShapeDtypeStruct(parts[0].shape, BF16),
        [(VMEM, a) for a in parts],
        4,
        FINAL_FLOPS,
    )


def spread_kernel(parts, out):
    total = parts[0]
    for i in range(1, parts.shape[0]):
        total = total + parts[i]
    for i in range(out.shape[0]):
        out[i] = total


def sum_and_spread(parts, copies):
    return kernel_call(
        spread_kernel,
        "sum_and_spread",
        jax.ShapeDtypeStruct((copies,) + parts.shape[1:], F32),
        [(VMEM, parts)],
        2,
        SPREAD_FLOPS,
    )


def summed_weight_grad(local_grad):
    channels = local_grad.shape[1]
    rows, dom = lax.axis_size("rows"), lax.axis_size("dom")
    outer = dom // INNER
    near = [[i * INNER + j for j in range(INNER)] for i in range(outer)]
    far = [[i * INNER + j for i in range(outer)] for j in range(INNER)]
    pieces = local_grad.reshape(rows, local_grad.shape[0] // rows, channels)
    piece = sum_and_spread(exchange(pieces, "rows"), INNER)
    piece = sum_and_spread(exchange(piece, "dom", near), outer)
    piece = sum_and_spread(exchange(piece, "dom", far), rows)
    return exchange(piece, "rows").reshape(local_grad.shape)


def per_device(
    features, weight, tile_values, tile_source, tile_slot, slot_block, tile_count, cotangent
):
    blocks_dev = features.shape[0] // BLOCK
    channels = features.shape[1]
    vals = tile_values.reshape(-1, BLOCK, BLOCK)
    src, slot, cnt = tile_source[0], tile_slot[0], tile_count
    rank = lax.axis_index("rows")
    me = jnp.stack([rank % YN, rank // YN]).astype(jnp.int32)
    id_rows = jnp.broadcast_to(
        jnp.pad(slot_block.reshape(XN, -1), ((0, 0), (0, ID_ROWS - YN * CAP)))[..., None],
        (XN, ID_ROWS, channels),
    ).astype(BF16)

    near = [dom_shift(features, -o) for o in OFFSETS]
    feats = [near[0], near[1], features, near[2], near[3]]
    feats = [f.reshape(blocks_dev, BLOCK, channels) for f in feats]
    sent = forward_products(src, slot, cnt, feats, vals, id_rows)
    sums, ids = gather_blocks(exchange(sent, "rows", X_GROUPS), blocks_dev)
    parts = exchange(sums, "rows", Y_GROUPS)
    activations, grad, local_grad = dense(parts, weight, cotangent)

    grads = [grad] + [y_shift(grad, k) for k in range(1, YN)]
    reply = reply_slots(me, grads, ids, blocks_dev)
    back = [reply[0]] + [x_shift(reply[k], -k) for k in range(1, XN)]
    terms = list(backward_products(src, slot, cnt, me, back, vals, blocks_dev))
    own = terms.pop(HALF)
    terms = [dom_shift(t, o) for t, o in zip(terms, OFFSETS)]
    weight_grad = summed_weight_grad(local_grad)
    feature_grad = final_sum([own, *terms])
    return (activations, feature_grad, weight_grad)


def solution(mesh):
    return jax.shard_map(
        per_device,
        mesh=mesh,
        in_specs=(
            P(("dom", "rows"), None),
            P(),
            P(("dom", "rows"), None, None, None, None),
            P(("dom", "rows"), None, None),
            P(("dom", "rows"), None, None),
            P(("dom", "rows"), None),
            P(("dom", "rows"), None),
            P(("dom", "rows"), None),
        ),
        out_specs=(P(("dom", "rows"), None), P(("dom", "rows"), None), P()),
        check_vma=False,
    )
```

time: 752 us -> 203 us (0.27)
  waiting for transfers between devices: 615 us -> 36.1 us
  blocking collectives: 0 us -> 64.5 us
  matrix products: 19.5 us -> 0 us
  local copies, waits for them, and re-layouts: 26.9 us -> 8.82 us
  starting transfers between devices: 65.2 us -> 79.6 us
  between operations: 14.6 us -> 0.88 us
  Pallas kernels: 0 us -> 11.6 us
  other arithmetic: 8.5 us -> 0.75 us
    psum x1 -> x0, waiting for transfers between devices: 464 us -> none  [per_device(): weight_grad = lax.psum(local_grad, ('dom', 'rows'))]
    all_to_all x3, waiting for transfers between devices: 97.2 us -> 4.47 us  [exchange(): lax.all_to_all(value, axis, split_axis=0, concat_axis=0, tiled=True, axis...]
    all_to_all x0 -> x3, blocking collectives: none -> 64.5 us  [exchange(): lax.all_to_all(value, axis, split_axis=0, concat_axis=0, tiled=True, axis...]
    ppermute x10 -> x14, waiting for transfers between devices: 53.3 us -> 31.6 us  [the longest x3 15.7 us: y_shift(): return lax.ppermute(value, 'rows', pairs)]
    dot_general x20 -> x0, matrix products: 19.5 us -> none  [the longest x5 5.52 us: source_terms(): jnp.einsum('tji,tjf->tif', values[step_idx], picked, preferred_element_ty...]
    ppermute x10 -> x14, starting transfers between devices: 40.3 us -> 58.1 us  [the longest x8 38 us: dom_shift(): lax.ppermute(value, 'dom', [(i, (i + steps) % count) for i in range(count)])]
    pallas_call x0 -> x9, Pallas kernels: none -> 11.6 us  [kernel_call(): pl.pallas_call(body, out_shape=outs, in_specs=[space for space, _ in ins]...]
  transfers between devices with their start and end apart: 14 -> 17, of which waited for: 13 -> 6; matrix products, arithmetic and copies ran while one was open for 5% -> 1% of each run, Pallas kernels for 0% -> 3%
where the time goes in v4:
time: 203 us; the launch traced here: 202 us
  starting transfers between devices  79.6 us (39%)
  blocking collectives  64.5 us (32%)
  waiting for transfers between devices  36.1 us (18%)
  Pallas kernels  11.6 us (6%)
  local copies, waits for them, and re-layouts  8.82 us (4%)
    all_to_all x3, blocking collectives, exchange(): lax.all_to_all(value, axis, split_axis=0, concat_axis=0, tiled=True, axis...  64.5 us
    ppermute x8, starting transfers between devices, dom_shift(): lax.ppermute(value, 'dom', [(i, (i + steps) % count) for i in range(count)])  38 us
    all_to_all x3, starting transfers between devices, exchange(): lax.all_to_all(value, axis, split_axis=0, concat_axis=0, tiled=True, axis...  21.5 us
    ppermute x3, waiting for transfers between devices, y_shift(): return lax.ppermute(value, 'rows', pairs)  15.7 us
    ppermute x8, waiting for transfers between devices, dom_shift(): lax.ppermute(value, 'dom', [(i, (i + steps) % count) for i in range(count)])  13.2 us
    ppermute x3, starting transfers between devices, y_shift(): return lax.ppermute(value, 'rows', pairs)  12.3 us
    pallas_call x9, Pallas kernels, kernel_call(): pl.pallas_call(body, out_shape=outs, in_specs=[space for space, _ in ins]...  11.6 us
    ppermute x3, starting transfers between devices, x_shift(): return lax.ppermute(value, 'rows', pairs)  7.82 us
  transfers between devices with their start and end apart: 17, of which 6 were waited for; matrix products, arithmetic and copies ran while one was open for 1% of the time, Pallas kernels for 3%

profile of v4, /device:TPU:1, one launch (start us, length us, event | category | flops | bytes accessed | tf_op | source)
XLA Modules:
  0.0 202.2 jit_solution(2231638134945707690)
XLA Ops:
  0.6 4.0 %collective-permute-start = (bf16[512,256]{1,0:T(8,128)(2,1)}, bf16[512,256]{1,0:T(8,128)(2,1)S(1)}, u32[]{:S(2)}, u32[]{:S(2)}) collective-permute-start(bf16[512,256]{1,0:T(8,128)(2,1)} %param.8), channel_id=1, source_target_pairs={{0,32},{16,48},{32,64},{48,80},{64,96},{80,112},{96,128},{112,144}... | collective-permute-start | bytes 786440 | tf_op jit(solution)/shard_map/ppermute | solution.py:49
  4.7 4.7 %collective-permute-start.1 = (bf16[512,256]{1,0:T(8,128)(2,1)}, bf16[512,256]{1,0:T(8,128)(2,1)S(1)}, u32[]{:S(2)}, u32[]{:S(2)}) collective-permute-start(bf16[512,256]{1,0:T(8,128)(2,1)} %param.8), channel_id=1, source_target_pairs={{0,16},{16,32},{32,48},{48,64},{64,80},{80,96},{96,112},{112,128},... | collective-permute-start | bytes 786440 | tf_op jit(solution)/shard_map/ppermute | solution.py:49
  9.4 11.1 %collective-permute-start.2 = (bf16[512,256]{1,0:T(8,128)(2,1)}, bf16[512,256]{1,0:T(8,128)(2,1)S(1)}, u32[]{:S(2)}, u32[]{:S(2)}) collective-permute-start(bf16[512,256]{1,0:T(8,128)(2,1)} %param.8), channel_id=1, source_target_pairs={{0,1008},{16,0},{32,16},{48,32},{64,48},{80,64},{96,80},{112,96},{... | collective-permute-start | bytes 786440 | tf_op jit(solution)/shard_map/ppermute | solution.py:49
  20.6 6.3 %collective-permute-start.3 = (bf16[512,256]{1,0:T(8,128)(2,1)}, bf16[512,256]{1,0:T(8,128)(2,1)S(1)}, u32[]{:S(2)}, u32[]{:S(2)}) collective-permute-start(bf16[512,256]{1,0:T(8,128)(2,1)} %param.8), channel_id=1, source_target_pairs={{0,992},{16,1008},{32,0},{48,16},{64,32},{80,48},{96,64},{112,80},... | collective-permute-start | bytes 786440 | tf_op jit(solution)/shard_map/ppermute | solution.py:49
  29.2 6.6 %collective-permute-done.3 = bf16[512,256]{1,0:T(8,128)(2,1)S(1)} collective-permute-done((bf16[512,256]{1,0:T(8,128)(2,1)}, bf16[512,256]{1,0:T(8,128)(2,1)S(1)}, u32[]{:S(2)}, u32[]{:S(2)}) %collective-permute-start.3) | collective-permute-done | bytes 262176 | tf_op jit(solution)/shard_map/ppermute | solution.py:49
  40.3 28.7 %all_to_all.30.recv = bf16[4,1040,256]{2,1,0:T(8,128)(2,1)S(1)} all-to-all(bf16[4,1040,256]{2,1,0:T(8,128)(2,1)S(1)} %tile_forward.1), channel_id=1, replica_groups={{0,4,8,12},{1,5,9,13},{2,6,10,14},{3,7,11,15},{16,20,24,28},{17,21,25,2..., dimensions={0} | all-to-all | bytes 4259840 | tf_op jit(solution)/shard_map/all_to_all | solution.py:67
  70.6 27.7 %all_to_all.31.parts = bf16[4,512,256]{2,1,0:T(8,128)(2,1)S(1)} all-to-all(bf16[4,512,256]{2,1,0:T(8,128)(2,1)S(1)} %get-tuple-element.17), channel_id=1, replica_groups={{0,1,2,3},{4,5,6,7},{8,9,10,11},{12,13,14,15},{16,17,18,19},{20,21,22,2..., dimensions={0} | all-to-all | bytes 2097152 | tf_op jit(solution)/shard_map/all_to_all | solution.py:67
  99.6 4.9 %collective-permute-start.4 = (bf16[512,256]{1,0:T(8,128)(2,1)S(1)}, bf16[512,256]{1,0:T(8,128)(2,1)S(1)}, u32[]{:S(2)}, u32[]{:S(2)}) collective-permute-start(bf16[512,256]{1,0:T(8,128)(2,1)S(1)} %get-tuple-element.19.g0), channel_id=1, source_target_pairs={{0,1},{1,2},{2,3},{3,0},{4,5},{5,6},{6,7},{7,4},{8,9},{9,10},{10,1... | collective-permute-start | bytes 786440 | tf_op jit(solution)/shard_map/ppermute | solution.py:54
  106.9 5.1 %collective-permute-start.6 = (bf16[512,256]{1,0:T(8,128)(2,1)S(1)}, bf16[512,256]{1,0:T(8,128)(2,1)S(1)}, u32[]{:S(2)}, u32[]{:S(2)}) collective-permute-start(bf16[512,256]{1,0:T(8,128)(2,1)S(1)} %get-tuple-element.19.g0), channel_id=1, source_target_pairs={{0,3},{1,0},{2,1},{3,2},{4,7},{5,4},{6,5},{7,6},{8,11},{9,8},{10,9... | collective-permute-start | bytes 786440 | tf_op jit(solution)/shard_map/ppermute | solution.py:54
  112.1 4.3 %all-to-all-start.2 = ((f32[16,16,256]{2,1,0:T(8,128)}), f32[16,16,256]{2,1,0:T(8,128)S(1)}, u32[]{:S(2)}, u32[]{:S(2)}) async-start(f32[16,16,256]{2,1,0:T(8,128)} %bitcast.10), calls=%async_computation.2 | async-start | bytes 524288 | tf_op jit(solution)/shard_map/all_to_all | solution.py:67
  116.4 6.7 %collective-permute-done.5.r2 = bf16[512,256]{1,0:T(8,128)(2,1)S(1)} collective-permute-done((bf16[512,256]{1,0:T(8,128)(2,1)S(1)}, bf16[512,256]{1,0:T(8,128)(2,1)S(1)}, u32[]{:S(2)}, u32[]{:S(2)}) %collective-permute-start.5) | collective-permute-done | bytes 262176 | tf_op jit(solution)/shard_map/ppermute | solution.py:54
  123.1 9.0 %collective-permute-done.6.r3 = bf16[512,256]{1,0:T(8,128)(2,1)S(1)} collective-permute-done((bf16[512,256]{1,0:T(8,128)(2,1)S(1)}, bf16[512,256]{1,0:T(8,128)(2,1)S(1)}, u32[]{:S(2)}, u32[]{:S(2)}) %collective-permute-start.6) | collective-permute-done | bytes 262176 | tf_op jit(solution)/shard_map/ppermute | solution.py:54
  132.1 2.3 %slot_replies.1 = (bf16[1024,256]{1,0:T(8,128)(2,1)S(1)}, bf16[1024,256]{1,0:T(8,128)(2,1)}, bf16[1024,256]{1,0:T(8,128)(2,1)}, bf16[1024,256]{1,0:T(8,128)(2,1)S(1)}) custom-call(s32[2]{0:T(128)S(1)} %pad_add_fusion.me, bf16[512,256]{1,0:T(8,128)(2,1)S(1)} %get-tuple-element.19.g0, bf16[512,256]{1,0:T(8,128)(2,1)S(1)} %collective-permute-done.4.r1, ...), custom_call_target="tpu_custom_call" | custom-call | flops 10000000000 | bytes 1081352 | tf_op jit(solution)/shard_map/slot_replies/pallas_call | solution.py:35
  135.2 2.8 %collective-permute-start.7 = (bf16[1024,256]{1,0:T(8,128)(2,1)}, bf16[1024,256]{1,0:T(8,128)(2,1)S(1)}, u32[]{:S(2)}, u32[]{:S(2)}) collective-permute-start(bf16[1024,256]{1,0:T(8,128)(2,1)} %get-tuple-element.22), channel_id=1, source_target_pairs={{0,12},{1,13},{2,14},{3,15},{4,0},{5,1},{6,2},{7,3},{8,4},{9,5},{1... | collective-permute-start | bytes 1572872 | tf_op jit(solution)/shard_map/ppermute | solution.py:59
  138.0 3.1 %collective-permute-start.8 = (bf16[1024,256]{1,0:T(8,128)(2,1)}, bf16[1024,256]{1,0:T(8,128)(2,1)S(1)}, u32[]{:S(2)}, u32[]{:S(2)}) collective-permute-start(bf16[1024,256]{1,0:T(8,128)(2,1)} %get-tuple-element.23), channel_id=1, source_target_pairs={{0,8},{1,9},{2,10},{3,11},{4,12},{5,13},{6,14},{7,15},{8,0},{9,1},... | collective-permute-start | bytes 1572872 | tf_op jit(solution)/shard_map/ppermute | solution.py:59
  143.1 8.1 %all_to_all.32.parts = f32[8,16,256]{2,1,0:T(8,128)S(1)} all-to-all(f32[8,16,256]{2,1,0:T(8,128)S(1)} %sum_and_spread.3), channel_id=1, replica_groups={{0,16,32,48,64,80,96,112},{128,144,160,176,192,208,224,240},{256,272,28..., dimensions={0} | all-to-all | bytes 262144 | tf_op jit(solution)/shard_map/all_to_all | solution.py:67
  151.9 12.1 %all-to-all-start.4 = ((f32[8,16,256]{2,1,0:T(8,128)}), f32[8,16,256]{2,1,0:T(8,128)S(1)}, u32[]{:S(2)}, u32[]{:S(2)}) async-start(f32[8,16,256]{2,1,0:T(8,128)} %sum_and_spread.4), calls=%async_computation.4 | async-start | bytes 262144 | tf_op jit(solution)/shard_map/all_to_all | solution.py:67
  164.0 2.7 %collective-permute-done.9.b3 = bf16[1024,256]{1,0:T(8,128)(2,1)S(1)} collective-permute-done((bf16[1024,256]{1,0:T(8,128)(2,1)S(1)}, bf16[1024,256]{1,0:T(8,128)(2,1)S(1)}, u32[]{:S(2)}, u32[]{:S(2)}) %collective-permute-start.9) | collective-permute-done | bytes 524320 | tf_op jit(solution)/shard_map/ppermute | solution.py:59
  167.8 2.4 %tile_backward.1 = (bf16[512,256]{1,0:T(8,128)(2,1)}, bf16[512,256]{1,0:T(8,128)(2,1)S(1)}, f32[512,256]{1,0:T(8,128)S(1)}, bf16[512,256]{1,0:T(8,128)(2,1)S(1)}, bf16[512,256]{1,0:T(8,128)(2,1)S(1)}) custom-call(s32[5,4]{1,0:T(8,128)S(1)} %copy.11.src, s32[5,4]{1,0:T(8,128)S(1)} %copy.12.slot, s32[1,5]{1,0:T(1,128)S(1)} %copy-done.6, s32[2]{0:T(128)S(1)} %pad_add_fusion.me, ...), custom_call_target="tpu_custom_call" | custom-call | flops 10000000000 | bytes 2752700 | tf_op jit(solution)/shard_map/tile_backward/pallas_call | solution.py:35
  173.3 3.3 %collective-permute-start.11 = (bf16[512,256]{1,0:T(8,128)(2,1)S(1)}, bf16[512,256]{1,0:T(8,128)(2,1)S(1)}, u32[]{:S(2)}, u32[]{:S(2)}) collective-permute-start(bf16[512,256]{1,0:T(8,128)(2,1)S(1)} %get-tuple-element.27), channel_id=1, source_target_pairs={{0,1008},{16,0},{32,16},{48,32},{64,48},{80,64},{96,80},{112,96},{... | collective-permute-start | bytes 786440 | tf_op jit(solution)/shard_map/ppermute | solution.py:49
  178.9 3.9 %collective-permute-start.13 = (bf16[512,256]{1,0:T(8,128)(2,1)S(1)}, bf16[512,256]{1,0:T(8,128)(2,1)S(1)}, u32[]{:S(2)}, u32[]{:S(2)}) collective-permute-start(bf16[512,256]{1,0:T(8,128)(2,1)S(1)} %get-tuple-element.29), channel_id=1, source_target_pairs={{0,32},{16,48},{32,64},{48,80},{64,96},{80,112},{96,128},{112,144}... | collective-permute-start | bytes 786440 | tf_op jit(solution)/shard_map/ppermute | solution.py:49
  183.5 5.0 %all-to-all-start.5 = ((f32[16,16,256]{2,1,0:T(8,128)}), f32[16,16,256]{2,1,0:T(8,128)S(1)}, u32[]{:S(2)}, u32[]{:S(2)}) async-start(f32[16,16,256]{2,1,0:T(8,128)} %sum_and_spread.5), calls=%async_computation.5 | async-start | bytes 524288 | tf_op jit(solution)/shard_map/all_to_all | solution.py:67
  188.6 6.6 %collective-permute-done.11.r2 = bf16[512,256]{1,0:T(8,128)(2,1)S(1)} collective-permute-done((bf16[512,256]{1,0:T(8,128)(2,1)S(1)}, bf16[512,256]{1,0:T(8,128)(2,1)S(1)}, u32[]{:S(2)}, u32[]{:S(2)}) %collective-permute-start.11) | collective-permute-done | bytes 262176 | tf_op jit(solution)/shard_map/ppermute | solution.py:49
  197.1 4.5 %all-to-all-done.5 = f32[16,16,256]{2,1,0:T(8,128)S(1)} async-done(((f32[16,16,256]{2,1,0:T(8,128)}), f32[16,16,256]{2,1,0:T(8,128)S(1)}, u32[]{:S(2)}, u32[]{:S(2)}) %all-to-all-start.5) | async-done | bytes 262176 | tf_op jit(solution)/shard_map/all_to_all | solution.py:67
  (52 shorter events, 25.3 us)
Async XLA Ops:
  0.6 28.6 %collective-permute-start = (bf16[512,256]{1,0:T(8,128)(2,1)}, bf16[512,256]{1,0:T(8,128)(2,1)S(1)}, u32[]{:S(2)}, u32[]{:S(2)}) collective-permute-start(bf16[512,256]{1,0:T(8,128)(2,1)} %param.8), channel_id=1, source_target_pairs={{0,32},{16,48},{32,64},{48,80},{64,96},{80,112},{96,128},{112,144}... | collective-permute-start | bytes 786440 | tf_op jit(solution)/shard_map/ppermute | solution.py:49
  4.7 24.5 %collective-permute-start.1 = (bf16[512,256]{1,0:T(8,128)(2,1)}, bf16[512,256]{1,0:T(8,128)(2,1)S(1)}, u32[]{:S(2)}, u32[]{:S(2)}) collective-permute-start(bf16[512,256]{1,0:T(8,128)(2,1)} %param.8), channel_id=1, source_target_pairs={{0,16},{16,32},{32,48},{48,64},{64,80},{80,96},{96,112},{112,128},... | collective-permute-start | bytes 786440 | tf_op jit(solution)/shard_map/ppermute | solution.py:49
  9.4 19.8 %collective-permute-start.2 = (bf16[512,256]{1,0:T(8,128)(2,1)}, bf16[512,256]{1,0:T(8,128)(2,1)S(1)}, u32[]{:S(2)}, u32[]{:S(2)}) collective-permute-start(bf16[512,256]{1,0:T(8,128)(2,1)} %param.8), channel_id=1, source_target_pairs={{0,1008},{16,0},{32,16},{48,32},{64,48},{80,64},{96,80},{112,96},{... | collective-permute-start | bytes 786440 | tf_op jit(solution)/shard_map/ppermute | solution.py:49
  20.6 15.3 %collective-permute-start.3 = (bf16[512,256]{1,0:T(8,128)(2,1)}, bf16[512,256]{1,0:T(8,128)(2,1)S(1)}, u32[]{:S(2)}, u32[]{:S(2)}) collective-permute-start(bf16[512,256]{1,0:T(8,128)(2,1)} %param.8), channel_id=1, source_target_pairs={{0,992},{16,1008},{32,0},{48,16},{64,32},{80,48},{96,64},{112,80},... | collective-permute-start | bytes 786440 | tf_op jit(solution)/shard_map/ppermute | solution.py:49
  35.9 1.1 copy-start
  69.0 29.3 %copy-start.3 = (bf16[512,256]{1,0:T(8,128)(2,1)S(1)}, bf16[512,256]{1,0:T(8,128)(2,1)}, u32[]{:S(2)}) copy-start(bf16[512,256]{1,0:T(8,128)(2,1)} %cot.1) | copy-start | bytes 786436
  69.0 29.3 %copy-start.4 = (bf16[256,256]{1,0:T(8,128)(2,1)S(1)}, bf16[256,256]{1,0:T(8,128)(2,1)}, u32[]{:S(2)}) copy-start(bf16[256,256]{1,0:T(8,128)(2,1)} %weight.1) | copy-start | bytes 393220
  99.6 16.8 %collective-permute-start.4 = (bf16[512,256]{1,0:T(8,128)(2,1)S(1)}, bf16[512,256]{1,0:T(8,128)(2,1)S(1)}, u32[]{:S(2)}, u32[]{:S(2)}) collective-permute-start(bf16[512,256]{1,0:T(8,128)(2,1)S(1)} %get-tuple-element.19.g0), channel_id=1, source_target_pairs={{0,1},{1,2},{2,3},{3,0},{4,5},{5,6},{6,7},{7,4},{8,9},{9,10},{10,1... | collective-permute-start | bytes 786440 | tf_op jit(solution)/shard_map/ppermute | solution.py:54
  104.5 18.5 %collective-permute-start.5 = (bf16[512,256]{1,0:T(8,128)(2,1)S(1)}, bf16[512,256]{1,0:T(8,128)(2,1)S(1)}, u32[]{:S(2)}, u32[]{:S(2)}) collective-permute-start(bf16[512,256]{1,0:T(8,128)(2,1)S(1)} %get-tuple-element.19.g0), channel_id=1, source_target_pairs={{0,2},{1,3},{2,0},{3,1},{4,6},{5,7},{6,4},{7,5},{8,10},{9,11},{10,... | collective-permute-start | bytes 786440 | tf_op jit(solution)/shard_map/ppermute | solution.py:54
  106.9 25.2 %collective-permute-start.6 = (bf16[512,256]{1,0:T(8,128)(2,1)S(1)}, bf16[512,256]{1,0:T(8,128)(2,1)S(1)}, u32[]{:S(2)}, u32[]{:S(2)}) collective-permute-start(bf16[512,256]{1,0:T(8,128)(2,1)S(1)} %get-tuple-element.19.g0), channel_id=1, source_target_pairs={{0,3},{1,0},{2,1},{3,2},{4,7},{5,4},{6,5},{7,6},{8,11},{9,8},{10,9... | collective-permute-start | bytes 786440 | tf_op jit(solution)/shard_map/ppermute | solution.py:54
  112.1 31.0 %all-to-all-start.2 = ((f32[16,16,256]{2,1,0:T(8,128)}), f32[16,16,256]{2,1,0:T(8,128)S(1)}, u32[]{:S(2)}, u32[]{:S(2)}) async-start(f32[16,16,256]{2,1,0:T(8,128)} %bitcast.10), calls=%async_computation.2 | async-start | bytes 524288 | tf_op jit(solution)/shard_map/all_to_all | solution.py:67
  132.1 34.7 %copy-start.1 = (bf16[1,5,4,128,128]{4,3,2,1,0:T(8,128)(2,1)S(1)}, bf16[1,5,4,128,128]{4,3,2,1,0:T(8,128)(2,1)}, u32[]{:S(2)}) copy-start(bf16[1,5,4,128,128]{4,3,2,1,0:T(8,128)(2,1)} %param.10) | copy-start | bytes 1966084
  132.1 34.7 %copy-start.6 = (s32[1,5]{1,0:T(1,128)S(1)}, s32[1,5]{1,0:T(1,128)}, u32[]{:S(2)}) copy-start(s32[1,5]{1,0:T(1,128)} %cnt.3) | copy-start | bytes 64
  135.2 28.8 %collective-permute-start.7 = (bf16[1024,256]{1,0:T(8,128)(2,1)}, bf16[1024,256]{1,0:T(8,128)(2,1)S(1)}, u32[]{:S(2)}, u32[]{:S(2)}) collective-permute-start(bf16[1024,256]{1,0:T(8,128)(2,1)} %get-tuple-element.22), channel_id=1, source_target_pairs={{0,12},{1,13},{2,14},{3,15},{4,0},{5,1},{6,2},{7,3},{8,4},{9,5},{1... | collective-permute-start | bytes 1572872 | tf_op jit(solution)/shard_map/ppermute | solution.py:59
  138.0 26.0 %collective-permute-start.8 = (bf16[1024,256]{1,0:T(8,128)(2,1)}, bf16[1024,256]{1,0:T(8,128)(2,1)S(1)}, u32[]{:S(2)}, u32[]{:S(2)}) collective-permute-start(bf16[1024,256]{1,0:T(8,128)(2,1)} %get-tuple-element.23), channel_id=1, source_target_pairs={{0,8},{1,9},{2,10},{3,11},{4,12},{5,13},{6,14},{7,15},{8,0},{9,1},... | collective-permute-start | bytes 1572872 | tf_op jit(solution)/shard_map/ppermute | solution.py:59
  141.1 25.6 %collective-permute-start.9 = (bf16[1024,256]{1,0:T(8,128)(2,1)S(1)}, bf16[1024,256]{1,0:T(8,128)(2,1)S(1)}, u32[]{:S(2)}, u32[]{:S(2)}) collective-permute-start(bf16[1024,256]{1,0:T(8,128)(2,1)S(1)} %get-tuple-element.24), channel_id=1, source_target_pairs={{0,4},{1,5},{2,6},{3,7},{4,8},{5,9},{6,10},{7,11},{8,12},{9,13},{1... | collective-permute-start | bytes 1572872 | tf_op jit(solution)/shard_map/ppermute | solution.py:59
  151.9 30.9 %all-to-all-start.4 = ((f32[8,16,256]{2,1,0:T(8,128)}), f32[8,16,256]{2,1,0:T(8,128)S(1)}, u32[]{:S(2)}, u32[]{:S(2)}) async-start(f32[8,16,256]{2,1,0:T(8,128)} %sum_and_spread.4), calls=%async_computation.4 | async-start | bytes 262144 | tf_op jit(solution)/shard_map/all_to_all | solution.py:67
  166.7 1.0 copy-start.8
  171.0 17.6 %collective-permute-start.10 = (bf16[512,256]{1,0:T(8,128)(2,1)}, bf16[512,256]{1,0:T(8,128)(2,1)S(1)}, u32[]{:S(2)}, u32[]{:S(2)}) collective-permute-start(bf16[512,256]{1,0:T(8,128)(2,1)} %get-tuple-element.26), channel_id=1, source_target_pairs={{0,992},{16,1008},{32,0},{48,16},{64,32},{80,48},{96,64},{112,80},... | collective-permute-start | bytes 786440 | tf_op jit(solution)/shard_map/ppermute | solution.py:49
  173.3 21.9 %collective-permute-start.11 = (bf16[512,256]{1,0:T(8,128)(2,1)S(1)}, bf16[512,256]{1,0:T(8,128)(2,1)S(1)}, u32[]{:S(2)}, u32[]{:S(2)}) collective-permute-start(bf16[512,256]{1,0:T(8,128)(2,1)S(1)} %get-tuple-element.27), channel_id=1, source_target_pairs={{0,1008},{16,0},{32,16},{48,32},{64,48},{80,64},{96,80},{112,96},{... | collective-permute-start | bytes 786440 | tf_op jit(solution)/shard_map/ppermute | solution.py:49
  176.6 18.6 %collective-permute-start.12 = (bf16[512,256]{1,0:T(8,128)(2,1)S(1)}, bf16[512,256]{1,0:T(8,128)(2,1)S(1)}, u32[]{:S(2)}, u32[]{:S(2)}) collective-permute-start(bf16[512,256]{1,0:T(8,128)(2,1)S(1)} %get-tuple-element.28), channel_id=1, source_target_pairs={{0,16},{16,32},{32,48},{48,64},{64,80},{80,96},{96,112},{112,128},... | collective-permute-start | bytes 786440 | tf_op jit(solution)/shard_map/ppermute | solution.py:49
  178.9 16.3 %collective-permute-start.13 = (bf16[512,256]{1,0:T(8,128)(2,1)S(1)}, bf16[512,256]{1,0:T(8,128)(2,1)S(1)}, u32[]{:S(2)}, u32[]{:S(2)}) collective-permute-start(bf16[512,256]{1,0:T(8,128)(2,1)S(1)} %get-tuple-element.29), channel_id=1, source_target_pairs={{0,32},{16,48},{32,64},{48,80},{64,96},{80,112},{96,128},{112,144}... | collective-permute-start | bytes 786440 | tf_op jit(solution)/shard_map/ppermute | solution.py:49
  183.5 18.0 %all-to-all-start.5 = ((f32[16,16,256]{2,1,0:T(8,128)}), f32[16,16,256]{2,1,0:T(8,128)S(1)}, u32[]{:S(2)}, u32[]{:S(2)}) async-start(f32[16,16,256]{2,1,0:T(8,128)} %sum_and_spread.5), calls=%async_computation.5 | async-start | bytes 524288 | tf_op jit(solution)/shard_map/all_to_all | solution.py:67
  195.2 1.0 copy-start.10
  (4 other events, 3.2 us)

commit v5 on v4

v5 whole, which is shorter than its diff:
```python
import functools

import jax
import jax.numpy as jnp
from jax import lax
from jax.experimental import pallas as pl
from jax.experimental.pallas import tpu as pltpu
from jax.sharding import PartitionSpec as P

BLOCK = 128
HALF = 2
CAP = 2
XN = 4
YN = 4
INNER = 8
LANES = 128
ID_ROWS = 8

OFFSETS = (-2, -1, 1, 2)
VMEM = pl.BlockSpec(memory_space=pltpu.VMEM)
HBM = pl.BlockSpec(memory_space=pltpu.HBM)
SMEM = pl.BlockSpec(memory_space=pltpu.SMEM)
BF16 = jnp.bfloat16
F32 = jnp.float32

GATHER_FLOPS = 1 << 20
DENSE_FLOPS = 1 << 28
REPLY_FLOPS = 2*10**9
BACK_FLOPS = 2*10**9
FINAL_FLOPS = 2*10**9
SPREAD_FLOPS = 1 << 16


def kernel_call(body, name, outs, ins, mib, flops, scratch=(), out_specs=None):
    nbytes = sum(a.size * a.dtype.itemsize for _, a in ins)
    return pl.pallas_call(
        body,
        out_shape=outs,
        in_specs=[space for space, _ in ins],
        out_specs=out_specs or jax.tree.map(lambda _: VMEM, outs),
        scratch_shapes=list(scratch),
        compiler_params=pltpu.CompilerParams(vmem_limit_bytes=mib << 20),
        cost_estimate=pl.CostEstimate(flops=flops, bytes_accessed=nbytes, transcendentals=0),
        name=name,
    )(*[a for _, a in ins])


def dom_shift(value, steps):
    count = lax.axis_size("dom")
    return lax.ppermute(value, "dom", [(i, (i + steps) % count) for i in range(count)])


def y_shift(value, steps):
    pairs = [(x * YN + y, x * YN + (y + steps) % YN) for x in range(XN) for y in range(YN)]
    return lax.ppermute(value, "rows", pairs)


def x_shift(value, steps):
    pairs = [(x * YN + y, (x + steps) % XN * YN + y) for x in range(XN) for y in range(YN)]
    return lax.ppermute(value, "rows", pairs)


X_GROUPS = [[x * YN + y for x in range(XN)] for y in range(YN)]
Y_GROUPS = [[x * YN + y for y in range(YN)] for x in range(XN)]


def exchange(value, axis, groups=None):
    return lax.all_to_all(
        value, axis, split_axis=0, concat_axis=0, tiled=True, axis_index_groups=groups
    )


def position():
    rank = lax.axis_index("rows")
    return lax.div(rank, YN), lax.rem(rank, YN)


def forward_kernel(src, slot, cnt, fm2, fm1, f0, fp1, fp2, vals, out, acc):
    acc[...] = jnp.zeros_like(acc)
    feats = (fm2, fm1, f0, fp1, fp2)
    tiles_step = vals.shape[0] // len(feats)
    for k, feat in enumerate(feats):
        for t in range(tiles_step):
            block = feat[src[t, k]]
            block = jnp.where(t < cnt[0, k], block, jnp.zeros_like(block))
            acc[slot[t, k]] += jnp.dot(
                vals[k * tiles_step + t], block, preferred_element_type=F32
            )
    for n in range(acc.shape[0]):
        out[n // CAP, pl.ds(n % CAP * BLOCK, BLOCK), :] = acc[n].astype(BF16)


def forward_products(src, slot, cnt, feats, vals):
    channels = feats[0].shape[2]
    return kernel_call(
        forward_kernel,
        "tile_forward",
        jax.ShapeDtypeStruct((XN * YN, CAP * BLOCK, channels), BF16),
        [(SMEM, a) for a in (src, slot, cnt)] + [(VMEM, a) for a in (*feats, vals)],
        12,
        vals.size * 2 * channels,
        [pltpu.VMEM((XN * YN * CAP, BLOCK, channels), F32)],
    )


def ids_kernel(own, i1, i2, i3, out):
    me_x, _ = position()
    out[...] = jnp.zeros_like(out)
    for k, ids in enumerate((own, i1, i2, i3)):
        out[pl.ds(lax.rem(me_x - k + XN, XN), 1), :] = ids[pl.ds(0, 1), :]


def column_ids(ids):
    return kernel_call(
        ids_kernel,
        "column_ids",
        jax.ShapeDtypeStruct(ids[0].shape, jnp.int32),
        [(VMEM, a) for a in ids],
        2,
        1 << 10,
    )


def dense_kernel(i0, i1, i2, i3, recv, weight, cot, act, grad, wgrad, acc):
    me_x, me_y = position()
    first = (me_x * YN + me_y) * CAP
    acc[...] = jnp.zeros_like(acc)
    for k, ids in enumerate((i0, i1, i2, i3)):
        y = lax.rem(me_y - k + YN, YN)
        for x in range(XN):
            for c in range(CAP):
                part = recv[x * YN + y, pl.ds(c * BLOCK, BLOCK), :]
                acc[ids[x, first + c]] += part.astype(F32)
    agg = acc[...].reshape(cot.shape).astype(BF16)
    w = weight[...]
    pre = jnp.dot(agg, w, preferred_element_type=F32)
    sig = 1.0 / (1.0 + jnp.exp(-pre))
    act[...] = (pre * sig).astype(BF16)
    slope = sig * (1.0 + pre * (1.0 - sig))
    pre_grad = (cot[...].astype(F32) * slope).astype(BF16)
    grad[...] = lax.dot_general(
        pre_grad, w, (((1,), (1,)), ((), ())), preferred_element_type=F32
    ).astype(BF16)
    wgrad[...] = lax.dot_general(
        agg, pre_grad, (((0,), (0,)), ((), ())), preferred_element_type=F32
    )


def dense(ids, recv, weight, cot):
    nodes, channels = cot.shape
    full = jax.ShapeDtypeStruct((nodes, channels), BF16)
    return kernel_call(
        dense_kernel,
        "dense_layer",
        (full, full, jax.ShapeDtypeStruct((channels, channels), F32)),
        [(SMEM, a) for a in ids] + [(VMEM, a) for a in (recv, weight, cot)],
        12,
        DENSE_FLOPS,
        [pltpu.VMEM((nodes // BLOCK, BLOCK, channels), F32)],
    )


def reply_kernel(ids, g0, r1, r2, r3, own, o1, o2, o3, held, sem):
    me_x, me_y = position()
    for k, grads in enumerate((g0, r1, r2, r3)):
        y = lax.rem(me_y - k + YN, YN)
        for i, out in enumerate((held, o1, o2, o3)):
            x = lax.rem(me_x - i + XN, XN)
            for c in range(CAP):
                block = ids[x, (me_x * YN + y) * CAP + c]
                spot = pl.multiple_of((y * CAP + c) * BLOCK, BLOCK)
                out[pl.ds(spot, BLOCK), :] = grads[block]
    store = pltpu.make_async_copy(held, own, sem)
    store.start()
    store.wait()


def reply_slots(ids, grads, blocks_dev):
    channels = grads[0].shape[1]
    out = jax.ShapeDtypeStruct((YN * CAP * BLOCK, channels), BF16)
    grads = [g.reshape(blocks_dev, BLOCK, channels) for g in grads]
    return kernel_call(
        reply_kernel,
        "slot_replies",
        (out,) * XN,
        [(SMEM, ids)] + [(VMEM, g) for g in grads],
        6,
        REPLY_FLOPS,
        [pltpu.VMEM(out.shape, BF16), pltpu.SemaphoreType.DMA],
        (HBM,) + (VMEM,) * (XN - 1),
    )


def backward_kernel(
    src, slot, cnt, b0, b1, b2, b3, vals, om2, om1, own, op1, op2, acc, ret, in_sem, out_sem
):
    per_x = YN * CAP
    me_x, _ = position()
    load = pltpu.make_async_copy(b0, ret.at[pl.ds(me_x * per_x, per_x)], in_sem)
    load.start()
    for k, back in ((1, b1), (2, b2), (3, b3)):
        x = lax.rem(me_x + k, XN)
        for j in range(per_x):
            ret[x * per_x + j] = back[pl.ds(j * BLOCK, BLOCK), :]
    load.wait()
    steps = cnt.shape[1]
    tiles_step = vals.shape[0] // steps
    acc[...] = jnp.zeros_like(acc)
    for k in range(steps):
        for t in range(tiles_step):
            block = ret[slot[t, k]]
            block = jnp.where(t < cnt[0, k], block, jnp.zeros_like(block))
            acc[k, src[t, k]] += lax.dot_general(
                vals[k * tiles_step + t],
                block,
                (((0,), (0,)), ((), ())),
                preferred_element_type=F32,
            )
    store = pltpu.make_async_copy(acc.at[HALF], own, out_sem)
    store.start()
    for k, out in ((0, om2), (1, om1), (3, op1), (4, op2)):
        for b in range(acc.shape[1]):
            out[pl.ds(b * BLOCK, BLOCK), :] = acc[k, b].astype(BF16)
    store.wait()


def backward_products(src, slot, cnt, back, vals, blocks_dev):
    nodes, channels = blocks_dev * BLOCK, back[0].shape[1]
    steps = cnt.shape[1]
    send = jax.ShapeDtypeStruct((nodes, channels), BF16)
    own = jax.ShapeDtypeStruct((blocks_dev, BLOCK, channels), F32)
    own_back = back[0].reshape(YN * CAP, BLOCK, channels)
    return kernel_call(
        backward_kernel,
        "tile_backward",
        (send, send, own, send, send),
        [(SMEM, a) for a in (src, slot, cnt)]
        + [(HBM, own_back)]
        + [(VMEM, a) for a in (*back[1:], vals)],
        12,
        BACK_FLOPS,
        [
            pltpu.VMEM((steps, blocks_dev, BLOCK, channels), F32),
            pltpu.VMEM((XN * YN * CAP, BLOCK, channels), BF16),
            pltpu.SemaphoreType.DMA,
            pltpu.SemaphoreType.DMA,
        ],
        (VMEM, VMEM, HBM, VMEM, VMEM),
    )


def final_kernel(own, r1, r2, r3, r4, out, held, sem):
    load = pltpu.make_async_copy(own, held, sem)
    load.start()
    load.wait()
    for b in range(held.shape[0]):
        spot = pl.ds(b * BLOCK, BLOCK)
        total = held[b]
        for r in (r1, r2, r3, r4):
            total = total + r[spot, :].astype(F32)
        out[spot, :] = total.astype(BF16)


def final_sum(own, parts):
    return kernel_call(
        final_kernel,
        "grad_sum",
        jax.ShapeDtypeStruct(parts[0].shape, BF16),
        [(HBM, own)] + [(VMEM, a) for a in parts],
        4,
        FINAL_FLOPS,
        [pltpu.VMEM(own.shape, F32), pltpu.SemaphoreType.DMA],
    )


def spread_kernel(parts, out):
    total = parts[0]
    for i in range(1, parts.shape[0]):
        total = total + parts[i]
    for i in range(out.shape[0]):
        out[i] = total


def sum_and_spread(parts, copies):
    return kernel_call(
        spread_kernel,
        "sum_and_spread",
        jax.ShapeDtypeStruct((copies,) + parts.shape[1:], F32),
        [(VMEM, parts)],
        2,
        SPREAD_FLOPS,
    )


def summed_weight_grad(local_grad):
    channels = local_grad.shape[1]
    rows, dom = lax.axis_size("rows"), lax.axis_size("dom")
    outer = dom // INNER
    near = [[i * INNER + j for j in range(INNER)] for i in range(outer)]
    far = [[i * INNER + j for i in range(outer)] for j in range(INNER)]
    pieces = local_grad.reshape(rows, local_grad.shape[0] // rows, channels)
    piece = sum_and_spread(exchange(pieces, "rows"), INNER)
    piece = sum_and_spread(exchange(piece, "dom", near), outer)
    piece = sum_and_spread(exchange(piece, "dom", far), rows)
    return exchange(piece, "rows").reshape(local_grad.shape)


def per_device(
    features, weight, tile_values, tile_source, tile_slot, slot_block, tile_count, cotangent
):
    blocks_dev = features.shape[0] // BLOCK
    channels = features.shape[1]
    vals = tile_values.reshape(-1, BLOCK, BLOCK)
    src, slot = tile_source[0].T, tile_slot[0].T
    cnt = tile_count

    near = [dom_shift(features, -o) for o in OFFSETS]
    feats = [near[0], near[1], features, near[2], near[3]]
    feats = [f.reshape(blocks_dev, BLOCK, channels) for f in feats]
    recv = exchange(forward_products(src, slot, cnt, feats, vals), "rows")
    ids = jnp.pad(slot_block, ((0, ID_ROWS - 1), (0, LANES - slot_block.shape[1])))
    column = column_ids([ids] + [x_shift(ids, k) for k in range(1, XN)])
    all_ids = [column] + [y_shift(column, k) for k in range(1, YN)]
    activations, grad, local_grad = dense(all_ids, recv, weight, cotangent)

    grads = [grad] + [y_shift(grad, k) for k in range(1, YN)]
    reply = reply_slots(column, grads, blocks_dev)
    back = [reply[0]] + [None] * (XN - 1)
    for k in (1, 3, 2):
        back[k] = x_shift(reply[k], -k)
    terms = list(backward_products(src, slot, cnt, back, vals, blocks_dev))
    own = terms.pop(HALF)
    terms = [dom_shift(t, o) for t, o in zip(terms, OFFSETS)]
    weight_grad = summed_weight_grad(local_grad)
    feature_grad = final_sum(own, terms)
    return (activations, feature_grad, weight_grad)


def solution(mesh):
    return jax.shard_map(
        per_device,
        mesh=mesh,
        in_specs=(
            P(("dom", "rows"), None),
            P(),
            P(("dom", "rows"), None, None, None, None),
            P(("dom", "rows"), None, None),
            P(("dom", "rows"), None, None),
            P(("dom", "rows"), None),
            P(("dom", "rows"), None),
            P(("dom", "rows"), None),
        ),
        out_specs=(P(("dom", "rows"), None), P(("dom", "rows"), None), P()),
        check_vma=False,
    )
```

time: 203 us -> 216 us (1.064)
  starting transfers between devices: 79.6 us -> 130 us
  blocking collectives: 64.5 us -> 15.9 us
  waiting for transfers between devices: 36.1 us -> 49.6 us
    all_to_all x3 -> x1, blocking collectives: 64.5 us -> 15.9 us  [exchange(): lax.all_to_all(value, axis, split_axis=0, concat_axis=0, tiled=True, axis...]
    all_to_all x3 -> x4, starting transfers between devices: 21.5 us -> 42.8 us  [exchange(): lax.all_to_all(value, axis, split_axis=0, concat_axis=0, tiled=True, axis...]
    ppermute x3 -> x6, starting transfers between devices: 12.3 us -> 28.1 us  [y_shift(): return lax.ppermute(value, 'rows', pairs)]
    ppermute x3 -> x6, waiting for transfers between devices: 15.7 us -> 26.9 us  [y_shift(): return lax.ppermute(value, 'rows', pairs)]
    ppermute x3 -> x6, starting transfers between devices: 7.82 us -> 19 us  [x_shift(): return lax.ppermute(value, 'rows', pairs)]
    ppermute x8, waiting for transfers between devices: 13.2 us -> 17.8 us  [dom_shift(): lax.ppermute(value, 'dom', [(i, (i + steps) % count) for i in range(count)])]
    all_to_all x3 -> x4, waiting for transfers between devices: 4.47 us -> 1.48 us  [exchange(): lax.all_to_all(value, axis, split_axis=0, concat_axis=0, tiled=True, axis...]
    unnamed x23 -> x29, local copies, waits for them, and re-layouts: 7.11 us -> 7.59 us
  transfers between devices with their start and end apart: 17 -> 24, of which waited for: 6 -> 10; matrix products, arithmetic and copies ran while one was open for 1% -> 0% of each run, Pallas kernels for 3% -> 3%
where the time goes in v5:
time: 216 us; the launch traced here: 215 us
  starting transfers between devices  130 us (60%)
  waiting for transfers between devices  49.6 us (23%)
  blocking collectives  15.9 us (7%)
  Pallas kernels  11.2 us (5%)
  local copies, waits for them, and re-layouts  7.6 us (4%)
    all_to_all x4, starting transfers between devices, exchange(): lax.all_to_all(value, axis, split_axis=0, concat_axis=0, tiled=True, axis...  42.8 us
    ppermute x8, starting transfers between devices, dom_shift(): lax.ppermute(value, 'dom', [(i, (i + steps) % count) for i in range(count)])  39.8 us
    ppermute x6, starting transfers between devices, y_shift(): return lax.ppermute(value, 'rows', pairs)  28.1 us
    ppermute x6, waiting for transfers between devices, y_shift(): return lax.ppermute(value, 'rows', pairs)  26.9 us
    ppermute x6, starting transfers between devices, x_shift(): return lax.ppermute(value, 'rows', pairs)  19 us
    ppermute x8, waiting for transfers between devices, dom_shift(): lax.ppermute(value, 'dom', [(i, (i + steps) % count) for i in range(count)])  17.8 us
    all_to_all x1, blocking collectives, exchange(): lax.all_to_all(value, axis, split_axis=0, concat_axis=0, tiled=True, axis...  15.9 us
    pallas_call x9, Pallas kernels, kernel_call(): pl.pallas_call(body, out_shape=outs, in_specs=[space for space, _ in ins]...  11.2 us
  transfers between devices with their start and end apart: 24, of which 10 were waited for; matrix products, arithmetic and copies ran while one was open for 0% of the time, Pallas kernels for 3%

profile of v5, /device:TPU:1, one launch (start us, length us, event | category | flops | bytes accessed | tf_op | source)
XLA Modules:
  0.0 214.9 jit_solution(8938392503626920694)
XLA Ops:
  0.6 4.6 %collective-permute-start.7 = (bf16[512,256]{1,0:T(8,128)(2,1)}, bf16[512,256]{1,0:T(8,128)(2,1)S(1)}, u32[]{:S(2)}, u32[]{:S(2)}) collective-permute-start(bf16[512,256]{1,0:T(8,128)(2,1)} %param.8), channel_id=1, source_target_pairs={{0,16},{16,32},{32,48},{48,64},{64,80},{80,96},{96,112},{112,128},... | collective-permute-start | bytes 786440 | tf_op jit(solution)/shard_map/ppermute | solution.py:50
  5.2 3.9 %collective-permute-start.6 = (bf16[512,256]{1,0:T(8,128)(2,1)}, bf16[512,256]{1,0:T(8,128)(2,1)S(1)}, u32[]{:S(2)}, u32[]{:S(2)}) collective-permute-start(bf16[512,256]{1,0:T(8,128)(2,1)} %param.8), channel_id=1, source_target_pairs={{0,32},{16,48},{32,64},{48,80},{64,96},{80,112},{96,128},{112,144}... | collective-permute-start | bytes 786440 | tf_op jit(solution)/shard_map/ppermute | solution.py:50
  9.1 15.1 %collective-permute-start.9 = (bf16[512,256]{1,0:T(8,128)(2,1)}, bf16[512,256]{1,0:T(8,128)(2,1)S(1)}, u32[]{:S(2)}, u32[]{:S(2)}) collective-permute-start(bf16[512,256]{1,0:T(8,128)(2,1)} %param.8), channel_id=1, source_target_pairs={{0,992},{16,1008},{32,0},{48,16},{64,32},{80,48},{96,64},{112,80},... | collective-permute-start | bytes 786440 | tf_op jit(solution)/shard_map/ppermute | solution.py:50
  27.2 3.1 %collective-permute-done.6 = bf16[512,256]{1,0:T(8,128)(2,1)S(1)} collective-permute-done((bf16[512,256]{1,0:T(8,128)(2,1)}, bf16[512,256]{1,0:T(8,128)(2,1)S(1)}, u32[]{:S(2)}, u32[]{:S(2)}) %collective-permute-start.6) | collective-permute-done | bytes 262176 | tf_op jit(solution)/shard_map/ppermute | solution.py:50
  30.3 5.3 %collective-permute-done.8 = bf16[512,256]{1,0:T(8,128)(2,1)S(1)} collective-permute-done((bf16[512,256]{1,0:T(8,128)(2,1)}, bf16[512,256]{1,0:T(8,128)(2,1)S(1)}, u32[]{:S(2)}, u32[]{:S(2)}) %collective-permute-start.8) | collective-permute-done | bytes 262176 | tf_op jit(solution)/shard_map/ppermute | solution.py:50
  42.8 5.8 %all-to-all-start = ((bf16[16,256,256]{2,1,0:T(8,128)(2,1)}), bf16[16,256,256]{2,1,0:T(8,128)(2,1)S(1)}, u32[]{:S(2)}, u32[]{:S(2)}) async-start(bf16[16,256,256]{2,1,0:T(8,128)(2,1)} %tile_forward.1), calls=%async_computation | async-start | bytes 4194304 | tf_op jit(solution)/shard_map/all_to_all | solution.py:68
  48.6 4.5 %collective-permute-start.2 = (s32[8,128]{1,0:T(8,128)S(1)}, s32[8,128]{1,0:T(8,128)S(1)}, u32[]{:S(2)}, u32[]{:S(2)}) collective-permute-start(s32[8,128]{1,0:T(8,128)S(1)} %pad.4.own), channel_id=1, source_target_pairs={{0,12},{1,13},{2,14},{3,15},{4,0},{5,1},{6,2},{7,3},{8,4},{9,5},{1... | collective-permute-start | bytes 12296 | tf_op jit(solution)/shard_map/ppermute | solution.py:60
  61.4 5.2 %collective-permute-start.5 = (s32[8,128]{1,0:T(8,128)S(1)}, s32[8,128]{1,0:T(8,128)S(1)}, u32[]{:S(2)}, u32[]{:S(2)}) collective-permute-start(s32[8,128]{1,0:T(8,128)S(1)} %column_ids.1.i0.ids), channel_id=1, source_target_pairs={{0,3},{1,0},{2,1},{3,2},{4,7},{5,4},{6,5},{7,6},{8,11},{9,8},{10,9... | collective-permute-start | bytes 12296 | tf_op jit(solution)/shard_map/ppermute | solution.py:55
  66.6 5.3 %collective-permute-start.4 = (s32[8,128]{1,0:T(8,128)S(1)}, s32[8,128]{1,0:T(8,128)S(1)}, u32[]{:S(2)}, u32[]{:S(2)}) collective-permute-start(s32[8,128]{1,0:T(8,128)S(1)} %column_ids.1.i0.ids), channel_id=1, source_target_pairs={{0,2},{1,3},{2,0},{3,1},{4,6},{5,7},{6,4},{7,5},{8,10},{9,11},{10,... | collective-permute-start | bytes 12296 | tf_op jit(solution)/shard_map/ppermute | solution.py:55
  71.9 4.3 %collective-permute-start.3 = (s32[8,128]{1,0:T(8,128)S(1)}, s32[8,128]{1,0:T(8,128)S(1)}, u32[]{:S(2)}, u32[]{:S(2)}) collective-permute-start(s32[8,128]{1,0:T(8,128)S(1)} %column_ids.1.i0.ids), channel_id=1, source_target_pairs={{0,1},{1,2},{2,3},{3,0},{4,5},{5,6},{6,7},{7,4},{8,9},{9,10},{10,1... | collective-permute-start | bytes 12296 | tf_op jit(solution)/shard_map/ppermute | solution.py:55
  76.2 19.2 %collective-permute-done.5.i3 = s32[8,128]{1,0:T(8,128)S(1)} collective-permute-done((s32[8,128]{1,0:T(8,128)S(1)}, s32[8,128]{1,0:T(8,128)S(1)}, u32[]{:S(2)}, u32[]{:S(2)}) %collective-permute-start.5) | collective-permute-done | bytes 4128 | tf_op jit(solution)/shard_map/ppermute | solution.py:55
  99.4 23.7 %all-to-all-start.1 = ((f32[16,16,256]{2,1,0:T(8,128)}), f32[16,16,256]{2,1,0:T(8,128)S(1)}, u32[]{:S(2)}, u32[]{:S(2)}) async-start(f32[16,16,256]{2,1,0:T(8,128)} %bitcast.17), calls=%async_computation.1 | async-start | bytes 524288 | tf_op jit(solution)/shard_map/all_to_all | solution.py:68
  123.1 5.4 %collective-permute-start.12 = (bf16[512,256]{1,0:T(8,128)(2,1)S(1)}, bf16[512,256]{1,0:T(8,128)(2,1)S(1)}, u32[]{:S(2)}, u32[]{:S(2)}) collective-permute-start(bf16[512,256]{1,0:T(8,128)(2,1)S(1)} %get-tuple-element.16), channel_id=1, source_target_pairs={{0,3},{1,0},{2,1},{3,2},{4,7},{5,4},{6,5},{7,6},{8,11},{9,8},{10,9... | collective-permute-start | bytes 786440 | tf_op jit(solution)/shard_map/ppermute | solution.py:55
  128.5 4.0 %collective-permute-start.11 = (bf16[512,256]{1,0:T(8,128)(2,1)S(1)}, bf16[512,256]{1,0:T(8,128)(2,1)S(1)}, u32[]{:S(2)}, u32[]{:S(2)}) collective-permute-start(bf16[512,256]{1,0:T(8,128)(2,1)S(1)} %get-tuple-element.16), channel_id=1, source_target_pairs={{0,2},{1,3},{2,0},{3,1},{4,6},{5,7},{6,4},{7,5},{8,10},{9,11},{10,... | collective-permute-start | bytes 786440 | tf_op jit(solution)/shard_map/ppermute | solution.py:55
  132.5 4.0 %collective-permute-start.10 = (bf16[512,256]{1,0:T(8,128)(2,1)S(1)}, bf16[512,256]{1,0:T(8,128)(2,1)S(1)}, u32[]{:S(2)}, u32[]{:S(2)}) collective-permute-start(bf16[512,256]{1,0:T(8,128)(2,1)S(1)} %get-tuple-element.16), channel_id=1, source_target_pairs={{0,1},{1,2},{2,3},{3,0},{4,5},{5,6},{6,7},{7,4},{8,9},{9,10},{10,1... | collective-permute-start | bytes 786440 | tf_op jit(solution)/shard_map/ppermute | solution.py:55
  137.2 5.3 %all-to-all-start.2 = ((f32[8,16,256]{2,1,0:T(8,128)}), f32[8,16,256]{2,1,0:T(8,128)S(1)}, u32[]{:S(2)}, u32[]{:S(2)}) async-start(f32[8,16,256]{2,1,0:T(8,128)} %sum_and_spread.3), calls=%async_computation.2 | async-start | bytes 262144 | tf_op jit(solution)/shard_map/all_to_all | solution.py:68
  143.7 6.4 %collective-permute-done.10 = bf16[512,256]{1,0:T(8,128)(2,1)S(1)} collective-permute-done((bf16[512,256]{1,0:T(8,128)(2,1)S(1)}, bf16[512,256]{1,0:T(8,128)(2,1)S(1)}, u32[]{:S(2)}, u32[]{:S(2)}) %collective-permute-start.10) | collective-permute-done | bytes 262176 | tf_op jit(solution)/shard_map/ppermute | solution.py:55
  152.6 4.6 %collective-permute-start.13 = (bf16[1024,256]{1,0:T(8,128)(2,1)}, bf16[1024,256]{1,0:T(8,128)(2,1)S(1)}, u32[]{:S(2)}, u32[]{:S(2)}) collective-permute-start(bf16[1024,256]{1,0:T(8,128)(2,1)} %get-tuple-element.18), channel_id=1, source_target_pairs={{0,12},{1,13},{2,14},{3,15},{4,0},{5,1},{6,2},{7,3},{8,4},{9,5},{1... | collective-permute-start | bytes 1572872 | tf_op jit(solution)/shard_map/ppermute | solution.py:60
  162.2 15.9 %all_to_all.25.parts = f32[8,16,256]{2,1,0:T(8,128)S(1)} all-to-all(f32[8,16,256]{2,1,0:T(8,128)S(1)} %sum_and_spread.4), channel_id=1, replica_groups={{0,128,256,384,512,640,768,896},{16,144,272,400,528,656,784,912},{32,16..., dimensions={0} | all-to-all | bytes 262144 | tf_op jit(solution)/shard_map/all_to_all | solution.py:68
  178.8 8.0 %all-to-all-start.4 = ((f32[16,16,256]{2,1,0:T(8,128)}), f32[16,16,256]{2,1,0:T(8,128)}, u32[]{:S(2)}, u32[]{:S(2)}) async-start(f32[16,16,256]{2,1,0:T(8,128)} %sum_and_spread.5), calls=%async_computation.4 | async-start | bytes 524288 | tf_op jit(solution)/shard_map/all_to_all | solution.py:68
  191.6 5.8 %collective-permute-start.17 = (bf16[512,256]{1,0:T(8,128)(2,1)S(1)}, bf16[512,256]{1,0:T(8,128)(2,1)S(1)}, u32[]{:S(2)}, u32[]{:S(2)}) collective-permute-start(bf16[512,256]{1,0:T(8,128)(2,1)S(1)} %get-tuple-element.23), channel_id=1, source_target_pairs={{0,1008},{16,0},{32,16},{48,32},{64,48},{80,64},{96,80},{112,96},{... | collective-permute-start | bytes 786440 | tf_op jit(solution)/shard_map/ppermute | solution.py:50
  197.4 3.5 %collective-permute-start.18 = (bf16[512,256]{1,0:T(8,128)(2,1)S(1)}, bf16[512,256]{1,0:T(8,128)(2,1)S(1)}, u32[]{:S(2)}, u32[]{:S(2)}) collective-permute-start(bf16[512,256]{1,0:T(8,128)(2,1)S(1)} %get-tuple-element.24), channel_id=1, source_target_pairs={{0,16},{16,32},{32,48},{48,64},{64,80},{80,96},{96,112},{112,128},... | collective-permute-start | bytes 786440 | tf_op jit(solution)/shard_map/ppermute | solution.py:50
  203.0 4.6 %collective-permute-done.17.r2 = bf16[512,256]{1,0:T(8,128)(2,1)S(1)} collective-permute-done((bf16[512,256]{1,0:T(8,128)(2,1)S(1)}, bf16[512,256]{1,0:T(8,128)(2,1)S(1)}, u32[]{:S(2)}, u32[]{:S(2)}) %collective-permute-start.17) | collective-permute-done | bytes 262176 | tf_op jit(solution)/shard_map/ppermute | solution.py:50
  207.5 4.8 %collective-permute-done.19.r4 = bf16[512,256]{1,0:T(8,128)(2,1)S(1)} collective-permute-done((bf16[512,256]{1,0:T(8,128)(2,1)S(1)}, bf16[512,256]{1,0:T(8,128)(2,1)S(1)}, u32[]{:S(2)}, u32[]{:S(2)}) %collective-permute-start.19) | collective-permute-done | bytes 262176 | tf_op jit(solution)/shard_map/ppermute | solution.py:50
  (64 shorter events, 41.7 us)
Async XLA Ops:
  0.6 26.5 %collective-permute-start.7 = (bf16[512,256]{1,0:T(8,128)(2,1)}, bf16[512,256]{1,0:T(8,128)(2,1)S(1)}, u32[]{:S(2)}, u32[]{:S(2)}) collective-permute-start(bf16[512,256]{1,0:T(8,128)(2,1)} %param.8), channel_id=1, source_target_pairs={{0,16},{16,32},{32,48},{48,64},{64,80},{80,96},{96,112},{112,128},... | collective-permute-start | bytes 786440 | tf_op jit(solution)/shard_map/ppermute | solution.py:50
  5.2 25.1 %collective-permute-start.6 = (bf16[512,256]{1,0:T(8,128)(2,1)}, bf16[512,256]{1,0:T(8,128)(2,1)S(1)}, u32[]{:S(2)}, u32[]{:S(2)}) collective-permute-start(bf16[512,256]{1,0:T(8,128)(2,1)} %param.8), channel_id=1, source_target_pairs={{0,32},{16,48},{32,64},{48,80},{64,96},{80,112},{96,128},{112,144}... | collective-permute-start | bytes 786440 | tf_op jit(solution)/shard_map/ppermute | solution.py:50
  9.1 21.2 %collective-permute-start.9 = (bf16[512,256]{1,0:T(8,128)(2,1)}, bf16[512,256]{1,0:T(8,128)(2,1)S(1)}, u32[]{:S(2)}, u32[]{:S(2)}) collective-permute-start(bf16[512,256]{1,0:T(8,128)(2,1)} %param.8), channel_id=1, source_target_pairs={{0,992},{16,1008},{32,0},{48,16},{64,32},{80,48},{96,64},{112,80},... | collective-permute-start | bytes 786440 | tf_op jit(solution)/shard_map/ppermute | solution.py:50
  24.3 11.3 %collective-permute-start.8 = (bf16[512,256]{1,0:T(8,128)(2,1)}, bf16[512,256]{1,0:T(8,128)(2,1)S(1)}, u32[]{:S(2)}, u32[]{:S(2)}) collective-permute-start(bf16[512,256]{1,0:T(8,128)(2,1)} %param.8), channel_id=1, source_target_pairs={{0,1008},{16,0},{32,16},{48,32},{64,48},{80,64},{96,80},{112,96},{... | collective-permute-start | bytes 786440 | tf_op jit(solution)/shard_map/ppermute | solution.py:50
  42.8 54.1 %all-to-all-start = ((bf16[16,256,256]{2,1,0:T(8,128)(2,1)}), bf16[16,256,256]{2,1,0:T(8,128)(2,1)S(1)}, u32[]{:S(2)}, u32[]{:S(2)}) async-start(bf16[16,256,256]{2,1,0:T(8,128)(2,1)} %tile_forward.1), calls=%async_computation | async-start | bytes 4194304 | tf_op jit(solution)/shard_map/all_to_all | solution.py:68
  48.6 9.5 %collective-permute-start.2 = (s32[8,128]{1,0:T(8,128)S(1)}, s32[8,128]{1,0:T(8,128)S(1)}, u32[]{:S(2)}, u32[]{:S(2)}) collective-permute-start(s32[8,128]{1,0:T(8,128)S(1)} %pad.4.own), channel_id=1, source_target_pairs={{0,12},{1,13},{2,14},{3,15},{4,0},{5,1},{6,2},{7,3},{8,4},{9,5},{1... | collective-permute-start | bytes 12296 | tf_op jit(solution)/shard_map/ppermute | solution.py:60
  53.1 6.5 %collective-permute-start.1 = (s32[8,128]{1,0:T(8,128)S(1)}, s32[8,128]{1,0:T(8,128)S(1)}, u32[]{:S(2)}, u32[]{:S(2)}) collective-permute-start(s32[8,128]{1,0:T(8,128)S(1)} %pad.4.own), channel_id=1, source_target_pairs={{0,8},{1,9},{2,10},{3,11},{4,12},{5,13},{6,14},{7,15},{8,0},{9,1},... | collective-permute-start | bytes 12296 | tf_op jit(solution)/shard_map/ppermute | solution.py:60
  55.6 5.9 %collective-permute-start = (s32[8,128]{1,0:T(8,128)S(1)}, s32[8,128]{1,0:T(8,128)S(1)}, u32[]{:S(2)}, u32[]{:S(2)}) collective-permute-start(s32[8,128]{1,0:T(8,128)S(1)} %pad.4.own), channel_id=1, source_target_pairs={{0,4},{1,5},{2,6},{3,7},{4,8},{5,9},{6,10},{7,11},{8,12},{9,13},{1... | collective-permute-start | bytes 12296 | tf_op jit(solution)/shard_map/ppermute | solution.py:60
  61.4 34.0 %collective-permute-start.5 = (s32[8,128]{1,0:T(8,128)S(1)}, s32[8,128]{1,0:T(8,128)S(1)}, u32[]{:S(2)}, u32[]{:S(2)}) collective-permute-start(s32[8,128]{1,0:T(8,128)S(1)} %column_ids.1.i0.ids), channel_id=1, source_target_pairs={{0,3},{1,0},{2,1},{3,2},{4,7},{5,4},{6,5},{7,6},{8,11},{9,8},{10,9... | collective-permute-start | bytes 12296 | tf_op jit(solution)/shard_map/ppermute | solution.py:55
  66.6 28.8 %collective-permute-start.4 = (s32[8,128]{1,0:T(8,128)S(1)}, s32[8,128]{1,0:T(8,128)S(1)}, u32[]{:S(2)}, u32[]{:S(2)}) collective-permute-start(s32[8,128]{1,0:T(8,128)S(1)} %column_ids.1.i0.ids), channel_id=1, source_target_pairs={{0,2},{1,3},{2,0},{3,1},{4,6},{5,7},{6,4},{7,5},{8,10},{9,11},{10,... | collective-permute-start | bytes 12296 | tf_op jit(solution)/shard_map/ppermute | solution.py:55
  71.9 23.5 %collective-permute-start.3 = (s32[8,128]{1,0:T(8,128)S(1)}, s32[8,128]{1,0:T(8,128)S(1)}, u32[]{:S(2)}, u32[]{:S(2)}) collective-permute-start(s32[8,128]{1,0:T(8,128)S(1)} %column_ids.1.i0.ids), channel_id=1, source_target_pairs={{0,1},{1,2},{2,3},{3,0},{4,5},{5,6},{6,7},{7,4},{8,9},{9,10},{10,1... | collective-permute-start | bytes 12296 | tf_op jit(solution)/shard_map/ppermute | solution.py:55
  99.4 37.1 %all-to-all-start.1 = ((f32[16,16,256]{2,1,0:T(8,128)}), f32[16,16,256]{2,1,0:T(8,128)S(1)}, u32[]{:S(2)}, u32[]{:S(2)}) async-start(f32[16,16,256]{2,1,0:T(8,128)} %bitcast.17), calls=%async_computation.1 | async-start | bytes 524288 | tf_op jit(solution)/shard_map/all_to_all | solution.py:68
  123.1 19.3 %collective-permute-start.12 = (bf16[512,256]{1,0:T(8,128)(2,1)S(1)}, bf16[512,256]{1,0:T(8,128)(2,1)S(1)}, u32[]{:S(2)}, u32[]{:S(2)}) collective-permute-start(bf16[512,256]{1,0:T(8,128)(2,1)S(1)} %get-tuple-element.16), channel_id=1, source_target_pairs={{0,3},{1,0},{2,1},{3,2},{4,7},{5,4},{6,5},{7,6},{8,11},{9,8},{10,9... | collective-permute-start | bytes 786440 | tf_op jit(solution)/shard_map/ppermute | solution.py:55
  128.5 15.2 %collective-permute-start.11 = (bf16[512,256]{1,0:T(8,128)(2,1)S(1)}, bf16[512,256]{1,0:T(8,128)(2,1)S(1)}, u32[]{:S(2)}, u32[]{:S(2)}) collective-permute-start(bf16[512,256]{1,0:T(8,128)(2,1)S(1)} %get-tuple-element.16), channel_id=1, source_target_pairs={{0,2},{1,3},{2,0},{3,1},{4,6},{5,7},{6,4},{7,5},{8,10},{9,11},{10,... | collective-permute-start | bytes 786440 | tf_op jit(solution)/shard_map/ppermute | solution.py:55
  132.5 17.6 %collective-permute-start.10 = (bf16[512,256]{1,0:T(8,128)(2,1)S(1)}, bf16[512,256]{1,0:T(8,128)(2,1)S(1)}, u32[]{:S(2)}, u32[]{:S(2)}) collective-permute-start(bf16[512,256]{1,0:T(8,128)(2,1)S(1)} %get-tuple-element.16), channel_id=1, source_target_pairs={{0,1},{1,2},{2,3},{3,0},{4,5},{5,6},{6,7},{7,4},{8,9},{9,10},{10,1... | collective-permute-start | bytes 786440 | tf_op jit(solution)/shard_map/ppermute | solution.py:55
  137.2 25.0 %all-to-all-start.2 = ((f32[8,16,256]{2,1,0:T(8,128)}), f32[8,16,256]{2,1,0:T(8,128)S(1)}, u32[]{:S(2)}, u32[]{:S(2)}) async-start(f32[8,16,256]{2,1,0:T(8,128)} %sum_and_spread.3), calls=%async_computation.2 | async-start | bytes 262144 | tf_op jit(solution)/shard_map/all_to_all | solution.py:68
  152.6 34.2 %collective-permute-start.13 = (bf16[1024,256]{1,0:T(8,128)(2,1)}, bf16[1024,256]{1,0:T(8,128)(2,1)S(1)}, u32[]{:S(2)}, u32[]{:S(2)}) collective-permute-start(bf16[1024,256]{1,0:T(8,128)(2,1)} %get-tuple-element.18), channel_id=1, source_target_pairs={{0,12},{1,13},{2,14},{3,15},{4,0},{5,1},{6,2},{7,3},{8,4},{9,5},{1... | collective-permute-start | bytes 1572872 | tf_op jit(solution)/shard_map/ppermute | solution.py:60
  157.2 29.6 %collective-permute-start.14 = (bf16[1024,256]{1,0:T(8,128)(2,1)S(1)}, bf16[1024,256]{1,0:T(8,128)(2,1)S(1)}, u32[]{:S(2)}, u32[]{:S(2)}) collective-permute-start(bf16[1024,256]{1,0:T(8,128)(2,1)S(1)} %get-tuple-element.19), channel_id=1, source_target_pairs={{0,8},{1,9},{2,10},{3,11},{4,12},{5,13},{6,14},{7,15},{8,0},{9,1},... | collective-permute-start | bytes 1572872 | tf_op jit(solution)/shard_map/ppermute | solution.py:60
  159.7 27.2 %collective-permute-start.15 = (bf16[1024,256]{1,0:T(8,128)(2,1)S(1)}, bf16[1024,256]{1,0:T(8,128)(2,1)S(1)}, u32[]{:S(2)}, u32[]{:S(2)}) collective-permute-start(bf16[1024,256]{1,0:T(8,128)(2,1)S(1)} %get-tuple-element.20), channel_id=1, source_target_pairs={{0,4},{1,5},{2,6},{3,7},{4,8},{5,9},{6,10},{7,11},{8,12},{9,13},{1... | collective-permute-start | bytes 1572872 | tf_op jit(solution)/shard_map/ppermute | solution.py:60
  178.8 34.5 %all-to-all-start.4 = ((f32[16,16,256]{2,1,0:T(8,128)}), f32[16,16,256]{2,1,0:T(8,128)}, u32[]{:S(2)}, u32[]{:S(2)}) async-start(f32[16,16,256]{2,1,0:T(8,128)} %sum_and_spread.5), calls=%async_computation.4 | async-start | bytes 524288 | tf_op jit(solution)/shard_map/all_to_all | solution.py:68
  189.6 13.3 %collective-permute-start.16 = (bf16[512,256]{1,0:T(8,128)(2,1)S(1)}, bf16[512,256]{1,0:T(8,128)(2,1)S(1)}, u32[]{:S(2)}, u32[]{:S(2)}) collective-permute-start(bf16[512,256]{1,0:T(8,128)(2,1)S(1)} %get-tuple-element.22), channel_id=1, source_target_pairs={{0,992},{16,1008},{32,0},{48,16},{64,32},{80,48},{96,64},{112,80},... | collective-permute-start | bytes 786440 | tf_op jit(solution)/shard_map/ppermute | solution.py:50
  191.6 16.0 %collective-permute-start.17 = (bf16[512,256]{1,0:T(8,128)(2,1)S(1)}, bf16[512,256]{1,0:T(8,128)(2,1)S(1)}, u32[]{:S(2)}, u32[]{:S(2)}) collective-permute-start(bf16[512,256]{1,0:T(8,128)(2,1)S(1)} %get-tuple-element.23), channel_id=1, source_target_pairs={{0,1008},{16,0},{32,16},{48,32},{64,48},{80,64},{96,80},{112,96},{... | collective-permute-start | bytes 786440 | tf_op jit(solution)/shard_map/ppermute | solution.py:50
  197.4 10.1 %collective-permute-start.18 = (bf16[512,256]{1,0:T(8,128)(2,1)S(1)}, bf16[512,256]{1,0:T(8,128)(2,1)S(1)}, u32[]{:S(2)}, u32[]{:S(2)}) collective-permute-start(bf16[512,256]{1,0:T(8,128)(2,1)S(1)} %get-tuple-element.24), channel_id=1, source_target_pairs={{0,16},{16,32},{32,48},{48,64},{64,80},{80,96},{96,112},{112,128},... | collective-permute-start | bytes 786440 | tf_op jit(solution)/shard_map/ppermute | solution.py:50
  200.9 11.4 %collective-permute-start.19 = (bf16[512,256]{1,0:T(8,128)(2,1)S(1)}, bf16[512,256]{1,0:T(8,128)(2,1)S(1)}, u32[]{:S(2)}, u32[]{:S(2)}) collective-permute-start(bf16[512,256]{1,0:T(8,128)(2,1)S(1)} %get-tuple-element.25), channel_id=1, source_target_pairs={{0,32},{16,48},{32,64},{48,80},{64,96},{80,112},{96,128},{112,144}... | collective-permute-start | bytes 786440 | tf_op jit(solution)/shard_map/ppermute | solution.py:50
  (14 other events, 266.8 us)

commit v6 on v5

--- a/solution.py
+++ b/solution.py
@@ -15,6 +15,7 @@
 INNER = 8
 LANES = 128
 ID_ROWS = 8
+FORWARD_MIB = 56
 
 OFFSETS = (-2, -1, 1, 2)
 VMEM = pl.BlockSpec(memory_space=pltpu.VMEM)
@@ -25,9 +26,9 @@
 
 GATHER_FLOPS = 1 << 20
 DENSE_FLOPS = 1 << 28
-REPLY_FLOPS = 2*10**9
-BACK_FLOPS = 2*10**9
-FINAL_FLOPS = 2*10**9
+REPLY_FLOPS = 10**10
+BACK_FLOPS = 10**10
+FINAL_FLOPS = 10**10
 SPREAD_FLOPS = 1 << 16
 
 
@@ -97,7 +98,7 @@
         "tile_forward",
         jax.ShapeDtypeStruct((XN * YN, CAP * BLOCK, channels), BF16),
         [(SMEM, a) for a in (src, slot, cnt)] + [(VMEM, a) for a in (*feats, vals)],
-        12,
+        FORWARD_MIB,
         vals.size * 2 * channels,
         [pltpu.VMEM((XN * YN * CAP, BLOCK, channels), F32)],
     )
@@ -143,7 +144,7 @@
     ).astype(BF16)
     wgrad[...] = lax.dot_general(
         agg, pre_grad, (((0,), (0,)), ((), ())), preferred_element_type=F32
-    )
+    ).astype(BF16)
 
 
 def dense(ids, recv, weight, cot):
@@ -152,7 +153,7 @@
     return kernel_call(
         dense_kernel,
         "dense_layer",
-        (full, full, jax.ShapeDtypeStruct((channels, channels), F32)),
+        (full, full, jax.ShapeDtypeStruct((channels, channels), BF16)),
         [(SMEM, a) for a in ids] + [(VMEM, a) for a in (recv, weight, cot)],
         12,
         DENSE_FLOPS,
@@ -274,18 +275,18 @@
 
 
 def spread_kernel(parts, out):
-    total = parts[0]
+    total = parts[0].astype(F32)
     for i in range(1, parts.shape[0]):
-        total = total + parts[i]
+        total = total + parts[i].astype(F32)
     for i in range(out.shape[0]):
-        out[i] = total
-
-
-def sum_and_spread(parts, copies):
+        out[i] = total.astype(out.dtype)
+
+
+def sum_and_spread(parts, copies, dtype=F32):
     return kernel_call(
         spread_kernel,
         "sum_and_spread",
-        jax.ShapeDtypeStruct((copies,) + parts.shape[1:], F32),
+        jax.ShapeDtypeStruct((copies,) + parts.shape[1:], dtype),
         [(VMEM, parts)],
         2,
         SPREAD_FLOPS,
@@ -301,8 +302,8 @@
     pieces = local_grad.reshape(rows, local_grad.shape[0] // rows, channels)
     piece = sum_and_spread(exchange(pieces, "rows"), INNER)
     piece = sum_and_spread(exchange(piece, "dom", near), outer)
-    piece = sum_and_spread(exchange(piece, "dom", far), rows)
-    return exchange(piece, "rows").reshape(local_grad.shape)
+    piece = sum_and_spread(exchange(piece, "dom", far), rows, BF16)
+    return exchange(piece, "rows").reshape(local_grad.shape).astype(F32)
 
 
 def per_device(

time: 216 us -> 207 us (0.958)
  blocking collectives: 15.9 us -> 8.41 us
  local copies, waits for them, and re-layouts: 7.6 us -> 4.42 us
  starting transfers between devices: 130 us -> 127 us
  waiting for transfers between devices: 49.6 us -> 51.8 us
    all_to_all x4, starting transfers between devices: 42.8 us -> 32 us  [exchange(): lax.all_to_all(value, axis, split_axis=0, concat_axis=0, tiled=True, axis...]
    ppermute x6, starting transfers between devices: 28.1 us -> 36.8 us  [y_shift(): return lax.ppermute(value, 'rows', pairs)]
    all_to_all x1, blocking collectives: 15.9 us -> 8.41 us  [exchange(): lax.all_to_all(value, axis, split_axis=0, concat_axis=0, tiled=True, axis...]
    ppermute x8, waiting for transfers between devices: 17.8 us -> 10.7 us  [dom_shift(): lax.ppermute(value, 'dom', [(i, (i + steps) % count) for i in range(count)])]
    all_to_all x4, waiting for transfers between devices: 1.48 us -> 8.51 us  [exchange(): lax.all_to_all(value, axis, split_axis=0, concat_axis=0, tiled=True, axis...]
    unnamed x29 -> x30, local copies, waits for them, and re-layouts: 7.59 us -> 4.41 us
    ppermute x6, waiting for transfers between devices: 3.36 us -> 6.3 us  [x_shift(): return lax.ppermute(value, 'rows', pairs)]
where the time goes in v6:
time: 207 us; the launch traced here: 206 us
  starting transfers between devices  127 us (61%)
  waiting for transfers between devices  51.8 us (25%)
  Pallas kernels  12 us (6%)
  blocking collectives  8.41 us (4%)
  local copies, waits for them, and re-layouts  4.42 us (2%)
    ppermute x8, starting transfers between devices, dom_shift(): lax.ppermute(value, 'dom', [(i, (i + steps) % count) for i in range(count)])  38.2 us
    ppermute x6, starting transfers between devices, y_shift(): return lax.ppermute(value, 'rows', pairs)  36.8 us
    all_to_all x4, starting transfers between devices, exchange(): lax.all_to_all(value, axis, split_axis=0, concat_axis=0, tiled=True, axis...  32 us
    ppermute x6, waiting for transfers between devices, y_shift(): return lax.ppermute(value, 'rows', pairs)  26.3 us
    ppermute x6, starting transfers between devices, x_shift(): return lax.ppermute(value, 'rows', pairs)  20.2 us
    pallas_call x9, Pallas kernels, kernel_call(): pl.pallas_call(body, out_shape=outs, in_specs=[space for space, _ in ins]...  12 us
    ppermute x8, waiting for transfers between devices, dom_shift(): lax.ppermute(value, 'dom', [(i, (i + steps) % count) for i in range(count)])  10.7 us
    all_to_all x4, waiting for transfers between devices, exchange(): lax.all_to_all(value, axis, split_axis=0, concat_axis=0, tiled=True, axis...  8.51 us
  transfers between devices with their start and end apart: 24, of which 10 were waited for; matrix products, arithmetic and copies ran while one was open for 0% of the time, Pallas kernels for 3%

profile of v6, /device:TPU:1, one launch (start us, length us, event | category | flops | bytes accessed | tf_op | source)
XLA Modules:
  0.0 205.6 jit_solution(4297892497564372004)
XLA Ops:
  0.6 4.6 %collective-permute-start.7 = (bf16[512,256]{1,0:T(8,128)(2,1)}, bf16[512,256]{1,0:T(8,128)(2,1)S(1)}, u32[]{:S(2)}, u32[]{:S(2)}) collective-permute-start(bf16[512,256]{1,0:T(8,128)(2,1)} %param.8), channel_id=1, source_target_pairs={{0,16},{16,32},{32,48},{48,64},{64,80},{80,96},{96,112},{112,128},... | collective-permute-start | bytes 786440 | tf_op jit(solution)/shard_map/ppermute | solution.py:51
  5.2 3.9 %collective-permute-start.6 = (bf16[512,256]{1,0:T(8,128)(2,1)}, bf16[512,256]{1,0:T(8,128)(2,1)S(1)}, u32[]{:S(2)}, u32[]{:S(2)}) collective-permute-start(bf16[512,256]{1,0:T(8,128)(2,1)} %param.8), channel_id=1, source_target_pairs={{0,32},{16,48},{32,64},{48,80},{64,96},{80,112},{96,128},{112,144}... | collective-permute-start | bytes 786440 | tf_op jit(solution)/shard_map/ppermute | solution.py:51
  9.1 15.1 %collective-permute-start.9 = (bf16[512,256]{1,0:T(8,128)(2,1)}, bf16[512,256]{1,0:T(8,128)(2,1)S(1)}, u32[]{:S(2)}, u32[]{:S(2)}) collective-permute-start(bf16[512,256]{1,0:T(8,128)(2,1)} %param.8), channel_id=1, source_target_pairs={{0,992},{16,1008},{32,0},{48,16},{64,32},{80,48},{96,64},{112,80},... | collective-permute-start | bytes 786440 | tf_op jit(solution)/shard_map/ppermute | solution.py:51
  27.2 3.1 %collective-permute-done.6 = bf16[512,256]{1,0:T(8,128)(2,1)S(1)} collective-permute-done((bf16[512,256]{1,0:T(8,128)(2,1)}, bf16[512,256]{1,0:T(8,128)(2,1)S(1)}, u32[]{:S(2)}, u32[]{:S(2)}) %collective-permute-start.6) | collective-permute-done | bytes 262176 | tf_op jit(solution)/shard_map/ppermute | solution.py:51
  30.3 5.3 %collective-permute-done.8 = bf16[512,256]{1,0:T(8,128)(2,1)S(1)} collective-permute-done((bf16[512,256]{1,0:T(8,128)(2,1)}, bf16[512,256]{1,0:T(8,128)(2,1)S(1)}, u32[]{:S(2)}, u32[]{:S(2)}) %collective-permute-start.8) | collective-permute-done | bytes 262176 | tf_op jit(solution)/shard_map/ppermute | solution.py:51
  36.3 3.9 %tile_forward.1 = bf16[16,256,256]{2,1,0:T(8,128)(2,1)} custom-call(s32[4,5]{1,0:T(4,128)} %bitcast.23, s32[4,5]{1,0:T(4,128)} %bitcast.25, s32[1,5]{1,0:T(1,128)} %cnt.3, bf16[4,128,256]{2,1,0:T(8,128)(2,1)} %bitcast.34, bf16[4,128,256]{2,1,0:T(8,128)(2,1)} %bitcast.33, bf16[4,128,256]{2,1,0:T(8,128)(2,1)} %bitcast.32, bf16[4,128,256]{2,1,0:T(8,128)(2,1)} %bitcast.36, ...), custom_call_target="tpu_custom_call" | custom-call | flops 167772160 | bytes 1966260 | tf_op jit(solution)/shard_map/tile_forward/pallas_call | solution.py:37
  40.3 5.8 %all-to-all-start = ((bf16[16,256,256]{2,1,0:T(8,128)(2,1)}), bf16[16,256,256]{2,1,0:T(8,128)(2,1)S(1)}, u32[]{:S(2)}, u32[]{:S(2)}) async-start(bf16[16,256,256]{2,1,0:T(8,128)(2,1)} %tile_forward.1), calls=%async_computation | async-start | bytes 4194304 | tf_op jit(solution)/shard_map/all_to_all | solution.py:69
  46.1 4.5 %collective-permute-start.2 = (s32[8,128]{1,0:T(8,128)S(1)}, s32[8,128]{1,0:T(8,128)S(1)}, u32[]{:S(2)}, u32[]{:S(2)}) collective-permute-start(s32[8,128]{1,0:T(8,128)S(1)} %pad.4.own), channel_id=1, source_target_pairs={{0,12},{1,13},{2,14},{3,15},{4,0},{5,1},{6,2},{7,3},{8,4},{9,5},{1... | collective-permute-start | bytes 12296 | tf_op jit(solution)/shard_map/ppermute | solution.py:61
  59.0 5.2 %collective-permute-start.5 = (s32[8,128]{1,0:T(8,128)S(1)}, s32[8,128]{1,0:T(8,128)S(1)}, u32[]{:S(2)}, u32[]{:S(2)}) collective-permute-start(s32[8,128]{1,0:T(8,128)S(1)} %column_ids.1.i0.ids), channel_id=1, source_target_pairs={{0,3},{1,0},{2,1},{3,2},{4,7},{5,4},{6,5},{7,6},{8,11},{9,8},{10,9... | collective-permute-start | bytes 12296 | tf_op jit(solution)/shard_map/ppermute | solution.py:56
  64.2 5.4 %collective-permute-start.4 = (s32[8,128]{1,0:T(8,128)S(1)}, s32[8,128]{1,0:T(8,128)S(1)}, u32[]{:S(2)}, u32[]{:S(2)}) collective-permute-start(s32[8,128]{1,0:T(8,128)S(1)} %column_ids.1.i0.ids), channel_id=1, source_target_pairs={{0,2},{1,3},{2,0},{3,1},{4,6},{5,7},{6,4},{7,5},{8,10},{9,11},{10,... | collective-permute-start | bytes 12296 | tf_op jit(solution)/shard_map/ppermute | solution.py:56
  69.5 4.3 %collective-permute-start.3 = (s32[8,128]{1,0:T(8,128)S(1)}, s32[8,128]{1,0:T(8,128)S(1)}, u32[]{:S(2)}, u32[]{:S(2)}) collective-permute-start(s32[8,128]{1,0:T(8,128)S(1)} %column_ids.1.i0.ids), channel_id=1, source_target_pairs={{0,1},{1,2},{2,3},{3,0},{4,5},{5,6},{6,7},{7,4},{8,9},{9,10},{10,1... | collective-permute-start | bytes 12296 | tf_op jit(solution)/shard_map/ppermute | solution.py:56
  73.8 19.3 %collective-permute-done.5.i3 = s32[8,128]{1,0:T(8,128)S(1)} collective-permute-done((s32[8,128]{1,0:T(8,128)S(1)}, s32[8,128]{1,0:T(8,128)S(1)}, u32[]{:S(2)}, u32[]{:S(2)}) %collective-permute-start.5) | collective-permute-done | bytes 4128 | tf_op jit(solution)/shard_map/ppermute | solution.py:56
  98.4 13.0 %collective-permute-start.12 = (bf16[512,256]{1,0:T(8,128)(2,1)S(1)}, bf16[512,256]{1,0:T(8,128)(2,1)S(1)}, u32[]{:S(2)}, u32[]{:S(2)}) collective-permute-start(bf16[512,256]{1,0:T(8,128)(2,1)S(1)} %get-tuple-element.16), channel_id=1, source_target_pairs={{0,3},{1,0},{2,1},{3,2},{4,7},{5,4},{6,5},{7,6},{8,11},{9,8},{10,9... | collective-permute-start | bytes 786440 | tf_op jit(solution)/shard_map/ppermute | solution.py:56
  111.4 5.9 %collective-permute-start.11 = (bf16[512,256]{1,0:T(8,128)(2,1)S(1)}, bf16[512,256]{1,0:T(8,128)(2,1)S(1)}, u32[]{:S(2)}, u32[]{:S(2)}) collective-permute-start(bf16[512,256]{1,0:T(8,128)(2,1)S(1)} %get-tuple-element.16), channel_id=1, source_target_pairs={{0,2},{1,3},{2,0},{3,1},{4,6},{5,7},{6,4},{7,5},{8,10},{9,11},{10,... | collective-permute-start | bytes 786440 | tf_op jit(solution)/shard_map/ppermute | solution.py:56
  117.4 3.1 %collective-permute-start.10 = (bf16[512,256]{1,0:T(8,128)(2,1)S(1)}, bf16[512,256]{1,0:T(8,128)(2,1)S(1)}, u32[]{:S(2)}, u32[]{:S(2)}) collective-permute-start(bf16[512,256]{1,0:T(8,128)(2,1)S(1)} %get-tuple-element.16), channel_id=1, source_target_pairs={{0,1},{1,2},{2,3},{3,0},{4,5},{5,6},{6,7},{7,4},{8,9},{9,10},{10,1... | collective-permute-start | bytes 786440 | tf_op jit(solution)/shard_map/ppermute | solution.py:56
  120.4 7.0 %all-to-all-start.1 = ((bf16[16,16,256]{2,1,0:T(8,128)(2,1)}), bf16[16,16,256]{2,1,0:T(8,128)(2,1)S(1)}, u32[]{:S(2)}, u32[]{:S(2)}) async-start(bf16[16,16,256]{2,1,0:T(8,128)(2,1)} %bitcast.17), calls=%async_computation.1 | async-start | bytes 262144 | tf_op jit(solution)/shard_map/all_to_all | solution.py:69
  127.5 7.1 %collective-permute-done.10 = bf16[512,256]{1,0:T(8,128)(2,1)S(1)} collective-permute-done((bf16[512,256]{1,0:T(8,128)(2,1)S(1)}, bf16[512,256]{1,0:T(8,128)(2,1)S(1)}, u32[]{:S(2)}, u32[]{:S(2)}) %collective-permute-start.10) | collective-permute-done | bytes 262176 | tf_op jit(solution)/shard_map/ppermute | solution.py:56
  137.0 6.4 %collective-permute-start.13 = (bf16[1024,256]{1,0:T(8,128)(2,1)}, bf16[1024,256]{1,0:T(8,128)(2,1)S(1)}, u32[]{:S(2)}, u32[]{:S(2)}) collective-permute-start(bf16[1024,256]{1,0:T(8,128)(2,1)} %get-tuple-element.18), channel_id=1, source_target_pairs={{0,12},{1,13},{2,14},{3,15},{4,0},{5,1},{6,2},{7,3},{8,4},{9,5},{1... | collective-permute-start | bytes 1572872 | tf_op jit(solution)/shard_map/ppermute | solution.py:61
  147.9 8.4 %all_to_all.25.parts = f32[8,16,256]{2,1,0:T(8,128)S(1)} all-to-all(f32[8,16,256]{2,1,0:T(8,128)S(1)} %sum_and_spread.3), channel_id=1, replica_groups={{0,16,32,48,64,80,96,112},{128,144,160,176,192,208,224,240},{256,272,28..., dimensions={0} | all-to-all | bytes 262144 | tf_op jit(solution)/shard_map/all_to_all | solution.py:69
  156.9 12.0 %all-to-all-start.3 = ((f32[8,16,256]{2,1,0:T(8,128)}), f32[8,16,256]{2,1,0:T(8,128)S(1)}, u32[]{:S(2)}, u32[]{:S(2)}) async-start(f32[8,16,256]{2,1,0:T(8,128)} %sum_and_spread.4), calls=%async_computation.3 | async-start | bytes 262144 | tf_op jit(solution)/shard_map/all_to_all | solution.py:69
  168.9 2.9 %collective-permute-done.15.b3 = bf16[1024,256]{1,0:T(8,128)(2,1)S(1)} collective-permute-done((bf16[1024,256]{1,0:T(8,128)(2,1)S(1)}, bf16[1024,256]{1,0:T(8,128)(2,1)S(1)}, u32[]{:S(2)}, u32[]{:S(2)}) %collective-permute-start.15) | collective-permute-done | bytes 524320 | tf_op jit(solution)/shard_map/ppermute | solution.py:61
  175.4 3.9 %collective-permute-start.16 = (bf16[512,256]{1,0:T(8,128)(2,1)S(1)}, bf16[512,256]{1,0:T(8,128)(2,1)S(1)}, u32[]{:S(2)}, u32[]{:S(2)}) collective-permute-start(bf16[512,256]{1,0:T(8,128)(2,1)S(1)} %get-tuple-element.22), channel_id=1, source_target_pairs={{0,992},{16,1008},{32,0},{48,16},{64,32},{80,48},{96,64},{112,80},... | collective-permute-start | bytes 786440 | tf_op jit(solution)/shard_map/ppermute | solution.py:51
  187.9 7.1 %all-to-all-start.4 = ((bf16[16,16,256]{2,1,0:T(8,128)(2,1)}), bf16[16,16,256]{2,1,0:T(8,128)(2,1)S(1)}, u32[]{:S(2)}, u32[]{:S(2)}) async-start(bf16[16,16,256]{2,1,0:T(8,128)(2,1)} %sum_and_spread.5), calls=%async_computation.4 | async-start | bytes 262144 | tf_op jit(solution)/shard_map/all_to_all | solution.py:69
  199.2 5.7 %all-to-all-done.4 = bf16[16,16,256]{2,1,0:T(8,128)(2,1)S(1)} async-done(((bf16[16,16,256]{2,1,0:T(8,128)(2,1)}), bf16[16,16,256]{2,1,0:T(8,128)(2,1)S(1)}, u32[]{:S(2)}, u32[]{:S(2)}) %all-to-all-start.4) | async-done | bytes 131104 | tf_op jit(solution)/shard_map/all_to_all | solution.py:69
  (66 shorter events, 41.6 us)
Async XLA Ops:
  0.6 26.5 %collective-permute-start.7 = (bf16[512,256]{1,0:T(8,128)(2,1)}, bf16[512,256]{1,0:T(8,128)(2,1)S(1)}, u32[]{:S(2)}, u32[]{:S(2)}) collective-permute-start(bf16[512,256]{1,0:T(8,128)(2,1)} %param.8), channel_id=1, source_target_pairs={{0,16},{16,32},{32,48},{48,64},{64,80},{80,96},{96,112},{112,128},... | collective-permute-start | bytes 786440 | tf_op jit(solution)/shard_map/ppermute | solution.py:51
  5.2 25.1 %collective-permute-start.6 = (bf16[512,256]{1,0:T(8,128)(2,1)}, bf16[512,256]{1,0:T(8,128)(2,1)S(1)}, u32[]{:S(2)}, u32[]{:S(2)}) collective-permute-start(bf16[512,256]{1,0:T(8,128)(2,1)} %param.8), channel_id=1, source_target_pairs={{0,32},{16,48},{32,64},{48,80},{64,96},{80,112},{96,128},{112,144}... | collective-permute-start | bytes 786440 | tf_op jit(solution)/shard_map/ppermute | solution.py:51
  9.1 21.2 %collective-permute-start.9 = (bf16[512,256]{1,0:T(8,128)(2,1)}, bf16[512,256]{1,0:T(8,128)(2,1)S(1)}, u32[]{:S(2)}, u32[]{:S(2)}) collective-permute-start(bf16[512,256]{1,0:T(8,128)(2,1)} %param.8), channel_id=1, source_target_pairs={{0,992},{16,1008},{32,0},{48,16},{64,32},{80,48},{96,64},{112,80},... | collective-permute-start | bytes 786440 | tf_op jit(solution)/shard_map/ppermute | solution.py:51
  24.3 11.3 %collective-permute-start.8 = (bf16[512,256]{1,0:T(8,128)(2,1)}, bf16[512,256]{1,0:T(8,128)(2,1)S(1)}, u32[]{:S(2)}, u32[]{:S(2)}) collective-permute-start(bf16[512,256]{1,0:T(8,128)(2,1)} %param.8), channel_id=1, source_target_pairs={{0,1008},{16,0},{32,16},{48,32},{64,48},{80,64},{96,80},{112,96},{... | collective-permute-start | bytes 786440 | tf_op jit(solution)/shard_map/ppermute | solution.py:51
  40.3 55.6 %all-to-all-start = ((bf16[16,256,256]{2,1,0:T(8,128)(2,1)}), bf16[16,256,256]{2,1,0:T(8,128)(2,1)S(1)}, u32[]{:S(2)}, u32[]{:S(2)}) async-start(bf16[16,256,256]{2,1,0:T(8,128)(2,1)} %tile_forward.1), calls=%async_computation | async-start | bytes 4194304 | tf_op jit(solution)/shard_map/all_to_all | solution.py:69
  46.1 9.5 %collective-permute-start.2 = (s32[8,128]{1,0:T(8,128)S(1)}, s32[8,128]{1,0:T(8,128)S(1)}, u32[]{:S(2)}, u32[]{:S(2)}) collective-permute-start(s32[8,128]{1,0:T(8,128)S(1)} %pad.4.own), channel_id=1, source_target_pairs={{0,12},{1,13},{2,14},{3,15},{4,0},{5,1},{6,2},{7,3},{8,4},{9,5},{1... | collective-permute-start | bytes 12296 | tf_op jit(solution)/shard_map/ppermute | solution.py:61
  50.6 6.4 %collective-permute-start.1 = (s32[8,128]{1,0:T(8,128)S(1)}, s32[8,128]{1,0:T(8,128)S(1)}, u32[]{:S(2)}, u32[]{:S(2)}) collective-permute-start(s32[8,128]{1,0:T(8,128)S(1)} %pad.4.own), channel_id=1, source_target_pairs={{0,8},{1,9},{2,10},{3,11},{4,12},{5,13},{6,14},{7,15},{8,0},{9,1},... | collective-permute-start | bytes 12296 | tf_op jit(solution)/shard_map/ppermute | solution.py:61
  53.1 5.9 %collective-permute-start = (s32[8,128]{1,0:T(8,128)S(1)}, s32[8,128]{1,0:T(8,128)S(1)}, u32[]{:S(2)}, u32[]{:S(2)}) collective-permute-start(s32[8,128]{1,0:T(8,128)S(1)} %pad.4.own), channel_id=1, source_target_pairs={{0,4},{1,5},{2,6},{3,7},{4,8},{5,9},{6,10},{7,11},{8,12},{9,13},{1... | collective-permute-start | bytes 12296 | tf_op jit(solution)/shard_map/ppermute | solution.py:61
  59.0 34.1 %collective-permute-start.5 = (s32[8,128]{1,0:T(8,128)S(1)}, s32[8,128]{1,0:T(8,128)S(1)}, u32[]{:S(2)}, u32[]{:S(2)}) collective-permute-start(s32[8,128]{1,0:T(8,128)S(1)} %column_ids.1.i0.ids), channel_id=1, source_target_pairs={{0,3},{1,0},{2,1},{3,2},{4,7},{5,4},{6,5},{7,6},{8,11},{9,8},{10,9... | collective-permute-start | bytes 12296 | tf_op jit(solution)/shard_map/ppermute | solution.py:56
  64.2 28.9 %collective-permute-start.4 = (s32[8,128]{1,0:T(8,128)S(1)}, s32[8,128]{1,0:T(8,128)S(1)}, u32[]{:S(2)}, u32[]{:S(2)}) collective-permute-start(s32[8,128]{1,0:T(8,128)S(1)} %column_ids.1.i0.ids), channel_id=1, source_target_pairs={{0,2},{1,3},{2,0},{3,1},{4,6},{5,7},{6,4},{7,5},{8,10},{9,11},{10,... | collective-permute-start | bytes 12296 | tf_op jit(solution)/shard_map/ppermute | solution.py:56
  69.5 23.6 %collective-permute-start.3 = (s32[8,128]{1,0:T(8,128)S(1)}, s32[8,128]{1,0:T(8,128)S(1)}, u32[]{:S(2)}, u32[]{:S(2)}) collective-permute-start(s32[8,128]{1,0:T(8,128)S(1)} %column_ids.1.i0.ids), channel_id=1, source_target_pairs={{0,1},{1,2},{2,3},{3,0},{4,5},{5,6},{6,7},{7,4},{8,9},{9,10},{10,1... | collective-permute-start | bytes 12296 | tf_op jit(solution)/shard_map/ppermute | solution.py:56
  98.4 29.1 %collective-permute-start.12 = (bf16[512,256]{1,0:T(8,128)(2,1)S(1)}, bf16[512,256]{1,0:T(8,128)(2,1)S(1)}, u32[]{:S(2)}, u32[]{:S(2)}) collective-permute-start(bf16[512,256]{1,0:T(8,128)(2,1)S(1)} %get-tuple-element.16), channel_id=1, source_target_pairs={{0,3},{1,0},{2,1},{3,2},{4,7},{5,4},{6,5},{7,6},{8,11},{9,8},{10,9... | collective-permute-start | bytes 786440 | tf_op jit(solution)/shard_map/ppermute | solution.py:56
  111.4 16.1 %collective-permute-start.11 = (bf16[512,256]{1,0:T(8,128)(2,1)S(1)}, bf16[512,256]{1,0:T(8,128)(2,1)S(1)}, u32[]{:S(2)}, u32[]{:S(2)}) collective-permute-start(bf16[512,256]{1,0:T(8,128)(2,1)S(1)} %get-tuple-element.16), channel_id=1, source_target_pairs={{0,2},{1,3},{2,0},{3,1},{4,6},{5,7},{6,4},{7,5},{8,10},{9,11},{10,... | collective-permute-start | bytes 786440 | tf_op jit(solution)/shard_map/ppermute | solution.py:56
  117.4 17.2 %collective-permute-start.10 = (bf16[512,256]{1,0:T(8,128)(2,1)S(1)}, bf16[512,256]{1,0:T(8,128)(2,1)S(1)}, u32[]{:S(2)}, u32[]{:S(2)}) collective-permute-start(bf16[512,256]{1,0:T(8,128)(2,1)S(1)} %get-tuple-element.16), channel_id=1, source_target_pairs={{0,1},{1,2},{2,3},{3,0},{4,5},{5,6},{6,7},{7,4},{8,9},{9,10},{10,1... | collective-permute-start | bytes 786440 | tf_op jit(solution)/shard_map/ppermute | solution.py:56
  120.4 27.4 %all-to-all-start.1 = ((bf16[16,16,256]{2,1,0:T(8,128)(2,1)}), bf16[16,16,256]{2,1,0:T(8,128)(2,1)S(1)}, u32[]{:S(2)}, u32[]{:S(2)}) async-start(bf16[16,16,256]{2,1,0:T(8,128)(2,1)} %bitcast.17), calls=%async_computation.1 | async-start | bytes 262144 | tf_op jit(solution)/shard_map/all_to_all | solution.py:69
  137.0 31.9 %collective-permute-start.13 = (bf16[1024,256]{1,0:T(8,128)(2,1)}, bf16[1024,256]{1,0:T(8,128)(2,1)S(1)}, u32[]{:S(2)}, u32[]{:S(2)}) collective-permute-start(bf16[1024,256]{1,0:T(8,128)(2,1)} %get-tuple-element.18), channel_id=1, source_target_pairs={{0,12},{1,13},{2,14},{3,15},{4,0},{5,1},{6,2},{7,3},{8,4},{9,5},{1... | collective-permute-start | bytes 1572872 | tf_op jit(solution)/shard_map/ppermute | solution.py:61
  143.4 25.5 %collective-permute-start.14 = (bf16[1024,256]{1,0:T(8,128)(2,1)S(1)}, bf16[1024,256]{1,0:T(8,128)(2,1)S(1)}, u32[]{:S(2)}, u32[]{:S(2)}) collective-permute-start(bf16[1024,256]{1,0:T(8,128)(2,1)S(1)} %get-tuple-element.19), channel_id=1, source_target_pairs={{0,8},{1,9},{2,10},{3,11},{4,12},{5,13},{6,14},{7,15},{8,0},{9,1},... | collective-permute-start | bytes 1572872 | tf_op jit(solution)/shard_map/ppermute | solution.py:61
  145.3 26.6 %collective-permute-start.15 = (bf16[1024,256]{1,0:T(8,128)(2,1)S(1)}, bf16[1024,256]{1,0:T(8,128)(2,1)S(1)}, u32[]{:S(2)}, u32[]{:S(2)}) collective-permute-start(bf16[1024,256]{1,0:T(8,128)(2,1)S(1)} %get-tuple-element.20), channel_id=1, source_target_pairs={{0,4},{1,5},{2,6},{3,7},{4,8},{5,9},{6,10},{7,11},{8,12},{9,13},{1... | collective-permute-start | bytes 1572872 | tf_op jit(solution)/shard_map/ppermute | solution.py:61
  156.9 30.3 %all-to-all-start.3 = ((f32[8,16,256]{2,1,0:T(8,128)}), f32[8,16,256]{2,1,0:T(8,128)S(1)}, u32[]{:S(2)}, u32[]{:S(2)}) async-start(f32[8,16,256]{2,1,0:T(8,128)} %sum_and_spread.4), calls=%async_computation.3 | async-start | bytes 262144 | tf_op jit(solution)/shard_map/all_to_all | solution.py:69
  175.4 19.6 %collective-permute-start.16 = (bf16[512,256]{1,0:T(8,128)(2,1)S(1)}, bf16[512,256]{1,0:T(8,128)(2,1)S(1)}, u32[]{:S(2)}, u32[]{:S(2)}) collective-permute-start(bf16[512,256]{1,0:T(8,128)(2,1)S(1)} %get-tuple-element.22), channel_id=1, source_target_pairs={{0,992},{16,1008},{32,0},{48,16},{64,32},{80,48},{96,64},{112,80},... | collective-permute-start | bytes 786440 | tf_op jit(solution)/shard_map/ppermute | solution.py:51
  179.4 15.7 %collective-permute-start.17 = (bf16[512,256]{1,0:T(8,128)(2,1)S(1)}, bf16[512,256]{1,0:T(8,128)(2,1)S(1)}, u32[]{:S(2)}, u32[]{:S(2)}) collective-permute-start(bf16[512,256]{1,0:T(8,128)(2,1)S(1)} %get-tuple-element.23), channel_id=1, source_target_pairs={{0,1008},{16,0},{32,16},{48,32},{64,48},{80,64},{96,80},{112,96},{... | collective-permute-start | bytes 786440 | tf_op jit(solution)/shard_map/ppermute | solution.py:51
  182.1 13.0 %collective-permute-start.18 = (bf16[512,256]{1,0:T(8,128)(2,1)S(1)}, bf16[512,256]{1,0:T(8,128)(2,1)S(1)}, u32[]{:S(2)}, u32[]{:S(2)}) collective-permute-start(bf16[512,256]{1,0:T(8,128)(2,1)S(1)} %get-tuple-element.24), channel_id=1, source_target_pairs={{0,16},{16,32},{32,48},{48,64},{64,80},{80,96},{96,112},{112,128},... | collective-permute-start | bytes 786440 | tf_op jit(solution)/shard_map/ppermute | solution.py:51
  184.9 12.3 %collective-permute-start.19 = (bf16[512,256]{1,0:T(8,128)(2,1)S(1)}, bf16[512,256]{1,0:T(8,128)(2,1)S(1)}, u32[]{:S(2)}, u32[]{:S(2)}) collective-permute-start(bf16[512,256]{1,0:T(8,128)(2,1)S(1)} %get-tuple-element.25), channel_id=1, source_target_pairs={{0,32},{16,48},{32,64},{48,80},{64,96},{80,112},{96,128},{112,144}... | collective-permute-start | bytes 786440 | tf_op jit(solution)/shard_map/ppermute | solution.py:51
  187.9 17.0 %all-to-all-start.4 = ((bf16[16,16,256]{2,1,0:T(8,128)(2,1)}), bf16[16,16,256]{2,1,0:T(8,128)(2,1)S(1)}, u32[]{:S(2)}, u32[]{:S(2)}) async-start(bf16[16,16,256]{2,1,0:T(8,128)(2,1)} %sum_and_spread.5), calls=%async_computation.4 | async-start | bytes 262144 | tf_op jit(solution)/shard_map/all_to_all | solution.py:69
  (15 other events, 289.9 us)

commit v7 on v6

--- a/solution.py
+++ b/solution.py
@@ -14,17 +14,18 @@
 YN = 4
 INNER = 8
 LANES = 128
-ID_ROWS = 8
+ID_ROWS = 16
 FORWARD_MIB = 56
 
 OFFSETS = (-2, -1, 1, 2)
 VMEM = pl.BlockSpec(memory_space=pltpu.VMEM)
 HBM = pl.BlockSpec(memory_space=pltpu.HBM)
+ANY = pl.BlockSpec(memory_space=pl.ANY)
 SMEM = pl.BlockSpec(memory_space=pltpu.SMEM)
 BF16 = jnp.bfloat16
 F32 = jnp.float32
 
-GATHER_FLOPS = 1 << 20
+GATHER_FLOPS = 10**11
 DENSE_FLOPS = 1 << 28
 REPLY_FLOPS = 10**10
 BACK_FLOPS = 10**10
@@ -76,7 +77,8 @@
     return lax.div(rank, YN), lax.rem(rank, YN)
 
 
-def forward_kernel(src, slot, cnt, fm2, fm1, f0, fp1, fp2, vals, out, acc):
+def forward_kernel(src, slot, cnt, ids, fm2, fm1, f0, fp1, fp2, vals, *refs):
+    outs, acc = refs[:-1], refs[-1]
     acc[...] = jnp.zeros_like(acc)
     feats = (fm2, fm1, f0, fp1, fp2)
     tiles_step = vals.shape[0] // len(feats)
@@ -87,52 +89,92 @@
             acc[slot[t, k]] += jnp.dot(
                 vals[k * tiles_step + t], block, preferred_element_type=F32
             )
-    for n in range(acc.shape[0]):
-        out[n // CAP, pl.ds(n % CAP * BLOCK, BLOCK), :] = acc[n].astype(BF16)
-
-
-def forward_products(src, slot, cnt, feats, vals):
-    channels = feats[0].shape[2]
+    me_x, _ = position()
+    per_x = YN * CAP
+    line = lax.broadcasted_iota(jnp.int32, (ID_ROWS, LANES), 0)
+    for k in range(XN):
+        x = lax.rem(me_x + k, XN)
+        rows = jnp.zeros_like(line)
+        for j in range(per_x):
+            total = acc[x * per_x + j].astype(BF16)
+            rows = jnp.where(line == j, ids[0, x * per_x + j], rows)
+            for h in range(2):
+                part = total[:, h * LANES : (h + 1) * LANES]
+                outs[h * XN + k][pl.ds(j * BLOCK, BLOCK), :] = part
+        outs[k][pl.ds(per_x * BLOCK, ID_ROWS), :] = rows.astype(F32).astype(BF16)
+
+
+def forward_products(src, slot, cnt, feats, vals, ids):
+    rows = YN * CAP * BLOCK
+    first = jax.ShapeDtypeStruct((rows + ID_ROWS, LANES), BF16)
+    second = jax.ShapeDtypeStruct((rows, LANES), BF16)
     return kernel_call(
         forward_kernel,
         "tile_forward",
-        jax.ShapeDtypeStruct((XN * YN, CAP * BLOCK, channels), BF16),
-        [(SMEM, a) for a in (src, slot, cnt)] + [(VMEM, a) for a in (*feats, vals)],
+        (first,) * XN + (second,) * XN,
+        [(SMEM, a) for a in (src, slot, cnt, ids)] + [(VMEM, a) for a in (*feats, vals)],
         FORWARD_MIB,
-        vals.size * 2 * channels,
-        [pltpu.VMEM((XN * YN * CAP, BLOCK, channels), F32)],
-    )
-
-
-def ids_kernel(own, i1, i2, i3, out):
-    me_x, _ = position()
-    out[...] = jnp.zeros_like(out)
-    for k, ids in enumerate((own, i1, i2, i3)):
-        out[pl.ds(lax.rem(me_x - k + XN, XN), 1), :] = ids[pl.ds(0, 1), :]
-
-
-def column_ids(ids):
-    return kernel_call(
-        ids_kernel,
-        "column_ids",
-        jax.ShapeDtypeStruct(ids[0].shape, jnp.int32),
-        [(VMEM, a) for a in ids],
-        2,
-        1 << 10,
-    )
-
-
-def dense_kernel(i0, i1, i2, i3, recv, weight, cot, act, grad, wgrad, acc):
-    me_x, me_y = position()
-    first = (me_x * YN + me_y) * CAP
-    acc[...] = jnp.zeros_like(acc)
-    for k, ids in enumerate((i0, i1, i2, i3)):
-        y = lax.rem(me_y - k + YN, YN)
-        for x in range(XN):
+        vals.size * 4 * LANES,
+        [pltpu.VMEM((XN * YN * CAP, BLOCK, 2 * LANES), F32)],
+    )
+
+
+def gather_kernel(blocks_dev, recv, ids, outs):
+    _, me_y = position()
+    chunk = 64
+    for i, out in enumerate(outs):
+        y = lax.rem(me_y + i, YN)
+        rows = {}
+        for k in range(XN):
             for c in range(CAP):
-                part = recv[x * YN + y, pl.ds(c * BLOCK, BLOCK), :]
-                acc[ids[x, first + c]] += part.astype(F32)
-    agg = acc[...].reshape(cot.shape).astype(BF16)
+                rows[k, c] = ids[pl.ds(k * YN * CAP + y * CAP + c, 1), :][:, :LANES]
+        for start in range(0, BLOCK, chunk):
+            totals = [jnp.zeros((chunk, LANES), F32) for _ in range(blocks_dev)]
+            for (k, c), row in rows.items():
+                spot = pl.multiple_of((y * CAP + c) * BLOCK + start, chunk)
+                part = recv[k][pl.ds(spot, chunk), :].astype(F32)
+                for b in range(blocks_dev):
+                    totals[b] = totals[b] + jnp.where(row == float(b), part, 0.0)
+            for b in range(blocks_dev):
+                out[pl.ds(b * BLOCK + start, chunk), :] = totals[b].astype(BF16)
+
+
+def gather0_kernel(blocks_dev, *refs):
+    recv, outs, ids = refs[:XN], refs[XN:-1], refs[-1]
+    per_x = YN * CAP
+    for k in range(XN):
+        got = recv[k][pl.ds(per_x * BLOCK, ID_ROWS), :].astype(F32)[:per_x]
+        ids[pl.ds(k * per_x, per_x), :] = jnp.concatenate([got, got], axis=1)
+    gather_kernel(blocks_dev, recv, ids, outs)
+
+
+def gather1_kernel(blocks_dev, *refs):
+    gather_kernel(blocks_dev, refs[:XN], refs[XN], refs[XN + 1 :])
+
+
+def gather_blocks(recv, blocks_dev, ids=None):
+    outs = (jax.ShapeDtypeStruct((blocks_dev * BLOCK, LANES), BF16),) * YN
+    if ids is None:
+        outs += (jax.ShapeDtypeStruct((XN * YN * CAP, 2 * LANES), F32),)
+    return kernel_call(
+        functools.partial(gather0_kernel if ids is None else gather1_kernel, blocks_dev),
+        "block_sums",
+        outs,
+        [(VMEM, a) for a in recv] + ([] if ids is None else [(VMEM, ids)]),
+        6,
+        GATHER_FLOPS,
+    )
+
+
+def dense_kernel(*refs):
+    parts, (weight, cot, act, grad, wgrad) = refs[: 2 * YN], refs[2 * YN :]
+    halves = []
+    for h in range(2):
+        total = parts[h * YN][...].astype(F32)
+        for k in range(1, YN):
+            total = total + parts[h * YN + k][...].astype(F32)
+        halves.append(total.astype(BF16))
+    agg = jnp.concatenate(halves, axis=1)
     w = weight[...]
     pre = jnp.dot(agg, w, preferred_element_type=F32)
     sig = 1.0 / (1.0 + jnp.exp(-pre))
@@ -147,30 +189,36 @@
     ).astype(BF16)
 
 
-def dense(ids, recv, weight, cot):
+def dense(parts, weight, cot):
     nodes, channels = cot.shape
     full = jax.ShapeDtypeStruct((nodes, channels), BF16)
     return kernel_call(
         dense_kernel,
         "dense_layer",
         (full, full, jax.ShapeDtypeStruct((channels, channels), BF16)),
-        [(SMEM, a) for a in ids] + [(VMEM, a) for a in (recv, weight, cot)],
-        12,
+        [(VMEM, a) for a in (*parts, weight, cot)],
+        10,
         DENSE_FLOPS,
-        [pltpu.VMEM((nodes // BLOCK, BLOCK, channels), F32)],
     )
 
 
 def reply_kernel(ids, g0, r1, r2, r3, own, o1, o2, o3, held, sem):
-    me_x, me_y = position()
+    _, me_y = position()
+    chunk = 32
     for k, grads in enumerate((g0, r1, r2, r3)):
         y = lax.rem(me_y - k + YN, YN)
-        for i, out in enumerate((held, o1, o2, o3)):
-            x = lax.rem(me_x - i + XN, XN)
+        rows = {}
+        for i in range(XN):
             for c in range(CAP):
-                block = ids[x, (me_x * YN + y) * CAP + c]
-                spot = pl.multiple_of((y * CAP + c) * BLOCK, BLOCK)
-                out[pl.ds(spot, BLOCK), :] = grads[block]
+                rows[i, c] = ids[pl.ds(i * YN * CAP + y * CAP + c, 1), :]
+        for start in range(0, BLOCK, chunk):
+            blocks = [grads[b, pl.ds(start, chunk), :].astype(F32) for b in range(grads.shape[0])]
+            for (i, c), row in rows.items():
+                picked = jnp.where(row == 0.0, blocks[0], 0.0)
+                for b in range(1, len(blocks)):
+                    picked = jnp.where(row == float(b), blocks[b], picked)
+                spot = pl.multiple_of((y * CAP + c) * BLOCK + start, chunk)
+                (held, o1, o2, o3)[i][pl.ds(spot, chunk), :] = picked.astype(BF16)
     store = pltpu.make_async_copy(held, own, sem)
     store.start()
     store.wait()
@@ -184,7 +232,7 @@
         reply_kernel,
         "slot_replies",
         (out,) * XN,
-        [(SMEM, ids)] + [(VMEM, g) for g in grads],
+        [(VMEM, a) for a in (ids, *grads)],
         6,
         REPLY_FLOPS,
         [pltpu.VMEM(out.shape, BF16), pltpu.SemaphoreType.DMA],
@@ -193,7 +241,7 @@
 
 
 def backward_kernel(
-    src, slot, cnt, b0, b1, b2, b3, vals, om2, om1, own, op1, op2, acc, ret, in_sem, out_sem
+    src, slot, cnt, after, b0, b1, b2, b3, vals, om2, om1, own, op1, op2, acc, ret, in_sem, out_sem
 ):
     per_x = YN * CAP
     me_x, _ = position()
@@ -225,7 +273,7 @@
     store.wait()
 
 
-def backward_products(src, slot, cnt, back, vals, blocks_dev):
+def backward_products(src, slot, cnt, back, vals, blocks_dev, after):
     nodes, channels = blocks_dev * BLOCK, back[0].shape[1]
     steps = cnt.shape[1]
     send = jax.ShapeDtypeStruct((nodes, channels), BF16)
@@ -236,7 +284,7 @@
         "tile_backward",
         (send, send, own, send, send),
         [(SMEM, a) for a in (src, slot, cnt)]
-        + [(HBM, own_back)]
+        + [(ANY, after), (HBM, own_back)]
         + [(VMEM, a) for a in (*back[1:], vals)],
         12,
         BACK_FLOPS,
@@ -293,17 +341,15 @@
     )
 
 
-def summed_weight_grad(local_grad):
-    channels = local_grad.shape[1]
+def weight_piece(local_grad):
     rows, dom = lax.axis_size("rows"), lax.axis_size("dom")
     outer = dom // INNER
     near = [[i * INNER + j for j in range(INNER)] for i in range(outer)]
     far = [[i * INNER + j for i in range(outer)] for j in range(INNER)]
-    pieces = local_grad.reshape(rows, local_grad.shape[0] // rows, channels)
+    pieces = local_grad.reshape(rows, local_grad.shape[0] // rows, local_grad.shape[1])
     piece = sum_and_spread(exchange(pieces, "rows"), INNER)
     piece = sum_and_spread(exchange(piece, "dom", near), outer)
-    piece = sum_and_spread(exchange(piece, "dom", far), rows, BF16)
-    return exchange(piece, "rows").reshape(local_grad.shape).astype(F32)
+    return sum_and_spread(exchange(piece, "dom", far), rows, BF16)
 
 
 def per_device(
@@ -318,21 +364,25 @@
     near = [dom_shift(features, -o) for o in OFFSETS]
     feats = [near[0], near[1], features, near[2], near[3]]
     feats = [f.reshape(blocks_dev, BLOCK, channels) for f in feats]
-    recv = exchange(forward_products(src, slot, cnt, feats, vals), "rows")
-    ids = jnp.pad(slot_block, ((0, ID_ROWS - 1), (0, LANES - slot_block.shape[1])))
-    column = column_ids([ids] + [x_shift(ids, k) for k in range(1, XN)])
-    all_ids = [column] + [y_shift(column, k) for k in range(1, YN)]
-    activations, grad, local_grad = dense(all_ids, recv, weight, cotangent)
-
+    sent = forward_products(src, slot, cnt, feats, vals, slot_block)
+    got0 = [sent[0]] + [x_shift(sent[k], k) for k in range(1, XN)]
+    got1 = [sent[XN]] + [x_shift(sent[XN + k], k) for k in range(1, XN)]
+    *sums0, ids = gather_blocks(got0, blocks_dev)
+    parts = [sums0[0]] + [y_shift(sums0[k], k) for k in range(1, YN)]
+    sums1 = gather_blocks(got1, blocks_dev, ids)
+    parts += [sums1[0]] + [y_shift(sums1[k], k) for k in range(1, YN)]
+    activations, grad, local_grad = dense(parts, weight, cotangent)
+
+    piece = weight_piece(local_grad)
     grads = [grad] + [y_shift(grad, k) for k in range(1, YN)]
-    reply = reply_slots(column, grads, blocks_dev)
+    reply = reply_slots(ids, grads, blocks_dev)
     back = [reply[0]] + [None] * (XN - 1)
     for k in (1, 3, 2):
         back[k] = x_shift(reply[k], -k)
-    terms = list(backward_products(src, slot, cnt, back, vals, blocks_dev))
+    terms = list(backward_products(src, slot, cnt, back, vals, blocks_dev, piece))
     own = terms.pop(HALF)
     terms = [dom_shift(t, o) for t, o in zip(terms, OFFSETS)]
-    weight_grad = summed_weight_grad(local_grad)
+    weight_grad = exchange(piece, "rows").reshape(local_grad.shape).astype(F32)
     feature_grad = final_sum(own, terms)
     return (activations, feature_grad, weight_grad)
 

time: 207 us -> 209 us (level)
  blocking collectives: 8.41 us -> 46 us
  waiting for transfers between devices: 51.8 us -> 27.6 us
  starting transfers between devices: 127 us -> 114 us
    all_to_all x1 -> x2, blocking collectives: 8.41 us -> 46 us  [exchange(): lax.all_to_all(value, axis, split_axis=0, concat_axis=0, tiled=True, axis...]
    all_to_all x4 -> x2, starting transfers between devices: 32 us -> 11.5 us  [exchange(): lax.all_to_all(value, axis, split_axis=0, concat_axis=0, tiled=True, axis...]
    ppermute x6 -> x9, waiting for transfers between devices: 26.3 us -> 7.51 us  [y_shift(): return lax.ppermute(value, 'rows', pairs)]
    all_to_all x4 -> x2, waiting for transfers between devices: 8.51 us -> 0.01 us  [exchange(): lax.all_to_all(value, axis, split_axis=0, concat_axis=0, tiled=True, axis...]
    ppermute x8, waiting for transfers between devices: 10.7 us -> 16.2 us  [dom_shift(): lax.ppermute(value, 'dom', [(i, (i + steps) % count) for i in range(count)])]
    ppermute x6 -> x9, starting transfers between devices: 20.2 us -> 25.1 us  [x_shift(): return lax.ppermute(value, 'rows', pairs)]
    ppermute x8, starting transfers between devices: 38.2 us -> 41.5 us  [dom_shift(): lax.ppermute(value, 'dom', [(i, (i + steps) % count) for i in range(count)])]
    ppermute x6 -> x9, waiting for transfers between devices: 6.3 us -> 3.9 us  [x_shift(): return lax.ppermute(value, 'rows', pairs)]
  transfers between devices with their start and end apart: 24 -> 28, of which waited for: 10 -> 8; matrix products, arithmetic and copies ran while one was open for 0% -> 0% of each run, Pallas kernels for 3% -> 3%
where the time goes in v7:
time: 209 us; the launch traced here: 208 us
  starting transfers between devices  114 us (55%)
  blocking collectives  46 us (22%)
  waiting for transfers between devices  27.6 us (13%)
  Pallas kernels  12.1 us (6%)
  local copies, waits for them, and re-layouts  6 us (3%)
    all_to_all x2, blocking collectives, exchange(): lax.all_to_all(value, axis, split_axis=0, concat_axis=0, tiled=True, axis...  46 us
    ppermute x8, starting transfers between devices, dom_shift(): lax.ppermute(value, 'dom', [(i, (i + steps) % count) for i in range(count)])  41.5 us
    ppermute x9, starting transfers between devices, y_shift(): return lax.ppermute(value, 'rows', pairs)  36.3 us
    ppermute x9, starting transfers between devices, x_shift(): return lax.ppermute(value, 'rows', pairs)  25.1 us
    ppermute x8, waiting for transfers between devices, dom_shift(): lax.ppermute(value, 'dom', [(i, (i + steps) % count) for i in range(count)])  16.2 us
    pallas_call x10, Pallas kernels, kernel_call(): pl.pallas_call(body, out_shape=outs, in_specs=[space for space, _ in ins]...  12.1 us
    all_to_all x2, starting transfers between devices, exchange(): lax.all_to_all(value, axis, split_axis=0, concat_axis=0, tiled=True, axis...  11.5 us
    ppermute x9, waiting for transfers between devices, y_shift(): return lax.ppermute(value, 'rows', pairs)  7.51 us
  transfers between devices with their start and end apart: 28, of which 8 were waited for; matrix products, arithmetic and copies ran while one was open for 0% of the time, Pallas kernels for 3%

profile of v7, /device:TPU:1, one launch (start us, length us, event | category | flops | bytes accessed | tf_op | source)
XLA Modules:
  0.0 207.9 jit_solution(14828574835063052443)
XLA Ops:
  0.6 4.0 %collective-permute-start = (bf16[512,256]{1,0:T(8,128)(2,1)}, bf16[512,256]{1,0:T(8,128)(2,1)S(1)}, u32[]{:S(2)}, u32[]{:S(2)}) collective-permute-start(bf16[512,256]{1,0:T(8,128)(2,1)} %param.8), channel_id=1, source_target_pairs={{0,32},{16,48},{32,64},{48,80},{64,96},{80,112},{96,128},{112,144}... | collective-permute-start | bytes 786440 | tf_op jit(solution)/shard_map/ppermute | solution.py:52
  4.7 4.7 %collective-permute-start.1 = (bf16[512,256]{1,0:T(8,128)(2,1)}, bf16[512,256]{1,0:T(8,128)(2,1)S(1)}, u32[]{:S(2)}, u32[]{:S(2)}) collective-permute-start(bf16[512,256]{1,0:T(8,128)(2,1)} %param.8), channel_id=1, source_target_pairs={{0,16},{16,32},{32,48},{48,64},{64,80},{80,96},{96,112},{112,128},... | collective-permute-start | bytes 786440 | tf_op jit(solution)/shard_map/ppermute | solution.py:52
  9.4 11.1 %collective-permute-start.2 = (bf16[512,256]{1,0:T(8,128)(2,1)}, bf16[512,256]{1,0:T(8,128)(2,1)S(1)}, u32[]{:S(2)}, u32[]{:S(2)}) collective-permute-start(bf16[512,256]{1,0:T(8,128)(2,1)} %param.8), channel_id=1, source_target_pairs={{0,1008},{16,0},{32,16},{48,32},{64,48},{80,64},{96,80},{112,96},{... | collective-permute-start | bytes 786440 | tf_op jit(solution)/shard_map/ppermute | solution.py:52
  20.6 6.3 %collective-permute-start.3 = (bf16[512,256]{1,0:T(8,128)(2,1)}, bf16[512,256]{1,0:T(8,128)(2,1)S(1)}, u32[]{:S(2)}, u32[]{:S(2)}) collective-permute-start(bf16[512,256]{1,0:T(8,128)(2,1)} %param.8), channel_id=1, source_target_pairs={{0,992},{16,1008},{32,0},{48,16},{64,32},{80,48},{96,64},{112,80},... | collective-permute-start | bytes 786440 | tf_op jit(solution)/shard_map/ppermute | solution.py:52
  26.9 8.9 %collective-permute-done.3 = bf16[512,256]{1,0:T(8,128)(2,1)S(1)} collective-permute-done((bf16[512,256]{1,0:T(8,128)(2,1)}, bf16[512,256]{1,0:T(8,128)(2,1)S(1)}, u32[]{:S(2)}, u32[]{:S(2)}) %collective-permute-start.3) | collective-permute-done | bytes 262176 | tf_op jit(solution)/shard_map/ppermute | solution.py:52
  36.5 3.8 %tile_forward.1 = (bf16[1040,128]{1,0:T(8,128)(2,1)}, bf16[1040,128]{1,0:T(8,128)(2,1)}, bf16[1040,128]{1,0:T(8,128)(2,1)}, bf16[1040,128]{1,0:T(8,128)(2,1)}, b...) custom-call(s32[4,5]{1,0:T(4,128)} %bitcast.24, ...), custom_call_target="tpu_custom_call" | custom-call | flops 167772160 | bytes 1966388 | tf_op jit(solution)/shard_map/tile_forward/pallas_call | solution.py:38
  44.6 4.1 %collective-permute-start.6 = (bf16[1040,128]{1,0:T(8,128)(2,1)}, bf16[1040,128]{1,0:T(8,128)(2,1)S(1)}, u32[]{:S(2)}, u32[]{:S(2)}) collective-permute-start(bf16[1040,128]{1,0:T(8,128)(2,1)} %get-tuple-element.35), channel_id=1, source_target_pairs={{0,12},{1,13},{2,14},{3,15},{4,0},{5,1},{6,2},{7,3},{8,4},{9,5},{1... | collective-permute-start | bytes 798728 | tf_op jit(solution)/shard_map/ppermute | solution.py:62
  51.2 3.7 %collective-permute-start.11 = (bf16[1024,128]{1,0:T(8,128)(2,1)}, bf16[1024,128]{1,0:T(8,128)(2,1)S(1)}, u32[]{:S(2)}, u32[]{:S(2)}) collective-permute-start(bf16[1024,128]{1,0:T(8,128)(2,1)} %get-tuple-element.42), channel_id=1, source_target_pairs={{0,8},{1,9},{2,10},{3,11},{4,12},{5,13},{6,14},{7,15},{8,0},{9,1},... | collective-permute-start | bytes 786440 | tf_op jit(solution)/shard_map/ppermute | solution.py:62
  63.4 3.5 %collective-permute-start.8 = (bf16[512,128]{1,0:T(8,128)(2,1)S(1)}, bf16[512,128]{1,0:T(8,128)(2,1)S(1)}, u32[]{:S(2)}, u32[]{:S(2)}) collective-permute-start(bf16[512,128]{1,0:T(8,128)(2,1)S(1)} %get-tuple-element.38), channel_id=1, source_target_pairs={{0,2},{1,3},{2,0},{3,1},{4,6},{5,7},{6,4},{7,5},{8,10},{9,11},{10,... | collective-permute-start | bytes 393224 | tf_op jit(solution)/shard_map/ppermute | solution.py:57
  68.0 3.9 %collective-permute-start.9 = (bf16[512,128]{1,0:T(8,128)(2,1)S(1)}, bf16[512,128]{1,0:T(8,128)(2,1)S(1)}, u32[]{:S(2)}, u32[]{:S(2)}) collective-permute-start(bf16[512,128]{1,0:T(8,128)(2,1)S(1)} %get-tuple-element.39), channel_id=1, source_target_pairs={{0,3},{1,0},{2,1},{3,2},{4,7},{5,4},{6,5},{7,6},{8,11},{9,8},{10,9... | collective-permute-start | bytes 393224 | tf_op jit(solution)/shard_map/ppermute | solution.py:57
  75.6 5.2 %collective-permute-start.14 = (bf16[512,128]{1,0:T(8,128)(2,1)S(1)}, bf16[512,128]{1,0:T(8,128)(2,1)S(1)}, u32[]{:S(2)}, u32[]{:S(2)}) collective-permute-start(bf16[512,128]{1,0:T(8,128)(2,1)S(1)} %get-tuple-element.47), channel_id=1, source_target_pairs={{0,2},{1,3},{2,0},{3,1},{4,6},{5,7},{6,4},{7,5},{8,10},{9,11},{10,... | collective-permute-start | bytes 393224 | tf_op jit(solution)/shard_map/ppermute | solution.py:57
  80.8 5.5 %collective-permute-start.15 = (bf16[512,128]{1,0:T(8,128)(2,1)S(1)}, bf16[512,128]{1,0:T(8,128)(2,1)S(1)}, u32[]{:S(2)}, u32[]{:S(2)}) collective-permute-start(bf16[512,128]{1,0:T(8,128)(2,1)S(1)} %get-tuple-element.48), channel_id=1, source_target_pairs={{0,3},{1,0},{2,1},{3,2},{4,7},{5,4},{6,5},{7,6},{8,11},{9,8},{10,9... | collective-permute-start | bytes 393224 | tf_op jit(solution)/shard_map/ppermute | solution.py:57
  87.3 6.5 %collective-permute-done.15.refs_7_ = bf16[512,128]{1,0:T(8,128)(2,1)S(1)} collective-permute-done((bf16[512,128]{1,0:T(8,128)(2,1)S(1)}, bf16[512,128]{1,0:T(8,128)(2,1)S(1)}, u32[]{:S(2)}, u32[]{:S(2)}) %collective-permute-start.15) | collective-permute-done | bytes 131104 | tf_op jit(solution)/shard_map/ppermute | solution.py:57
  94.9 3.8 %collective-permute-start.16 = (bf16[512,256]{1,0:T(8,128)(2,1)S(1)}, bf16[512,256]{1,0:T(8,128)(2,1)S(1)}, u32[]{:S(2)}, u32[]{:S(2)}) collective-permute-start(bf16[512,256]{1,0:T(8,128)(2,1)S(1)} %get-tuple-element.51), channel_id=1, source_target_pairs={{0,1},{1,2},{2,3},{3,0},{4,5},{5,6},{6,7},{7,4},{8,9},{9,10},{10,1... | collective-permute-start | bytes 786440 | tf_op jit(solution)/shard_map/ppermute | solution.py:57
  98.7 4.1 %collective-permute-start.17 = (bf16[512,256]{1,0:T(8,128)(2,1)S(1)}, bf16[512,256]{1,0:T(8,128)(2,1)S(1)}, u32[]{:S(2)}, u32[]{:S(2)}) collective-permute-start(bf16[512,256]{1,0:T(8,128)(2,1)S(1)} %get-tuple-element.51), channel_id=1, source_target_pairs={{0,2},{1,3},{2,0},{3,1},{4,6},{5,7},{6,4},{7,5},{8,10},{9,11},{10,... | collective-permute-start | bytes 786440 | tf_op jit(solution)/shard_map/ppermute | solution.py:57
  102.9 5.5 %collective-permute-start.18 = (bf16[512,256]{1,0:T(8,128)(2,1)S(1)}, bf16[512,256]{1,0:T(8,128)(2,1)S(1)}, u32[]{:S(2)}, u32[]{:S(2)}) collective-permute-start(bf16[512,256]{1,0:T(8,128)(2,1)S(1)} %get-tuple-element.51), channel_id=1, source_target_pairs={{0,3},{1,0},{2,1},{3,2},{4,7},{5,4},{6,5},{7,6},{8,11},{9,8},{10,9... | collective-permute-start | bytes 786440 | tf_op jit(solution)/shard_map/ppermute | solution.py:57
  108.3 21.3 %all_to_all.20.parts = bf16[16,16,256]{2,1,0:T(8,128)(2,1)S(1)} all-to-all(bf16[16,16,256]{2,1,0:T(8,128)(2,1)S(1)} %bitcast.23), channel_id=1, replica_groups=mesh['dom'=64,'rows'=16] {'rows'}, dimensions={0} | all-to-all | bytes 262144 | tf_op jit(solution)/shard_map/all_to_all | solution.py:70
  130.3 4.2 %all-to-all-start.1 = ((f32[8,16,256]{2,1,0:T(8,128)}), f32[8,16,256]{2,1,0:T(8,128)S(1)}, u32[]{:S(2)}, u32[]{:S(2)}) async-start(f32[8,16,256]{2,1,0:T(8,128)} %sum_and_spread.3), calls=%async_computation.1 | async-start | bytes 262144 | tf_op jit(solution)/shard_map/all_to_all | solution.py:70
  139.9 3.7 %collective-permute-start.20 = (bf16[1024,256]{1,0:T(8,128)(2,1)S(1)}, bf16[1024,256]{1,0:T(8,128)(2,1)S(1)}, u32[]{:S(2)}, u32[]{:S(2)}) collective-permute-start(bf16[1024,256]{1,0:T(8,128)(2,1)S(1)} %get-tuple-element.54), channel_id=1, source_target_pairs={{0,8},{1,9},{2,10},{3,11},{4,12},{5,13},{6,14},{7,15},{8,0},{9,1},... | collective-permute-start | bytes 1572872 | tf_op jit(solution)/shard_map/ppermute | solution.py:62
  145.6 24.6 %all_to_all.21.parts = f32[8,16,256]{2,1,0:T(8,128)S(1)} all-to-all(f32[8,16,256]{2,1,0:T(8,128)S(1)} %sum_and_spread.4), channel_id=1, replica_groups={{0,128,256,384,512,640,768,896},{16,144,272,400,528,656,784,912},{32,16..., dimensions={0} | all-to-all | bytes 262144 | tf_op jit(solution)/shard_map/all_to_all | solution.py:70
  170.9 7.4 %all-to-all-start.3 = ((bf16[16,16,256]{2,1,0:T(8,128)(2,1)}), bf16[16,16,256]{2,1,0:T(8,128)(2,1)S(1)}, u32[]{:S(2)}, u32[]{:S(2)}) async-start(bf16[16,16,256]{2,1,0:T(8,128)(2,1)} %sum_and_spread.5.after), calls=%async_computation.3 | async-start | bytes 262144 | tf_op jit(solution)/shard_map/all_to_all | solution.py:70
  185.5 5.6 %collective-permute-start.23 = (bf16[512,256]{1,0:T(8,128)(2,1)S(1)}, bf16[512,256]{1,0:T(8,128)(2,1)S(1)}, u32[]{:S(2)}, u32[]{:S(2)}) collective-permute-start(bf16[512,256]{1,0:T(8,128)(2,1)S(1)} %get-tuple-element.58), channel_id=1, source_target_pairs={{0,1008},{16,0},{32,16},{48,32},{64,48},{80,64},{96,80},{112,96},{... | collective-permute-start | bytes 786440 | tf_op jit(solution)/shard_map/ppermute | solution.py:52
  193.7 4.2 %collective-permute-start.25 = (bf16[512,256]{1,0:T(8,128)(2,1)S(1)}, bf16[512,256]{1,0:T(8,128)(2,1)S(1)}, u32[]{:S(2)}, u32[]{:S(2)}) collective-permute-start(bf16[512,256]{1,0:T(8,128)(2,1)S(1)} %get-tuple-element.60), channel_id=1, source_target_pairs={{0,32},{16,48},{32,64},{48,80},{64,96},{80,112},{96,128},{112,144}... | collective-permute-start | bytes 786440 | tf_op jit(solution)/shard_map/ppermute | solution.py:52
  198.7 3.9 %collective-permute-done.24.r3 = bf16[512,256]{1,0:T(8,128)(2,1)S(1)} collective-permute-done((bf16[512,256]{1,0:T(8,128)(2,1)S(1)}, bf16[512,256]{1,0:T(8,128)(2,1)S(1)}, u32[]{:S(2)}, u32[]{:S(2)}) %collective-permute-start.24) | collective-permute-done | bytes 262176 | tf_op jit(solution)/shard_map/ppermute | solution.py:52
  (77 shorter events, 47.2 us)
Async XLA Ops:
  0.6 26.2 %collective-permute-start = (bf16[512,256]{1,0:T(8,128)(2,1)}, bf16[512,256]{1,0:T(8,128)(2,1)S(1)}, u32[]{:S(2)}, u32[]{:S(2)}) collective-permute-start(bf16[512,256]{1,0:T(8,128)(2,1)} %param.8), channel_id=1, source_target_pairs={{0,32},{16,48},{32,64},{48,80},{64,96},{80,112},{96,128},{112,144}... | collective-permute-start | bytes 786440 | tf_op jit(solution)/shard_map/ppermute | solution.py:52
  4.7 22.2 %collective-permute-start.1 = (bf16[512,256]{1,0:T(8,128)(2,1)}, bf16[512,256]{1,0:T(8,128)(2,1)S(1)}, u32[]{:S(2)}, u32[]{:S(2)}) collective-permute-start(bf16[512,256]{1,0:T(8,128)(2,1)} %param.8), channel_id=1, source_target_pairs={{0,16},{16,32},{32,48},{48,64},{64,80},{80,96},{96,112},{112,128},... | collective-permute-start | bytes 786440 | tf_op jit(solution)/shard_map/ppermute | solution.py:52
  9.4 17.5 %collective-permute-start.2 = (bf16[512,256]{1,0:T(8,128)(2,1)}, bf16[512,256]{1,0:T(8,128)(2,1)S(1)}, u32[]{:S(2)}, u32[]{:S(2)}) collective-permute-start(bf16[512,256]{1,0:T(8,128)(2,1)} %param.8), channel_id=1, source_target_pairs={{0,1008},{16,0},{32,16},{48,32},{64,48},{80,64},{96,80},{112,96},{... | collective-permute-start | bytes 786440 | tf_op jit(solution)/shard_map/ppermute | solution.py:52
  20.6 15.3 %collective-permute-start.3 = (bf16[512,256]{1,0:T(8,128)(2,1)}, bf16[512,256]{1,0:T(8,128)(2,1)S(1)}, u32[]{:S(2)}, u32[]{:S(2)}) collective-permute-start(bf16[512,256]{1,0:T(8,128)(2,1)} %param.8), channel_id=1, source_target_pairs={{0,992},{16,1008},{32,0},{48,16},{64,32},{80,48},{96,64},{112,80},... | collective-permute-start | bytes 786440 | tf_op jit(solution)/shard_map/ppermute | solution.py:52
  40.3 16.5 %collective-permute-start.4 = (bf16[1040,128]{1,0:T(8,128)(2,1)}, bf16[1040,128]{1,0:T(8,128)(2,1)S(1)}, u32[]{:S(2)}, u32[]{:S(2)}) collective-permute-start(bf16[1040,128]{1,0:T(8,128)(2,1)} %get-tuple-element.33), channel_id=1, source_target_pairs={{0,4},{1,5},{2,6},{3,7},{4,8},{5,9},{6,10},{7,11},{8,12},{9,13},{1... | collective-permute-start | bytes 798728 | tf_op jit(solution)/shard_map/ppermute | solution.py:62
  42.2 16.7 %collective-permute-start.5 = (bf16[1040,128]{1,0:T(8,128)(2,1)}, bf16[1040,128]{1,0:T(8,128)(2,1)S(1)}, u32[]{:S(2)}, u32[]{:S(2)}) collective-permute-start(bf16[1040,128]{1,0:T(8,128)(2,1)} %get-tuple-element.34), channel_id=1, source_target_pairs={{0,8},{1,9},{2,10},{3,11},{4,12},{5,13},{6,14},{7,15},{8,0},{9,1},... | collective-permute-start | bytes 798728 | tf_op jit(solution)/shard_map/ppermute | solution.py:62
  44.6 15.2 %collective-permute-start.6 = (bf16[1040,128]{1,0:T(8,128)(2,1)}, bf16[1040,128]{1,0:T(8,128)(2,1)S(1)}, u32[]{:S(2)}, u32[]{:S(2)}) collective-permute-start(bf16[1040,128]{1,0:T(8,128)(2,1)} %get-tuple-element.35), channel_id=1, source_target_pairs={{0,12},{1,13},{2,14},{3,15},{4,0},{5,1},{6,2},{7,3},{8,4},{9,5},{1... | collective-permute-start | bytes 798728 | tf_op jit(solution)/shard_map/ppermute | solution.py:62
  48.7 19.3 %collective-permute-start.10 = (bf16[1024,128]{1,0:T(8,128)(2,1)}, bf16[1024,128]{1,0:T(8,128)(2,1)S(1)}, u32[]{:S(2)}, u32[]{:S(2)}) collective-permute-start(bf16[1024,128]{1,0:T(8,128)(2,1)} %get-tuple-element.41), channel_id=1, source_target_pairs={{0,4},{1,5},{2,6},{3,7},{4,8},{5,9},{6,10},{7,11},{8,12},{9,13},{1... | collective-permute-start | bytes 786440 | tf_op jit(solution)/shard_map/ppermute | solution.py:62
  51.2 20.7 %collective-permute-start.11 = (bf16[1024,128]{1,0:T(8,128)(2,1)}, bf16[1024,128]{1,0:T(8,128)(2,1)S(1)}, u32[]{:S(2)}, u32[]{:S(2)}) collective-permute-start(bf16[1024,128]{1,0:T(8,128)(2,1)} %get-tuple-element.42), channel_id=1, source_target_pairs={{0,8},{1,9},{2,10},{3,11},{4,12},{5,13},{6,14},{7,15},{8,0},{9,1},... | collective-permute-start | bytes 786440 | tf_op jit(solution)/shard_map/ppermute | solution.py:62
  56.7 15.1 %collective-permute-start.12 = (bf16[1024,128]{1,0:T(8,128)(2,1)}, bf16[1024,128]{1,0:T(8,128)(2,1)S(1)}, u32[]{:S(2)}, u32[]{:S(2)}) collective-permute-start(bf16[1024,128]{1,0:T(8,128)(2,1)} %get-tuple-element.43), channel_id=1, source_target_pairs={{0,12},{1,13},{2,14},{3,15},{4,0},{5,1},{6,2},{7,3},{8,4},{9,5},{1... | collective-permute-start | bytes 786440 | tf_op jit(solution)/shard_map/ppermute | solution.py:62
  61.5 19.3 %collective-permute-start.7 = (bf16[512,128]{1,0:T(8,128)(2,1)S(1)}, bf16[512,128]{1,0:T(8,128)(2,1)S(1)}, u32[]{:S(2)}, u32[]{:S(2)}) collective-permute-start(bf16[512,128]{1,0:T(8,128)(2,1)S(1)} %get-tuple-element.37), channel_id=1, source_target_pairs={{0,1},{1,2},{2,3},{3,0},{4,5},{5,6},{6,7},{7,4},{8,9},{9,10},{10,1... | collective-permute-start | bytes 393224 | tf_op jit(solution)/shard_map/ppermute | solution.py:57
  63.4 22.9 %collective-permute-start.8 = (bf16[512,128]{1,0:T(8,128)(2,1)S(1)}, bf16[512,128]{1,0:T(8,128)(2,1)S(1)}, u32[]{:S(2)}, u32[]{:S(2)}) collective-permute-start(bf16[512,128]{1,0:T(8,128)(2,1)S(1)} %get-tuple-element.38), channel_id=1, source_target_pairs={{0,2},{1,3},{2,0},{3,1},{4,6},{5,7},{6,4},{7,5},{8,10},{9,11},{10,... | collective-permute-start | bytes 393224 | tf_op jit(solution)/shard_map/ppermute | solution.py:57
  68.0 18.3 %collective-permute-start.9 = (bf16[512,128]{1,0:T(8,128)(2,1)S(1)}, bf16[512,128]{1,0:T(8,128)(2,1)S(1)}, u32[]{:S(2)}, u32[]{:S(2)}) collective-permute-start(bf16[512,128]{1,0:T(8,128)(2,1)S(1)} %get-tuple-element.39), channel_id=1, source_target_pairs={{0,3},{1,0},{2,1},{3,2},{4,7},{5,4},{6,5},{7,6},{8,11},{9,8},{10,9... | collective-permute-start | bytes 393224 | tf_op jit(solution)/shard_map/ppermute | solution.py:57
  72.6 13.7 %collective-permute-start.13 = (bf16[512,128]{1,0:T(8,128)(2,1)S(1)}, bf16[512,128]{1,0:T(8,128)(2,1)S(1)}, u32[]{:S(2)}, u32[]{:S(2)}) collective-permute-start(bf16[512,128]{1,0:T(8,128)(2,1)S(1)} %get-tuple-element.46), channel_id=1, source_target_pairs={{0,1},{1,2},{2,3},{3,0},{4,5},{5,6},{6,7},{7,4},{8,9},{9,10},{10,1... | collective-permute-start | bytes 393224 | tf_op jit(solution)/shard_map/ppermute | solution.py:57
  94.9 39.6 %collective-permute-start.16 = (bf16[512,256]{1,0:T(8,128)(2,1)S(1)}, bf16[512,256]{1,0:T(8,128)(2,1)S(1)}, u32[]{:S(2)}, u32[]{:S(2)}) collective-permute-start(bf16[512,256]{1,0:T(8,128)(2,1)S(1)} %get-tuple-element.51), channel_id=1, source_target_pairs={{0,1},{1,2},{2,3},{3,0},{4,5},{5,6},{6,7},{7,4},{8,9},{9,10},{10,1... | collective-permute-start | bytes 786440 | tf_op jit(solution)/shard_map/ppermute | solution.py:57
  98.7 35.8 %collective-permute-start.17 = (bf16[512,256]{1,0:T(8,128)(2,1)S(1)}, bf16[512,256]{1,0:T(8,128)(2,1)S(1)}, u32[]{:S(2)}, u32[]{:S(2)}) collective-permute-start(bf16[512,256]{1,0:T(8,128)(2,1)S(1)} %get-tuple-element.51), channel_id=1, source_target_pairs={{0,2},{1,3},{2,0},{3,1},{4,6},{5,7},{6,4},{7,5},{8,10},{9,11},{10,... | collective-permute-start | bytes 786440 | tf_op jit(solution)/shard_map/ppermute | solution.py:57
  102.9 31.6 %collective-permute-start.18 = (bf16[512,256]{1,0:T(8,128)(2,1)S(1)}, bf16[512,256]{1,0:T(8,128)(2,1)S(1)}, u32[]{:S(2)}, u32[]{:S(2)}) collective-permute-start(bf16[512,256]{1,0:T(8,128)(2,1)S(1)} %get-tuple-element.51), channel_id=1, source_target_pairs={{0,3},{1,0},{2,1},{3,2},{4,7},{5,4},{6,5},{7,6},{8,11},{9,8},{10,9... | collective-permute-start | bytes 786440 | tf_op jit(solution)/shard_map/ppermute | solution.py:57
  130.3 15.2 %all-to-all-start.1 = ((f32[8,16,256]{2,1,0:T(8,128)}), f32[8,16,256]{2,1,0:T(8,128)S(1)}, u32[]{:S(2)}, u32[]{:S(2)}) async-start(f32[8,16,256]{2,1,0:T(8,128)} %sum_and_spread.3), calls=%async_computation.1 | async-start | bytes 262144 | tf_op jit(solution)/shard_map/all_to_all | solution.py:70
  137.1 41.2 %collective-permute-start.19 = (bf16[1024,256]{1,0:T(8,128)(2,1)}, bf16[1024,256]{1,0:T(8,128)(2,1)S(1)}, u32[]{:S(2)}, u32[]{:S(2)}) collective-permute-start(bf16[1024,256]{1,0:T(8,128)(2,1)} %get-tuple-element.53), channel_id=1, source_target_pairs={{0,12},{1,13},{2,14},{3,15},{4,0},{5,1},{6,2},{7,3},{8,4},{9,5},{1... | collective-permute-start | bytes 1572872 | tf_op jit(solution)/shard_map/ppermute | solution.py:62
  139.9 38.4 %collective-permute-start.20 = (bf16[1024,256]{1,0:T(8,128)(2,1)S(1)}, bf16[1024,256]{1,0:T(8,128)(2,1)S(1)}, u32[]{:S(2)}, u32[]{:S(2)}) collective-permute-start(bf16[1024,256]{1,0:T(8,128)(2,1)S(1)} %get-tuple-element.54), channel_id=1, source_target_pairs={{0,8},{1,9},{2,10},{3,11},{4,12},{5,13},{6,14},{7,15},{8,0},{9,1},... | collective-permute-start | bytes 1572872 | tf_op jit(solution)/shard_map/ppermute | solution.py:62
  143.6 34.7 %collective-permute-start.21 = (bf16[1024,256]{1,0:T(8,128)(2,1)S(1)}, bf16[1024,256]{1,0:T(8,128)(2,1)S(1)}, u32[]{:S(2)}, u32[]{:S(2)}) collective-permute-start(bf16[1024,256]{1,0:T(8,128)(2,1)S(1)} %get-tuple-element.55), channel_id=1, source_target_pairs={{0,4},{1,5},{2,6},{3,7},{4,8},{5,9},{6,10},{7,11},{8,12},{9,13},{1... | collective-permute-start | bytes 1572872 | tf_op jit(solution)/shard_map/ppermute | solution.py:62
  170.9 27.0 %all-to-all-start.3 = ((bf16[16,16,256]{2,1,0:T(8,128)(2,1)}), bf16[16,16,256]{2,1,0:T(8,128)(2,1)S(1)}, u32[]{:S(2)}, u32[]{:S(2)}) async-start(bf16[16,16,256]{2,1,0:T(8,128)(2,1)} %sum_and_spread.5.after), calls=%async_computation.3 | async-start | bytes 262144 | tf_op jit(solution)/shard_map/all_to_all | solution.py:70
  182.6 16.1 %collective-permute-start.22 = (bf16[512,256]{1,0:T(8,128)(2,1)S(1)}, bf16[512,256]{1,0:T(8,128)(2,1)S(1)}, u32[]{:S(2)}, u32[]{:S(2)}) collective-permute-start(bf16[512,256]{1,0:T(8,128)(2,1)S(1)} %get-tuple-element.57), channel_id=1, source_target_pairs={{0,992},{16,1008},{32,0},{48,16},{64,32},{80,48},{96,64},{112,80},... | collective-permute-start | bytes 786440 | tf_op jit(solution)/shard_map/ppermute | solution.py:52
  185.5 13.2 %collective-permute-start.23 = (bf16[512,256]{1,0:T(8,128)(2,1)S(1)}, bf16[512,256]{1,0:T(8,128)(2,1)S(1)}, u32[]{:S(2)}, u32[]{:S(2)}) collective-permute-start(bf16[512,256]{1,0:T(8,128)(2,1)S(1)} %get-tuple-element.58), channel_id=1, source_target_pairs={{0,1008},{16,0},{32,16},{48,32},{64,48},{80,64},{96,80},{112,96},{... | collective-permute-start | bytes 786440 | tf_op jit(solution)/shard_map/ppermute | solution.py:52
  (20 other events, 185.4 us)

commit v8 on v7

--- a/solution.py
+++ b/solution.py
@@ -20,7 +20,6 @@
 OFFSETS = (-2, -1, 1, 2)
 VMEM = pl.BlockSpec(memory_space=pltpu.VMEM)
 HBM = pl.BlockSpec(memory_space=pltpu.HBM)
-ANY = pl.BlockSpec(memory_space=pl.ANY)
 SMEM = pl.BlockSpec(memory_space=pltpu.SMEM)
 BF16 = jnp.bfloat16
 F32 = jnp.float32
@@ -241,7 +240,7 @@
 
 
 def backward_kernel(
-    src, slot, cnt, after, b0, b1, b2, b3, vals, om2, om1, own, op1, op2, acc, ret, in_sem, out_sem
+    src, slot, cnt, b0, b1, b2, b3, vals, om2, om1, own, op1, op2, acc, ret, in_sem, out_sem
 ):
     per_x = YN * CAP
     me_x, _ = position()
@@ -273,7 +272,7 @@
     store.wait()
 
 
-def backward_products(src, slot, cnt, back, vals, blocks_dev, after):
+def backward_products(src, slot, cnt, back, vals, blocks_dev):
     nodes, channels = blocks_dev * BLOCK, back[0].shape[1]
     steps = cnt.shape[1]
     send = jax.ShapeDtypeStruct((nodes, channels), BF16)
@@ -284,7 +283,7 @@
         "tile_backward",
         (send, send, own, send, send),
         [(SMEM, a) for a in (src, slot, cnt)]
-        + [(ANY, after), (HBM, own_back)]
+        + [(HBM, own_back)]
         + [(VMEM, a) for a in (*back[1:], vals)],
         12,
         BACK_FLOPS,
@@ -379,7 +378,7 @@
     back = [reply[0]] + [None] * (XN - 1)
     for k in (1, 3, 2):
         back[k] = x_shift(reply[k], -k)
-    terms = list(backward_products(src, slot, cnt, back, vals, blocks_dev, piece))
+    terms = list(backward_products(src, slot, cnt, back, vals, blocks_dev))
     own = terms.pop(HALF)
     terms = [dom_shift(t, o) for t, o in zip(terms, OFFSETS)]
     weight_grad = exchange(piece, "rows").reshape(local_grad.shape).astype(F32)

time: 209 us -> 207 us (level)
  blocking collectives: 46 us -> 8.09 us
  waiting for transfers between devices: 27.6 us -> 55 us
  starting transfers between devices: 114 us -> 122 us
    all_to_all x2 -> x1, blocking collectives: 46 us -> 8.09 us  [exchange(): lax.all_to_all(value, axis, split_axis=0, concat_axis=0, tiled=True, axis...]
    ppermute x9, waiting for transfers between devices: 7.51 us -> 20.7 us  [y_shift(): return lax.ppermute(value, 'rows', pairs)]
    ppermute x9, waiting for transfers between devices: 3.9 us -> 16.7 us  [x_shift(): return lax.ppermute(value, 'rows', pairs)]
    all_to_all x2 -> x3, starting transfers between devices: 11.5 us -> 19.9 us  [exchange(): lax.all_to_all(value, axis, split_axis=0, concat_axis=0, tiled=True, axis...]
    ppermute x8, starting transfers between devices: 41.5 us -> 38.1 us  [dom_shift(): lax.ppermute(value, 'dom', [(i, (i + steps) % count) for i in range(count)])]
    ppermute x9, starting transfers between devices: 25.1 us -> 27.7 us  [x_shift(): return lax.ppermute(value, 'rows', pairs)]
  transfers between devices with their start and end apart: 28 -> 29, of which waited for: 8 -> 12; matrix products, arithmetic and copies ran while one was open for 0% -> 0% of each run, Pallas kernels for 3% -> 3%
where the time goes in v8:
time: 207 us; the launch traced here: 205 us
  starting transfers between devices  122 us (59%)
  waiting for transfers between devices  55 us (27%)
  Pallas kernels  12.2 us (6%)
  blocking collectives  8.09 us (4%)
  local copies, waits for them, and re-layouts  4.95 us (2%)
    ppermute x8, starting transfers between devices, dom_shift(): lax.ppermute(value, 'dom', [(i, (i + steps) % count) for i in range(count)])  38.1 us
    ppermute x9, starting transfers between devices, y_shift(): return lax.ppermute(value, 'rows', pairs)  36.8 us
    ppermute x9, starting transfers between devices, x_shift(): return lax.ppermute(value, 'rows', pairs)  27.7 us
    ppermute x9, waiting for transfers between devices, y_shift(): return lax.ppermute(value, 'rows', pairs)  20.7 us
    all_to_all x3, starting transfers between devices, exchange(): lax.all_to_all(value, axis, split_axis=0, concat_axis=0, tiled=True, axis...  19.9 us
    ppermute x9, waiting for transfers between devices, x_shift(): return lax.ppermute(value, 'rows', pairs)  16.7 us
    ppermute x8, waiting for transfers between devices, dom_shift(): lax.ppermute(value, 'dom', [(i, (i + steps) % count) for i in range(count)])  16.3 us
    pallas_call x10, Pallas kernels, kernel_call(): pl.pallas_call(body, out_shape=outs, in_specs=[space for space, _ in ins]...  12.2 us
  transfers between devices with their start and end apart: 29, of which 12 were waited for; matrix products, arithmetic and copies ran while one was open for 0% of the time, Pallas kernels for 3%

profile of v8, /device:TPU:1, one launch (start us, length us, event | category | flops | bytes accessed | tf_op | source)
XLA Modules:
  0.0 204.6 jit_solution(90765958274230835)
XLA Ops:
  0.6 4.0 %collective-permute-start = (bf16[512,256]{1,0:T(8,128)(2,1)}, bf16[512,256]{1,0:T(8,128)(2,1)S(1)}, u32[]{:S(2)}, u32[]{:S(2)}) collective-permute-start(bf16[512,256]{1,0:T(8,128)(2,1)} %param.8), channel_id=1, source_target_pairs={{0,32},{16,48},{32,64},{48,80},{64,96},{80,112},{96,128},{112,144}... | collective-permute-start | bytes 786440 | tf_op jit(solution)/shard_map/ppermute | solution.py:51
  4.7 4.7 %collective-permute-start.1 = (bf16[512,256]{1,0:T(8,128)(2,1)}, bf16[512,256]{1,0:T(8,128)(2,1)S(1)}, u32[]{:S(2)}, u32[]{:S(2)}) collective-permute-start(bf16[512,256]{1,0:T(8,128)(2,1)} %param.8), channel_id=1, source_target_pairs={{0,16},{16,32},{32,48},{48,64},{64,80},{80,96},{96,112},{112,128},... | collective-permute-start | bytes 786440 | tf_op jit(solution)/shard_map/ppermute | solution.py:51
  9.4 11.1 %collective-permute-start.2 = (bf16[512,256]{1,0:T(8,128)(2,1)}, bf16[512,256]{1,0:T(8,128)(2,1)S(1)}, u32[]{:S(2)}, u32[]{:S(2)}) collective-permute-start(bf16[512,256]{1,0:T(8,128)(2,1)} %param.8), channel_id=1, source_target_pairs={{0,1008},{16,0},{32,16},{48,32},{64,48},{80,64},{96,80},{112,96},{... | collective-permute-start | bytes 786440 | tf_op jit(solution)/shard_map/ppermute | solution.py:51
  20.6 6.3 %collective-permute-start.3 = (bf16[512,256]{1,0:T(8,128)(2,1)}, bf16[512,256]{1,0:T(8,128)(2,1)S(1)}, u32[]{:S(2)}, u32[]{:S(2)}) collective-permute-start(bf16[512,256]{1,0:T(8,128)(2,1)} %param.8), channel_id=1, source_target_pairs={{0,992},{16,1008},{32,0},{48,16},{64,32},{80,48},{96,64},{112,80},... | collective-permute-start | bytes 786440 | tf_op jit(solution)/shard_map/ppermute | solution.py:51
  26.9 8.9 %collective-permute-done.3 = bf16[512,256]{1,0:T(8,128)(2,1)S(1)} collective-permute-done((bf16[512,256]{1,0:T(8,128)(2,1)}, bf16[512,256]{1,0:T(8,128)(2,1)S(1)}, u32[]{:S(2)}, u32[]{:S(2)}) %collective-permute-start.3) | collective-permute-done | bytes 262176 | tf_op jit(solution)/shard_map/ppermute | solution.py:51
  36.5 3.8 %tile_forward.1 = (bf16[1040,128]{1,0:T(8,128)(2,1)}, bf16[1040,128]{1,0:T(8,128)(2,1)}, bf16[1040,128]{1,0:T(8,128)(2,1)}, bf16[1040,128]{1,0:T(8,128)(2,1)}, b...) custom-call(s32[4,5]{1,0:T(4,128)} %bitcast.23, ...), custom_call_target="tpu_custom_call" | custom-call | flops 167772160 | bytes 1966388 | tf_op jit(solution)/shard_map/tile_forward/pallas_call | solution.py:37
  44.6 4.1 %collective-permute-start.6 = (bf16[1040,128]{1,0:T(8,128)(2,1)}, bf16[1040,128]{1,0:T(8,128)(2,1)S(1)}, u32[]{:S(2)}, u32[]{:S(2)}) collective-permute-start(bf16[1040,128]{1,0:T(8,128)(2,1)} %get-tuple-element.35), channel_id=1, source_target_pairs={{0,12},{1,13},{2,14},{3,15},{4,0},{5,1},{6,2},{7,3},{8,4},{9,5},{1... | collective-permute-start | bytes 798728 | tf_op jit(solution)/shard_map/ppermute | solution.py:61
  61.5 6.5 %collective-permute-done.10.refs_1_ = bf16[1024,128]{1,0:T(8,128)(2,1)S(1)} collective-permute-done((bf16[1024,128]{1,0:T(8,128)(2,1)}, bf16[1024,128]{1,0:T(8,128)(2,1)S(1)}, u32[]{:S(2)}, u32[]{:S(2)}) %collective-permute-start.10) | collective-permute-done | bytes 262176 | tf_op jit(solution)/shard_map/ppermute | solution.py:61
  76.4 5.0 %collective-permute-start.15 = (bf16[512,128]{1,0:T(8,128)(2,1)S(1)}, bf16[512,128]{1,0:T(8,128)(2,1)S(1)}, u32[]{:S(2)}, u32[]{:S(2)}) collective-permute-start(bf16[512,128]{1,0:T(8,128)(2,1)S(1)} %get-tuple-element.48), channel_id=1, source_target_pairs={{0,3},{1,0},{2,1},{3,2},{4,7},{5,4},{6,5},{7,6},{8,11},{9,8},{10,9... | collective-permute-start | bytes 393224 | tf_op jit(solution)/shard_map/ppermute | solution.py:56
  84.4 5.2 %collective-permute-start.8 = (bf16[512,128]{1,0:T(8,128)(2,1)S(1)}, bf16[512,128]{1,0:T(8,128)(2,1)S(1)}, u32[]{:S(2)}, u32[]{:S(2)}) collective-permute-start(bf16[512,128]{1,0:T(8,128)(2,1)S(1)} %get-tuple-element.38), channel_id=1, source_target_pairs={{0,2},{1,3},{2,0},{3,1},{4,6},{5,7},{6,4},{7,5},{8,10},{9,11},{10,... | collective-permute-start | bytes 393224 | tf_op jit(solution)/shard_map/ppermute | solution.py:56
  89.6 5.5 %collective-permute-start.9 = (bf16[512,128]{1,0:T(8,128)(2,1)S(1)}, bf16[512,128]{1,0:T(8,128)(2,1)S(1)}, u32[]{:S(2)}, u32[]{:S(2)}) collective-permute-start(bf16[512,128]{1,0:T(8,128)(2,1)S(1)} %get-tuple-element.39), channel_id=1, source_target_pairs={{0,3},{1,0},{2,1},{3,2},{4,7},{5,4},{6,5},{7,6},{8,11},{9,8},{10,9... | collective-permute-start | bytes 393224 | tf_op jit(solution)/shard_map/ppermute | solution.py:56
  97.3 5.8 %collective-permute-done.9.refs_3_ = bf16[512,128]{1,0:T(8,128)(2,1)S(1)} collective-permute-done((bf16[512,128]{1,0:T(8,128)(2,1)S(1)}, bf16[512,128]{1,0:T(8,128)(2,1)S(1)}, u32[]{:S(2)}, u32[]{:S(2)}) %collective-permute-start.9) | collective-permute-done | bytes 131104 | tf_op jit(solution)/shard_map/ppermute | solution.py:56
  104.3 3.7 %collective-permute-start.16 = (bf16[512,256]{1,0:T(8,128)(2,1)S(1)}, bf16[512,256]{1,0:T(8,128)(2,1)S(1)}, u32[]{:S(2)}, u32[]{:S(2)}) collective-permute-start(bf16[512,256]{1,0:T(8,128)(2,1)S(1)} %get-tuple-element.50), channel_id=1, source_target_pairs={{0,1},{1,2},{2,3},{3,0},{4,5},{5,6},{6,7},{7,4},{8,9},{9,10},{10,1... | collective-permute-start | bytes 786440 | tf_op jit(solution)/shard_map/ppermute | solution.py:56
  108.0 4.5 %collective-permute-start.17 = (bf16[512,256]{1,0:T(8,128)(2,1)S(1)}, bf16[512,256]{1,0:T(8,128)(2,1)S(1)}, u32[]{:S(2)}, u32[]{:S(2)}) collective-permute-start(bf16[512,256]{1,0:T(8,128)(2,1)S(1)} %get-tuple-element.50), channel_id=1, source_target_pairs={{0,2},{1,3},{2,0},{3,1},{4,6},{5,7},{6,4},{7,5},{8,10},{9,11},{10,... | collective-permute-start | bytes 786440 | tf_op jit(solution)/shard_map/ppermute | solution.py:56
  112.6 4.6 %collective-permute-start.18 = (bf16[512,256]{1,0:T(8,128)(2,1)S(1)}, bf16[512,256]{1,0:T(8,128)(2,1)S(1)}, u32[]{:S(2)}, u32[]{:S(2)}) collective-permute-start(bf16[512,256]{1,0:T(8,128)(2,1)S(1)} %get-tuple-element.50), channel_id=1, source_target_pairs={{0,3},{1,0},{2,1},{3,2},{4,7},{5,4},{6,5},{7,6},{8,11},{9,8},{10,9... | collective-permute-start | bytes 786440 | tf_op jit(solution)/shard_map/ppermute | solution.py:56
  117.2 6.2 %all-to-all-start = ((bf16[16,16,256]{2,1,0:T(8,128)(2,1)}), bf16[16,16,256]{2,1,0:T(8,128)(2,1)S(1)}, u32[]{:S(2)}, u32[]{:S(2)}) async-start(bf16[16,16,256]{2,1,0:T(8,128)(2,1)} %bitcast.17), calls=%async_computation | async-start | bytes 262144 | tf_op jit(solution)/shard_map/all_to_all | solution.py:69
  123.5 8.6 %collective-permute-done.17 = bf16[512,256]{1,0:T(8,128)(2,1)S(1)} collective-permute-done((bf16[512,256]{1,0:T(8,128)(2,1)S(1)}, bf16[512,256]{1,0:T(8,128)(2,1)S(1)}, u32[]{:S(2)}, u32[]{:S(2)}) %collective-permute-start.17) | collective-permute-done | bytes 262176 | tf_op jit(solution)/shard_map/ppermute | solution.py:56
  132.0 4.2 %collective-permute-done.18 = bf16[512,256]{1,0:T(8,128)(2,1)S(1)} collective-permute-done((bf16[512,256]{1,0:T(8,128)(2,1)S(1)}, bf16[512,256]{1,0:T(8,128)(2,1)S(1)}, u32[]{:S(2)}, u32[]{:S(2)}) %collective-permute-start.18) | collective-permute-done | bytes 262176 | tf_op jit(solution)/shard_map/ppermute | solution.py:56
  138.8 6.6 %collective-permute-start.19 = (bf16[1024,256]{1,0:T(8,128)(2,1)}, bf16[1024,256]{1,0:T(8,128)(2,1)S(1)}, u32[]{:S(2)}, u32[]{:S(2)}) collective-permute-start(bf16[1024,256]{1,0:T(8,128)(2,1)} %get-tuple-element.52), channel_id=1, source_target_pairs={{0,12},{1,13},{2,14},{3,15},{4,0},{5,1},{6,2},{7,3},{8,4},{9,5},{1... | collective-permute-start | bytes 1572872 | tf_op jit(solution)/shard_map/ppermute | solution.py:61
  149.9 8.1 %all_to_all.20.parts = f32[8,16,256]{2,1,0:T(8,128)S(1)} all-to-all(f32[8,16,256]{2,1,0:T(8,128)S(1)} %sum_and_spread.3), channel_id=1, replica_groups={{0,16,32,48,64,80,96,112},{128,144,160,176,192,208,224,240},{256,272,28..., dimensions={0} | all-to-all | bytes 262144 | tf_op jit(solution)/shard_map/all_to_all | solution.py:69
  158.6 10.1 %all-to-all-start.2 = ((f32[8,16,256]{2,1,0:T(8,128)}), f32[8,16,256]{2,1,0:T(8,128)S(1)}, u32[]{:S(2)}, u32[]{:S(2)}) async-start(f32[8,16,256]{2,1,0:T(8,128)} %sum_and_spread.4), calls=%async_computation.2 | async-start | bytes 262144 | tf_op jit(solution)/shard_map/all_to_all | solution.py:69
  168.8 5.1 %collective-permute-done.21.b3 = bf16[1024,256]{1,0:T(8,128)(2,1)S(1)} collective-permute-done((bf16[1024,256]{1,0:T(8,128)(2,1)S(1)}, bf16[1024,256]{1,0:T(8,128)(2,1)S(1)}, u32[]{:S(2)}, u32[]{:S(2)}) %collective-permute-start.21) | collective-permute-done | bytes 524320 | tf_op jit(solution)/shard_map/ppermute | solution.py:61
  186.1 3.9 %collective-permute-start.25 = (bf16[512,256]{1,0:T(8,128)(2,1)S(1)}, bf16[512,256]{1,0:T(8,128)(2,1)S(1)}, u32[]{:S(2)}, u32[]{:S(2)}) collective-permute-start(bf16[512,256]{1,0:T(8,128)(2,1)S(1)} %get-tuple-element.59), channel_id=1, source_target_pairs={{0,32},{16,48},{32,64},{48,80},{64,96},{80,112},{96,128},{112,144}... | collective-permute-start | bytes 786440 | tf_op jit(solution)/shard_map/ppermute | solution.py:51
  194.2 7.4 %collective-permute-done.25.r4 = bf16[512,256]{1,0:T(8,128)(2,1)S(1)} collective-permute-done((bf16[512,256]{1,0:T(8,128)(2,1)S(1)}, bf16[512,256]{1,0:T(8,128)(2,1)S(1)}, u32[]{:S(2)}, u32[]{:S(2)}) %collective-permute-start.25) | collective-permute-done | bytes 262176 | tf_op jit(solution)/shard_map/ppermute | solution.py:51
  (78 shorter events, 59.6 us)
Async XLA Ops:
  0.6 26.2 %collective-permute-start = (bf16[512,256]{1,0:T(8,128)(2,1)}, bf16[512,256]{1,0:T(8,128)(2,1)S(1)}, u32[]{:S(2)}, u32[]{:S(2)}) collective-permute-start(bf16[512,256]{1,0:T(8,128)(2,1)} %param.8), channel_id=1, source_target_pairs={{0,32},{16,48},{32,64},{48,80},{64,96},{80,112},{96,128},{112,144}... | collective-permute-start | bytes 786440 | tf_op jit(solution)/shard_map/ppermute | solution.py:51
  4.7 22.2 %collective-permute-start.1 = (bf16[512,256]{1,0:T(8,128)(2,1)}, bf16[512,256]{1,0:T(8,128)(2,1)S(1)}, u32[]{:S(2)}, u32[]{:S(2)}) collective-permute-start(bf16[512,256]{1,0:T(8,128)(2,1)} %param.8), channel_id=1, source_target_pairs={{0,16},{16,32},{32,48},{48,64},{64,80},{80,96},{96,112},{112,128},... | collective-permute-start | bytes 786440 | tf_op jit(solution)/shard_map/ppermute | solution.py:51
  9.4 17.5 %collective-permute-start.2 = (bf16[512,256]{1,0:T(8,128)(2,1)}, bf16[512,256]{1,0:T(8,128)(2,1)S(1)}, u32[]{:S(2)}, u32[]{:S(2)}) collective-permute-start(bf16[512,256]{1,0:T(8,128)(2,1)} %param.8), channel_id=1, source_target_pairs={{0,1008},{16,0},{32,16},{48,32},{64,48},{80,64},{96,80},{112,96},{... | collective-permute-start | bytes 786440 | tf_op jit(solution)/shard_map/ppermute | solution.py:51
  20.6 15.3 %collective-permute-start.3 = (bf16[512,256]{1,0:T(8,128)(2,1)}, bf16[512,256]{1,0:T(8,128)(2,1)S(1)}, u32[]{:S(2)}, u32[]{:S(2)}) collective-permute-start(bf16[512,256]{1,0:T(8,128)(2,1)} %param.8), channel_id=1, source_target_pairs={{0,992},{16,1008},{32,0},{48,16},{64,32},{80,48},{96,64},{112,80},... | collective-permute-start | bytes 786440 | tf_op jit(solution)/shard_map/ppermute | solution.py:51
  40.3 16.5 %collective-permute-start.4 = (bf16[1040,128]{1,0:T(8,128)(2,1)}, bf16[1040,128]{1,0:T(8,128)(2,1)S(1)}, u32[]{:S(2)}, u32[]{:S(2)}) collective-permute-start(bf16[1040,128]{1,0:T(8,128)(2,1)} %get-tuple-element.33), channel_id=1, source_target_pairs={{0,4},{1,5},{2,6},{3,7},{4,8},{5,9},{6,10},{7,11},{8,12},{9,13},{1... | collective-permute-start | bytes 798728 | tf_op jit(solution)/shard_map/ppermute | solution.py:61
  42.2 16.7 %collective-permute-start.5 = (bf16[1040,128]{1,0:T(8,128)(2,1)}, bf16[1040,128]{1,0:T(8,128)(2,1)S(1)}, u32[]{:S(2)}, u32[]{:S(2)}) collective-permute-start(bf16[1040,128]{1,0:T(8,128)(2,1)} %get-tuple-element.34), channel_id=1, source_target_pairs={{0,8},{1,9},{2,10},{3,11},{4,12},{5,13},{6,14},{7,15},{8,0},{9,1},... | collective-permute-start | bytes 798728 | tf_op jit(solution)/shard_map/ppermute | solution.py:61
  44.6 15.2 %collective-permute-start.6 = (bf16[1040,128]{1,0:T(8,128)(2,1)}, bf16[1040,128]{1,0:T(8,128)(2,1)S(1)}, u32[]{:S(2)}, u32[]{:S(2)}) collective-permute-start(bf16[1040,128]{1,0:T(8,128)(2,1)} %get-tuple-element.35), channel_id=1, source_target_pairs={{0,12},{1,13},{2,14},{3,15},{4,0},{5,1},{6,2},{7,3},{8,4},{9,5},{1... | collective-permute-start | bytes 798728 | tf_op jit(solution)/shard_map/ppermute | solution.py:61
  48.7 19.3 %collective-permute-start.10 = (bf16[1024,128]{1,0:T(8,128)(2,1)}, bf16[1024,128]{1,0:T(8,128)(2,1)S(1)}, u32[]{:S(2)}, u32[]{:S(2)}) collective-permute-start(bf16[1024,128]{1,0:T(8,128)(2,1)} %get-tuple-element.41), channel_id=1, source_target_pairs={{0,4},{1,5},{2,6},{3,7},{4,8},{5,9},{6,10},{7,11},{8,12},{9,13},{1... | collective-permute-start | bytes 786440 | tf_op jit(solution)/shard_map/ppermute | solution.py:61
  51.2 16.8 %collective-permute-start.11 = (bf16[1024,128]{1,0:T(8,128)(2,1)}, bf16[1024,128]{1,0:T(8,128)(2,1)S(1)}, u32[]{:S(2)}, u32[]{:S(2)}) collective-permute-start(bf16[1024,128]{1,0:T(8,128)(2,1)} %get-tuple-element.42), channel_id=1, source_target_pairs={{0,8},{1,9},{2,10},{3,11},{4,12},{5,13},{6,14},{7,15},{8,0},{9,1},... | collective-permute-start | bytes 786440 | tf_op jit(solution)/shard_map/ppermute | solution.py:61
  71.0 18.5 %collective-permute-start.13 = (bf16[512,128]{1,0:T(8,128)(2,1)S(1)}, bf16[512,128]{1,0:T(8,128)(2,1)S(1)}, u32[]{:S(2)}, u32[]{:S(2)}) collective-permute-start(bf16[512,128]{1,0:T(8,128)(2,1)S(1)} %get-tuple-element.46), channel_id=1, source_target_pairs={{0,1},{1,2},{2,3},{3,0},{4,5},{5,6},{6,7},{7,4},{8,9},{9,10},{10,1... | collective-permute-start | bytes 393224 | tf_op jit(solution)/shard_map/ppermute | solution.py:56
  72.9 22.1 %collective-permute-start.14 = (bf16[512,128]{1,0:T(8,128)(2,1)S(1)}, bf16[512,128]{1,0:T(8,128)(2,1)S(1)}, u32[]{:S(2)}, u32[]{:S(2)}) collective-permute-start(bf16[512,128]{1,0:T(8,128)(2,1)S(1)} %get-tuple-element.47), channel_id=1, source_target_pairs={{0,2},{1,3},{2,0},{3,1},{4,6},{5,7},{6,4},{7,5},{8,10},{9,11},{10,... | collective-permute-start | bytes 393224 | tf_op jit(solution)/shard_map/ppermute | solution.py:56
  76.4 18.7 %collective-permute-start.15 = (bf16[512,128]{1,0:T(8,128)(2,1)S(1)}, bf16[512,128]{1,0:T(8,128)(2,1)S(1)}, u32[]{:S(2)}, u32[]{:S(2)}) collective-permute-start(bf16[512,128]{1,0:T(8,128)(2,1)S(1)} %get-tuple-element.48), channel_id=1, source_target_pairs={{0,3},{1,0},{2,1},{3,2},{4,7},{5,4},{6,5},{7,6},{8,11},{9,8},{10,9... | collective-permute-start | bytes 393224 | tf_op jit(solution)/shard_map/ppermute | solution.py:56
  81.4 13.7 %collective-permute-start.7 = (bf16[512,128]{1,0:T(8,128)(2,1)S(1)}, bf16[512,128]{1,0:T(8,128)(2,1)S(1)}, u32[]{:S(2)}, u32[]{:S(2)}) collective-permute-start(bf16[512,128]{1,0:T(8,128)(2,1)S(1)} %get-tuple-element.37), channel_id=1, source_target_pairs={{0,1},{1,2},{2,3},{3,0},{4,5},{5,6},{6,7},{7,4},{8,9},{9,10},{10,1... | collective-permute-start | bytes 393224 | tf_op jit(solution)/shard_map/ppermute | solution.py:56
  104.3 19.1 %collective-permute-start.16 = (bf16[512,256]{1,0:T(8,128)(2,1)S(1)}, bf16[512,256]{1,0:T(8,128)(2,1)S(1)}, u32[]{:S(2)}, u32[]{:S(2)}) collective-permute-start(bf16[512,256]{1,0:T(8,128)(2,1)S(1)} %get-tuple-element.50), channel_id=1, source_target_pairs={{0,1},{1,2},{2,3},{3,0},{4,5},{5,6},{6,7},{7,4},{8,9},{9,10},{10,1... | collective-permute-start | bytes 786440 | tf_op jit(solution)/shard_map/ppermute | solution.py:56
  108.0 24.0 %collective-permute-start.17 = (bf16[512,256]{1,0:T(8,128)(2,1)S(1)}, bf16[512,256]{1,0:T(8,128)(2,1)S(1)}, u32[]{:S(2)}, u32[]{:S(2)}) collective-permute-start(bf16[512,256]{1,0:T(8,128)(2,1)S(1)} %get-tuple-element.50), channel_id=1, source_target_pairs={{0,2},{1,3},{2,0},{3,1},{4,6},{5,7},{6,4},{7,5},{8,10},{9,11},{10,... | collective-permute-start | bytes 786440 | tf_op jit(solution)/shard_map/ppermute | solution.py:56
  112.6 23.6 %collective-permute-start.18 = (bf16[512,256]{1,0:T(8,128)(2,1)S(1)}, bf16[512,256]{1,0:T(8,128)(2,1)S(1)}, u32[]{:S(2)}, u32[]{:S(2)}) collective-permute-start(bf16[512,256]{1,0:T(8,128)(2,1)S(1)} %get-tuple-element.50), channel_id=1, source_target_pairs={{0,3},{1,0},{2,1},{3,2},{4,7},{5,4},{6,5},{7,6},{8,11},{9,8},{10,9... | collective-permute-start | bytes 786440 | tf_op jit(solution)/shard_map/ppermute | solution.py:56
  117.2 32.6 %all-to-all-start = ((bf16[16,16,256]{2,1,0:T(8,128)(2,1)}), bf16[16,16,256]{2,1,0:T(8,128)(2,1)S(1)}, u32[]{:S(2)}, u32[]{:S(2)}) async-start(bf16[16,16,256]{2,1,0:T(8,128)(2,1)} %bitcast.17), calls=%async_computation | async-start | bytes 262144 | tf_op jit(solution)/shard_map/all_to_all | solution.py:69
  138.8 30.0 %collective-permute-start.19 = (bf16[1024,256]{1,0:T(8,128)(2,1)}, bf16[1024,256]{1,0:T(8,128)(2,1)S(1)}, u32[]{:S(2)}, u32[]{:S(2)}) collective-permute-start(bf16[1024,256]{1,0:T(8,128)(2,1)} %get-tuple-element.52), channel_id=1, source_target_pairs={{0,12},{1,13},{2,14},{3,15},{4,0},{5,1},{6,2},{7,3},{8,4},{9,5},{1... | collective-permute-start | bytes 1572872 | tf_op jit(solution)/shard_map/ppermute | solution.py:61
  145.4 23.4 %collective-permute-start.20 = (bf16[1024,256]{1,0:T(8,128)(2,1)S(1)}, bf16[1024,256]{1,0:T(8,128)(2,1)S(1)}, u32[]{:S(2)}, u32[]{:S(2)}) collective-permute-start(bf16[1024,256]{1,0:T(8,128)(2,1)S(1)} %get-tuple-element.53), channel_id=1, source_target_pairs={{0,8},{1,9},{2,10},{3,11},{4,12},{5,13},{6,14},{7,15},{8,0},{9,1},... | collective-permute-start | bytes 1572872 | tf_op jit(solution)/shard_map/ppermute | solution.py:61
  147.3 26.6 %collective-permute-start.21 = (bf16[1024,256]{1,0:T(8,128)(2,1)S(1)}, bf16[1024,256]{1,0:T(8,128)(2,1)S(1)}, u32[]{:S(2)}, u32[]{:S(2)}) collective-permute-start(bf16[1024,256]{1,0:T(8,128)(2,1)S(1)} %get-tuple-element.54), channel_id=1, source_target_pairs={{0,4},{1,5},{2,6},{3,7},{4,8},{5,9},{6,10},{7,11},{8,12},{9,13},{1... | collective-permute-start | bytes 1572872 | tf_op jit(solution)/shard_map/ppermute | solution.py:61
  158.6 31.4 %all-to-all-start.2 = ((f32[8,16,256]{2,1,0:T(8,128)}), f32[8,16,256]{2,1,0:T(8,128)S(1)}, u32[]{:S(2)}, u32[]{:S(2)}) async-start(f32[8,16,256]{2,1,0:T(8,128)} %sum_and_spread.4), calls=%async_computation.2 | async-start | bytes 262144 | tf_op jit(solution)/shard_map/all_to_all | solution.py:69
  178.1 16.1 %collective-permute-start.22 = (bf16[512,256]{1,0:T(8,128)(2,1)S(1)}, bf16[512,256]{1,0:T(8,128)(2,1)S(1)}, u32[]{:S(2)}, u32[]{:S(2)}) collective-permute-start(bf16[512,256]{1,0:T(8,128)(2,1)S(1)} %get-tuple-element.56), channel_id=1, source_target_pairs={{0,992},{16,1008},{32,0},{48,16},{64,32},{80,48},{96,64},{112,80},... | collective-permute-start | bytes 786440 | tf_op jit(solution)/shard_map/ppermute | solution.py:51
  180.1 14.1 %collective-permute-start.23 = (bf16[512,256]{1,0:T(8,128)(2,1)S(1)}, bf16[512,256]{1,0:T(8,128)(2,1)S(1)}, u32[]{:S(2)}, u32[]{:S(2)}) collective-permute-start(bf16[512,256]{1,0:T(8,128)(2,1)S(1)} %get-tuple-element.57), channel_id=1, source_target_pairs={{0,1008},{16,0},{32,16},{48,32},{64,48},{80,64},{96,80},{112,96},{... | collective-permute-start | bytes 786440 | tf_op jit(solution)/shard_map/ppermute | solution.py:51
  186.1 15.6 %collective-permute-start.25 = (bf16[512,256]{1,0:T(8,128)(2,1)S(1)}, bf16[512,256]{1,0:T(8,128)(2,1)S(1)}, u32[]{:S(2)}, u32[]{:S(2)}) collective-permute-start(bf16[512,256]{1,0:T(8,128)(2,1)S(1)} %get-tuple-element.59), channel_id=1, source_target_pairs={{0,32},{16,48},{32,64},{48,80},{64,96},{80,112},{96,128},{112,144}... | collective-permute-start | bytes 786440 | tf_op jit(solution)/shard_map/ppermute | solution.py:51
  (21 other events, 250.8 us)

commit v9 on v8

--- a/solution.py
+++ b/solution.py
@@ -25,6 +25,7 @@
 F32 = jnp.float32
 
 GATHER_FLOPS = 10**11
+HALF_FLOPS = 10**10
 DENSE_FLOPS = 1 << 28
 REPLY_FLOPS = 10**10
 BACK_FLOPS = 10**10
@@ -165,15 +166,31 @@
     )
 
 
+def summed(parts):
+    total = parts[0][...].astype(F32)
+    for part in parts[1:]:
+        total = total + part[...].astype(F32)
+    return total.astype(BF16)
+
+
+def half_kernel(*refs):
+    refs[-1][...] = summed(refs[:-1])
+
+
+def half_sum(parts):
+    return kernel_call(
+        half_kernel,
+        "half_sum",
+        jax.ShapeDtypeStruct(parts[0].shape, BF16),
+        [(VMEM, a) for a in parts],
+        4,
+        HALF_FLOPS,
+    )
+
+
 def dense_kernel(*refs):
-    parts, (weight, cot, act, grad, wgrad) = refs[: 2 * YN], refs[2 * YN :]
-    halves = []
-    for h in range(2):
-        total = parts[h * YN][...].astype(F32)
-        for k in range(1, YN):
-            total = total + parts[h * YN + k][...].astype(F32)
-        halves.append(total.astype(BF16))
-    agg = jnp.concatenate(halves, axis=1)
+    agg0, parts, (weight, cot, act, grad, wgrad) = refs[0], refs[1 : 1 + YN], refs[1 + YN :]
+    agg = jnp.concatenate([agg0[...], summed(parts)], axis=1)
     w = weight[...]
     pre = jnp.dot(agg, w, preferred_element_type=F32)
     sig = 1.0 / (1.0 + jnp.exp(-pre))
@@ -188,14 +205,14 @@
     ).astype(BF16)
 
 
-def dense(parts, weight, cot):
+def dense(agg0, parts, weight, cot):
     nodes, channels = cot.shape
     full = jax.ShapeDtypeStruct((nodes, channels), BF16)
     return kernel_call(
         dense_kernel,
         "dense_layer",
         (full, full, jax.ShapeDtypeStruct((channels, channels), BF16)),
-        [(VMEM, a) for a in (*parts, weight, cot)],
+        [(VMEM, a) for a in (agg0, *parts, weight, cot)],
         10,
         DENSE_FLOPS,
     )
@@ -367,10 +384,10 @@
     got0 = [sent[0]] + [x_shift(sent[k], k) for k in range(1, XN)]
     got1 = [sent[XN]] + [x_shift(sent[XN + k], k) for k in range(1, XN)]
     *sums0, ids = gather_blocks(got0, blocks_dev)
-    parts = [sums0[0]] + [y_shift(sums0[k], k) for k in range(1, YN)]
+    agg0 = half_sum([sums0[0]] + [y_shift(sums0[k], k) for k in range(1, YN)])
     sums1 = gather_blocks(got1, blocks_dev, ids)
-    parts += [sums1[0]] + [y_shift(sums1[k], k) for k in range(1, YN)]
-    activations, grad, local_grad = dense(parts, weight, cotangent)
+    parts = [sums1[0]] + [y_shift(sums1[k], k) for k in range(1, YN)]
+    activations, grad, local_grad = dense(agg0, parts, weight, cotangent)
 
     piece = weight_piece(local_grad)
     grads = [grad] + [y_shift(grad, k) for k in range(1, YN)]

time: 207 us -> 197 us (0.952)
  waiting for transfers between devices: 55 us -> 43.1 us
  starting transfers between devices: 122 us -> 125 us
    ppermute x9, waiting for transfers between devices: 16.7 us -> 7.25 us  [x_shift(): return lax.ppermute(value, 'rows', pairs)]
    all_to_all x3, starting transfers between devices: 19.9 us -> 23 us  [exchange(): lax.all_to_all(value, axis, split_axis=0, concat_axis=0, tiled=True, axis...]
    ppermute x9, waiting for transfers between devices: 20.7 us -> 18.4 us  [y_shift(): return lax.ppermute(value, 'rows', pairs)]
    pallas_call x10 -> x11, Pallas kernels: 12.2 us -> 12.3 us  [kernel_call(): pl.pallas_call(body, out_shape=outs, in_specs=[space for space, _ in ins]...]
  transfers between devices with their start and end apart: 29 -> 29, of which waited for: 12 -> 11; matrix products, arithmetic and copies ran while one was open for 0% -> 0% of each run, Pallas kernels for 3% -> 4%
where the time goes in v9:
time: 197 us; the launch traced here: 196 us
  starting transfers between devices  125 us (63%)
  waiting for transfers between devices  43.1 us (22%)
  Pallas kernels  12.3 us (6%)
  blocking collectives  8.09 us (4%)
  local copies, waits for them, and re-layouts  4.96 us (3%)
    ppermute x8, starting transfers between devices, dom_shift(): lax.ppermute(value, 'dom', [(i, (i + steps) % count) for i in range(count)])  38.1 us
    ppermute x9, starting transfers between devices, y_shift(): return lax.ppermute(value, 'rows', pairs)  36.3 us
    ppermute x9, starting transfers between devices, x_shift(): return lax.ppermute(value, 'rows', pairs)  27.8 us
    all_to_all x3, starting transfers between devices, exchange(): lax.all_to_all(value, axis, split_axis=0, concat_axis=0, tiled=True, axis...  23 us
    ppermute x9, waiting for transfers between devices, y_shift(): return lax.ppermute(value, 'rows', pairs)  18.4 us
    ppermute x8, waiting for transfers between devices, dom_shift(): lax.ppermute(value, 'dom', [(i, (i + steps) % count) for i in range(count)])  14.2 us
    pallas_call x11, Pallas kernels, kernel_call(): pl.pallas_call(body, out_shape=outs, in_specs=[space for space, _ in ins]...  12.3 us
    all_to_all x1, blocking collectives, exchange(): lax.all_to_all(value, axis, split_axis=0, concat_axis=0, tiled=True, axis...  8.09 us
  transfers between devices with their start and end apart: 29, of which 11 were waited for; matrix products, arithmetic and copies ran while one was open for 0% of the time, Pallas kernels for 4%

profile of v9, /device:TPU:1, one launch (start us, length us, event | category | flops | bytes accessed | tf_op | source)
XLA Modules:
  0.0 195.6 jit_solution(11866724998759068644)
XLA Ops:
  0.6 4.0 %collective-permute-start = (bf16[512,256]{1,0:T(8,128)(2,1)}, bf16[512,256]{1,0:T(8,128)(2,1)S(1)}, u32[]{:S(2)}, u32[]{:S(2)}) collective-permute-start(bf16[512,256]{1,0:T(8,128)(2,1)} %param.8), channel_id=1, source_target_pairs={{0,32},{16,48},{32,64},{48,80},{64,96},{80,112},{96,128},{112,144}... | collective-permute-start | bytes 786440 | tf_op jit(solution)/shard_map/ppermute | solution.py:52
  4.7 4.7 %collective-permute-start.1 = (bf16[512,256]{1,0:T(8,128)(2,1)}, bf16[512,256]{1,0:T(8,128)(2,1)S(1)}, u32[]{:S(2)}, u32[]{:S(2)}) collective-permute-start(bf16[512,256]{1,0:T(8,128)(2,1)} %param.8), channel_id=1, source_target_pairs={{0,16},{16,32},{32,48},{48,64},{64,80},{80,96},{96,112},{112,128},... | collective-permute-start | bytes 786440 | tf_op jit(solution)/shard_map/ppermute | solution.py:52
  9.4 11.1 %collective-permute-start.2 = (bf16[512,256]{1,0:T(8,128)(2,1)}, bf16[512,256]{1,0:T(8,128)(2,1)S(1)}, u32[]{:S(2)}, u32[]{:S(2)}) collective-permute-start(bf16[512,256]{1,0:T(8,128)(2,1)} %param.8), channel_id=1, source_target_pairs={{0,1008},{16,0},{32,16},{48,32},{64,48},{80,64},{96,80},{112,96},{... | collective-permute-start | bytes 786440 | tf_op jit(solution)/shard_map/ppermute | solution.py:52
  20.6 6.3 %collective-permute-start.3 = (bf16[512,256]{1,0:T(8,128)(2,1)}, bf16[512,256]{1,0:T(8,128)(2,1)S(1)}, u32[]{:S(2)}, u32[]{:S(2)}) collective-permute-start(bf16[512,256]{1,0:T(8,128)(2,1)} %param.8), channel_id=1, source_target_pairs={{0,992},{16,1008},{32,0},{48,16},{64,32},{80,48},{96,64},{112,80},... | collective-permute-start | bytes 786440 | tf_op jit(solution)/shard_map/ppermute | solution.py:52
  26.9 8.9 %collective-permute-done.3 = bf16[512,256]{1,0:T(8,128)(2,1)S(1)} collective-permute-done((bf16[512,256]{1,0:T(8,128)(2,1)}, bf16[512,256]{1,0:T(8,128)(2,1)S(1)}, u32[]{:S(2)}, u32[]{:S(2)}) %collective-permute-start.3) | collective-permute-done | bytes 262176 | tf_op jit(solution)/shard_map/ppermute | solution.py:52
  36.5 3.8 %tile_forward.1 = (bf16[1040,128]{1,0:T(8,128)(2,1)}, bf16[1040,128]{1,0:T(8,128)(2,1)}, bf16[1040,128]{1,0:T(8,128)(2,1)}, bf16[1040,128]{1,0:T(8,128)(2,1)}, b...) custom-call(s32[4,5]{1,0:T(4,128)} %bitcast.23, ...), custom_call_target="tpu_custom_call" | custom-call | flops 167772160 | bytes 1966388 | tf_op jit(solution)/shard_map/tile_forward/pallas_call | solution.py:38
  44.6 4.1 %collective-permute-start.6 = (bf16[1040,128]{1,0:T(8,128)(2,1)}, bf16[1040,128]{1,0:T(8,128)(2,1)S(1)}, u32[]{:S(2)}, u32[]{:S(2)}) collective-permute-start(bf16[1040,128]{1,0:T(8,128)(2,1)} %get-tuple-element.35), channel_id=1, source_target_pairs={{0,12},{1,13},{2,14},{3,15},{4,0},{5,1},{6,2},{7,3},{8,4},{9,5},{1... | collective-permute-start | bytes 798728 | tf_op jit(solution)/shard_map/ppermute | solution.py:62
  51.2 3.7 %collective-permute-start.11 = (bf16[1024,128]{1,0:T(8,128)(2,1)}, bf16[1024,128]{1,0:T(8,128)(2,1)S(1)}, u32[]{:S(2)}, u32[]{:S(2)}) collective-permute-start(bf16[1024,128]{1,0:T(8,128)(2,1)} %get-tuple-element.42), channel_id=1, source_target_pairs={{0,8},{1,9},{2,10},{3,11},{4,12},{5,13},{6,14},{7,15},{8,0},{9,1},... | collective-permute-start | bytes 786440 | tf_op jit(solution)/shard_map/ppermute | solution.py:62
  68.0 3.9 %collective-permute-start.9 = (bf16[512,128]{1,0:T(8,128)(2,1)S(1)}, bf16[512,128]{1,0:T(8,128)(2,1)S(1)}, u32[]{:S(2)}, u32[]{:S(2)}) collective-permute-start(bf16[512,128]{1,0:T(8,128)(2,1)S(1)} %get-tuple-element.39), channel_id=1, source_target_pairs={{0,3},{1,0},{2,1},{3,2},{4,7},{5,4},{6,5},{7,6},{8,11},{9,8},{10,9... | collective-permute-start | bytes 393224 | tf_op jit(solution)/shard_map/ppermute | solution.py:57
  75.6 5.2 %collective-permute-start.14 = (bf16[512,128]{1,0:T(8,128)(2,1)S(1)}, bf16[512,128]{1,0:T(8,128)(2,1)S(1)}, u32[]{:S(2)}, u32[]{:S(2)}) collective-permute-start(bf16[512,128]{1,0:T(8,128)(2,1)S(1)} %get-tuple-element.47), channel_id=1, source_target_pairs={{0,2},{1,3},{2,0},{3,1},{4,6},{5,7},{6,4},{7,5},{8,10},{9,11},{10,... | collective-permute-start | bytes 393224 | tf_op jit(solution)/shard_map/ppermute | solution.py:57
  80.8 5.5 %collective-permute-start.15 = (bf16[512,128]{1,0:T(8,128)(2,1)S(1)}, bf16[512,128]{1,0:T(8,128)(2,1)S(1)}, u32[]{:S(2)}, u32[]{:S(2)}) collective-permute-start(bf16[512,128]{1,0:T(8,128)(2,1)S(1)} %get-tuple-element.48), channel_id=1, source_target_pairs={{0,3},{1,0},{2,1},{3,2},{4,7},{5,4},{6,5},{7,6},{8,11},{9,8},{10,9... | collective-permute-start | bytes 393224 | tf_op jit(solution)/shard_map/ppermute | solution.py:57
  87.3 6.6 %collective-permute-done.15.refs_4_ = bf16[512,128]{1,0:T(8,128)(2,1)S(1)} collective-permute-done((bf16[512,128]{1,0:T(8,128)(2,1)S(1)}, bf16[512,128]{1,0:T(8,128)(2,1)S(1)}, u32[]{:S(2)}, u32[]{:S(2)}) %collective-permute-start.15) | collective-permute-done | bytes 131104 | tf_op jit(solution)/shard_map/ppermute | solution.py:57
  95.1 3.8 %collective-permute-start.16 = (bf16[512,256]{1,0:T(8,128)(2,1)S(1)}, bf16[512,256]{1,0:T(8,128)(2,1)S(1)}, u32[]{:S(2)}, u32[]{:S(2)}) collective-permute-start(bf16[512,256]{1,0:T(8,128)(2,1)S(1)} %get-tuple-element.50), channel_id=1, source_target_pairs={{0,1},{1,2},{2,3},{3,0},{4,5},{5,6},{6,7},{7,4},{8,9},{9,10},{10,1... | collective-permute-start | bytes 786440 | tf_op jit(solution)/shard_map/ppermute | solution.py:57
  98.9 4.2 %collective-permute-start.17 = (bf16[512,256]{1,0:T(8,128)(2,1)S(1)}, bf16[512,256]{1,0:T(8,128)(2,1)S(1)}, u32[]{:S(2)}, u32[]{:S(2)}) collective-permute-start(bf16[512,256]{1,0:T(8,128)(2,1)S(1)} %get-tuple-element.50), channel_id=1, source_target_pairs={{0,2},{1,3},{2,0},{3,1},{4,6},{5,7},{6,4},{7,5},{8,10},{9,11},{10,... | collective-permute-start | bytes 786440 | tf_op jit(solution)/shard_map/ppermute | solution.py:57
  103.0 5.5 %collective-permute-start.18 = (bf16[512,256]{1,0:T(8,128)(2,1)S(1)}, bf16[512,256]{1,0:T(8,128)(2,1)S(1)}, u32[]{:S(2)}, u32[]{:S(2)}) collective-permute-start(bf16[512,256]{1,0:T(8,128)(2,1)S(1)} %get-tuple-element.50), channel_id=1, source_target_pairs={{0,3},{1,0},{2,1},{3,2},{4,7},{5,4},{6,5},{7,6},{8,11},{9,8},{10,9... | collective-permute-start | bytes 786440 | tf_op jit(solution)/shard_map/ppermute | solution.py:57
  108.5 6.1 %all-to-all-start = ((bf16[16,16,256]{2,1,0:T(8,128)(2,1)}), bf16[16,16,256]{2,1,0:T(8,128)(2,1)S(1)}, u32[]{:S(2)}, u32[]{:S(2)}) async-start(bf16[16,16,256]{2,1,0:T(8,128)(2,1)} %bitcast.17), calls=%async_computation | async-start | bytes 262144 | tf_op jit(solution)/shard_map/all_to_all | solution.py:70
  114.6 4.6 %collective-permute-done.17 = bf16[512,256]{1,0:T(8,128)(2,1)S(1)} collective-permute-done((bf16[512,256]{1,0:T(8,128)(2,1)S(1)}, bf16[512,256]{1,0:T(8,128)(2,1)S(1)}, u32[]{:S(2)}, u32[]{:S(2)}) %collective-permute-start.17) | collective-permute-done | bytes 262176 | tf_op jit(solution)/shard_map/ppermute | solution.py:57
  119.2 6.4 %collective-permute-done.18 = bf16[512,256]{1,0:T(8,128)(2,1)S(1)} collective-permute-done((bf16[512,256]{1,0:T(8,128)(2,1)S(1)}, bf16[512,256]{1,0:T(8,128)(2,1)S(1)}, u32[]{:S(2)}, u32[]{:S(2)}) %collective-permute-start.18) | collective-permute-done | bytes 262176 | tf_op jit(solution)/shard_map/ppermute | solution.py:57
  128.1 6.7 %collective-permute-start.19 = (bf16[1024,256]{1,0:T(8,128)(2,1)}, bf16[1024,256]{1,0:T(8,128)(2,1)S(1)}, u32[]{:S(2)}, u32[]{:S(2)}) collective-permute-start(bf16[1024,256]{1,0:T(8,128)(2,1)} %get-tuple-element.52), channel_id=1, source_target_pairs={{0,12},{1,13},{2,14},{3,15},{4,0},{5,1},{6,2},{7,3},{8,4},{9,5},{1... | collective-permute-start | bytes 1572872 | tf_op jit(solution)/shard_map/ppermute | solution.py:62
  139.4 8.1 %all_to_all.20.parts = f32[8,16,256]{2,1,0:T(8,128)S(1)} all-to-all(f32[8,16,256]{2,1,0:T(8,128)S(1)} %sum_and_spread.3), channel_id=1, replica_groups={{0,16,32,48,64,80,96,112},{128,144,160,176,192,208,224,240},{256,272,28..., dimensions={0} | all-to-all | bytes 262144 | tf_op jit(solution)/shard_map/all_to_all | solution.py:70
  148.1 11.9 %all-to-all-start.2 = ((f32[8,16,256]{2,1,0:T(8,128)}), f32[8,16,256]{2,1,0:T(8,128)S(1)}, u32[]{:S(2)}, u32[]{:S(2)}) async-start(f32[8,16,256]{2,1,0:T(8,128)} %sum_and_spread.4), calls=%async_computation.2 | async-start | bytes 262144 | tf_op jit(solution)/shard_map/all_to_all | solution.py:70
  175.6 3.9 %collective-permute-start.25 = (bf16[512,256]{1,0:T(8,128)(2,1)S(1)}, bf16[512,256]{1,0:T(8,128)(2,1)S(1)}, u32[]{:S(2)}, u32[]{:S(2)}) collective-permute-start(bf16[512,256]{1,0:T(8,128)(2,1)S(1)} %get-tuple-element.59), channel_id=1, source_target_pairs={{0,32},{16,48},{32,64},{48,80},{64,96},{80,112},{96,128},{112,144}... | collective-permute-start | bytes 786440 | tf_op jit(solution)/shard_map/ppermute | solution.py:52
  180.2 5.1 %all-to-all-start.3 = ((bf16[16,16,256]{2,1,0:T(8,128)(2,1)}), bf16[16,16,256]{2,1,0:T(8,128)(2,1)S(1)}, u32[]{:S(2)}, u32[]{:S(2)}) async-start(bf16[16,16,256]{2,1,0:T(8,128)(2,1)} %sum_and_spread.5), calls=%async_computation.3 | async-start | bytes 262144 | tf_op jit(solution)/shard_map/all_to_all | solution.py:70
  185.3 5.4 %collective-permute-done.23.r2 = bf16[512,256]{1,0:T(8,128)(2,1)S(1)} collective-permute-done((bf16[512,256]{1,0:T(8,128)(2,1)S(1)}, bf16[512,256]{1,0:T(8,128)(2,1)S(1)}, u32[]{:S(2)}, u32[]{:S(2)}) %collective-permute-start.23) | collective-permute-done | bytes 262176 | tf_op jit(solution)/shard_map/ppermute | solution.py:52
  (79 shorter events, 55.3 us)
Async XLA Ops:
  0.6 26.2 %collective-permute-start = (bf16[512,256]{1,0:T(8,128)(2,1)}, bf16[512,256]{1,0:T(8,128)(2,1)S(1)}, u32[]{:S(2)}, u32[]{:S(2)}) collective-permute-start(bf16[512,256]{1,0:T(8,128)(2,1)} %param.8), channel_id=1, source_target_pairs={{0,32},{16,48},{32,64},{48,80},{64,96},{80,112},{96,128},{112,144}... | collective-permute-start | bytes 786440 | tf_op jit(solution)/shard_map/ppermute | solution.py:52
  4.7 22.2 %collective-permute-start.1 = (bf16[512,256]{1,0:T(8,128)(2,1)}, bf16[512,256]{1,0:T(8,128)(2,1)S(1)}, u32[]{:S(2)}, u32[]{:S(2)}) collective-permute-start(bf16[512,256]{1,0:T(8,128)(2,1)} %param.8), channel_id=1, source_target_pairs={{0,16},{16,32},{32,48},{48,64},{64,80},{80,96},{96,112},{112,128},... | collective-permute-start | bytes 786440 | tf_op jit(solution)/shard_map/ppermute | solution.py:52
  9.4 17.5 %collective-permute-start.2 = (bf16[512,256]{1,0:T(8,128)(2,1)}, bf16[512,256]{1,0:T(8,128)(2,1)S(1)}, u32[]{:S(2)}, u32[]{:S(2)}) collective-permute-start(bf16[512,256]{1,0:T(8,128)(2,1)} %param.8), channel_id=1, source_target_pairs={{0,1008},{16,0},{32,16},{48,32},{64,48},{80,64},{96,80},{112,96},{... | collective-permute-start | bytes 786440 | tf_op jit(solution)/shard_map/ppermute | solution.py:52
  20.6 15.3 %collective-permute-start.3 = (bf16[512,256]{1,0:T(8,128)(2,1)}, bf16[512,256]{1,0:T(8,128)(2,1)S(1)}, u32[]{:S(2)}, u32[]{:S(2)}) collective-permute-start(bf16[512,256]{1,0:T(8,128)(2,1)} %param.8), channel_id=1, source_target_pairs={{0,992},{16,1008},{32,0},{48,16},{64,32},{80,48},{96,64},{112,80},... | collective-permute-start | bytes 786440 | tf_op jit(solution)/shard_map/ppermute | solution.py:52
  40.3 16.5 %collective-permute-start.4 = (bf16[1040,128]{1,0:T(8,128)(2,1)}, bf16[1040,128]{1,0:T(8,128)(2,1)S(1)}, u32[]{:S(2)}, u32[]{:S(2)}) collective-permute-start(bf16[1040,128]{1,0:T(8,128)(2,1)} %get-tuple-element.33), channel_id=1, source_target_pairs={{0,4},{1,5},{2,6},{3,7},{4,8},{5,9},{6,10},{7,11},{8,12},{9,13},{1... | collective-permute-start | bytes 798728 | tf_op jit(solution)/shard_map/ppermute | solution.py:62
  42.2 16.7 %collective-permute-start.5 = (bf16[1040,128]{1,0:T(8,128)(2,1)}, bf16[1040,128]{1,0:T(8,128)(2,1)S(1)}, u32[]{:S(2)}, u32[]{:S(2)}) collective-permute-start(bf16[1040,128]{1,0:T(8,128)(2,1)} %get-tuple-element.34), channel_id=1, source_target_pairs={{0,8},{1,9},{2,10},{3,11},{4,12},{5,13},{6,14},{7,15},{8,0},{9,1},... | collective-permute-start | bytes 798728 | tf_op jit(solution)/shard_map/ppermute | solution.py:62
  44.6 15.2 %collective-permute-start.6 = (bf16[1040,128]{1,0:T(8,128)(2,1)}, bf16[1040,128]{1,0:T(8,128)(2,1)S(1)}, u32[]{:S(2)}, u32[]{:S(2)}) collective-permute-start(bf16[1040,128]{1,0:T(8,128)(2,1)} %get-tuple-element.35), channel_id=1, source_target_pairs={{0,12},{1,13},{2,14},{3,15},{4,0},{5,1},{6,2},{7,3},{8,4},{9,5},{1... | collective-permute-start | bytes 798728 | tf_op jit(solution)/shard_map/ppermute | solution.py:62
  48.7 19.3 %collective-permute-start.10 = (bf16[1024,128]{1,0:T(8,128)(2,1)}, bf16[1024,128]{1,0:T(8,128)(2,1)S(1)}, u32[]{:S(2)}, u32[]{:S(2)}) collective-permute-start(bf16[1024,128]{1,0:T(8,128)(2,1)} %get-tuple-element.41), channel_id=1, source_target_pairs={{0,4},{1,5},{2,6},{3,7},{4,8},{5,9},{6,10},{7,11},{8,12},{9,13},{1... | collective-permute-start | bytes 786440 | tf_op jit(solution)/shard_map/ppermute | solution.py:62
  51.2 20.7 %collective-permute-start.11 = (bf16[1024,128]{1,0:T(8,128)(2,1)}, bf16[1024,128]{1,0:T(8,128)(2,1)S(1)}, u32[]{:S(2)}, u32[]{:S(2)}) collective-permute-start(bf16[1024,128]{1,0:T(8,128)(2,1)} %get-tuple-element.42), channel_id=1, source_target_pairs={{0,8},{1,9},{2,10},{3,11},{4,12},{5,13},{6,14},{7,15},{8,0},{9,1},... | collective-permute-start | bytes 786440 | tf_op jit(solution)/shard_map/ppermute | solution.py:62
  56.8 15.1 %collective-permute-start.12 = (bf16[1024,128]{1,0:T(8,128)(2,1)}, bf16[1024,128]{1,0:T(8,128)(2,1)S(1)}, u32[]{:S(2)}, u32[]{:S(2)}) collective-permute-start(bf16[1024,128]{1,0:T(8,128)(2,1)} %get-tuple-element.43), channel_id=1, source_target_pairs={{0,12},{1,13},{2,14},{3,15},{4,0},{5,1},{6,2},{7,3},{8,4},{9,5},{1... | collective-permute-start | bytes 786440 | tf_op jit(solution)/shard_map/ppermute | solution.py:62
  61.5 19.3 %collective-permute-start.7 = (bf16[512,128]{1,0:T(8,128)(2,1)S(1)}, bf16[512,128]{1,0:T(8,128)(2,1)S(1)}, u32[]{:S(2)}, u32[]{:S(2)}) collective-permute-start(bf16[512,128]{1,0:T(8,128)(2,1)S(1)} %get-tuple-element.37), channel_id=1, source_target_pairs={{0,1},{1,2},{2,3},{3,0},{4,5},{5,6},{6,7},{7,4},{8,9},{9,10},{10,1... | collective-permute-start | bytes 393224 | tf_op jit(solution)/shard_map/ppermute | solution.py:57
  63.4 22.9 %collective-permute-start.8 = (bf16[512,128]{1,0:T(8,128)(2,1)S(1)}, bf16[512,128]{1,0:T(8,128)(2,1)S(1)}, u32[]{:S(2)}, u32[]{:S(2)}) collective-permute-start(bf16[512,128]{1,0:T(8,128)(2,1)S(1)} %get-tuple-element.38), channel_id=1, source_target_pairs={{0,2},{1,3},{2,0},{3,1},{4,6},{5,7},{6,4},{7,5},{8,10},{9,11},{10,... | collective-permute-start | bytes 393224 | tf_op jit(solution)/shard_map/ppermute | solution.py:57
  68.0 18.3 %collective-permute-start.9 = (bf16[512,128]{1,0:T(8,128)(2,1)S(1)}, bf16[512,128]{1,0:T(8,128)(2,1)S(1)}, u32[]{:S(2)}, u32[]{:S(2)}) collective-permute-start(bf16[512,128]{1,0:T(8,128)(2,1)S(1)} %get-tuple-element.39), channel_id=1, source_target_pairs={{0,3},{1,0},{2,1},{3,2},{4,7},{5,4},{6,5},{7,6},{8,11},{9,8},{10,9... | collective-permute-start | bytes 393224 | tf_op jit(solution)/shard_map/ppermute | solution.py:57
  95.1 19.5 %collective-permute-start.16 = (bf16[512,256]{1,0:T(8,128)(2,1)S(1)}, bf16[512,256]{1,0:T(8,128)(2,1)S(1)}, u32[]{:S(2)}, u32[]{:S(2)}) collective-permute-start(bf16[512,256]{1,0:T(8,128)(2,1)S(1)} %get-tuple-element.50), channel_id=1, source_target_pairs={{0,1},{1,2},{2,3},{3,0},{4,5},{5,6},{6,7},{7,4},{8,9},{9,10},{10,1... | collective-permute-start | bytes 786440 | tf_op jit(solution)/shard_map/ppermute | solution.py:57
  98.9 20.3 %collective-permute-start.17 = (bf16[512,256]{1,0:T(8,128)(2,1)S(1)}, bf16[512,256]{1,0:T(8,128)(2,1)S(1)}, u32[]{:S(2)}, u32[]{:S(2)}) collective-permute-start(bf16[512,256]{1,0:T(8,128)(2,1)S(1)} %get-tuple-element.50), channel_id=1, source_target_pairs={{0,2},{1,3},{2,0},{3,1},{4,6},{5,7},{6,4},{7,5},{8,10},{9,11},{10,... | collective-permute-start | bytes 786440 | tf_op jit(solution)/shard_map/ppermute | solution.py:57
  103.0 22.5 %collective-permute-start.18 = (bf16[512,256]{1,0:T(8,128)(2,1)S(1)}, bf16[512,256]{1,0:T(8,128)(2,1)S(1)}, u32[]{:S(2)}, u32[]{:S(2)}) collective-permute-start(bf16[512,256]{1,0:T(8,128)(2,1)S(1)} %get-tuple-element.50), channel_id=1, source_target_pairs={{0,3},{1,0},{2,1},{3,2},{4,7},{5,4},{6,5},{7,6},{8,11},{9,8},{10,9... | collective-permute-start | bytes 786440 | tf_op jit(solution)/shard_map/ppermute | solution.py:57
  108.5 30.8 %all-to-all-start = ((bf16[16,16,256]{2,1,0:T(8,128)(2,1)}), bf16[16,16,256]{2,1,0:T(8,128)(2,1)S(1)}, u32[]{:S(2)}, u32[]{:S(2)}) async-start(bf16[16,16,256]{2,1,0:T(8,128)(2,1)} %bitcast.17), calls=%async_computation | async-start | bytes 262144 | tf_op jit(solution)/shard_map/all_to_all | solution.py:70
  128.1 31.8 %collective-permute-start.19 = (bf16[1024,256]{1,0:T(8,128)(2,1)}, bf16[1024,256]{1,0:T(8,128)(2,1)S(1)}, u32[]{:S(2)}, u32[]{:S(2)}) collective-permute-start(bf16[1024,256]{1,0:T(8,128)(2,1)} %get-tuple-element.52), channel_id=1, source_target_pairs={{0,12},{1,13},{2,14},{3,15},{4,0},{5,1},{6,2},{7,3},{8,4},{9,5},{1... | collective-permute-start | bytes 1572872 | tf_op jit(solution)/shard_map/ppermute | solution.py:62
  134.9 25.1 %collective-permute-start.20 = (bf16[1024,256]{1,0:T(8,128)(2,1)S(1)}, bf16[1024,256]{1,0:T(8,128)(2,1)S(1)}, u32[]{:S(2)}, u32[]{:S(2)}) collective-permute-start(bf16[1024,256]{1,0:T(8,128)(2,1)S(1)} %get-tuple-element.53), channel_id=1, source_target_pairs={{0,8},{1,9},{2,10},{3,11},{4,12},{5,13},{6,14},{7,15},{8,0},{9,1},... | collective-permute-start | bytes 1572872 | tf_op jit(solution)/shard_map/ppermute | solution.py:62
  136.8 26.6 %collective-permute-start.21 = (bf16[1024,256]{1,0:T(8,128)(2,1)S(1)}, bf16[1024,256]{1,0:T(8,128)(2,1)S(1)}, u32[]{:S(2)}, u32[]{:S(2)}) collective-permute-start(bf16[1024,256]{1,0:T(8,128)(2,1)S(1)} %get-tuple-element.54), channel_id=1, source_target_pairs={{0,4},{1,5},{2,6},{3,7},{4,8},{5,9},{6,10},{7,11},{8,12},{9,13},{1... | collective-permute-start | bytes 1572872 | tf_op jit(solution)/shard_map/ppermute | solution.py:62
  148.1 31.4 %all-to-all-start.2 = ((f32[8,16,256]{2,1,0:T(8,128)}), f32[8,16,256]{2,1,0:T(8,128)S(1)}, u32[]{:S(2)}, u32[]{:S(2)}) async-start(f32[8,16,256]{2,1,0:T(8,128)} %sum_and_spread.4), calls=%async_computation.2 | async-start | bytes 262144 | tf_op jit(solution)/shard_map/all_to_all | solution.py:70
  167.6 17.7 %collective-permute-start.22 = (bf16[512,256]{1,0:T(8,128)(2,1)S(1)}, bf16[512,256]{1,0:T(8,128)(2,1)S(1)}, u32[]{:S(2)}, u32[]{:S(2)}) collective-permute-start(bf16[512,256]{1,0:T(8,128)(2,1)S(1)} %get-tuple-element.56), channel_id=1, source_target_pairs={{0,992},{16,1008},{32,0},{48,16},{64,32},{80,48},{96,64},{112,80},... | collective-permute-start | bytes 786440 | tf_op jit(solution)/shard_map/ppermute | solution.py:52
  169.6 21.0 %collective-permute-start.23 = (bf16[512,256]{1,0:T(8,128)(2,1)S(1)}, bf16[512,256]{1,0:T(8,128)(2,1)S(1)}, u32[]{:S(2)}, u32[]{:S(2)}) collective-permute-start(bf16[512,256]{1,0:T(8,128)(2,1)S(1)} %get-tuple-element.57), channel_id=1, source_target_pairs={{0,1008},{16,0},{32,16},{48,32},{64,48},{80,64},{96,80},{112,96},{... | collective-permute-start | bytes 786440 | tf_op jit(solution)/shard_map/ppermute | solution.py:52
  172.7 18.0 %collective-permute-start.24 = (bf16[512,256]{1,0:T(8,128)(2,1)S(1)}, bf16[512,256]{1,0:T(8,128)(2,1)S(1)}, u32[]{:S(2)}, u32[]{:S(2)}) collective-permute-start(bf16[512,256]{1,0:T(8,128)(2,1)S(1)} %get-tuple-element.58), channel_id=1, source_target_pairs={{0,16},{16,32},{32,48},{48,64},{64,80},{80,96},{96,112},{112,128},... | collective-permute-start | bytes 786440 | tf_op jit(solution)/shard_map/ppermute | solution.py:52
  (21 other events, 203.0 us)

commit v10 on v9

--- a/solution.py
+++ b/solution.py
@@ -365,7 +365,7 @@
     pieces = local_grad.reshape(rows, local_grad.shape[0] // rows, local_grad.shape[1])
     piece = sum_and_spread(exchange(pieces, "rows"), INNER)
     piece = sum_and_spread(exchange(piece, "dom", near), outer)
-    return sum_and_spread(exchange(piece, "dom", far), rows, BF16)
+    return sum_and_spread(exchange(piece, "dom", far), XN, BF16)
 
 
 def per_device(
@@ -381,8 +381,10 @@
     feats = [near[0], near[1], features, near[2], near[3]]
     feats = [f.reshape(blocks_dev, BLOCK, channels) for f in feats]
     sent = forward_products(src, slot, cnt, feats, vals, slot_block)
-    got0 = [sent[0]] + [x_shift(sent[k], k) for k in range(1, XN)]
-    got1 = [sent[XN]] + [x_shift(sent[XN + k], k) for k in range(1, XN)]
+    got0, got1 = list(sent[:XN]), list(sent[XN:])
+    for got in (got0, got1):
+        for k in (1, 3, 2):
+            got[k] = x_shift(got[k], k)
     *sums0, ids = gather_blocks(got0, blocks_dev)
     agg0 = half_sum([sums0[0]] + [y_shift(sums0[k], k) for k in range(1, YN)])
     sums1 = gather_blocks(got1, blocks_dev, ids)
@@ -398,7 +400,10 @@
     terms = list(backward_products(src, slot, cnt, back, vals, blocks_dev))
     own = terms.pop(HALF)
     terms = [dom_shift(t, o) for t, o in zip(terms, OFFSETS)]
-    weight_grad = exchange(piece, "rows").reshape(local_grad.shape).astype(F32)
+    column = exchange(piece, "rows", X_GROUPS)
+    column = jnp.broadcast_to(column.reshape(1, -1, channels), (YN, channels // YN, channels))
+    whole = exchange(column, "rows", Y_GROUPS).reshape(YN, XN, -1, channels)
+    weight_grad = whole.transpose(1, 0, 2, 3).reshape(local_grad.shape).astype(F32)
     feature_grad = final_sum(own, terms)
     return (activations, feature_grad, weight_grad)
 

time: 197 us -> 202 us (1.025)
  blocking collectives: 8.09 us -> 15 us
  waiting for transfers between devices: 43.1 us -> 40.8 us
    all_to_all x1 -> x2, blocking collectives: 8.09 us -> 15 us  [exchange(): lax.all_to_all(value, axis, split_axis=0, concat_axis=0, tiled=True, axis...]
    ppermute x8, waiting for transfers between devices: 14.2 us -> 8.89 us  [dom_shift(): lax.ppermute(value, 'dom', [(i, (i + steps) % count) for i in range(count)])]
    all_to_all x3, waiting for transfers between devices: 3.26 us -> 6.28 us  [exchange(): lax.all_to_all(value, axis, split_axis=0, concat_axis=0, tiled=True, axis...]
  transfers between devices with their start and end apart: 29 -> 29, of which waited for: 11 -> 10; matrix products, arithmetic and copies ran while one was open for 0% -> 0% of each run, Pallas kernels for 4% -> 3%
where the time goes in v10:
time: 202 us; the launch traced here: 200 us
  starting transfers between devices  125 us (62%)
  waiting for transfers between devices  40.8 us (20%)
  blocking collectives  15 us (7%)
  Pallas kernels  11.7 us (6%)
  local copies, waits for them, and re-layouts  6.34 us (3%)
    ppermute x8, starting transfers between devices, dom_shift(): lax.ppermute(value, 'dom', [(i, (i + steps) % count) for i in range(count)])  38.1 us
    ppermute x9, starting transfers between devices, y_shift(): return lax.ppermute(value, 'rows', pairs)  36.3 us
    ppermute x9, starting transfers between devices, x_shift(): return lax.ppermute(value, 'rows', pairs)  27.8 us
    all_to_all x3, starting transfers between devices, exchange(): lax.all_to_all(value, axis, split_axis=0, concat_axis=0, tiled=True, axis...  23.1 us
    ppermute x9, waiting for transfers between devices, y_shift(): return lax.ppermute(value, 'rows', pairs)  18.4 us
    all_to_all x2, blocking collectives, exchange(): lax.all_to_all(value, axis, split_axis=0, concat_axis=0, tiled=True, axis...  15 us
    pallas_call x11, Pallas kernels, kernel_call(): pl.pallas_call(body, out_shape=outs, in_specs=[space for space, _ in ins]...  11.7 us
    ppermute x8, waiting for transfers between devices, dom_shift(): lax.ppermute(value, 'dom', [(i, (i + steps) % count) for i in range(count)])  8.89 us
  transfers between devices with their start and end apart: 29, of which 10 were waited for; matrix products, arithmetic and copies ran while one was open for 0% of the time, Pallas kernels for 3%

profile of v10, /device:TPU:1, one launch (start us, length us, event | category | flops | bytes accessed | tf_op | source)
XLA Modules:
  0.0 200.3 jit_solution(9398041837668203363)
XLA Ops:
  0.6 4.0 %collective-permute-start = (bf16[512,256]{1,0:T(8,128)(2,1)}, bf16[512,256]{1,0:T(8,128)(2,1)S(1)}, u32[]{:S(2)}, u32[]{:S(2)}) collective-permute-start(bf16[512,256]{1,0:T(8,128)(2,1)} %param.8), channel_id=1, source_target_pairs={{0,32},{16,48},{32,64},{48,80},{64,96},{80,112},{96,128},{112,144}... | collective-permute-start | bytes 786440 | tf_op jit(solution)/shard_map/ppermute | solution.py:52
  4.7 4.7 %collective-permute-start.1 = (bf16[512,256]{1,0:T(8,128)(2,1)}, bf16[512,256]{1,0:T(8,128)(2,1)S(1)}, u32[]{:S(2)}, u32[]{:S(2)}) collective-permute-start(bf16[512,256]{1,0:T(8,128)(2,1)} %param.8), channel_id=1, source_target_pairs={{0,16},{16,32},{32,48},{48,64},{64,80},{80,96},{96,112},{112,128},... | collective-permute-start | bytes 786440 | tf_op jit(solution)/shard_map/ppermute | solution.py:52
  9.4 11.1 %collective-permute-start.2 = (bf16[512,256]{1,0:T(8,128)(2,1)}, bf16[512,256]{1,0:T(8,128)(2,1)S(1)}, u32[]{:S(2)}, u32[]{:S(2)}) collective-permute-start(bf16[512,256]{1,0:T(8,128)(2,1)} %param.8), channel_id=1, source_target_pairs={{0,1008},{16,0},{32,16},{48,32},{64,48},{80,64},{96,80},{112,96},{... | collective-permute-start | bytes 786440 | tf_op jit(solution)/shard_map/ppermute | solution.py:52
  20.6 6.3 %collective-permute-start.3 = (bf16[512,256]{1,0:T(8,128)(2,1)}, bf16[512,256]{1,0:T(8,128)(2,1)S(1)}, u32[]{:S(2)}, u32[]{:S(2)}) collective-permute-start(bf16[512,256]{1,0:T(8,128)(2,1)} %param.8), channel_id=1, source_target_pairs={{0,992},{16,1008},{32,0},{48,16},{64,32},{80,48},{96,64},{112,80},... | collective-permute-start | bytes 786440 | tf_op jit(solution)/shard_map/ppermute | solution.py:52
  26.9 8.9 %collective-permute-done.3 = bf16[512,256]{1,0:T(8,128)(2,1)S(1)} collective-permute-done((bf16[512,256]{1,0:T(8,128)(2,1)}, bf16[512,256]{1,0:T(8,128)(2,1)S(1)}, u32[]{:S(2)}, u32[]{:S(2)}) %collective-permute-start.3) | collective-permute-done | bytes 262176 | tf_op jit(solution)/shard_map/ppermute | solution.py:52
  36.5 3.8 %tile_forward.1 = (bf16[1040,128]{1,0:T(8,128)(2,1)}, bf16[1040,128]{1,0:T(8,128)(2,1)}, bf16[1040,128]{1,0:T(8,128)(2,1)}, bf16[1040,128]{1,0:T(8,128)(2,1)}, b...) custom-call(s32[4,5]{1,0:T(4,128)} %bitcast.26, ...), custom_call_target="tpu_custom_call" | custom-call | flops 167772160 | bytes 1966388 | tf_op jit(solution)/shard_map/tile_forward/pallas_call | solution.py:38
  44.6 4.1 %collective-permute-start.6 = (bf16[1040,128]{1,0:T(8,128)(2,1)}, bf16[1040,128]{1,0:T(8,128)(2,1)S(1)}, u32[]{:S(2)}, u32[]{:S(2)}) collective-permute-start(bf16[1040,128]{1,0:T(8,128)(2,1)} %get-tuple-element.35), channel_id=1, source_target_pairs={{0,12},{1,13},{2,14},{3,15},{4,0},{5,1},{6,2},{7,3},{8,4},{9,5},{1... | collective-permute-start | bytes 798728 | tf_op jit(solution)/shard_map/ppermute | solution.py:62
  68.0 3.9 %collective-permute-start.9 = (bf16[512,128]{1,0:T(8,128)(2,1)S(1)}, bf16[512,128]{1,0:T(8,128)(2,1)S(1)}, u32[]{:S(2)}, u32[]{:S(2)}) collective-permute-start(bf16[512,128]{1,0:T(8,128)(2,1)S(1)} %get-tuple-element.39), channel_id=1, source_target_pairs={{0,3},{1,0},{2,1},{3,2},{4,7},{5,4},{6,5},{7,6},{8,11},{9,8},{10,9... | collective-permute-start | bytes 393224 | tf_op jit(solution)/shard_map/ppermute | solution.py:57
  75.6 5.2 %collective-permute-start.14 = (bf16[512,128]{1,0:T(8,128)(2,1)S(1)}, bf16[512,128]{1,0:T(8,128)(2,1)S(1)}, u32[]{:S(2)}, u32[]{:S(2)}) collective-permute-start(bf16[512,128]{1,0:T(8,128)(2,1)S(1)} %get-tuple-element.47), channel_id=1, source_target_pairs={{0,2},{1,3},{2,0},{3,1},{4,6},{5,7},{6,4},{7,5},{8,10},{9,11},{10,... | collective-permute-start | bytes 393224 | tf_op jit(solution)/shard_map/ppermute | solution.py:57
  80.8 5.5 %collective-permute-start.15 = (bf16[512,128]{1,0:T(8,128)(2,1)S(1)}, bf16[512,128]{1,0:T(8,128)(2,1)S(1)}, u32[]{:S(2)}, u32[]{:S(2)}) collective-permute-start(bf16[512,128]{1,0:T(8,128)(2,1)S(1)} %get-tuple-element.48), channel_id=1, source_target_pairs={{0,3},{1,0},{2,1},{3,2},{4,7},{5,4},{6,5},{7,6},{8,11},{9,8},{10,9... | collective-permute-start | bytes 393224 | tf_op jit(solution)/shard_map/ppermute | solution.py:57
  87.3 6.6 %collective-permute-done.15.refs_4_ = bf16[512,128]{1,0:T(8,128)(2,1)S(1)} collective-permute-done((bf16[512,128]{1,0:T(8,128)(2,1)S(1)}, bf16[512,128]{1,0:T(8,128)(2,1)S(1)}, u32[]{:S(2)}, u32[]{:S(2)}) %collective-permute-start.15) | collective-permute-done | bytes 131104 | tf_op jit(solution)/shard_map/ppermute | solution.py:57
  95.1 3.8 %collective-permute-start.16 = (bf16[512,256]{1,0:T(8,128)(2,1)S(1)}, bf16[512,256]{1,0:T(8,128)(2,1)S(1)}, u32[]{:S(2)}, u32[]{:S(2)}) collective-permute-start(bf16[512,256]{1,0:T(8,128)(2,1)S(1)} %get-tuple-element.50), channel_id=1, source_target_pairs={{0,1},{1,2},{2,3},{3,0},{4,5},{5,6},{6,7},{7,4},{8,9},{9,10},{10,1... | collective-permute-start | bytes 786440 | tf_op jit(solution)/shard_map/ppermute | solution.py:57
  98.9 4.2 %collective-permute-start.17 = (bf16[512,256]{1,0:T(8,128)(2,1)S(1)}, bf16[512,256]{1,0:T(8,128)(2,1)S(1)}, u32[]{:S(2)}, u32[]{:S(2)}) collective-permute-start(bf16[512,256]{1,0:T(8,128)(2,1)S(1)} %get-tuple-element.50), channel_id=1, source_target_pairs={{0,2},{1,3},{2,0},{3,1},{4,6},{5,7},{6,4},{7,5},{8,10},{9,11},{10,... | collective-permute-start | bytes 786440 | tf_op jit(solution)/shard_map/ppermute | solution.py:57
  103.0 5.5 %collective-permute-start.18 = (bf16[512,256]{1,0:T(8,128)(2,1)S(1)}, bf16[512,256]{1,0:T(8,128)(2,1)S(1)}, u32[]{:S(2)}, u32[]{:S(2)}) collective-permute-start(bf16[512,256]{1,0:T(8,128)(2,1)S(1)} %get-tuple-element.50), channel_id=1, source_target_pairs={{0,3},{1,0},{2,1},{3,2},{4,7},{5,4},{6,5},{7,6},{8,11},{9,8},{10,9... | collective-permute-start | bytes 786440 | tf_op jit(solution)/shard_map/ppermute | solution.py:57
  108.5 6.1 %all-to-all-start = ((bf16[16,16,256]{2,1,0:T(8,128)(2,1)}), bf16[16,16,256]{2,1,0:T(8,128)(2,1)S(1)}, u32[]{:S(2)}, u32[]{:S(2)}) async-start(bf16[16,16,256]{2,1,0:T(8,128)(2,1)} %bitcast.17), calls=%async_computation | async-start | bytes 262144 | tf_op jit(solution)/shard_map/all_to_all | solution.py:70
  114.6 4.6 %collective-permute-done.17 = bf16[512,256]{1,0:T(8,128)(2,1)S(1)} collective-permute-done((bf16[512,256]{1,0:T(8,128)(2,1)S(1)}, bf16[512,256]{1,0:T(8,128)(2,1)S(1)}, u32[]{:S(2)}, u32[]{:S(2)}) %collective-permute-start.17) | collective-permute-done | bytes 262176 | tf_op jit(solution)/shard_map/ppermute | solution.py:57
  119.2 6.4 %collective-permute-done.18 = bf16[512,256]{1,0:T(8,128)(2,1)S(1)} collective-permute-done((bf16[512,256]{1,0:T(8,128)(2,1)S(1)}, bf16[512,256]{1,0:T(8,128)(2,1)S(1)}, u32[]{:S(2)}, u32[]{:S(2)}) %collective-permute-start.18) | collective-permute-done | bytes 262176 | tf_op jit(solution)/shard_map/ppermute | solution.py:57
  128.1 6.7 %collective-permute-start.19 = (bf16[1024,256]{1,0:T(8,128)(2,1)}, bf16[1024,256]{1,0:T(8,128)(2,1)S(1)}, u32[]{:S(2)}, u32[]{:S(2)}) collective-permute-start(bf16[1024,256]{1,0:T(8,128)(2,1)} %get-tuple-element.52), channel_id=1, source_target_pairs={{0,12},{1,13},{2,14},{3,15},{4,0},{5,1},{6,2},{7,3},{8,4},{9,5},{1... | collective-permute-start | bytes 1572872 | tf_op jit(solution)/shard_map/ppermute | solution.py:62
  139.4 8.1 %all_to_all.25.parts = f32[8,16,256]{2,1,0:T(8,128)S(1)} all-to-all(f32[8,16,256]{2,1,0:T(8,128)S(1)} %sum_and_spread.3), channel_id=1, replica_groups={{0,16,32,48,64,80,96,112},{128,144,160,176,192,208,224,240},{256,272,28..., dimensions={0} | all-to-all | bytes 262144 | tf_op jit(solution)/shard_map/all_to_all | solution.py:70
  148.1 11.9 %all-to-all-start.2 = ((f32[8,16,256]{2,1,0:T(8,128)}), f32[8,16,256]{2,1,0:T(8,128)S(1)}, u32[]{:S(2)}, u32[]{:S(2)}) async-start(f32[8,16,256]{2,1,0:T(8,128)} %sum_and_spread.4), calls=%async_computation.2 | async-start | bytes 262144 | tf_op jit(solution)/shard_map/all_to_all | solution.py:70
  175.6 3.9 %collective-permute-start.25 = (bf16[512,256]{1,0:T(8,128)(2,1)S(1)}, bf16[512,256]{1,0:T(8,128)(2,1)S(1)}, u32[]{:S(2)}, u32[]{:S(2)}) collective-permute-start(bf16[512,256]{1,0:T(8,128)(2,1)S(1)} %get-tuple-element.59), channel_id=1, source_target_pairs={{0,32},{16,48},{32,64},{48,80},{64,96},{80,112},{96,128},{112,144}... | collective-permute-start | bytes 786440 | tf_op jit(solution)/shard_map/ppermute | solution.py:52
  179.5 7.0 %all_to_all.26 = bf16[4,16,256]{2,1,0:T(8,128)(2,1)S(1)} all-to-all(bf16[4,16,256]{2,1,0:T(8,128)(2,1)S(1)} %sum_and_spread.5), channel_id=1, replica_groups={{0,4,8,12},{1,5,9,13},{2,6,10,14},{3,7,11,15},{16,20,24,28},{17,21,25,2..., dimensions={0} | all-to-all | bytes 65536 | tf_op jit(solution)/shard_map/all_to_all | solution.py:70
  187.1 5.1 %all-to-all-start.4 = ((bf16[4,64,256]{2,1,0:T(8,128)(2,1)}), bf16[4,64,256]{2,1,0:T(8,128)(2,1)S(1)}, u32[]{:S(2)}, u32[]{:S(2)}) async-start(bf16[4,64,256]{2,1,0:T(8,128)(2,1)} %broadcast_in_dim.8), calls=%async_computation.4 | async-start | bytes 262144 | tf_op jit(solution)/shard_map/all_to_all | solution.py:70
  193.2 6.3 %all-to-all-done.4 = bf16[4,64,256]{2,1,0:T(8,128)(2,1)S(1)} async-done(((bf16[4,64,256]{2,1,0:T(8,128)(2,1)}), bf16[4,64,256]{2,1,0:T(8,128)(2,1)S(1)}, u32[]{:S(2)}, u32[]{:S(2)}) %all-to-all-start.4) | async-done | bytes 131104 | tf_op jit(solution)/shard_map/all_to_all | solution.py:70
  (82 shorter events, 55.8 us)
Async XLA Ops:
  0.6 26.2 %collective-permute-start = (bf16[512,256]{1,0:T(8,128)(2,1)}, bf16[512,256]{1,0:T(8,128)(2,1)S(1)}, u32[]{:S(2)}, u32[]{:S(2)}) collective-permute-start(bf16[512,256]{1,0:T(8,128)(2,1)} %param.8), channel_id=1, source_target_pairs={{0,32},{16,48},{32,64},{48,80},{64,96},{80,112},{96,128},{112,144}... | collective-permute-start | bytes 786440 | tf_op jit(solution)/shard_map/ppermute | solution.py:52
  4.7 22.2 %collective-permute-start.1 = (bf16[512,256]{1,0:T(8,128)(2,1)}, bf16[512,256]{1,0:T(8,128)(2,1)S(1)}, u32[]{:S(2)}, u32[]{:S(2)}) collective-permute-start(bf16[512,256]{1,0:T(8,128)(2,1)} %param.8), channel_id=1, source_target_pairs={{0,16},{16,32},{32,48},{48,64},{64,80},{80,96},{96,112},{112,128},... | collective-permute-start | bytes 786440 | tf_op jit(solution)/shard_map/ppermute | solution.py:52
  9.4 17.5 %collective-permute-start.2 = (bf16[512,256]{1,0:T(8,128)(2,1)}, bf16[512,256]{1,0:T(8,128)(2,1)S(1)}, u32[]{:S(2)}, u32[]{:S(2)}) collective-permute-start(bf16[512,256]{1,0:T(8,128)(2,1)} %param.8), channel_id=1, source_target_pairs={{0,1008},{16,0},{32,16},{48,32},{64,48},{80,64},{96,80},{112,96},{... | collective-permute-start | bytes 786440 | tf_op jit(solution)/shard_map/ppermute | solution.py:52
  20.6 15.3 %collective-permute-start.3 = (bf16[512,256]{1,0:T(8,128)(2,1)}, bf16[512,256]{1,0:T(8,128)(2,1)S(1)}, u32[]{:S(2)}, u32[]{:S(2)}) collective-permute-start(bf16[512,256]{1,0:T(8,128)(2,1)} %param.8), channel_id=1, source_target_pairs={{0,992},{16,1008},{32,0},{48,16},{64,32},{80,48},{96,64},{112,80},... | collective-permute-start | bytes 786440 | tf_op jit(solution)/shard_map/ppermute | solution.py:52
  40.3 16.5 %collective-permute-start.4 = (bf16[1040,128]{1,0:T(8,128)(2,1)}, bf16[1040,128]{1,0:T(8,128)(2,1)S(1)}, u32[]{:S(2)}, u32[]{:S(2)}) collective-permute-start(bf16[1040,128]{1,0:T(8,128)(2,1)} %get-tuple-element.33), channel_id=1, source_target_pairs={{0,4},{1,5},{2,6},{3,7},{4,8},{5,9},{6,10},{7,11},{8,12},{9,13},{1... | collective-permute-start | bytes 798728 | tf_op jit(solution)/shard_map/ppermute | solution.py:62
  42.2 16.7 %collective-permute-start.5 = (bf16[1040,128]{1,0:T(8,128)(2,1)}, bf16[1040,128]{1,0:T(8,128)(2,1)S(1)}, u32[]{:S(2)}, u32[]{:S(2)}) collective-permute-start(bf16[1040,128]{1,0:T(8,128)(2,1)} %get-tuple-element.34), channel_id=1, source_target_pairs={{0,8},{1,9},{2,10},{3,11},{4,12},{5,13},{6,14},{7,15},{8,0},{9,1},... | collective-permute-start | bytes 798728 | tf_op jit(solution)/shard_map/ppermute | solution.py:62
  44.6 15.2 %collective-permute-start.6 = (bf16[1040,128]{1,0:T(8,128)(2,1)}, bf16[1040,128]{1,0:T(8,128)(2,1)S(1)}, u32[]{:S(2)}, u32[]{:S(2)}) collective-permute-start(bf16[1040,128]{1,0:T(8,128)(2,1)} %get-tuple-element.35), channel_id=1, source_target_pairs={{0,12},{1,13},{2,14},{3,15},{4,0},{5,1},{6,2},{7,3},{8,4},{9,5},{1... | collective-permute-start | bytes 798728 | tf_op jit(solution)/shard_map/ppermute | solution.py:62
  48.7 19.3 %collective-permute-start.10 = (bf16[1024,128]{1,0:T(8,128)(2,1)}, bf16[1024,128]{1,0:T(8,128)(2,1)S(1)}, u32[]{:S(2)}, u32[]{:S(2)}) collective-permute-start(bf16[1024,128]{1,0:T(8,128)(2,1)} %get-tuple-element.41), channel_id=1, source_target_pairs={{0,4},{1,5},{2,6},{3,7},{4,8},{5,9},{6,10},{7,11},{8,12},{9,13},{1... | collective-permute-start | bytes 786440 | tf_op jit(solution)/shard_map/ppermute | solution.py:62
  51.2 20.7 %collective-permute-start.11 = (bf16[1024,128]{1,0:T(8,128)(2,1)}, bf16[1024,128]{1,0:T(8,128)(2,1)S(1)}, u32[]{:S(2)}, u32[]{:S(2)}) collective-permute-start(bf16[1024,128]{1,0:T(8,128)(2,1)} %get-tuple-element.42), channel_id=1, source_target_pairs={{0,8},{1,9},{2,10},{3,11},{4,12},{5,13},{6,14},{7,15},{8,0},{9,1},... | collective-permute-start | bytes 786440 | tf_op jit(solution)/shard_map/ppermute | solution.py:62
  61.5 19.3 %collective-permute-start.7 = (bf16[512,128]{1,0:T(8,128)(2,1)S(1)}, bf16[512,128]{1,0:T(8,128)(2,1)S(1)}, u32[]{:S(2)}, u32[]{:S(2)}) collective-permute-start(bf16[512,128]{1,0:T(8,128)(2,1)S(1)} %get-tuple-element.37), channel_id=1, source_target_pairs={{0,1},{1,2},{2,3},{3,0},{4,5},{5,6},{6,7},{7,4},{8,9},{9,10},{10,1... | collective-permute-start | bytes 393224 | tf_op jit(solution)/shard_map/ppermute | solution.py:57
  63.4 22.9 %collective-permute-start.8 = (bf16[512,128]{1,0:T(8,128)(2,1)S(1)}, bf16[512,128]{1,0:T(8,128)(2,1)S(1)}, u32[]{:S(2)}, u32[]{:S(2)}) collective-permute-start(bf16[512,128]{1,0:T(8,128)(2,1)S(1)} %get-tuple-element.38), channel_id=1, source_target_pairs={{0,2},{1,3},{2,0},{3,1},{4,6},{5,7},{6,4},{7,5},{8,10},{9,11},{10,... | collective-permute-start | bytes 393224 | tf_op jit(solution)/shard_map/ppermute | solution.py:57
  68.0 18.3 %collective-permute-start.9 = (bf16[512,128]{1,0:T(8,128)(2,1)S(1)}, bf16[512,128]{1,0:T(8,128)(2,1)S(1)}, u32[]{:S(2)}, u32[]{:S(2)}) collective-permute-start(bf16[512,128]{1,0:T(8,128)(2,1)S(1)} %get-tuple-element.39), channel_id=1, source_target_pairs={{0,3},{1,0},{2,1},{3,2},{4,7},{5,4},{6,5},{7,6},{8,11},{9,8},{10,9... | collective-permute-start | bytes 393224 | tf_op jit(solution)/shard_map/ppermute | solution.py:57
  95.1 19.5 %collective-permute-start.16 = (bf16[512,256]{1,0:T(8,128)(2,1)S(1)}, bf16[512,256]{1,0:T(8,128)(2,1)S(1)}, u32[]{:S(2)}, u32[]{:S(2)}) collective-permute-start(bf16[512,256]{1,0:T(8,128)(2,1)S(1)} %get-tuple-element.50), channel_id=1, source_target_pairs={{0,1},{1,2},{2,3},{3,0},{4,5},{5,6},{6,7},{7,4},{8,9},{9,10},{10,1... | collective-permute-start | bytes 786440 | tf_op jit(solution)/shard_map/ppermute | solution.py:57
  98.9 20.3 %collective-permute-start.17 = (bf16[512,256]{1,0:T(8,128)(2,1)S(1)}, bf16[512,256]{1,0:T(8,128)(2,1)S(1)}, u32[]{:S(2)}, u32[]{:S(2)}) collective-permute-start(bf16[512,256]{1,0:T(8,128)(2,1)S(1)} %get-tuple-element.50), channel_id=1, source_target_pairs={{0,2},{1,3},{2,0},{3,1},{4,6},{5,7},{6,4},{7,5},{8,10},{9,11},{10,... | collective-permute-start | bytes 786440 | tf_op jit(solution)/shard_map/ppermute | solution.py:57
  103.0 22.5 %collective-permute-start.18 = (bf16[512,256]{1,0:T(8,128)(2,1)S(1)}, bf16[512,256]{1,0:T(8,128)(2,1)S(1)}, u32[]{:S(2)}, u32[]{:S(2)}) collective-permute-start(bf16[512,256]{1,0:T(8,128)(2,1)S(1)} %get-tuple-element.50), channel_id=1, source_target_pairs={{0,3},{1,0},{2,1},{3,2},{4,7},{5,4},{6,5},{7,6},{8,11},{9,8},{10,9... | collective-permute-start | bytes 786440 | tf_op jit(solution)/shard_map/ppermute | solution.py:57
  108.5 30.8 %all-to-all-start = ((bf16[16,16,256]{2,1,0:T(8,128)(2,1)}), bf16[16,16,256]{2,1,0:T(8,128)(2,1)S(1)}, u32[]{:S(2)}, u32[]{:S(2)}) async-start(bf16[16,16,256]{2,1,0:T(8,128)(2,1)} %bitcast.17), calls=%async_computation | async-start | bytes 262144 | tf_op jit(solution)/shard_map/all_to_all | solution.py:70
  128.1 31.8 %collective-permute-start.19 = (bf16[1024,256]{1,0:T(8,128)(2,1)}, bf16[1024,256]{1,0:T(8,128)(2,1)S(1)}, u32[]{:S(2)}, u32[]{:S(2)}) collective-permute-start(bf16[1024,256]{1,0:T(8,128)(2,1)} %get-tuple-element.52), channel_id=1, source_target_pairs={{0,12},{1,13},{2,14},{3,15},{4,0},{5,1},{6,2},{7,3},{8,4},{9,5},{1... | collective-permute-start | bytes 1572872 | tf_op jit(solution)/shard_map/ppermute | solution.py:62
  134.9 25.1 %collective-permute-start.20 = (bf16[1024,256]{1,0:T(8,128)(2,1)S(1)}, bf16[1024,256]{1,0:T(8,128)(2,1)S(1)}, u32[]{:S(2)}, u32[]{:S(2)}) collective-permute-start(bf16[1024,256]{1,0:T(8,128)(2,1)S(1)} %get-tuple-element.53), channel_id=1, source_target_pairs={{0,8},{1,9},{2,10},{3,11},{4,12},{5,13},{6,14},{7,15},{8,0},{9,1},... | collective-permute-start | bytes 1572872 | tf_op jit(solution)/shard_map/ppermute | solution.py:62
  136.8 26.6 %collective-permute-start.21 = (bf16[1024,256]{1,0:T(8,128)(2,1)S(1)}, bf16[1024,256]{1,0:T(8,128)(2,1)S(1)}, u32[]{:S(2)}, u32[]{:S(2)}) collective-permute-start(bf16[1024,256]{1,0:T(8,128)(2,1)S(1)} %get-tuple-element.54), channel_id=1, source_target_pairs={{0,4},{1,5},{2,6},{3,7},{4,8},{5,9},{6,10},{7,11},{8,12},{9,13},{1... | collective-permute-start | bytes 1572872 | tf_op jit(solution)/shard_map/ppermute | solution.py:62
  148.1 31.4 %all-to-all-start.2 = ((f32[8,16,256]{2,1,0:T(8,128)}), f32[8,16,256]{2,1,0:T(8,128)S(1)}, u32[]{:S(2)}, u32[]{:S(2)}) async-start(f32[8,16,256]{2,1,0:T(8,128)} %sum_and_spread.4), calls=%async_computation.2 | async-start | bytes 262144 | tf_op jit(solution)/shard_map/all_to_all | solution.py:70
  167.6 24.7 %collective-permute-start.22 = (bf16[512,256]{1,0:T(8,128)(2,1)S(1)}, bf16[512,256]{1,0:T(8,128)(2,1)S(1)}, u32[]{:S(2)}, u32[]{:S(2)}) collective-permute-start(bf16[512,256]{1,0:T(8,128)(2,1)S(1)} %get-tuple-element.56), channel_id=1, source_target_pairs={{0,992},{16,1008},{32,0},{48,16},{64,32},{80,48},{96,64},{112,80},... | collective-permute-start | bytes 786440 | tf_op jit(solution)/shard_map/ppermute | solution.py:52
  169.6 22.6 %collective-permute-start.23 = (bf16[512,256]{1,0:T(8,128)(2,1)S(1)}, bf16[512,256]{1,0:T(8,128)(2,1)S(1)}, u32[]{:S(2)}, u32[]{:S(2)}) collective-permute-start(bf16[512,256]{1,0:T(8,128)(2,1)S(1)} %get-tuple-element.57), channel_id=1, source_target_pairs={{0,1008},{16,0},{32,16},{48,32},{64,48},{80,64},{96,80},{112,96},{... | collective-permute-start | bytes 786440 | tf_op jit(solution)/shard_map/ppermute | solution.py:52
  172.7 19.6 %collective-permute-start.24 = (bf16[512,256]{1,0:T(8,128)(2,1)S(1)}, bf16[512,256]{1,0:T(8,128)(2,1)S(1)}, u32[]{:S(2)}, u32[]{:S(2)}) collective-permute-start(bf16[512,256]{1,0:T(8,128)(2,1)S(1)} %get-tuple-element.58), channel_id=1, source_target_pairs={{0,16},{16,32},{32,48},{48,64},{64,80},{80,96},{96,112},{112,128},... | collective-permute-start | bytes 786440 | tf_op jit(solution)/shard_map/ppermute | solution.py:52
  175.6 16.7 %collective-permute-start.25 = (bf16[512,256]{1,0:T(8,128)(2,1)S(1)}, bf16[512,256]{1,0:T(8,128)(2,1)S(1)}, u32[]{:S(2)}, u32[]{:S(2)}) collective-permute-start(bf16[512,256]{1,0:T(8,128)(2,1)S(1)} %get-tuple-element.59), channel_id=1, source_target_pairs={{0,32},{16,48},{32,64},{48,80},{64,96},{80,112},{96,128},{112,144}... | collective-permute-start | bytes 786440 | tf_op jit(solution)/shard_map/ppermute | solution.py:52
  (21 other events, 202.4 us)

commit v11 on v9

--- a/solution.py
+++ b/solution.py
@@ -149,18 +149,24 @@
 
 
 def gather1_kernel(blocks_dev, *refs):
-    gather_kernel(blocks_dev, refs[:XN], refs[XN], refs[XN + 1 :])
-
-
-def gather_blocks(recv, blocks_dev, ids=None):
-    outs = (jax.ShapeDtypeStruct((blocks_dev * BLOCK, LANES), BF16),) * YN
+    recv, ids, first = refs[:XN], refs[XN], refs[XN + 1]
+    own, o1, o2, o3 = refs[XN + 2 :]
+    nodes = blocks_dev * BLOCK
+    o2[pl.ds(0, nodes), :] = first[...]
+    gather_kernel(blocks_dev, recv, ids, (own, o1, o2.at[pl.ds(nodes, nodes)], o3))
+
+
+def gather_blocks(recv, blocks_dev, ids=None, first=None):
+    half = jax.ShapeDtypeStruct((blocks_dev * BLOCK, LANES), BF16)
     if ids is None:
-        outs += (jax.ShapeDtypeStruct((XN * YN * CAP, 2 * LANES), F32),)
+        outs = (half,) * YN + (jax.ShapeDtypeStruct((XN * YN * CAP, 2 * LANES), F32),)
+    else:
+        outs = (half, half, jax.ShapeDtypeStruct((2 * blocks_dev * BLOCK, LANES), BF16), half)
     return kernel_call(
         functools.partial(gather0_kernel if ids is None else gather1_kernel, blocks_dev),
         "block_sums",
         outs,
-        [(VMEM, a) for a in recv] + ([] if ids is None else [(VMEM, ids)]),
+        [(VMEM, a) for a in recv] + ([] if ids is None else [(VMEM, ids), (VMEM, first)]),
         6,
         GATHER_FLOPS,
     )
@@ -170,7 +176,7 @@
     total = parts[0][...].astype(F32)
     for part in parts[1:]:
         total = total + part[...].astype(F32)
-    return total.astype(BF16)
+    return total
 
 
 def half_kernel(*refs):
@@ -181,7 +187,7 @@
     return kernel_call(
         half_kernel,
         "half_sum",
-        jax.ShapeDtypeStruct(parts[0].shape, BF16),
+        jax.ShapeDtypeStruct(parts[0].shape, F32),
         [(VMEM, a) for a in parts],
         4,
         HALF_FLOPS,
@@ -189,8 +195,12 @@
 
 
 def dense_kernel(*refs):
-    agg0, parts, (weight, cot, act, grad, wgrad) = refs[0], refs[1 : 1 + YN], refs[1 + YN :]
-    agg = jnp.concatenate([agg0[...], summed(parts)], axis=1)
+    sum0, both, parts = refs[0], refs[1], refs[2 : 1 + YN]
+    weight, cot, act, grad, wgrad = refs[1 + YN :]
+    nodes = cot.shape[0]
+    left = sum0[...] + both[pl.ds(0, nodes), :].astype(F32)
+    right = summed(parts) + both[pl.ds(nodes, nodes), :].astype(F32)
+    agg = jnp.concatenate([left, right], axis=1).astype(BF16)
     w = weight[...]
     pre = jnp.dot(agg, w, preferred_element_type=F32)
     sig = 1.0 / (1.0 + jnp.exp(-pre))
@@ -205,14 +215,14 @@
     ).astype(BF16)
 
 
-def dense(agg0, parts, weight, cot):
+def dense(sum0, both, parts, weight, cot):
     nodes, channels = cot.shape
     full = jax.ShapeDtypeStruct((nodes, channels), BF16)
     return kernel_call(
         dense_kernel,
         "dense_layer",
         (full, full, jax.ShapeDtypeStruct((channels, channels), BF16)),
-        [(VMEM, a) for a in (agg0, *parts, weight, cot)],
+        [(VMEM, a) for a in (sum0, both, *parts, weight, cot)],
         10,
         DENSE_FLOPS,
     )
@@ -384,10 +394,11 @@
     got0 = [sent[0]] + [x_shift(sent[k], k) for k in range(1, XN)]
     got1 = [sent[XN]] + [x_shift(sent[XN + k], k) for k in range(1, XN)]
     *sums0, ids = gather_blocks(got0, blocks_dev)
-    agg0 = half_sum([sums0[0]] + [y_shift(sums0[k], k) for k in range(1, YN)])
-    sums1 = gather_blocks(got1, blocks_dev, ids)
-    parts = [sums1[0]] + [y_shift(sums1[k], k) for k in range(1, YN)]
-    activations, grad, local_grad = dense(agg0, parts, weight, cotangent)
+    sum0 = half_sum([sums0[0], y_shift(sums0[1], 1), y_shift(sums0[3], 3)])
+    sums1 = gather_blocks(got1, blocks_dev, ids, sums0[2])
+    both = y_shift(sums1[2], 2)
+    parts = [sums1[0], y_shift(sums1[1], 1), y_shift(sums1[3], 3)]
+    activations, grad, local_grad = dense(sum0, both, parts, weight, cotangent)
 
     piece = weight_piece(local_grad)
     grads = [grad] + [y_shift(grad, k) for k in range(1, YN)]

time: 197 us -> 204 us (1.036)
  waiting for transfers between devices: 43.1 us -> 65.3 us
  starting transfers between devices: 125 us -> 110 us
    ppermute x9 -> x8, waiting for transfers between devices: 18.4 us -> 30.1 us  [y_shift(): return lax.ppermute(value, 'rows', pairs)]
    ppermute x9, waiting for transfers between devices: 7.25 us -> 16.5 us  [x_shift(): return lax.ppermute(value, 'rows', pairs)]
    ppermute x9 -> x8, starting transfers between devices: 36.3 us -> 29.4 us  [y_shift(): return lax.ppermute(value, 'rows', pairs)]
    all_to_all x3, starting transfers between devices: 23 us -> 16.3 us  [exchange(): lax.all_to_all(value, axis, split_axis=0, concat_axis=0, tiled=True, axis...]
  transfers between devices with their start and end apart: 29 -> 28, of which waited for: 11 -> 9; matrix products, arithmetic and copies ran while one was open for 0% -> 0% of each run, Pallas kernels for 4% -> 4%
where the time goes in v11:
time: 204 us; the launch traced here: 202 us
  starting transfers between devices  110 us (54%)
  waiting for transfers between devices  65.3 us (32%)
  Pallas kernels  12.3 us (6%)
  blocking collectives  8.09 us (4%)
  local copies, waits for them, and re-layouts  4.98 us (2%)
    ppermute x8, starting transfers between devices, dom_shift(): lax.ppermute(value, 'dom', [(i, (i + steps) % count) for i in range(count)])  38.1 us
    ppermute x8, waiting for transfers between devices, y_shift(): return lax.ppermute(value, 'rows', pairs)  30.1 us
    ppermute x8, starting transfers between devices, y_shift(): return lax.ppermute(value, 'rows', pairs)  29.4 us
    ppermute x9, starting transfers between devices, x_shift(): return lax.ppermute(value, 'rows', pairs)  26.2 us
    ppermute x9, waiting for transfers between devices, x_shift(): return lax.ppermute(value, 'rows', pairs)  16.5 us
    all_to_all x3, starting transfers between devices, exchange(): lax.all_to_all(value, axis, split_axis=0, concat_axis=0, tiled=True, axis...  16.3 us
    ppermute x8, waiting for transfers between devices, dom_shift(): lax.ppermute(value, 'dom', [(i, (i + steps) % count) for i in range(count)])  16.2 us
    pallas_call x11, Pallas kernels, kernel_call(): pl.pallas_call(body, out_shape=outs, in_specs=[space for space, _ in ins]...  12.3 us
  transfers between devices with their start and end apart: 28, of which 9 were waited for; matrix products, arithmetic and copies ran while one was open for 0% of the time, Pallas kernels for 4%

profile of v11, /device:TPU:1, one launch (start us, length us, event | category | flops | bytes accessed | tf_op | source)
XLA Modules:
  0.0 202.4 jit_solution(12277793433840404903)
XLA Ops:
  0.6 4.0 %collective-permute-start = (bf16[512,256]{1,0:T(8,128)(2,1)}, bf16[512,256]{1,0:T(8,128)(2,1)S(1)}, u32[]{:S(2)}, u32[]{:S(2)}) collective-permute-start(bf16[512,256]{1,0:T(8,128)(2,1)} %param.8), channel_id=1, source_target_pairs={{0,32},{16,48},{32,64},{48,80},{64,96},{80,112},{96,128},{112,144}... | collective-permute-start | bytes 786440 | tf_op jit(solution)/shard_map/ppermute | solution.py:52
  4.7 4.7 %collective-permute-start.1 = (bf16[512,256]{1,0:T(8,128)(2,1)}, bf16[512,256]{1,0:T(8,128)(2,1)S(1)}, u32[]{:S(2)}, u32[]{:S(2)}) collective-permute-start(bf16[512,256]{1,0:T(8,128)(2,1)} %param.8), channel_id=1, source_target_pairs={{0,16},{16,32},{32,48},{48,64},{64,80},{80,96},{96,112},{112,128},... | collective-permute-start | bytes 786440 | tf_op jit(solution)/shard_map/ppermute | solution.py:52
  9.4 11.1 %collective-permute-start.2 = (bf16[512,256]{1,0:T(8,128)(2,1)}, bf16[512,256]{1,0:T(8,128)(2,1)S(1)}, u32[]{:S(2)}, u32[]{:S(2)}) collective-permute-start(bf16[512,256]{1,0:T(8,128)(2,1)} %param.8), channel_id=1, source_target_pairs={{0,1008},{16,0},{32,16},{48,32},{64,48},{80,64},{96,80},{112,96},{... | collective-permute-start | bytes 786440 | tf_op jit(solution)/shard_map/ppermute | solution.py:52
  20.6 6.3 %collective-permute-start.3 = (bf16[512,256]{1,0:T(8,128)(2,1)}, bf16[512,256]{1,0:T(8,128)(2,1)S(1)}, u32[]{:S(2)}, u32[]{:S(2)}) collective-permute-start(bf16[512,256]{1,0:T(8,128)(2,1)} %param.8), channel_id=1, source_target_pairs={{0,992},{16,1008},{32,0},{48,16},{64,32},{80,48},{96,64},{112,80},... | collective-permute-start | bytes 786440 | tf_op jit(solution)/shard_map/ppermute | solution.py:52
  26.9 8.9 %collective-permute-done.3 = bf16[512,256]{1,0:T(8,128)(2,1)S(1)} collective-permute-done((bf16[512,256]{1,0:T(8,128)(2,1)}, bf16[512,256]{1,0:T(8,128)(2,1)S(1)}, u32[]{:S(2)}, u32[]{:S(2)}) %collective-permute-start.3) | collective-permute-done | bytes 262176 | tf_op jit(solution)/shard_map/ppermute | solution.py:52
  44.7 4.0 %collective-permute-start.6 = (bf16[1040,128]{1,0:T(8,128)(2,1)}, bf16[1040,128]{1,0:T(8,128)(2,1)S(1)}, u32[]{:S(2)}, u32[]{:S(2)}) collective-permute-start(bf16[1040,128]{1,0:T(8,128)(2,1)} %get-tuple-element.35), channel_id=1, source_target_pairs={{0,12},{1,13},{2,14},{3,15},{4,0},{5,1},{6,2},{7,3},{8,4},{9,5},{1... | collective-permute-start | bytes 798728 | tf_op jit(solution)/shard_map/ppermute | solution.py:62
  48.7 4.3 %collective-permute-start.10 = (bf16[1024,128]{1,0:T(8,128)(2,1)}, bf16[1024,128]{1,0:T(8,128)(2,1)S(1)}, u32[]{:S(2)}, u32[]{:S(2)}) collective-permute-start(bf16[1024,128]{1,0:T(8,128)(2,1)} %get-tuple-element.41), channel_id=1, source_target_pairs={{0,8},{1,9},{2,10},{3,11},{4,12},{5,13},{6,14},{7,15},{8,0},{9,1},... | collective-permute-start | bytes 786440 | tf_op jit(solution)/shard_map/ppermute | solution.py:62
  55.5 6.9 %collective-permute-done.4.refs_1_ = bf16[1040,128]{1,0:T(8,128)(2,1)S(1)} collective-permute-done((bf16[1040,128]{1,0:T(8,128)(2,1)}, bf16[1040,128]{1,0:T(8,128)(2,1)S(1)}, u32[]{:S(2)}, u32[]{:S(2)}) %collective-permute-start.4) | collective-permute-done | bytes 266272 | tf_op jit(solution)/shard_map/ppermute | solution.py:62
  67.9 5.5 %collective-permute-start.8 = (bf16[512,128]{1,0:T(8,128)(2,1)S(1)}, bf16[512,128]{1,0:T(8,128)(2,1)S(1)}, u32[]{:S(2)}, u32[]{:S(2)}) collective-permute-start(bf16[512,128]{1,0:T(8,128)(2,1)S(1)} %get-tuple-element.38), channel_id=1, source_target_pairs={{0,3},{1,0},{2,1},{3,2},{4,7},{5,4},{6,5},{7,6},{8,11},{9,8},{10,9... | collective-permute-start | bytes 393224 | tf_op jit(solution)/shard_map/ppermute | solution.py:57
  76.1 4.0 %collective-permute-start.13 = (bf16[512,128]{1,0:T(8,128)(2,1)S(1)}, bf16[512,128]{1,0:T(8,128)(2,1)S(1)}, u32[]{:S(2)}, u32[]{:S(2)}) collective-permute-start(bf16[512,128]{1,0:T(8,128)(2,1)S(1)} %get-tuple-element.47), channel_id=1, source_target_pairs={{0,1},{1,2},{2,3},{3,0},{4,5},{5,6},{6,7},{7,4},{8,9},{9,10},{10,1... | collective-permute-start | bytes 393224 | tf_op jit(solution)/shard_map/ppermute | solution.py:57
  83.6 4.9 %collective-permute-done.13.refs_3_ = bf16[512,128]{1,0:T(8,128)(2,1)S(1)} collective-permute-done((bf16[512,128]{1,0:T(8,128)(2,1)S(1)}, bf16[512,128]{1,0:T(8,128)(2,1)S(1)}, u32[]{:S(2)}, u32[]{:S(2)}) %collective-permute-start.13) | collective-permute-done | bytes 131104 | tf_op jit(solution)/shard_map/ppermute | solution.py:57
  88.5 8.0 %collective-permute-done.14.refs_4_ = bf16[512,128]{1,0:T(8,128)(2,1)S(1)} collective-permute-done((bf16[512,128]{1,0:T(8,128)(2,1)S(1)}, bf16[512,128]{1,0:T(8,128)(2,1)S(1)}, u32[]{:S(2)}, u32[]{:S(2)}) %collective-permute-start.14) | collective-permute-done | bytes 131104 | tf_op jit(solution)/shard_map/ppermute | solution.py:57
  97.8 3.9 %collective-permute-start.15 = (bf16[512,256]{1,0:T(8,128)(2,1)S(1)}, bf16[512,256]{1,0:T(8,128)(2,1)S(1)}, u32[]{:S(2)}, u32[]{:S(2)}) collective-permute-start(bf16[512,256]{1,0:T(8,128)(2,1)S(1)} %get-tuple-element.50), channel_id=1, source_target_pairs={{0,1},{1,2},{2,3},{3,0},{4,5},{5,6},{6,7},{7,4},{8,9},{9,10},{10,1... | collective-permute-start | bytes 786440 | tf_op jit(solution)/shard_map/ppermute | solution.py:57
  101.7 5.4 %collective-permute-start.16 = (bf16[512,256]{1,0:T(8,128)(2,1)S(1)}, bf16[512,256]{1,0:T(8,128)(2,1)S(1)}, u32[]{:S(2)}, u32[]{:S(2)}) collective-permute-start(bf16[512,256]{1,0:T(8,128)(2,1)S(1)} %get-tuple-element.50), channel_id=1, source_target_pairs={{0,2},{1,3},{2,0},{3,1},{4,6},{5,7},{6,4},{7,5},{8,10},{9,11},{10,... | collective-permute-start | bytes 786440 | tf_op jit(solution)/shard_map/ppermute | solution.py:57
  110.5 5.9 %all-to-all-start = ((bf16[16,16,256]{2,1,0:T(8,128)(2,1)}), bf16[16,16,256]{2,1,0:T(8,128)(2,1)S(1)}, u32[]{:S(2)}, u32[]{:S(2)}) async-start(bf16[16,16,256]{2,1,0:T(8,128)(2,1)} %bitcast.17), calls=%async_computation | async-start | bytes 262144 | tf_op jit(solution)/shard_map/all_to_all | solution.py:70
  116.4 9.1 %collective-permute-done.16 = bf16[512,256]{1,0:T(8,128)(2,1)S(1)} collective-permute-done((bf16[512,256]{1,0:T(8,128)(2,1)S(1)}, bf16[512,256]{1,0:T(8,128)(2,1)S(1)}, u32[]{:S(2)}, u32[]{:S(2)}) %collective-permute-start.16) | collective-permute-done | bytes 262176 | tf_op jit(solution)/shard_map/ppermute | solution.py:57
  125.5 8.1 %collective-permute-done.17 = bf16[512,256]{1,0:T(8,128)(2,1)S(1)} collective-permute-done((bf16[512,256]{1,0:T(8,128)(2,1)S(1)}, bf16[512,256]{1,0:T(8,128)(2,1)S(1)}, u32[]{:S(2)}, u32[]{:S(2)}) %collective-permute-start.17) | collective-permute-done | bytes 262176 | tf_op jit(solution)/shard_map/ppermute | solution.py:57
  136.2 4.7 %collective-permute-start.18 = (bf16[1024,256]{1,0:T(8,128)(2,1)}, bf16[1024,256]{1,0:T(8,128)(2,1)S(1)}, u32[]{:S(2)}, u32[]{:S(2)}) collective-permute-start(bf16[1024,256]{1,0:T(8,128)(2,1)} %get-tuple-element.52), channel_id=1, source_target_pairs={{0,12},{1,13},{2,14},{3,15},{4,0},{5,1},{6,2},{7,3},{8,4},{9,5},{1... | collective-permute-start | bytes 1572872 | tf_op jit(solution)/shard_map/ppermute | solution.py:62
  145.4 8.1 %all_to_all.20.parts = f32[8,16,256]{2,1,0:T(8,128)S(1)} all-to-all(f32[8,16,256]{2,1,0:T(8,128)S(1)} %sum_and_spread.3), channel_id=1, replica_groups={{0,16,32,48,64,80,96,112},{128,144,160,176,192,208,224,240},{256,272,28..., dimensions={0} | all-to-all | bytes 262144 | tf_op jit(solution)/shard_map/all_to_all | solution.py:70
  154.1 5.6 %all-to-all-start.2 = ((f32[8,16,256]{2,1,0:T(8,128)}), f32[8,16,256]{2,1,0:T(8,128)S(1)}, u32[]{:S(2)}, u32[]{:S(2)}) async-start(f32[8,16,256]{2,1,0:T(8,128)} %sum_and_spread.4), calls=%async_computation.2 | async-start | bytes 262144 | tf_op jit(solution)/shard_map/all_to_all | solution.py:70
  159.8 9.6 %collective-permute-done.20.b3 = bf16[1024,256]{1,0:T(8,128)(2,1)S(1)} collective-permute-done((bf16[1024,256]{1,0:T(8,128)(2,1)S(1)}, bf16[1024,256]{1,0:T(8,128)(2,1)S(1)}, u32[]{:S(2)}, u32[]{:S(2)}) %collective-permute-start.20) | collective-permute-done | bytes 524320 | tf_op jit(solution)/shard_map/ppermute | solution.py:62
  181.6 3.9 %collective-permute-start.24 = (bf16[512,256]{1,0:T(8,128)(2,1)S(1)}, bf16[512,256]{1,0:T(8,128)(2,1)S(1)}, u32[]{:S(2)}, u32[]{:S(2)}) collective-permute-start(bf16[512,256]{1,0:T(8,128)(2,1)S(1)} %get-tuple-element.59), channel_id=1, source_target_pairs={{0,32},{16,48},{32,64},{48,80},{64,96},{80,112},{96,128},{112,144}... | collective-permute-start | bytes 786440 | tf_op jit(solution)/shard_map/ppermute | solution.py:52
  186.2 4.8 %all-to-all-start.3 = ((bf16[16,16,256]{2,1,0:T(8,128)(2,1)}), bf16[16,16,256]{2,1,0:T(8,128)(2,1)S(1)}, u32[]{:S(2)}, u32[]{:S(2)}) async-start(bf16[16,16,256]{2,1,0:T(8,128)(2,1)} %sum_and_spread.5), calls=%async_computation.3 | async-start | bytes 262144 | tf_op jit(solution)/shard_map/all_to_all | solution.py:70
  191.0 7.3 %collective-permute-done.24.r4 = bf16[512,256]{1,0:T(8,128)(2,1)S(1)} collective-permute-done((bf16[512,256]{1,0:T(8,128)(2,1)S(1)}, bf16[512,256]{1,0:T(8,128)(2,1)S(1)}, u32[]{:S(2)}, u32[]{:S(2)}) %collective-permute-start.24) | collective-permute-done | bytes 262176 | tf_op jit(solution)/shard_map/ppermute | solution.py:52
  (77 shorter events, 52.3 us)
Async XLA Ops:
  0.6 26.2 %collective-permute-start = (bf16[512,256]{1,0:T(8,128)(2,1)}, bf16[512,256]{1,0:T(8,128)(2,1)S(1)}, u32[]{:S(2)}, u32[]{:S(2)}) collective-permute-start(bf16[512,256]{1,0:T(8,128)(2,1)} %param.8), channel_id=1, source_target_pairs={{0,32},{16,48},{32,64},{48,80},{64,96},{80,112},{96,128},{112,144}... | collective-permute-start | bytes 786440 | tf_op jit(solution)/shard_map/ppermute | solution.py:52
  4.7 22.2 %collective-permute-start.1 = (bf16[512,256]{1,0:T(8,128)(2,1)}, bf16[512,256]{1,0:T(8,128)(2,1)S(1)}, u32[]{:S(2)}, u32[]{:S(2)}) collective-permute-start(bf16[512,256]{1,0:T(8,128)(2,1)} %param.8), channel_id=1, source_target_pairs={{0,16},{16,32},{32,48},{48,64},{64,80},{80,96},{96,112},{112,128},... | collective-permute-start | bytes 786440 | tf_op jit(solution)/shard_map/ppermute | solution.py:52
  9.4 17.5 %collective-permute-start.2 = (bf16[512,256]{1,0:T(8,128)(2,1)}, bf16[512,256]{1,0:T(8,128)(2,1)S(1)}, u32[]{:S(2)}, u32[]{:S(2)}) collective-permute-start(bf16[512,256]{1,0:T(8,128)(2,1)} %param.8), channel_id=1, source_target_pairs={{0,1008},{16,0},{32,16},{48,32},{64,48},{80,64},{96,80},{112,96},{... | collective-permute-start | bytes 786440 | tf_op jit(solution)/shard_map/ppermute | solution.py:52
  40.3 22.1 %collective-permute-start.4 = (bf16[1040,128]{1,0:T(8,128)(2,1)}, bf16[1040,128]{1,0:T(8,128)(2,1)S(1)}, u32[]{:S(2)}, u32[]{:S(2)}) collective-permute-start(bf16[1040,128]{1,0:T(8,128)(2,1)} %get-tuple-element.33), channel_id=1, source_target_pairs={{0,4},{1,5},{2,6},{3,7},{4,8},{5,9},{6,10},{7,11},{8,12},{9,13},{1... | collective-permute-start | bytes 798728 | tf_op jit(solution)/shard_map/ppermute | solution.py:62
  42.2 22.1 %collective-permute-start.5 = (bf16[1040,128]{1,0:T(8,128)(2,1)}, bf16[1040,128]{1,0:T(8,128)(2,1)S(1)}, u32[]{:S(2)}, u32[]{:S(2)}) collective-permute-start(bf16[1040,128]{1,0:T(8,128)(2,1)} %get-tuple-element.34), channel_id=1, source_target_pairs={{0,8},{1,9},{2,10},{3,11},{4,12},{5,13},{6,14},{7,15},{8,0},{9,1},... | collective-permute-start | bytes 798728 | tf_op jit(solution)/shard_map/ppermute | solution.py:62
  44.7 19.6 %collective-permute-start.6 = (bf16[1040,128]{1,0:T(8,128)(2,1)}, bf16[1040,128]{1,0:T(8,128)(2,1)S(1)}, u32[]{:S(2)}, u32[]{:S(2)}) collective-permute-start(bf16[1040,128]{1,0:T(8,128)(2,1)} %get-tuple-element.35), channel_id=1, source_target_pairs={{0,12},{1,13},{2,14},{3,15},{4,0},{5,1},{6,2},{7,3},{8,4},{9,5},{1... | collective-permute-start | bytes 798728 | tf_op jit(solution)/shard_map/ppermute | solution.py:62
  48.7 24.7 %collective-permute-start.10 = (bf16[1024,128]{1,0:T(8,128)(2,1)}, bf16[1024,128]{1,0:T(8,128)(2,1)S(1)}, u32[]{:S(2)}, u32[]{:S(2)}) collective-permute-start(bf16[1024,128]{1,0:T(8,128)(2,1)} %get-tuple-element.41), channel_id=1, source_target_pairs={{0,8},{1,9},{2,10},{3,11},{4,12},{5,13},{6,14},{7,15},{8,0},{9,1},... | collective-permute-start | bytes 786440 | tf_op jit(solution)/shard_map/ppermute | solution.py:62
  53.0 20.4 %collective-permute-start.11 = (bf16[1024,128]{1,0:T(8,128)(2,1)}, bf16[1024,128]{1,0:T(8,128)(2,1)S(1)}, u32[]{:S(2)}, u32[]{:S(2)}) collective-permute-start(bf16[1024,128]{1,0:T(8,128)(2,1)} %get-tuple-element.42), channel_id=1, source_target_pairs={{0,12},{1,13},{2,14},{3,15},{4,0},{5,1},{6,2},{7,3},{8,4},{9,5},{1... | collective-permute-start | bytes 786440 | tf_op jit(solution)/shard_map/ppermute | solution.py:62
  66.0 17.5 %collective-permute-start.7 = (bf16[512,128]{1,0:T(8,128)(2,1)S(1)}, bf16[512,128]{1,0:T(8,128)(2,1)S(1)}, u32[]{:S(2)}, u32[]{:S(2)}) collective-permute-start(bf16[512,128]{1,0:T(8,128)(2,1)S(1)} %get-tuple-element.37), channel_id=1, source_target_pairs={{0,1},{1,2},{2,3},{3,0},{4,5},{5,6},{6,7},{7,4},{8,9},{9,10},{10,1... | collective-permute-start | bytes 393224 | tf_op jit(solution)/shard_map/ppermute | solution.py:57
  67.9 15.6 %collective-permute-start.8 = (bf16[512,128]{1,0:T(8,128)(2,1)S(1)}, bf16[512,128]{1,0:T(8,128)(2,1)S(1)}, u32[]{:S(2)}, u32[]{:S(2)}) collective-permute-start(bf16[512,128]{1,0:T(8,128)(2,1)S(1)} %get-tuple-element.38), channel_id=1, source_target_pairs={{0,3},{1,0},{2,1},{3,2},{4,7},{5,4},{6,5},{7,6},{8,11},{9,8},{10,9... | collective-permute-start | bytes 393224 | tf_op jit(solution)/shard_map/ppermute | solution.py:57
  74.2 22.4 %collective-permute-start.12 = (bf16[1024,128]{1,0:T(8,128)(2,1)S(1)}, bf16[1024,128]{1,0:T(8,128)(2,1)S(1)}, u32[]{:S(2)}, u32[]{:S(2)}) collective-permute-start(bf16[1024,128]{1,0:T(8,128)(2,1)S(1)} %get-tuple-element.45), channel_id=1, source_target_pairs={{0,2},{1,3},{2,0},{3,1},{4,6},{5,7},{6,4},{7,5},{8,10},{9,11},{10,... | collective-permute-start | bytes 786440 | tf_op jit(solution)/shard_map/ppermute | solution.py:57
  80.1 16.4 %collective-permute-start.14 = (bf16[512,128]{1,0:T(8,128)(2,1)S(1)}, bf16[512,128]{1,0:T(8,128)(2,1)S(1)}, u32[]{:S(2)}, u32[]{:S(2)}) collective-permute-start(bf16[512,128]{1,0:T(8,128)(2,1)S(1)} %get-tuple-element.48), channel_id=1, source_target_pairs={{0,3},{1,0},{2,1},{3,2},{4,7},{5,4},{6,5},{7,6},{8,11},{9,8},{10,9... | collective-permute-start | bytes 393224 | tf_op jit(solution)/shard_map/ppermute | solution.py:57
  97.8 18.6 %collective-permute-start.15 = (bf16[512,256]{1,0:T(8,128)(2,1)S(1)}, bf16[512,256]{1,0:T(8,128)(2,1)S(1)}, u32[]{:S(2)}, u32[]{:S(2)}) collective-permute-start(bf16[512,256]{1,0:T(8,128)(2,1)S(1)} %get-tuple-element.50), channel_id=1, source_target_pairs={{0,1},{1,2},{2,3},{3,0},{4,5},{5,6},{6,7},{7,4},{8,9},{9,10},{10,1... | collective-permute-start | bytes 786440 | tf_op jit(solution)/shard_map/ppermute | solution.py:57
  101.7 23.8 %collective-permute-start.16 = (bf16[512,256]{1,0:T(8,128)(2,1)S(1)}, bf16[512,256]{1,0:T(8,128)(2,1)S(1)}, u32[]{:S(2)}, u32[]{:S(2)}) collective-permute-start(bf16[512,256]{1,0:T(8,128)(2,1)S(1)} %get-tuple-element.50), channel_id=1, source_target_pairs={{0,2},{1,3},{2,0},{3,1},{4,6},{5,7},{6,4},{7,5},{8,10},{9,11},{10,... | collective-permute-start | bytes 786440 | tf_op jit(solution)/shard_map/ppermute | solution.py:57
  107.1 26.5 %collective-permute-start.17 = (bf16[512,256]{1,0:T(8,128)(2,1)S(1)}, bf16[512,256]{1,0:T(8,128)(2,1)S(1)}, u32[]{:S(2)}, u32[]{:S(2)}) collective-permute-start(bf16[512,256]{1,0:T(8,128)(2,1)S(1)} %get-tuple-element.50), channel_id=1, source_target_pairs={{0,3},{1,0},{2,1},{3,2},{4,7},{5,4},{6,5},{7,6},{8,11},{9,8},{10,9... | collective-permute-start | bytes 786440 | tf_op jit(solution)/shard_map/ppermute | solution.py:57
  110.5 34.9 %all-to-all-start = ((bf16[16,16,256]{2,1,0:T(8,128)(2,1)}), bf16[16,16,256]{2,1,0:T(8,128)(2,1)S(1)}, u32[]{:S(2)}, u32[]{:S(2)}) async-start(bf16[16,16,256]{2,1,0:T(8,128)(2,1)} %bitcast.17), calls=%async_computation | async-start | bytes 262144 | tf_op jit(solution)/shard_map/all_to_all | solution.py:70
  136.2 23.5 %collective-permute-start.18 = (bf16[1024,256]{1,0:T(8,128)(2,1)}, bf16[1024,256]{1,0:T(8,128)(2,1)S(1)}, u32[]{:S(2)}, u32[]{:S(2)}) collective-permute-start(bf16[1024,256]{1,0:T(8,128)(2,1)} %get-tuple-element.52), channel_id=1, source_target_pairs={{0,12},{1,13},{2,14},{3,15},{4,0},{5,1},{6,2},{7,3},{8,4},{9,5},{1... | collective-permute-start | bytes 1572872 | tf_op jit(solution)/shard_map/ppermute | solution.py:62
  140.9 18.9 %collective-permute-start.19 = (bf16[1024,256]{1,0:T(8,128)(2,1)S(1)}, bf16[1024,256]{1,0:T(8,128)(2,1)S(1)}, u32[]{:S(2)}, u32[]{:S(2)}) collective-permute-start(bf16[1024,256]{1,0:T(8,128)(2,1)S(1)} %get-tuple-element.53), channel_id=1, source_target_pairs={{0,8},{1,9},{2,10},{3,11},{4,12},{5,13},{6,14},{7,15},{8,0},{9,1},... | collective-permute-start | bytes 1572872 | tf_op jit(solution)/shard_map/ppermute | solution.py:62
  142.8 26.6 %collective-permute-start.20 = (bf16[1024,256]{1,0:T(8,128)(2,1)S(1)}, bf16[1024,256]{1,0:T(8,128)(2,1)S(1)}, u32[]{:S(2)}, u32[]{:S(2)}) collective-permute-start(bf16[1024,256]{1,0:T(8,128)(2,1)S(1)} %get-tuple-element.54), channel_id=1, source_target_pairs={{0,4},{1,5},{2,6},{3,7},{4,8},{5,9},{6,10},{7,11},{8,12},{9,13},{1... | collective-permute-start | bytes 1572872 | tf_op jit(solution)/shard_map/ppermute | solution.py:62
  154.1 31.4 %all-to-all-start.2 = ((f32[8,16,256]{2,1,0:T(8,128)}), f32[8,16,256]{2,1,0:T(8,128)S(1)}, u32[]{:S(2)}, u32[]{:S(2)}) async-start(f32[8,16,256]{2,1,0:T(8,128)} %sum_and_spread.4), calls=%async_computation.2 | async-start | bytes 262144 | tf_op jit(solution)/shard_map/all_to_all | solution.py:70
  173.6 17.4 %collective-permute-start.21 = (bf16[512,256]{1,0:T(8,128)(2,1)S(1)}, bf16[512,256]{1,0:T(8,128)(2,1)S(1)}, u32[]{:S(2)}, u32[]{:S(2)}) collective-permute-start(bf16[512,256]{1,0:T(8,128)(2,1)S(1)} %get-tuple-element.56), channel_id=1, source_target_pairs={{0,992},{16,1008},{32,0},{48,16},{64,32},{80,48},{96,64},{112,80},... | collective-permute-start | bytes 786440 | tf_op jit(solution)/shard_map/ppermute | solution.py:52
  175.6 15.4 %collective-permute-start.22 = (bf16[512,256]{1,0:T(8,128)(2,1)S(1)}, bf16[512,256]{1,0:T(8,128)(2,1)S(1)}, u32[]{:S(2)}, u32[]{:S(2)}) collective-permute-start(bf16[512,256]{1,0:T(8,128)(2,1)S(1)} %get-tuple-element.57), channel_id=1, source_target_pairs={{0,1008},{16,0},{32,16},{48,32},{64,48},{80,64},{96,80},{112,96},{... | collective-permute-start | bytes 786440 | tf_op jit(solution)/shard_map/ppermute | solution.py:52
  181.6 16.8 %collective-permute-start.24 = (bf16[512,256]{1,0:T(8,128)(2,1)S(1)}, bf16[512,256]{1,0:T(8,128)(2,1)S(1)}, u32[]{:S(2)}, u32[]{:S(2)}) collective-permute-start(bf16[512,256]{1,0:T(8,128)(2,1)S(1)} %get-tuple-element.59), channel_id=1, source_target_pairs={{0,32},{16,48},{32,64},{48,80},{64,96},{80,112},{96,128},{112,144}... | collective-permute-start | bytes 786440 | tf_op jit(solution)/shard_map/ppermute | solution.py:52
  186.2 15.5 %all-to-all-start.3 = ((bf16[16,16,256]{2,1,0:T(8,128)(2,1)}), bf16[16,16,256]{2,1,0:T(8,128)(2,1)S(1)}, u32[]{:S(2)}, u32[]{:S(2)}) async-start(bf16[16,16,256]{2,1,0:T(8,128)(2,1)} %sum_and_spread.5), calls=%async_computation.3 | async-start | bytes 262144 | tf_op jit(solution)/shard_map/all_to_all | solution.py:70
  (20 other events, 200.4 us)

commit v12 on v9

--- a/solution.py
+++ b/solution.py
@@ -257,7 +257,7 @@
 
 
 def backward_kernel(
-    src, slot, cnt, b0, b1, b2, b3, vals, om2, om1, own, op1, op2, acc, ret, in_sem, out_sem
+    src, slot, cnt, b0, b1, b2, b3, vals, om2, om1, own, op1, op2, acc, ret, in_sem
 ):
     per_x = YN * CAP
     me_x, _ = position()
@@ -281,24 +281,20 @@
                 (((0,), (0,)), ((), ())),
                 preferred_element_type=F32,
             )
-    store = pltpu.make_async_copy(acc.at[HALF], own, out_sem)
-    store.start()
-    for k, out in ((0, om2), (1, om1), (3, op1), (4, op2)):
+    for k, out in enumerate((om2, om1, own, op1, op2)):
         for b in range(acc.shape[1]):
             out[pl.ds(b * BLOCK, BLOCK), :] = acc[k, b].astype(BF16)
-    store.wait()
 
 
 def backward_products(src, slot, cnt, back, vals, blocks_dev):
     nodes, channels = blocks_dev * BLOCK, back[0].shape[1]
     steps = cnt.shape[1]
     send = jax.ShapeDtypeStruct((nodes, channels), BF16)
-    own = jax.ShapeDtypeStruct((blocks_dev, BLOCK, channels), F32)
     own_back = back[0].reshape(YN * CAP, BLOCK, channels)
     return kernel_call(
         backward_kernel,
         "tile_backward",
-        (send, send, own, send, send),
+        (send,) * 5,
         [(SMEM, a) for a in (src, slot, cnt)]
         + [(HBM, own_back)]
         + [(VMEM, a) for a in (*back[1:], vals)],
@@ -308,33 +304,22 @@
             pltpu.VMEM((steps, blocks_dev, BLOCK, channels), F32),
             pltpu.VMEM((XN * YN * CAP, BLOCK, channels), BF16),
             pltpu.SemaphoreType.DMA,
-            pltpu.SemaphoreType.DMA,
         ],
-        (VMEM, VMEM, HBM, VMEM, VMEM),
-    )
-
-
-def final_kernel(own, r1, r2, r3, r4, out, held, sem):
-    load = pltpu.make_async_copy(own, held, sem)
-    load.start()
-    load.wait()
-    for b in range(held.shape[0]):
-        spot = pl.ds(b * BLOCK, BLOCK)
-        total = held[b]
-        for r in (r1, r2, r3, r4):
-            total = total + r[spot, :].astype(F32)
-        out[spot, :] = total.astype(BF16)
+    )
+
+
+def final_kernel(*refs):
+    refs[-1][...] = summed(refs[:-1]).astype(BF16)
 
 
 def final_sum(own, parts):
     return kernel_call(
         final_kernel,
         "grad_sum",
-        jax.ShapeDtypeStruct(parts[0].shape, BF16),
-        [(HBM, own)] + [(VMEM, a) for a in parts],
+        jax.ShapeDtypeStruct(own.shape, BF16),
+        [(VMEM, a) for a in (own, *parts)],
         4,
         FINAL_FLOPS,
-        [pltpu.VMEM(own.shape, F32), pltpu.SemaphoreType.DMA],
     )
 
 

time: 197 us -> 197 us (level)
  no operation moved by 1% of the time
where the time goes in v12:
time: 197 us; the launch traced here: 195 us
  starting transfers between devices  125 us (63%)
  waiting for transfers between devices  43.2 us (22%)
  Pallas kernels  12.3 us (6%)
  blocking collectives  8.09 us (4%)
  local copies, waits for them, and re-layouts  4.88 us (2%)
    ppermute x8, starting transfers between devices, dom_shift(): lax.ppermute(value, 'dom', [(i, (i + steps) % count) for i in range(count)])  38.1 us
    ppermute x9, starting transfers between devices, y_shift(): return lax.ppermute(value, 'rows', pairs)  36.3 us
    ppermute x9, starting transfers between devices, x_shift(): return lax.ppermute(value, 'rows', pairs)  27.8 us
    all_to_all x3, starting transfers between devices, exchange(): lax.all_to_all(value, axis, split_axis=0, concat_axis=0, tiled=True, axis...  23 us
    ppermute x9, waiting for transfers between devices, y_shift(): return lax.ppermute(value, 'rows', pairs)  18.4 us
    ppermute x8, waiting for transfers between devices, dom_shift(): lax.ppermute(value, 'dom', [(i, (i + steps) % count) for i in range(count)])  14.1 us
    pallas_call x11, Pallas kernels, kernel_call(): pl.pallas_call(body, out_shape=outs, in_specs=[space for space, _ in ins]...  12.3 us
    all_to_all x1, blocking collectives, exchange(): lax.all_to_all(value, axis, split_axis=0, concat_axis=0, tiled=True, axis...  8.09 us
  transfers between devices with their start and end apart: 29, of which 11 were waited for; matrix products, arithmetic and copies ran while one was open for 0% of the time, Pallas kernels for 4%

profile of v12, /device:TPU:1, one launch (start us, length us, event | category | flops | bytes accessed | tf_op | source)
XLA Modules:
  0.0 195.5 jit_solution(7778999352358610294)
XLA Ops:
  0.6 4.0 %collective-permute-start = (bf16[512,256]{1,0:T(8,128)(2,1)}, bf16[512,256]{1,0:T(8,128)(2,1)S(1)}, u32[]{:S(2)}, u32[]{:S(2)}) collective-permute-start(bf16[512,256]{1,0:T(8,128)(2,1)} %param.8), channel_id=1, source_target_pairs={{0,32},{16,48},{32,64},{48,80},{64,96},{80,112},{96,128},{112,144}... | collective-permute-start | bytes 786440 | tf_op jit(solution)/shard_map/ppermute | solution.py:52
  4.7 4.7 %collective-permute-start.1 = (bf16[512,256]{1,0:T(8,128)(2,1)}, bf16[512,256]{1,0:T(8,128)(2,1)S(1)}, u32[]{:S(2)}, u32[]{:S(2)}) collective-permute-start(bf16[512,256]{1,0:T(8,128)(2,1)} %param.8), channel_id=1, source_target_pairs={{0,16},{16,32},{32,48},{48,64},{64,80},{80,96},{96,112},{112,128},... | collective-permute-start | bytes 786440 | tf_op jit(solution)/shard_map/ppermute | solution.py:52
  9.4 11.1 %collective-permute-start.2 = (bf16[512,256]{1,0:T(8,128)(2,1)}, bf16[512,256]{1,0:T(8,128)(2,1)S(1)}, u32[]{:S(2)}, u32[]{:S(2)}) collective-permute-start(bf16[512,256]{1,0:T(8,128)(2,1)} %param.8), channel_id=1, source_target_pairs={{0,1008},{16,0},{32,16},{48,32},{64,48},{80,64},{96,80},{112,96},{... | collective-permute-start | bytes 786440 | tf_op jit(solution)/shard_map/ppermute | solution.py:52
  20.6 6.3 %collective-permute-start.3 = (bf16[512,256]{1,0:T(8,128)(2,1)}, bf16[512,256]{1,0:T(8,128)(2,1)S(1)}, u32[]{:S(2)}, u32[]{:S(2)}) collective-permute-start(bf16[512,256]{1,0:T(8,128)(2,1)} %param.8), channel_id=1, source_target_pairs={{0,992},{16,1008},{32,0},{48,16},{64,32},{80,48},{96,64},{112,80},... | collective-permute-start | bytes 786440 | tf_op jit(solution)/shard_map/ppermute | solution.py:52
  26.9 8.9 %collective-permute-done.3 = bf16[512,256]{1,0:T(8,128)(2,1)S(1)} collective-permute-done((bf16[512,256]{1,0:T(8,128)(2,1)}, bf16[512,256]{1,0:T(8,128)(2,1)S(1)}, u32[]{:S(2)}, u32[]{:S(2)}) %collective-permute-start.3) | collective-permute-done | bytes 262176 | tf_op jit(solution)/shard_map/ppermute | solution.py:52
  36.5 3.8 %tile_forward.1 = (bf16[1040,128]{1,0:T(8,128)(2,1)}, bf16[1040,128]{1,0:T(8,128)(2,1)}, bf16[1040,128]{1,0:T(8,128)(2,1)}, bf16[1040,128]{1,0:T(8,128)(2,1)}, b...) custom-call(s32[4,5]{1,0:T(4,128)} %bitcast.23, ...), custom_call_target="tpu_custom_call" | custom-call | flops 167772160 | bytes 1966388 | tf_op jit(solution)/shard_map/tile_forward/pallas_call | solution.py:38
  44.6 4.1 %collective-permute-start.6 = (bf16[1040,128]{1,0:T(8,128)(2,1)}, bf16[1040,128]{1,0:T(8,128)(2,1)S(1)}, u32[]{:S(2)}, u32[]{:S(2)}) collective-permute-start(bf16[1040,128]{1,0:T(8,128)(2,1)} %get-tuple-element.35), channel_id=1, source_target_pairs={{0,12},{1,13},{2,14},{3,15},{4,0},{5,1},{6,2},{7,3},{8,4},{9,5},{1... | collective-permute-start | bytes 798728 | tf_op jit(solution)/shard_map/ppermute | solution.py:62
  51.2 3.7 %collective-permute-start.11 = (bf16[1024,128]{1,0:T(8,128)(2,1)}, bf16[1024,128]{1,0:T(8,128)(2,1)S(1)}, u32[]{:S(2)}, u32[]{:S(2)}) collective-permute-start(bf16[1024,128]{1,0:T(8,128)(2,1)} %get-tuple-element.42), channel_id=1, source_target_pairs={{0,8},{1,9},{2,10},{3,11},{4,12},{5,13},{6,14},{7,15},{8,0},{9,1},... | collective-permute-start | bytes 786440 | tf_op jit(solution)/shard_map/ppermute | solution.py:62
  68.0 3.9 %collective-permute-start.9 = (bf16[512,128]{1,0:T(8,128)(2,1)S(1)}, bf16[512,128]{1,0:T(8,128)(2,1)S(1)}, u32[]{:S(2)}, u32[]{:S(2)}) collective-permute-start(bf16[512,128]{1,0:T(8,128)(2,1)S(1)} %get-tuple-element.39), channel_id=1, source_target_pairs={{0,3},{1,0},{2,1},{3,2},{4,7},{5,4},{6,5},{7,6},{8,11},{9,8},{10,9... | collective-permute-start | bytes 393224 | tf_op jit(solution)/shard_map/ppermute | solution.py:57
  75.6 5.2 %collective-permute-start.14 = (bf16[512,128]{1,0:T(8,128)(2,1)S(1)}, bf16[512,128]{1,0:T(8,128)(2,1)S(1)}, u32[]{:S(2)}, u32[]{:S(2)}) collective-permute-start(bf16[512,128]{1,0:T(8,128)(2,1)S(1)} %get-tuple-element.47), channel_id=1, source_target_pairs={{0,2},{1,3},{2,0},{3,1},{4,6},{5,7},{6,4},{7,5},{8,10},{9,11},{10,... | collective-permute-start | bytes 393224 | tf_op jit(solution)/shard_map/ppermute | solution.py:57
  80.8 5.5 %collective-permute-start.15 = (bf16[512,128]{1,0:T(8,128)(2,1)S(1)}, bf16[512,128]{1,0:T(8,128)(2,1)S(1)}, u32[]{:S(2)}, u32[]{:S(2)}) collective-permute-start(bf16[512,128]{1,0:T(8,128)(2,1)S(1)} %get-tuple-element.48), channel_id=1, source_target_pairs={{0,3},{1,0},{2,1},{3,2},{4,7},{5,4},{6,5},{7,6},{8,11},{9,8},{10,9... | collective-permute-start | bytes 393224 | tf_op jit(solution)/shard_map/ppermute | solution.py:57
  87.3 6.6 %collective-permute-done.15.refs_4_ = bf16[512,128]{1,0:T(8,128)(2,1)S(1)} collective-permute-done((bf16[512,128]{1,0:T(8,128)(2,1)S(1)}, bf16[512,128]{1,0:T(8,128)(2,1)S(1)}, u32[]{:S(2)}, u32[]{:S(2)}) %collective-permute-start.15) | collective-permute-done | bytes 131104 | tf_op jit(solution)/shard_map/ppermute | solution.py:57
  95.1 3.8 %collective-permute-start.16 = (bf16[512,256]{1,0:T(8,128)(2,1)S(1)}, bf16[512,256]{1,0:T(8,128)(2,1)S(1)}, u32[]{:S(2)}, u32[]{:S(2)}) collective-permute-start(bf16[512,256]{1,0:T(8,128)(2,1)S(1)} %get-tuple-element.50), channel_id=1, source_target_pairs={{0,1},{1,2},{2,3},{3,0},{4,5},{5,6},{6,7},{7,4},{8,9},{9,10},{10,1... | collective-permute-start | bytes 786440 | tf_op jit(solution)/shard_map/ppermute | solution.py:57
  98.9 4.2 %collective-permute-start.17 = (bf16[512,256]{1,0:T(8,128)(2,1)S(1)}, bf16[512,256]{1,0:T(8,128)(2,1)S(1)}, u32[]{:S(2)}, u32[]{:S(2)}) collective-permute-start(bf16[512,256]{1,0:T(8,128)(2,1)S(1)} %get-tuple-element.50), channel_id=1, source_target_pairs={{0,2},{1,3},{2,0},{3,1},{4,6},{5,7},{6,4},{7,5},{8,10},{9,11},{10,... | collective-permute-start | bytes 786440 | tf_op jit(solution)/shard_map/ppermute | solution.py:57
  103.0 5.5 %collective-permute-start.18 = (bf16[512,256]{1,0:T(8,128)(2,1)S(1)}, bf16[512,256]{1,0:T(8,128)(2,1)S(1)}, u32[]{:S(2)}, u32[]{:S(2)}) collective-permute-start(bf16[512,256]{1,0:T(8,128)(2,1)S(1)} %get-tuple-element.50), channel_id=1, source_target_pairs={{0,3},{1,0},{2,1},{3,2},{4,7},{5,4},{6,5},{7,6},{8,11},{9,8},{10,9... | collective-permute-start | bytes 786440 | tf_op jit(solution)/shard_map/ppermute | solution.py:57
  108.5 6.1 %all-to-all-start = ((bf16[16,16,256]{2,1,0:T(8,128)(2,1)}), bf16[16,16,256]{2,1,0:T(8,128)(2,1)S(1)}, u32[]{:S(2)}, u32[]{:S(2)}) async-start(bf16[16,16,256]{2,1,0:T(8,128)(2,1)} %bitcast.17), calls=%async_computation | async-start | bytes 262144 | tf_op jit(solution)/shard_map/all_to_all | solution.py:70
  114.6 4.6 %collective-permute-done.17 = bf16[512,256]{1,0:T(8,128)(2,1)S(1)} collective-permute-done((bf16[512,256]{1,0:T(8,128)(2,1)S(1)}, bf16[512,256]{1,0:T(8,128)(2,1)S(1)}, u32[]{:S(2)}, u32[]{:S(2)}) %collective-permute-start.17) | collective-permute-done | bytes 262176 | tf_op jit(solution)/shard_map/ppermute | solution.py:57
  119.2 6.4 %collective-permute-done.18 = bf16[512,256]{1,0:T(8,128)(2,1)S(1)} collective-permute-done((bf16[512,256]{1,0:T(8,128)(2,1)S(1)}, bf16[512,256]{1,0:T(8,128)(2,1)S(1)}, u32[]{:S(2)}, u32[]{:S(2)}) %collective-permute-start.18) | collective-permute-done | bytes 262176 | tf_op jit(solution)/shard_map/ppermute | solution.py:57
  128.1 6.7 %collective-permute-start.19 = (bf16[1024,256]{1,0:T(8,128)(2,1)}, bf16[1024,256]{1,0:T(8,128)(2,1)S(1)}, u32[]{:S(2)}, u32[]{:S(2)}) collective-permute-start(bf16[1024,256]{1,0:T(8,128)(2,1)} %get-tuple-element.52), channel_id=1, source_target_pairs={{0,12},{1,13},{2,14},{3,15},{4,0},{5,1},{6,2},{7,3},{8,4},{9,5},{1... | collective-permute-start | bytes 1572872 | tf_op jit(solution)/shard_map/ppermute | solution.py:62
  139.4 8.1 %all_to_all.20.parts = f32[8,16,256]{2,1,0:T(8,128)S(1)} all-to-all(f32[8,16,256]{2,1,0:T(8,128)S(1)} %sum_and_spread.3), channel_id=1, replica_groups={{0,16,32,48,64,80,96,112},{128,144,160,176,192,208,224,240},{256,272,28..., dimensions={0} | all-to-all | bytes 262144 | tf_op jit(solution)/shard_map/all_to_all | solution.py:70
  148.1 11.9 %all-to-all-start.2 = ((f32[8,16,256]{2,1,0:T(8,128)}), f32[8,16,256]{2,1,0:T(8,128)S(1)}, u32[]{:S(2)}, u32[]{:S(2)}) async-start(f32[8,16,256]{2,1,0:T(8,128)} %sum_and_spread.4), calls=%async_computation.2 | async-start | bytes 262144 | tf_op jit(solution)/shard_map/all_to_all | solution.py:70
  175.4 4.0 %collective-permute-start.25 = (bf16[512,256]{1,0:T(8,128)(2,1)S(1)}, bf16[512,256]{1,0:T(8,128)(2,1)S(1)}, u32[]{:S(2)}, u32[]{:S(2)}) collective-permute-start(bf16[512,256]{1,0:T(8,128)(2,1)S(1)} %get-tuple-element.59), channel_id=1, source_target_pairs={{0,32},{16,48},{32,64},{48,80},{64,96},{80,112},{96,128},{112,144}... | collective-permute-start | bytes 786440 | tf_op jit(solution)/shard_map/ppermute | solution.py:52
  180.1 5.1 %all-to-all-start.3 = ((bf16[16,16,256]{2,1,0:T(8,128)(2,1)}), bf16[16,16,256]{2,1,0:T(8,128)(2,1)S(1)}, u32[]{:S(2)}, u32[]{:S(2)}) async-start(bf16[16,16,256]{2,1,0:T(8,128)(2,1)} %sum_and_spread.5), calls=%async_computation.3 | async-start | bytes 262144 | tf_op jit(solution)/shard_map/all_to_all | solution.py:70
  185.2 5.2 %collective-permute-done.23.refs_2_ = bf16[512,256]{1,0:T(8,128)(2,1)S(1)} collective-permute-done((bf16[512,256]{1,0:T(8,128)(2,1)S(1)}, bf16[512,256]{1,0:T(8,128)(2,1)S(1)}, u32[]{:S(2)}, u32[]{:S(2)}) %collective-permute-start.23) | collective-permute-done | bytes 262176 | tf_op jit(solution)/shard_map/ppermute | solution.py:52
  (79 shorter events, 55.2 us)
Async XLA Ops:
  0.6 26.2 %collective-permute-start = (bf16[512,256]{1,0:T(8,128)(2,1)}, bf16[512,256]{1,0:T(8,128)(2,1)S(1)}, u32[]{:S(2)}, u32[]{:S(2)}) collective-permute-start(bf16[512,256]{1,0:T(8,128)(2,1)} %param.8), channel_id=1, source_target_pairs={{0,32},{16,48},{32,64},{48,80},{64,96},{80,112},{96,128},{112,144}... | collective-permute-start | bytes 786440 | tf_op jit(solution)/shard_map/ppermute | solution.py:52
  4.7 22.2 %collective-permute-start.1 = (bf16[512,256]{1,0:T(8,128)(2,1)}, bf16[512,256]{1,0:T(8,128)(2,1)S(1)}, u32[]{:S(2)}, u32[]{:S(2)}) collective-permute-start(bf16[512,256]{1,0:T(8,128)(2,1)} %param.8), channel_id=1, source_target_pairs={{0,16},{16,32},{32,48},{48,64},{64,80},{80,96},{96,112},{112,128},... | collective-permute-start | bytes 786440 | tf_op jit(solution)/shard_map/ppermute | solution.py:52
  9.4 17.5 %collective-permute-start.2 = (bf16[512,256]{1,0:T(8,128)(2,1)}, bf16[512,256]{1,0:T(8,128)(2,1)S(1)}, u32[]{:S(2)}, u32[]{:S(2)}) collective-permute-start(bf16[512,256]{1,0:T(8,128)(2,1)} %param.8), channel_id=1, source_target_pairs={{0,1008},{16,0},{32,16},{48,32},{64,48},{80,64},{96,80},{112,96},{... | collective-permute-start | bytes 786440 | tf_op jit(solution)/shard_map/ppermute | solution.py:52
  20.6 15.3 %collective-permute-start.3 = (bf16[512,256]{1,0:T(8,128)(2,1)}, bf16[512,256]{1,0:T(8,128)(2,1)S(1)}, u32[]{:S(2)}, u32[]{:S(2)}) collective-permute-start(bf16[512,256]{1,0:T(8,128)(2,1)} %param.8), channel_id=1, source_target_pairs={{0,992},{16,1008},{32,0},{48,16},{64,32},{80,48},{96,64},{112,80},... | collective-permute-start | bytes 786440 | tf_op jit(solution)/shard_map/ppermute | solution.py:52
  40.3 16.5 %collective-permute-start.4 = (bf16[1040,128]{1,0:T(8,128)(2,1)}, bf16[1040,128]{1,0:T(8,128)(2,1)S(1)}, u32[]{:S(2)}, u32[]{:S(2)}) collective-permute-start(bf16[1040,128]{1,0:T(8,128)(2,1)} %get-tuple-element.33), channel_id=1, source_target_pairs={{0,4},{1,5},{2,6},{3,7},{4,8},{5,9},{6,10},{7,11},{8,12},{9,13},{1... | collective-permute-start | bytes 798728 | tf_op jit(solution)/shard_map/ppermute | solution.py:62
  42.2 16.7 %collective-permute-start.5 = (bf16[1040,128]{1,0:T(8,128)(2,1)}, bf16[1040,128]{1,0:T(8,128)(2,1)S(1)}, u32[]{:S(2)}, u32[]{:S(2)}) collective-permute-start(bf16[1040,128]{1,0:T(8,128)(2,1)} %get-tuple-element.34), channel_id=1, source_target_pairs={{0,8},{1,9},{2,10},{3,11},{4,12},{5,13},{6,14},{7,15},{8,0},{9,1},... | collective-permute-start | bytes 798728 | tf_op jit(solution)/shard_map/ppermute | solution.py:62
  44.6 15.2 %collective-permute-start.6 = (bf16[1040,128]{1,0:T(8,128)(2,1)}, bf16[1040,128]{1,0:T(8,128)(2,1)S(1)}, u32[]{:S(2)}, u32[]{:S(2)}) collective-permute-start(bf16[1040,128]{1,0:T(8,128)(2,1)} %get-tuple-element.35), channel_id=1, source_target_pairs={{0,12},{1,13},{2,14},{3,15},{4,0},{5,1},{6,2},{7,3},{8,4},{9,5},{1... | collective-permute-start | bytes 798728 | tf_op jit(solution)/shard_map/ppermute | solution.py:62
  48.7 19.3 %collective-permute-start.10 = (bf16[1024,128]{1,0:T(8,128)(2,1)}, bf16[1024,128]{1,0:T(8,128)(2,1)S(1)}, u32[]{:S(2)}, u32[]{:S(2)}) collective-permute-start(bf16[1024,128]{1,0:T(8,128)(2,1)} %get-tuple-element.41), channel_id=1, source_target_pairs={{0,4},{1,5},{2,6},{3,7},{4,8},{5,9},{6,10},{7,11},{8,12},{9,13},{1... | collective-permute-start | bytes 786440 | tf_op jit(solution)/shard_map/ppermute | solution.py:62
  51.2 20.7 %collective-permute-start.11 = (bf16[1024,128]{1,0:T(8,128)(2,1)}, bf16[1024,128]{1,0:T(8,128)(2,1)S(1)}, u32[]{:S(2)}, u32[]{:S(2)}) collective-permute-start(bf16[1024,128]{1,0:T(8,128)(2,1)} %get-tuple-element.42), channel_id=1, source_target_pairs={{0,8},{1,9},{2,10},{3,11},{4,12},{5,13},{6,14},{7,15},{8,0},{9,1},... | collective-permute-start | bytes 786440 | tf_op jit(solution)/shard_map/ppermute | solution.py:62
  56.8 15.1 %collective-permute-start.12 = (bf16[1024,128]{1,0:T(8,128)(2,1)}, bf16[1024,128]{1,0:T(8,128)(2,1)S(1)}, u32[]{:S(2)}, u32[]{:S(2)}) collective-permute-start(bf16[1024,128]{1,0:T(8,128)(2,1)} %get-tuple-element.43), channel_id=1, source_target_pairs={{0,12},{1,13},{2,14},{3,15},{4,0},{5,1},{6,2},{7,3},{8,4},{9,5},{1... | collective-permute-start | bytes 786440 | tf_op jit(solution)/shard_map/ppermute | solution.py:62
  61.5 19.3 %collective-permute-start.7 = (bf16[512,128]{1,0:T(8,128)(2,1)S(1)}, bf16[512,128]{1,0:T(8,128)(2,1)S(1)}, u32[]{:S(2)}, u32[]{:S(2)}) collective-permute-start(bf16[512,128]{1,0:T(8,128)(2,1)S(1)} %get-tuple-element.37), channel_id=1, source_target_pairs={{0,1},{1,2},{2,3},{3,0},{4,5},{5,6},{6,7},{7,4},{8,9},{9,10},{10,1... | collective-permute-start | bytes 393224 | tf_op jit(solution)/shard_map/ppermute | solution.py:57
  63.4 22.9 %collective-permute-start.8 = (bf16[512,128]{1,0:T(8,128)(2,1)S(1)}, bf16[512,128]{1,0:T(8,128)(2,1)S(1)}, u32[]{:S(2)}, u32[]{:S(2)}) collective-permute-start(bf16[512,128]{1,0:T(8,128)(2,1)S(1)} %get-tuple-element.38), channel_id=1, source_target_pairs={{0,2},{1,3},{2,0},{3,1},{4,6},{5,7},{6,4},{7,5},{8,10},{9,11},{10,... | collective-permute-start | bytes 393224 | tf_op jit(solution)/shard_map/ppermute | solution.py:57
  68.0 18.3 %collective-permute-start.9 = (bf16[512,128]{1,0:T(8,128)(2,1)S(1)}, bf16[512,128]{1,0:T(8,128)(2,1)S(1)}, u32[]{:S(2)}, u32[]{:S(2)}) collective-permute-start(bf16[512,128]{1,0:T(8,128)(2,1)S(1)} %get-tuple-element.39), channel_id=1, source_target_pairs={{0,3},{1,0},{2,1},{3,2},{4,7},{5,4},{6,5},{7,6},{8,11},{9,8},{10,9... | collective-permute-start | bytes 393224 | tf_op jit(solution)/shard_map/ppermute | solution.py:57
  95.1 19.5 %collective-permute-start.16 = (bf16[512,256]{1,0:T(8,128)(2,1)S(1)}, bf16[512,256]{1,0:T(8,128)(2,1)S(1)}, u32[]{:S(2)}, u32[]{:S(2)}) collective-permute-start(bf16[512,256]{1,0:T(8,128)(2,1)S(1)} %get-tuple-element.50), channel_id=1, source_target_pairs={{0,1},{1,2},{2,3},{3,0},{4,5},{5,6},{6,7},{7,4},{8,9},{9,10},{10,1... | collective-permute-start | bytes 786440 | tf_op jit(solution)/shard_map/ppermute | solution.py:57
  98.9 20.3 %collective-permute-start.17 = (bf16[512,256]{1,0:T(8,128)(2,1)S(1)}, bf16[512,256]{1,0:T(8,128)(2,1)S(1)}, u32[]{:S(2)}, u32[]{:S(2)}) collective-permute-start(bf16[512,256]{1,0:T(8,128)(2,1)S(1)} %get-tuple-element.50), channel_id=1, source_target_pairs={{0,2},{1,3},{2,0},{3,1},{4,6},{5,7},{6,4},{7,5},{8,10},{9,11},{10,... | collective-permute-start | bytes 786440 | tf_op jit(solution)/shard_map/ppermute | solution.py:57
  103.0 22.5 %collective-permute-start.18 = (bf16[512,256]{1,0:T(8,128)(2,1)S(1)}, bf16[512,256]{1,0:T(8,128)(2,1)S(1)}, u32[]{:S(2)}, u32[]{:S(2)}) collective-permute-start(bf16[512,256]{1,0:T(8,128)(2,1)S(1)} %get-tuple-element.50), channel_id=1, source_target_pairs={{0,3},{1,0},{2,1},{3,2},{4,7},{5,4},{6,5},{7,6},{8,11},{9,8},{10,9... | collective-permute-start | bytes 786440 | tf_op jit(solution)/shard_map/ppermute | solution.py:57
  108.5 30.8 %all-to-all-start = ((bf16[16,16,256]{2,1,0:T(8,128)(2,1)}), bf16[16,16,256]{2,1,0:T(8,128)(2,1)S(1)}, u32[]{:S(2)}, u32[]{:S(2)}) async-start(bf16[16,16,256]{2,1,0:T(8,128)(2,1)} %bitcast.17), calls=%async_computation | async-start | bytes 262144 | tf_op jit(solution)/shard_map/all_to_all | solution.py:70
  128.1 31.8 %collective-permute-start.19 = (bf16[1024,256]{1,0:T(8,128)(2,1)}, bf16[1024,256]{1,0:T(8,128)(2,1)S(1)}, u32[]{:S(2)}, u32[]{:S(2)}) collective-permute-start(bf16[1024,256]{1,0:T(8,128)(2,1)} %get-tuple-element.52), channel_id=1, source_target_pairs={{0,12},{1,13},{2,14},{3,15},{4,0},{5,1},{6,2},{7,3},{8,4},{9,5},{1... | collective-permute-start | bytes 1572872 | tf_op jit(solution)/shard_map/ppermute | solution.py:62
  134.9 25.1 %collective-permute-start.20 = (bf16[1024,256]{1,0:T(8,128)(2,1)S(1)}, bf16[1024,256]{1,0:T(8,128)(2,1)S(1)}, u32[]{:S(2)}, u32[]{:S(2)}) collective-permute-start(bf16[1024,256]{1,0:T(8,128)(2,1)S(1)} %get-tuple-element.53), channel_id=1, source_target_pairs={{0,8},{1,9},{2,10},{3,11},{4,12},{5,13},{6,14},{7,15},{8,0},{9,1},... | collective-permute-start | bytes 1572872 | tf_op jit(solution)/shard_map/ppermute | solution.py:62
  136.8 26.6 %collective-permute-start.21 = (bf16[1024,256]{1,0:T(8,128)(2,1)S(1)}, bf16[1024,256]{1,0:T(8,128)(2,1)S(1)}, u32[]{:S(2)}, u32[]{:S(2)}) collective-permute-start(bf16[1024,256]{1,0:T(8,128)(2,1)S(1)} %get-tuple-element.54), channel_id=1, source_target_pairs={{0,4},{1,5},{2,6},{3,7},{4,8},{5,9},{6,10},{7,11},{8,12},{9,13},{1... | collective-permute-start | bytes 1572872 | tf_op jit(solution)/shard_map/ppermute | solution.py:62
  148.1 31.3 %all-to-all-start.2 = ((f32[8,16,256]{2,1,0:T(8,128)}), f32[8,16,256]{2,1,0:T(8,128)S(1)}, u32[]{:S(2)}, u32[]{:S(2)}) async-start(f32[8,16,256]{2,1,0:T(8,128)} %sum_and_spread.4), calls=%async_computation.2 | async-start | bytes 262144 | tf_op jit(solution)/shard_map/all_to_all | solution.py:70
  167.5 17.7 %collective-permute-start.22 = (bf16[512,256]{1,0:T(8,128)(2,1)S(1)}, bf16[512,256]{1,0:T(8,128)(2,1)S(1)}, u32[]{:S(2)}, u32[]{:S(2)}) collective-permute-start(bf16[512,256]{1,0:T(8,128)(2,1)S(1)} %get-tuple-element.56), channel_id=1, source_target_pairs={{0,992},{16,1008},{32,0},{48,16},{64,32},{80,48},{96,64},{112,80},... | collective-permute-start | bytes 786440 | tf_op jit(solution)/shard_map/ppermute | solution.py:52
  169.4 21.0 %collective-permute-start.23 = (bf16[512,256]{1,0:T(8,128)(2,1)S(1)}, bf16[512,256]{1,0:T(8,128)(2,1)S(1)}, u32[]{:S(2)}, u32[]{:S(2)}) collective-permute-start(bf16[512,256]{1,0:T(8,128)(2,1)S(1)} %get-tuple-element.57), channel_id=1, source_target_pairs={{0,1008},{16,0},{32,16},{48,32},{64,48},{80,64},{96,80},{112,96},{... | collective-permute-start | bytes 786440 | tf_op jit(solution)/shard_map/ppermute | solution.py:52
  172.4 18.0 %collective-permute-start.24 = (bf16[512,256]{1,0:T(8,128)(2,1)S(1)}, bf16[512,256]{1,0:T(8,128)(2,1)S(1)}, u32[]{:S(2)}, u32[]{:S(2)}) collective-permute-start(bf16[512,256]{1,0:T(8,128)(2,1)S(1)} %get-tuple-element.58), channel_id=1, source_target_pairs={{0,16},{16,32},{32,48},{48,64},{64,80},{80,96},{96,112},{112,128},... | collective-permute-start | bytes 786440 | tf_op jit(solution)/shard_map/ppermute | solution.py:52
  (21 other events, 194.9 us)
